TPU v7x, 128 devices: a whole 4x4x4 slice. The times are simulated.
128 devices in a mesh: seq: 32 (over z, y, x_lo), narrow: 2 (over core), wide: 2 (over x_hi).
Axes of the slice: x: 4 (x_hi: 2, x_lo: 2; x = x_hi * 2 + x_lo), y: 4, z: 4, core: 2. Of those that a mesh axis runs over, the one named last changes fastest.
Arguments:
- block_input: bfloat16 [8192, 2048], P(('seq', 'wide'), 'narrow'), may hold values from -6 to 6
- out_grad: bfloat16 [8192, 2048], P(('seq', 'wide'), 'narrow'), may hold values from -6 to 6
- qkv_weight: float32 [2048, 8, 384], P(('narrow', 'seq'), 'wide'), may hold values from -0.0625 to 0.0625
- qkv_moment: float32 [2048, 8, 384], P(('narrow', 'seq'), 'wide'), may hold values from -0.00021362305 to 0.00021362305
- qkv_second: float32 [2048, 8, 384], P(('narrow', 'seq'), 'wide'), may hold values from 4.2748038e-10 to 6.905452e-09
- gate_up_weight: float32 [2048, 2, 8192], P(('narrow', 'seq'), None, 'wide'), may hold values from -0.0625 to 0.0625
- gate_up_moment: float32 [2048, 2, 8192], P(('narrow', 'seq'), None, 'wide'), may hold values from -0.00021362305 to 0.00021362305
- gate_up_second: float32 [2048, 2, 8192], P(('narrow', 'seq'), None, 'wide'), may hold values from 4.2748038e-10 to 6.905452e-09
- out_weight: float32 [2048, 2048], P(('wide', 'seq'), 'narrow')
- out_moment: float32 [2048, 2048], P(('wide', 'seq'), 'narrow'), may hold values from -3.8146973e-06 to 3.8146973e-06
- out_second: float32 [2048, 2048], P(('wide', 'seq'), 'narrow'), may hold values from 3.2883107e-14 to 3.2883107e-13
- down_weight: float32 [8192, 2048], P(('wide', 'seq'), 'narrow')
- down_moment: float32 [8192, 2048], P(('wide', 'seq'), 'narrow'), may hold values from -4.5776367e-05 to 4.5776367e-05
- down_second: float32 [8192, 2048], P(('wide', 'seq'), 'narrow'), may hold values from 4.274804e-12 to 4.2748038e-11
- norm_gains: float32 [2, 2048], P(None, 'narrow')
- gains_moment: float32 [2, 2048], P(None, 'narrow'), may hold values from -0.00012207031 to 0.00012207031
- gains_second: float32 [2, 2048], P(None, 'narrow'), may hold values from 2.9594795e-11 to 2.9594796e-10
- doc_lengths: int32 [4], replicated, may hold values from 1 to 8064, as said below
Outputs:
- layer_output: bfloat16 [8192, 2048], P(('seq', 'wide'), 'narrow')
- input_grad: float32 [8192, 2048], P(('seq', 'wide'), 'narrow')
- grad_norm: float32 [], replicated
- qkv_next: float32 [2048, 8, 384], P(('narrow', 'seq'), 'wide')
- qkv_moment_next: float32 [2048, 8, 384], P(('narrow', 'seq'), 'wide')
- qkv_second_next: float32 [2048, 8, 384], P(('narrow', 'seq'), 'wide')
- gate_up_next: float32 [2048, 2, 8192], P(('narrow', 'seq'), None, 'wide')
- gate_up_moment_next: float32 [2048, 2, 8192], P(('narrow', 'seq'), None, 'wide')
- gate_up_second_next: float32 [2048, 2, 8192], P(('narrow', 'seq'), None, 'wide')
- out_next: float32 [2048, 2048], P(('wide', 'seq'), 'narrow')
- out_moment_next: float32 [2048, 2048], P(('wide', 'seq'), 'narrow')
- out_second_next: float32 [2048, 2048], P(('wide', 'seq'), 'narrow')
- down_next: float32 [8192, 2048], P(('wide', 'seq'), 'narrow')
- down_moment_next: float32 [8192, 2048], P(('wide', 'seq'), 'narrow')
- down_second_next: float32 [8192, 2048], P(('wide', 'seq'), 'narrow')
- gains_next: float32 [2, 2048], P(None, 'narrow')
- gains_moment_next: float32 [2, 2048], P(None, 'narrow')
- gains_second_next: float32 [2, 2048], P(None, 'narrow')
Inputs may be any that keep to these rules, and one draw needn't show every extreme that they name: `doc_lengths`: four documents packed in order over the 8192 tokens: the second holds exactly 8064 tokens and runs from the first block of 128 tokens into the last; the first lies in the first block, the third and fourth at the end of the pack, the first, third and fourth together exactly 128; the third and the fourth are shorter than 64 each, and one of them is a single token.
All inputs are finite; a program needn't handle non-finite values.
Results may differ from a plain program's by a relative error of at most 0.04.
Values may be sent and summed in bfloat16 or wider, within the bound.
A program may use at most 192 MiB of HBM per device.

v0:
```python
import math

import jax
import jax.numpy as jnp
from jax import lax
from jax.sharding import PartitionSpec as P

D = 2048
HQ = 32
HD = 64
FF = 8192
ADAM_STEP = 10


NORM_EPS = 1e-05
ADAM_EPS = 1e-08
BETA_ONE = 0.9
BETA_TWO = 0.95
WEIGHT_DECAY = 0.1
MATRIX_RATE = 0.01
OUTPUT_RATE = 0.9
DOWN_RATE = 3.0
GAIN_RATE = 2.5
CLIP_NORM = 1.0
ROPE_THETA = 500000.0
ROPE_FACTOR = 32.0
LOW_FREQ = 1.0
HIGH_FREQ = 4.0
OLD_CONTEXT = 8192.0


def doc_tables(doc_lengths, count):
    ends = jnp.cumsum(doc_lengths)
    places = jnp.arange(count, dtype=jnp.int32)
    passed = (places[:, None] >= ends[None, :]).astype(jnp.int32)
    segment = jnp.sum(passed, axis=1)
    starts = jnp.sum(passed * doc_lengths[None, :], axis=1)
    return (places, segment, places - starts)


def rope_tables(position, head_size):
    half_size = head_size // 2
    column = jnp.arange(half_size, dtype=jnp.float32)
    inverse = jnp.exp(-(2.0 * column / head_size) * math.log(ROPE_THETA))
    wavelength = 2.0 * math.pi / inverse
    smooth = (OLD_CONTEXT / wavelength - LOW_FREQ) / (HIGH_FREQ - LOW_FREQ)
    blended = (1.0 - smooth) * inverse / ROPE_FACTOR + smooth * inverse
    inverse = jnp.where(
        wavelength < OLD_CONTEXT / HIGH_FREQ,
        inverse,
        jnp.where(wavelength > OLD_CONTEXT / LOW_FREQ, inverse / ROPE_FACTOR, blended),
    )
    angles = position.astype(jnp.float32)[:, None] * inverse[None, :]
    return (jnp.cos(angles), jnp.sin(angles))


def rotate(values, cosine, sine):
    half_size = values.shape[-1] // 2
    table_shape = (cosine.shape[0],) + (1,) * (values.ndim - 2) + (half_size,)
    cos_part = cosine.reshape(table_shape)
    sin_part = sine.reshape(table_shape)
    first_half = values[..., :half_size]
    second_half = values[..., half_size:]
    return jnp.concatenate(
        [
            first_half * cos_part - second_half * sin_part,
            second_half * cos_part + first_half * sin_part,
        ],
        axis=-1,
    )


def across_width(values):
    return lax.psum(values, "narrow")


def widen(values):
    return lax.all_gather(values, "wide", axis=0, tiled=True)


def collect_rows(values):
    return lax.all_gather(values, "narrow", axis=0, tiled=True)


def into_narrow(left, apply):
    share = left.shape[0] // lax.axis_size("narrow")

    def term(start, count):
        return apply(left)

    return lax.psum_scatter(
        term(jnp.int32(0), share * lax.axis_size("narrow")),
        "narrow",
        scatter_dimension=0,
        tiled=True,
    )


def into_wide(left, apply):
    share = left.shape[0] // lax.axis_size("wide")

    def term(start, count):
        return apply(left)

    return lax.psum_scatter(
        term(jnp.int32(0), share * lax.axis_size("wide")).astype(jnp.bfloat16),
        "wide",
        scatter_dimension=0,
        tiled=True,
    ).astype(jnp.float32)


def times_weight(weight):

    def apply(pieces):
        return jnp.dot(pieces, weight, preferred_element_type=jnp.float32)

    return apply


def times_transpose(weight):

    def apply(pieces):
        return lax.dot_general(
            pieces, weight, (((1,), (1,)), ((), ())), preferred_element_type=jnp.float32
        )

    return apply


def outer_rows(left, right):
    return lax.dot_general(
        left, right, (((0,), (0,)), ((), ())), preferred_element_type=jnp.float32
    )


def norm_forward(values, gain_row):
    totals = across_width(jnp.sum(values * values, axis=1))
    scale = lax.rsqrt(totals / D + NORM_EPS)
    return (values * scale[:, None] * gain_row[None, :], scale)


def norm_backward(values, scale, gain_row, incoming):
    weighted = incoming * gain_row[None, :]
    inner = across_width(jnp.sum(weighted * values, axis=1)) / D
    back = scale[:, None] * weighted - values * (scale * scale * scale * inner)[:, None]
    return (back, jnp.sum(incoming * values * scale[:, None], axis=0))


def masked_scores(queries, keys_block, query_place, query_seg, key_place, key_seg):
    scores = jnp.einsum(
        "bkgd,tkd->bkgt", queries, keys_block, preferred_element_type=jnp.float32
    ) * queries.shape[-1] ** (-0.5)
    allowed = (key_place[None, :] <= query_place[:, None]) & (
        key_seg[None, :] == query_seg[:, None]
    )
    return (scores, allowed[:, None, None, :])


def adam(weight, moment, second, gradient, rate, decay):
    moment_next = BETA_ONE * moment + (1.0 - BETA_ONE) * gradient
    second_next = BETA_TWO * second + (1.0 - BETA_TWO) * gradient * gradient
    unbiased = moment_next / (1.0 - BETA_ONE**ADAM_STEP)
    divisor = jnp.sqrt(second_next / (1.0 - BETA_TWO**ADAM_STEP)) + ADAM_EPS
    return (weight - rate * (unbiased / divisor + decay * weight), moment_next, second_next)


def shards(
    block_input,
    out_grad,
    qkv_weight,
    qkv_moment,
    qkv_second,
    gate_up_weight,
    gate_up_moment,
    gate_up_second,
    out_weight,
    out_moment,
    out_second,
    down_weight,
    down_moment,
    down_second,
    norm_gains,
    gains_moment,
    gains_second,
    doc_lengths,
):
    qkv_whole, gate_up_whole, out_low, down_low = (
        lax.all_gather(qkv_weight.astype(jnp.bfloat16), "seq", axis=0, tiled=True),
        lax.all_gather(gate_up_weight.astype(jnp.bfloat16), "seq", axis=0, tiled=True),
        lax.all_gather(out_weight.astype(jnp.bfloat16), "seq", axis=0, tiled=True),
        lax.all_gather(down_weight.astype(jnp.bfloat16), "seq", axis=0, tiled=True),
    )
    width_local = block_input.shape[1]
    groups = qkv_whole.shape[1]
    group_cols = qkv_whole.shape[2]
    group_size = (group_cols - 2 * HD) // HD
    hidden_cols = down_low.shape[0]
    inputs = block_input.astype(jnp.float32)
    qkv_low = qkv_whole.reshape(width_local, groups * group_cols)
    gate_up_low = gate_up_whole.reshape(width_local, 2 * hidden_cols)
    normed, scale_one = norm_forward(inputs, norm_gains[0])
    normed_wide = widen(normed.astype(jnp.bfloat16))
    projected = into_narrow(normed_wide, times_weight(qkv_low))
    block_rows = projected.shape[0]
    projected = projected.reshape(block_rows, groups, group_cols)
    mine = lax.axis_index("seq") * lax.axis_size("narrow") + lax.axis_index("narrow")
    total_rows = block_rows * lax.axis_size("seq") * lax.axis_size("narrow")
    places, segment, position = doc_tables(doc_lengths, total_rows)
    query_place = lax.dynamic_slice_in_dim(places, mine * block_rows, block_rows, 0)
    query_seg = lax.dynamic_slice_in_dim(segment, mine * block_rows, block_rows, 0)
    query_pos = lax.dynamic_slice_in_dim(position, mine * block_rows, block_rows, 0)
    cosine, sine = rope_tables(query_pos, HD)
    query_cols = group_size * HD
    queries = rotate(
        projected[:, :, :query_cols].reshape(block_rows, groups, group_size, HD), cosine, sine
    ).astype(jnp.bfloat16)
    keys_mine = rotate(projected[:, :, query_cols : query_cols + HD], cosine, sine).astype(
        jnp.bfloat16
    )
    values_mine = projected[:, :, query_cols + HD :].astype(jnp.bfloat16)
    keys_all, values_all = (
        lax.all_gather(keys_mine, ("seq", "narrow"), axis=0, tiled=True),
        lax.all_gather(values_mine, ("seq", "narrow"), axis=0, tiled=True),
    )

    def key_slices(block_at):
        start = block_at * block_rows
        return (
            lax.dynamic_slice_in_dim(keys_all, start, block_rows, 0),
            lax.dynamic_slice_in_dim(values_all, start, block_rows, 0),
            lax.dynamic_slice_in_dim(places, start, block_rows, 0),
            lax.dynamic_slice_in_dim(segment, start, block_rows, 0),
        )

    def stats_step(block_at, carry):
        highest, totals = carry
        keys_block, values_block, key_place, key_seg = key_slices(block_at)
        scores, allowed = masked_scores(
            queries, keys_block, query_place, query_seg, key_place, key_seg
        )
        scores = jnp.where(allowed, scores, -1e30)
        raised_top = jnp.maximum(highest, jnp.max(scores, axis=-1))
        weights_now = jnp.where(allowed, jnp.exp(scores - raised_top[..., None]), 0.0)
        return (raised_top, totals * jnp.exp(highest - raised_top) + jnp.sum(weights_now, axis=-1))

    stat_shape = (block_rows, groups, group_size)
    highest, totals = lax.fori_loop(
        0,
        mine + 1,
        stats_step,
        (jnp.full(stat_shape, -1e30, jnp.float32), jnp.zeros(stat_shape, jnp.float32)),
    )
    log_total = highest + jnp.log(totals)

    def mix_step(block_at, carry):
        rounded_sum, remainder_sum = carry
        keys_block, values_block, key_place, key_seg = key_slices(block_at)
        scores, allowed = masked_scores(
            queries, keys_block, query_place, query_seg, key_place, key_seg
        )
        probs = jnp.where(allowed, jnp.exp(scores - log_total[..., None]), 0.0)
        probs_high = probs.astype(jnp.bfloat16)
        probs_rest = (probs - probs_high.astype(jnp.float32)).astype(jnp.bfloat16)
        rounded_sum = rounded_sum + jnp.einsum(
            "bkgt,tkd->bkgd", probs_high, values_block, preferred_element_type=jnp.float32
        )
        remainder_sum = remainder_sum + jnp.einsum(
            "bkgt,tkd->bkgd", probs_rest, values_block, preferred_element_type=jnp.float32
        )
        return (rounded_sum, remainder_sum)

    mix_shape = (block_rows, groups, group_size, HD)
    rounded_sum, remainder_sum = lax.fori_loop(
        0,
        mine + 1,
        mix_step,
        (jnp.zeros(mix_shape, jnp.float32), jnp.zeros(mix_shape, jnp.float32)),
    )
    exact_sum = rounded_sum + remainder_sum
    attended = rounded_sum.astype(jnp.bfloat16).reshape(block_rows, groups * group_size * HD)
    attended_rows = collect_rows(attended)
    middle = inputs + into_wide(attended_rows, times_weight(out_low))
    normed_two, scale_two = norm_forward(middle, norm_gains[1])
    normed_two_wide = widen(normed_two.astype(jnp.bfloat16))
    gate_up = into_narrow(normed_two_wide, times_weight(gate_up_low))
    gate_part = gate_up[:, :hidden_cols]
    up_part = gate_up[:, hidden_cols:]
    sigmoid_gate = jax.nn.sigmoid(gate_part)
    hidden = (gate_part * sigmoid_gate * up_part).astype(jnp.bfloat16)
    hidden_rows = collect_rows(hidden)
    output = middle + into_wide(hidden_rows, times_weight(down_low))
    cotangent_rows = widen(out_grad)
    grad_down = outer_rows(hidden_rows, cotangent_rows)
    hidden_grad = into_narrow(cotangent_rows, times_transpose(down_low))
    gate_grad = hidden_grad * up_part * sigmoid_gate * (1.0 + gate_part * (1.0 - sigmoid_gate))
    up_grad = hidden_grad * gate_part * sigmoid_gate
    gate_up_back = jnp.concatenate([gate_grad, up_grad], axis=1).astype(jnp.bfloat16)
    gate_up_rows = collect_rows(gate_up_back)
    grad_gate_up = outer_rows(normed_two_wide, gate_up_rows).reshape(gate_up_whole.shape)
    middle_back, gain_two = norm_backward(
        middle, scale_two, norm_gains[1], into_wide(gate_up_rows, times_transpose(gate_up_low))
    )
    middle_grad = out_grad.astype(jnp.float32) + middle_back
    middle_rows = widen(middle_grad.astype(jnp.bfloat16))
    grad_out = outer_rows(attended_rows, middle_rows)
    attended_grad = (
        into_narrow(middle_rows, times_transpose(out_low)).astype(jnp.bfloat16).reshape(mix_shape)
    )
    delta = jnp.sum(attended_grad.astype(jnp.float32) * exact_sum, axis=-1)
    head_scale = HD ** (-0.5)

    def back_step(block_at, carry):
        query_back, key_terms = carry
        keys_block, values_block, key_place, key_seg = key_slices(block_at)
        scores, allowed = masked_scores(
            queries, keys_block, query_place, query_seg, key_place, key_seg
        )
        probs = jnp.where(allowed, jnp.exp(scores - log_total[..., None]), 0.0)
        prob_grad = jnp.einsum(
            "bkgd,tkd->bkgt", attended_grad, values_block, preferred_element_type=jnp.float32
        )
        score_grad = (probs * (prob_grad - delta[..., None])).astype(jnp.bfloat16)
        query_back = (
            query_back
            + jnp.einsum(
                "bkgt,tkd->bkgd", score_grad, keys_block, preferred_element_type=jnp.float32
            )
            * head_scale
        )
        key_back = (
            jnp.einsum("bkgt,bkgd->tkd", score_grad, queries, preferred_element_type=jnp.float32)
            * head_scale
        )
        value_back = jnp.einsum(
            "bkgt,bkgd->tkd",
            probs.astype(jnp.bfloat16),
            attended_grad,
            preferred_element_type=jnp.float32,
        )
        key_terms = lax.dynamic_update_slice_in_dim(
            key_terms, jnp.concatenate([key_back, value_back], axis=-1), block_at * block_rows, 0
        )
        return (query_back, key_terms)

    query_back, key_terms = lax.fori_loop(
        0,
        mine + 1,
        back_step,
        (jnp.zeros(mix_shape, jnp.float32), jnp.zeros((total_rows, groups, 2 * HD), jnp.float32)),
    )
    key_grads = lax.psum_scatter(key_terms, ("seq", "narrow"), scatter_dimension=0, tiled=True)
    query_grad = rotate(query_back, cosine, -sine).reshape(block_rows, groups, query_cols)
    key_grad = rotate(key_grads[:, :, :HD], cosine, -sine)
    projected_back = jnp.concatenate([query_grad, key_grad, key_grads[:, :, HD:]], axis=2)
    projected_back = projected_back.astype(jnp.bfloat16).reshape(block_rows, groups * group_cols)
    projected_rows = collect_rows(projected_back)
    grad_qkv = outer_rows(normed_wide, projected_rows).reshape(qkv_whole.shape)
    input_back, gain_one = norm_backward(
        inputs, scale_one, norm_gains[0], into_wide(projected_rows, times_transpose(qkv_low))
    )
    input_grad = middle_grad + input_back
    gains_grad = lax.psum(jnp.stack([gain_one, gain_two]), ("seq", "wide"))
    weights = (qkv_weight, gate_up_weight, out_weight, down_weight)
    moments = (qkv_moment, gate_up_moment, out_moment, down_moment)
    seconds = (qkv_second, gate_up_second, out_second, down_second)
    out_rate = OUTPUT_RATE * (total_rows / (HQ * HD)) ** 0.5
    down_rate = DOWN_RATE * FF ** (-0.5)
    rates = (MATRIX_RATE, MATRIX_RATE, out_rate, down_rate)
    summed = (
        lax.psum(grad_qkv.astype(jnp.bfloat16), "seq").astype(jnp.float32),
        lax.psum(grad_gate_up.astype(jnp.bfloat16), "seq").astype(jnp.float32),
        lax.psum(grad_out.astype(jnp.bfloat16), "seq").astype(jnp.float32),
        lax.psum(grad_down.astype(jnp.bfloat16), "seq").astype(jnp.float32),
    )
    seq_place = lax.axis_index("seq")
    shares = tuple(
        (
            lax.dynamic_slice_in_dim(member, seq_place * weight.shape[0], weight.shape[0], 0)
            for member, weight in zip(summed, weights)
        )
    )
    local_square = sum((jnp.sum(member * member) for member in shares))
    local_square = local_square + jnp.sum(gains_grad * gains_grad) / (
        lax.axis_size("wide") * lax.axis_size("seq")
    )
    grad_norm = jnp.sqrt(lax.psum(local_square, ("seq", "narrow", "wide")))
    factor = CLIP_NORM / jnp.maximum(grad_norm, CLIP_NORM)
    results = []
    for weight, moment, second, gradient, rate in zip(weights, moments, seconds, shares, rates):
        results.extend(adam(weight, moment, second, gradient * factor, rate, WEIGHT_DECAY))
    gains_new = adam(norm_gains, gains_moment, gains_second, gains_grad * factor, GAIN_RATE, 0.0)
    return (
        output.astype(jnp.bfloat16),
        input_grad,
        grad_norm,
        results[0],
        results[1],
        results[2],
        results[3],
        results[4],
        results[5],
        results[6],
        results[7],
        results[8],
        results[9],
        results[10],
        results[11],
        gains_new[0],
        gains_new[1],
        gains_new[2],
    )


def solution(mesh):
    placed = (
        P(("seq", "wide"), "narrow"),
        P(("seq", "wide"), "narrow"),
        P(("narrow", "seq"), "wide", None),
        P(("narrow", "seq"), "wide", None),
        P(("narrow", "seq"), "wide", None),
        P(("narrow", "seq"), None, "wide"),
        P(("narrow", "seq"), None, "wide"),
        P(("narrow", "seq"), None, "wide"),
        P(("wide", "seq"), "narrow"),
        P(("wide", "seq"), "narrow"),
        P(("wide", "seq"), "narrow"),
        P(("wide", "seq"), "narrow"),
        P(("wide", "seq"), "narrow"),
        P(("wide", "seq"), "narrow"),
        P(None, "narrow"),
        P(None, "narrow"),
        P(None, "narrow"),
        P(),
    )
    return jax.shard_map(
        shards,
        mesh=mesh,
        in_specs=placed,
        out_specs=(
            P(("seq", "wide"), "narrow"),
            P(("seq", "wide"), "narrow"),
            P(),
            P(("narrow", "seq"), "wide", None),
            P(("narrow", "seq"), "wide", None),
            P(("narrow", "seq"), "wide", None),
            P(("narrow", "seq"), None, "wide"),
            P(("narrow", "seq"), None, "wide"),
            P(("narrow", "seq"), None, "wide"),
            P(("wide", "seq"), "narrow"),
            P(("wide", "seq"), "narrow"),
            P(("wide", "seq"), "narrow"),
            P(("wide", "seq"), "narrow"),
            P(("wide", "seq"), "narrow"),
            P(("wide", "seq"), "narrow"),
            P(None, "narrow"),
            P(None, "narrow"),
            P(None, "narrow"),
        ),
        check_vma=False,
    )
```

profile of v0, /device:TPU:1, one launch (start us, length us, event | category | flops | bytes accessed | tf_op | source)
XLA Modules:
  0.0 3570.7 jit_solution(7346102953513261361)
XLA Ops:
  7.2 1.6 convert_element_type.128
  10.0 3.5 psum.70
  13.6 1.4 fusion.92
  16.6 11.0 all_gather.42
  27.6 130.6 %all-gather.9.cloned.1.call-done = bf16[1024,4,384]{2,1,0:T(4,128)(2,1)} async-done(((bf16[32,4,384]{2,1,0:T(4,128)(2,1)}), bf16[1024,4,384]{2,1,0:T(4,128)(2,1)}) %all-gather.9.cloned.1.call-update) | async-done | bytes 3145744 | tf_op jit(solution)/shard_map/all_gather | solution.py:189
  158.2 4.1 copy.92
  162.3 4.1 fusion.93
  168.3 25.1 reduce-scatter.10.cloned.1.call-done
  193.4 1.4 reshape.400
  200.8 111.7 %all-gather.13.cloned.1.call-done = bf16[8192,4,64]{0,2,1:T(8,128)(2,1)} async-done(((bf16[128,4,64]{0,2,1:T(8,128)(2,1)}), bf16[8192,4,64]{0,2,1:T(8,128)(2,1)}) %all-gather.13.cloned.1.call-update) | async-done | bytes 4194320 | tf_op jit(solution)/shard_map/all_gather | solution.py:223
  312.5 6.2 while.36
  319.3 108.8 %all-gather.11.cloned.1.call-done = bf16[8192,4,64]{0,2,1:T(8,128)(2,1)} async-done(((bf16[128,4,64]{0,2,1:T(8,128)(2,1)}), bf16[8192,4,64]{0,2,1:T(8,128)(2,1)}) %all-gather.11.cloned.1.call-update) | async-done | bytes 4194320 | tf_op jit(solution)/shard_map/all_gather | solution.py:224
  428.3 10.2 while.37
  438.5 2.3 all_gather.46
  440.8 123.7 %all-gather.15.cloned.1.call-done = bf16[1024,1024]{1,0:T(8,128)(2,1)} async-done(((bf16[32,1024]{1,0:T(8,128)(2,1)}), bf16[1024,1024]{1,0:T(8,128)(2,1)}) %all-gather.15.cloned.1.call-update) | async-done | bytes 2097168 | tf_op jit(solution)/shard_map/all_gather | solution.py:191
  564.5 3.1 convolution_convert_fusion.5
  569.0 8.3 all_gather.52
  577.3 224.6 %all-gather.21.cloned.1.call-done = bf16[4096,1024]{1,0:T(8,128)(2,1)} async-done(((bf16[128,1024]{1,0:T(8,128)(2,1)}), bf16[4096,1024]{1,0:T(8,128)(2,1)}) %all-gather.21.cloned.1.call-update) | async-done | bytes 8388624 | tf_op jit(solution)/shard_map/all_gather | solution.py:192
  801.9 7.7 fusion.95
  809.7 48.8 %reduce-scatter.12.cloned.1.call-done = bf16[128,1024]{1,0:T(8,128)(2,1)} async-done(((bf16[256,1024]{1,0:T(8,128)(2,1)}), bf16[128,1024]{1,0:T(8,128)(2,1)}) %reduce-scatter.12.cloned.1.call-update) | async-done | bytes 262160 | tf_op jit(solution)/shard_map/reduce_scatter | solution.py:105
  859.6 2.8 psum.71
  863.5 10.2 all_gather.48
  873.7 356.3 %all-gather.17.cloned.1.call-done = bf16[1024,2,4096]{2,1,0:T(2,128)(2,1)} async-done(((bf16[32,2,4096]{2,1,0:T(2,128)(2,1)}), bf16[1024,2,4096]{2,1,0:T(2,128)(2,1)}) %all-gather.17.cloned.1.call-update) | async-done | bytes 16777232 | tf_op jit(solution)/shard_map/all_gather | solution.py:190
  1230.0 15.5 copy.93
  1245.4 5.7 copy-done
  1251.2 6.7 fusion.94
  1257.9 15.8 reduce-scatter.14.cloned.1.call-done
  1273.7 5.2 multiply_convert_fusion.1
  1278.9 1.5 pad_maximum_fusion
  1280.5 17.9 all-gather.23.cloned.1.call-done
  1298.4 12.4 convolution_convert_fusion.7
  1310.8 19.6 reduce-scatter.20.cloned.1.call-done
  1330.4 1.8 fusion.58
  1332.2 2.8 psum.72
  1336.6 9.7 all_gather.54
  1346.4 3.3 fusion.96
  1350.5 11.0 reduce-scatter.22.cloned.1.call-done
  1361.5 1.8 convert_element_type.146
  1365.1 7.8 broadcast_in_dim.61
  1373.0 13.1 while.38
  1387.2 7.2 convolution_convert_fusion.1
  1394.5 705.7 %reduce-scatter.24.cloned.1.call-done = f32[128,4,128]{0,2,1:T(8,128)} async-done(((f32[8192,4,128]{0,2,1:T(8,128)}), f32[128,4,128]{0,2,1:T(8,128)}) %reduce-scatter.24.cloned.1.call-update) | async-done | bytes 262160 | tf_op jit(solution)/shard_map/reduce_scatter | solution.py:352
  2102.1 6.7 all_gather.55
  2109.7 3.7 convolution_convert_fusion.6
  2113.4 10.3 convolution_convert_fusion
  2123.8 27.7 convert_element_type.155
  2151.5 2.1 convolution_convert_fusion.3
  2153.6 2.3 convolution_convert_fusion.2
  2155.9 2.4 convert_element_type.152
  2159.9 6.5 convolution_convert_fusion.4
  2167.8 153.5 %psum.78 = f32[2,1024]{1,0:T(2,128)S(1)} all-reduce(f32[2,1024]{1,0:T(2,128)S(1)} %pad_maximum_fusion.5), channel_id=1, replica_groups=mesh['seq'=32,'narrow'=2,'wide'=2] {'seq','wide'}, use_global_device_ids=true, to_apply=%region_39.40 | all-reduce | flops 2048 | bytes 16384 | tf_op jit(solution)/shard_map/psum | solution.py:363
  2322.6 29.0 psum.73
  2351.6 1109.1 %all-reduce.3.cloned.1.call-done = (bf16[1024,4,384]{2,1,0:T(4,128)(2,1)}, bf16[1024,2,4096]{2,1,0:T(2,128)(2,1)}, bf16[1024,1024]{1,0:T(8,128)(2,1)}, bf16[4096,1024]{1,0:T(8,128)(2,1)}) async-done(((bf16[1024,4,384]{2,1,0:T(4,128)(2,1)}, bf16[1024,2,4096]{2,1,0:T(2,128)(2,1)}, bf16[1024,1024]{1,0:T(8,128)(2,1)}, bf16[4096,1024]{1,0:T(8,128)(2,1)}), (bf16[1024,4,384]{2,1,0:T(4,128)(2,1)}, ...) | async-done | bytes 30408720 | tf_op jit(solution)/shard_map/psum | solution.py:371
  3460.7 1.6 fusion.69
  3462.3 2.7 fusion.45
  3466.3 1.5 fusion.73
  3468.5 1.7 fusion.59
  3470.8 10.4 reduce-scatter.16.cloned.1.call-done
  3481.3 2.3 fusion.53
  3483.6 65.0 %psum.79 = f32[]{:T(128)} all-reduce(f32[]{:T(128)S(6)} %add.262), channel_id=1, replica_groups=mesh['seq'=32,'narrow'=2,'wide'=2] {'seq','narrow','wide'}, use_global_device_ids=true, to_apply=%region_41.42 | all-reduce | flops 1 | bytes 8 | tf_op jit(solution)/shard_map/psum | solution.py:387
  3550.0 2.7 multiply_subtract_fusion.1
  3552.7 1.9 multiply_subtract_fusion.3
  3554.5 5.8 multiply_subtract_fusion
  3560.3 2.0 multiply_subtract_fusion.2
  (219 shorter events, 56.8 us)
Async XLA Ops:
  7.2 151.0 %all-gather.9.cloned.1.call-start = ((), (), s32[]{:S(2)}) async-start(), calls=%async_computation.9 | async-start | bytes 3244032 | tf_op jit(solution)/shard_map/all_gather | solution.py:189
  8.9 184.5 %reduce-scatter.10.cloned.1.call-start = ((), (), s32[]{:S(2)}) async-start(), calls=%async_computation.10 | async-start | bytes 2359296 | tf_op jit(solution)/shard_map/reduce_scatter | solution.py:91
  13.5 1.4 copy-start.40
  13.5 3.1 copy-start.35
  14.9 0.6 copy-start.27
  27.6 138.8 %copy-start.2 = (bf16[256,1024]{1,0:T(8,128)(2,1)}, bf16[256,1024]{1,0:T(8,128)(2,1)S(1)}, u32[]{:S(2)}) copy-start(bf16[256,1024]{1,0:T(8,128)(2,1)S(1)} %all_gather.42) | copy-start | bytes 1572868
  162.3 4.1 copy-start.39
  166.3 30.6 copy-start.20
  166.3 31.3 copy-start.15
  166.4 146.1 %all-gather.13.cloned.1.call-start = ((), (), s32[]{:S(2)}) async-start(), calls=%async_computation.12 | async-start | bytes 4259840 | tf_op jit(solution)/shard_map/all_gather | solution.py:223
  195.9 232.2 %all-gather.11.cloned.1.call-start = ((), (), s32[]{:S(2)}) async-start(), calls=%async_computation.11 | async-start | bytes 4259840 | tf_op jit(solution)/shard_map/all_gather | solution.py:224
  196.9 367.6 %all-gather.15.cloned.1.call-start = ((), (), s32[]{:S(2)}) async-start(), calls=%async_computation.13 | async-start | bytes 2162688 | tf_op jit(solution)/shard_map/all_gather | solution.py:191
  197.6 604.3 %all-gather.21.cloned.1.call-start = ((), (), s32[]{:S(2)}) async-start(), calls=%async_computation.18 | async-start | bytes 8650752 | tf_op jit(solution)/shard_map/all_gather | solution.py:192
  198.4 660.1 %reduce-scatter.12.cloned.1.call-start = ((), (), s32[]{:S(2)}) async-start(), calls=%async_computation.14 | async-start | bytes 786432 | tf_op jit(solution)/shard_map/reduce_scatter | solution.py:105
  438.4 129.2 %copy-start.5 = (f32[32,2,4096]{2,1,0:T(2,128)S(1)}, f32[32,2,4096]{2,1,0:T(2,128)}, u32[]{:S(2)}) copy-start(f32[32,2,4096]{2,1,0:T(2,128)} %param.29) | copy-start | bytes 3145732
  438.5 130.5 %copy-start.9 = (bf16[128,1024]{1,0:T(8,128)(2,1)S(1)}, bf16[128,1024]{1,0:T(8,128)(2,1)}, u32[]{:S(2)}) copy-start(bf16[128,1024]{1,0:T(8,128)(2,1)} %param.25) | copy-start | bytes 786436
  567.6 662.3 %all-gather.17.cloned.1.call-start = ((), (), s32[]{:S(2)}) async-start(), calls=%async_computation.15 | async-start | bytes 17301504 | tf_op jit(solution)/shard_map/all_gather | solution.py:190
  569.0 689.0 %reduce-scatter.18.cloned.1.call-start = ((), (), s32[]{:S(2)}) async-start(), calls=%async_computation.20 | async-start | bytes 6291456 | tf_op jit(solution)/shard_map/reduce_scatter | solution.py:91
  577.3 232.3 %copy-start.13 = (bf16[256,1024]{1,0:T(8,128)(2,1)}, bf16[256,1024]{1,0:T(8,128)(2,1)S(1)}, u32[]{:S(2)}) copy-start(bf16[256,1024]{1,0:T(8,128)(2,1)S(1)} %all_gather.52) | copy-start | bytes 1572868
  809.6 48.9 %copy-start.1 = (bf16[128,1024]{1,0:T(8,128)(2,1)S(1)}, bf16[128,1024]{1,0:T(8,128)(2,1)}, u32[]{:S(2)}) copy-start(bf16[128,1024]{1,0:T(8,128)(2,1)} %param.24) | copy-start | bytes 786436
  809.6 52.8 %copy-start.25 = (f32[1,1024]{1,0:T(1,128)S(1)}, f32[1,1024]{1,0:T(1,128)}, u32[]{:S(2)}) copy-start(f32[1,1024]{1,0:T(1,128)} %get-tuple-element.344) | copy-start | bytes 12292
  809.6 464.1 %reduce-scatter.14.cloned.1.call-start = ((), (), s32[]{:S(2)}) async-start(), calls=%async_computation.16 | async-start | bytes 12582912 | tf_op jit(solution)/shard_map/reduce_scatter | solution.py:91
  862.4 472.5 %copy-start.33 = (f32[128]{0:T(128)}, f32[128]{0:T(128)S(1)}, u32[]{:S(2)}) copy-start(f32[128]{0:T(128)S(1)} %add_rsqrt_fusion) | copy-start | bytes 1540
  1245.4 5.7 copy-start
  1257.9 40.5 %all-gather.23.cloned.1.call-start = ((), (), s32[]{:S(2)}) async-start(), calls=%async_computation.21 | async-start | bytes 6291456 | tf_op jit(solution)/shard_map/all_gather | solution.py:82
  1280.4 50.0 %copy-start.3 = (bf16[128,1024]{1,0:T(8,128)(2,1)S(1)}, bf16[128,1024]{1,0:T(8,128)(2,1)}, u32[]{:S(2)}) copy-start(bf16[128,1024]{1,0:T(8,128)(2,1)} %reduce-scatter.12.cloned.1.call-done) | copy-start | bytes 786436
  1280.5 55.0 %copy-start.10 = (bf16[128,1024]{1,0:T(8,128)(2,1)S(1)}, bf16[128,1024]{1,0:T(8,128)(2,1)}, u32[]{:S(2)}) copy-start(bf16[128,1024]{1,0:T(8,128)(2,1)} %param.25) | copy-start | bytes 786436
  1280.5 50.0 %reduce-scatter.20.cloned.1.call-start = ((), (), s32[]{:S(2)}) async-start(), calls=%async_computation.22 | async-start | bytes 786432 | tf_op jit(solution)/shard_map/reduce_scatter | solution.py:105
  1310.8 50.7 %reduce-scatter.22.cloned.1.call-start = ((), (), s32[]{:S(2)}) async-start(), calls=%async_computation.23 | async-start | bytes 1572864 | tf_op jit(solution)/shard_map/reduce_scatter | solution.py:91
  1335.0 0.5 copy-start.37
  1349.7 36.5 %all-gather.19.cloned.1.call-start = ((), (), s32[]{:S(2)}) async-start(), calls=%async_computation.17 | async-start | bytes 3145728 | tf_op jit(solution)/shard_map/all_gather | solution.py:82
  1350.3 749.9 %reduce-scatter.24.cloned.1.call-start = ((), (), s32[]{:S(2)}) async-start(), calls=%async_computation.24 | async-start | bytes 17039360 | tf_op jit(solution)/shard_map/reduce_scatter | solution.py:352
  1365.1 7.8 copy-start.21
  1386.1 1.0 copy-start.14
  1386.2 8.2 copy-start.24
  1386.2 780.4 %reduce-scatter.26.cloned.1.call-start = ((), (), s32[]{:S(2)}) async-start(), calls=%async_computation.25 | async-start | bytes 786432 | tf_op jit(solution)/shard_map/reduce_scatter | solution.py:105
  2108.8 0.9 copy-start.8
  2113.4 1347.3 %all-reduce.3.cloned.1.call-start = ((), (), s32[]{:S(2)}) async-start(), calls=%async_computation.26 | async-start | bytes 60817408 | tf_op jit(solution)/shard_map/psum | solution.py:371
  2158.4 1.6 copy-start.7
  2158.4 8.2 copy-start.28
  2158.4 8.1 copy-start.36
  2158.4 9.4 copy-start.30
  2158.4 193.1 %copy-start.41 = (f32[128]{0:T(128)S(1)}, f32[128]{0:T(128)}, u32[]{:S(2)}) copy-start(f32[128]{0:T(128)} %copy-done.40) | copy-start | bytes 1540
  2158.4 1322.8 %copy-start.4 = (bf16[128,1024]{1,0:T(8,128)(2,1)S(1)}, bf16[128,1024]{1,0:T(8,128)(2,1)}, u32[]{:S(2)}) copy-start(bf16[128,1024]{1,0:T(8,128)(2,1)} %reduce-scatter.12.cloned.1.call-done) | copy-start | bytes 786436
  2158.4 1322.8 %copy-start.11 = (bf16[128,1024]{1,0:T(8,128)(2,1)S(1)}, bf16[128,1024]{1,0:T(8,128)(2,1)}, u32[]{:S(2)}) copy-start(bf16[128,1024]{1,0:T(8,128)(2,1)} %param.25) | copy-start | bytes 786436
  2158.4 1322.8 %copy-start.12 = (bf16[128,1024]{1,0:T(8,128)(2,1)S(1)}, bf16[128,1024]{1,0:T(8,128)(2,1)}, u32[]{:S(2)}) copy-start(bf16[128,1024]{1,0:T(8,128)(2,1)} %reduce-scatter.20.cloned.1.call-done) | copy-start | bytes 786436
  2158.5 1322.8 %copy-start.26 = (f32[1,1024]{1,0:T(1,128)S(1)}, f32[1,1024]{1,0:T(1,128)}, u32[]{:S(2)}) copy-start(f32[1,1024]{1,0:T(1,128)} %get-tuple-element.344) | copy-start | bytes 12292
  2158.5 1322.8 %copy-start.34 = (f32[128]{0:T(128)S(1)}, f32[128]{0:T(128)}, u32[]{:S(2)}) copy-start(f32[128]{0:T(128)} %copy-done.33) | copy-start | bytes 1540
  2158.5 1322.8 %copy-start.38 = (f32[128]{0:T(128)S(1)}, f32[128]{0:T(128)}, u32[]{:S(2)}) copy-start(f32[128]{0:T(128)} %copy-done.37) | copy-start | bytes 1540
  2158.5 1322.8 %reduce-scatter.16.cloned.1.call-start = ((), (), s32[]{:S(2)}) async-start(), calls=%async_computation.19 | async-start | bytes 786432 | tf_op jit(solution)/shard_map/reduce_scatter | solution.py:105
  2166.4 1382.8 %copy-start.29 = (f32[2,1024]{1,0:T(2,128)S(1)}, f32[2,1024]{1,0:T(2,128)}, u32[]{:S(2)}) copy-start(f32[2,1024]{1,0:T(2,128)} %param.38) | copy-start | bytes 24580
  2166.4 1382.8 %copy-start.31 = (f32[2,1024]{1,0:T(2,128)S(1)}, f32[2,1024]{1,0:T(2,128)}, u32[]{:S(2)}) copy-start(f32[2,1024]{1,0:T(2,128)} %param.39) | copy-start | bytes 24580
  2166.4 1382.9 %copy-start.32 = (f32[2,1024]{1,0:T(2,128)S(1)}, f32[2,1024]{1,0:T(2,128)}, u32[]{:S(2)}) copy-start(f32[2,1024]{1,0:T(2,128)} %param.40) | copy-start | bytes 24580
  2166.5 1383.5 %copy-start.16 = (f32[128,1024]{1,0:T(8,128)S(1)}, f32[128,1024]{1,0:T(8,128)}, u32[]{:S(2)}) copy-start(f32[128,1024]{1,0:T(8,128)} %param.35) | copy-start | bytes 1572868
  2166.5 1388.1 %copy-start.6 = (f32[32,2,4096]{2,1,0:T(2,128)S(1)}, f32[32,2,4096]{2,1,0:T(2,128)}, u32[]{:S(2)}) copy-start(f32[32,2,4096]{2,1,0:T(2,128)} %param.29) | copy-start | bytes 3145732
  3483.6 71.0 %copy-start.17 = (f32[32,2,4096]{2,1,0:T(2,128)S(1)}, f32[32,2,4096]{2,1,0:T(2,128)}, u32[]{:S(2)}) copy-start(f32[32,2,4096]{2,1,0:T(2,128)} %param.30) | copy-start | bytes 3145732
  3549.3 5.2 copy-start.18
  3552.7 7.7 copy-start.19
  3552.7 7.7 copy-start.22
  3552.7 7.7 copy-start.23
Sparse Core Ops, SparseCore 0:
  10.2 147.9 all-gather.8
  166.5 26.8 reduce-scatter.9
  196.0 116.3 all-gather.12
  314.6 113.4 all-gather.10
  430.3 134.1 all-gather.14
  566.7 235.2 all-gather.20
  805.0 53.4 reduce-scatter.11
  860.7 369.2 all-gather.16
  1232.4 10.8 reduce-scatter.17
  1258.0 15.6 reduce-scatter.13
  1280.6 17.7 all-gather.22
  1310.9 19.4 reduce-scatter.19
  1349.8 11.6 reduce-scatter.21
  1363.6 14.6 all-gather.18
  1386.3 713.8 reduce-scatter.23
  2113.5 16.5 reduce-scatter.25
  2158.5 1302.1 all-reduce.2
  3463.6 17.6 reduce-scatter.15
where the time goes:
time: 3610 us; the launch traced here: 3570 us
  waiting for transfers between devices  3020 us (84%)
  blocking collectives  305 us (8%)
  matrix products  86.8 us (2%)
  local copies, waits for them, and re-layouts  80.3 us (2%)
  other arithmetic  57 us (2%)
    psum x1, waiting for transfers between devices, shards(): lax.psum(grad_qkv.astype(jnp.bfloat16), 'seq').astype(jnp.float32)  1110 us
    reduce_scatter x1, waiting for transfers between devices, shards(): lax.psum_scatter(key_terms, ('seq', 'narrow'), scatter_dimension=0, tiled...  706 us
    all_gather x1, waiting for transfers between devices, shards(): lax.all_gather(gate_up_weight.astype(jnp.bfloat16), 'seq', axis=0, tiled=...  356 us
    all_gather x1, waiting for transfers between devices, shards(): lax.all_gather(down_weight.astype(jnp.bfloat16), 'seq', axis=0, tiled=True)  225 us
    psum x1, blocking collectives, shards(): gains_grad = lax.psum(jnp.stack([gain_one, gain_two]), ('seq', 'wide'))  153 us
    all_gather x1, waiting for transfers between devices, shards(): lax.all_gather(qkv_weight.astype(jnp.bfloat16), 'seq', axis=0, tiled=True)  131 us
    all_gather x1, waiting for transfers between devices, shards(): lax.all_gather(out_weight.astype(jnp.bfloat16), 'seq', axis=0, tiled=True)  124 us
    all_gather x1, waiting for transfers between devices, shards(): lax.all_gather(keys_mine, ('seq', 'narrow'), axis=0, tiled=True)  112 us
  transfers between devices with their start and end apart: 18, of which 15 were waited for; matrix products, arithmetic and copies ran while one was open for 4% of the time, Pallas kernels for 0%

commit v1 on v0

v1 whole, which is shorter than its diff:
```python
import functools
import math

import jax
import jax.numpy as jnp
from jax import lax
from jax.experimental import pallas as pl
from jax.experimental.pallas import tpu as pltpu
from jax.sharding import PartitionSpec as P

D = 2048
HQ = 32
HD = 64
FF = 8192
ADAM_STEP = 10


NORM_EPS = 1e-05
ADAM_EPS = 1e-08
BETA_ONE = 0.9
BETA_TWO = 0.95
WEIGHT_DECAY = 0.1
MATRIX_RATE = 0.01
OUTPUT_RATE = 0.9
DOWN_RATE = 3.0
GAIN_RATE = 2.5
CLIP_NORM = 1.0
ROPE_THETA = 500000.0
ROPE_FACTOR = 32.0
LOW_FREQ = 1.0
HIGH_FREQ = 4.0
OLD_CONTEXT = 8192.0

TOKENS = 8192
HALF = 256
HALVES = TOKENS // HALF
ROWS = 128
LINE = 512
WIDTH = 1024
GROUP = 4
PIECE = 32
HIDDEN = 1024
MESH = pl.DeviceIdType.MESH
ANY = pl.ANY
BF = jnp.bfloat16
F32 = jnp.float32
VMEM_LIMIT = 56 * 1024 * 1024
NEVER = -1e30


def place():
    seq = lax.axis_index("seq")
    return (
        seq // 8,
        lax.rem(seq // 2, 4),
        lax.rem(seq, 2),
        lax.axis_index("wide"),
        lax.axis_index("narrow"),
    )


def device(z, y, x, c):
    return (lax.rem(z, 4) * 8 + lax.rem(y, 4) * 2 + lax.rem(x, 2), c, x // 2)


def block_of(at):
    spot, x = at // 4, (at % 2) * 2 + (at // 2) % 2
    return 2 * spot + x if x < 2 else 2 * (HALVES - 1 - spot) + x - 2


class Wires:
    def __init__(self, send_sem, recv_sem):
        self.send_sem, self.recv_sem, self.used, self.sent = send_sem, recv_sem, 0, []

    def send(self, src, dst, target, start=True):
        at = self.used
        self.used += 1
        copy = pltpu.make_async_remote_copy(
            src_ref=src,
            dst_ref=dst,
            send_sem=self.send_sem.at[at],
            recv_sem=self.recv_sem.at[at],
            device_id=target,
            device_id_type=MESH,
        )
        if start:
            copy.start()
        self.sent.append(copy)
        return at

    def landed(self, at, region):
        pltpu.make_async_copy(region, region, self.recv_sem.at[at]).wait()

    def close(self):
        for copy in self.sent:
            copy.wait_send()


def greet(targets):
    barrier = pltpu.get_barrier_semaphore()
    for target in targets:
        pl.semaphore_signal(barrier, inc=1, device_id=target, device_id_type=MESH)
    pl.semaphore_wait(barrier, len(targets))


def line_targets(z, y, x, c):
    return [device(z, y, lax.rem(x + o, 4), c) for o in (1, 2, 3)] + [device(z, y, x, 1 - c)]


def plane_targets(z, y, x, c):
    return [device(z + o, y, x, c) for o in (1, 2, 3)] + [device(z, y + o, x, c) for o in (1, 2, 3)]


def wire_scratch(count):
    return [pltpu.SemaphoreType.DMA((count,)), pltpu.SemaphoreType.DMA((count,))]


def comm_params(number):
    return pltpu.CompilerParams(
        collective_id=number, has_side_effects=True, vmem_limit_bytes=VMEM_LIMIT
    )


def row_span(at):
    return pl.ds(pl.multiple_of(at * ROWS, ROWS), ROWS)


def col_span(c):
    return pl.ds(pl.multiple_of(c * WIDTH, WIDTH), WIDTH)


def gather_sends(wires, own, out, here):
    z, y, x, c = here
    spot = out.at[row_span(x), col_span(c)]
    across = {o: wires.send(own, spot, device(z, y, lax.rem(x + o, 4), c)) for o in (2, 1, 3)}
    return across, wires.send(own, spot, device(z, y, x, 1 - c))


def gather_relay(wires, numbers, out, here):
    z, y, x, c = here
    across, direct = numbers
    relays = []
    for o in (1, 3, 2):
        rows = row_span(lax.rem(x + 4 - o, 4))
        spot = out.at[rows, col_span(c)]
        wires.landed(across[o], spot)
        relays.append((wires.send(spot, spot, device(z, y, x, 1 - c)), rows))
    wires.landed(direct, out.at[row_span(x), col_span(1 - c)])
    for at, rows in relays:
        wires.landed(at, out.at[rows, col_span(1 - c)])


FOLD_ORDER = (2, 1, 3, 0)


def fold_sends(wires, part, folded, here):
    z, y, x, c = here
    return [
        wires.send(
            part.at[row_span(lax.rem(x + o, 4)), col_span(1 - c)],
            folded.at[k],
            device(z, y, x, 1 - c),
        )
        for k, o in enumerate(FOLD_ORDER)
    ]


def fold_moves(wires, numbers, part, folded, leaving, arriving, here, total):
    z, y, x, c = here
    moves = []
    for k, o in enumerate(FOLD_ORDER):
        wires.landed(numbers[k], folded.at[k])
        both = part[row_span(lax.rem(x + o, 4)), col_span(c)].astype(F32) + folded[k].astype(F32)
        if o:
            leaving[k] = both.astype(BF)
            moves.append(
                wires.send(leaving.at[k], arriving.at[k], device(z, y, lax.rem(x + o, 4), c))
            )
        else:
            total[...] = both
    return moves


def fold_finish(wires, moves, arriving, total):
    for k, at in enumerate(moves):
        wires.landed(at, arriving.at[k])
    total[...] = (
        total[...]
        + arriving[0].astype(F32)
        + arriving[1].astype(F32)
        + arriving[2].astype(F32)
    )


def fold_scratch():
    return [
        pltpu.VMEM((4, ROWS, WIDTH), BF),
        pltpu.VMEM((3, ROWS, WIDTH), BF),
        pltpu.VMEM((3, ROWS, WIDTH), BF),
        pltpu.VMEM((ROWS, WIDTH), F32),
    ]


def both_cores(wires, mine, theirs, value, here):
    z, y, x, c = here
    mine[...] = jnp.broadcast_to(value, mine.shape)
    at = wires.send(mine, theirs, device(z, y, x, 1 - c))
    wires.landed(at, theirs)
    return value + theirs[:, :1]


def middle_kernel(
    part, inputs, gains, middle_out, scale_out, out,
    folded, leaving, arriving, total, mine, theirs, own, send_sem, recv_sem, local_sem,
):
    z, y, xl, xh, c = place()
    x = xh * 2 + xl
    here = (z, y, x, c)
    greet(line_targets(z, y, x, c))
    wires = Wires(send_sem, recv_sem)
    numbers = fold_sends(wires, part, folded, here)
    moves = fold_moves(wires, numbers, part, folded, leaving, arriving, here, total)
    fold_finish(wires, moves, arriving, total)
    middle = total[...] + inputs[...].astype(F32)
    middle_out[...] = middle
    square = both_cores(
        wires, mine, theirs, jnp.sum(middle * middle, axis=1, keepdims=True), here
    )
    scale = lax.rsqrt(square / D + NORM_EPS)
    scale_out[...] = jnp.broadcast_to(scale, scale_out.shape)
    own[...] = (middle_out[...] * scale * gains[1:2, :]).astype(BF)
    local = pltpu.make_async_copy(own, out.at[row_span(x), col_span(c)], local_sem.at[0])
    local.start()
    gather_relay(wires, gather_sends(wires, own, out, here), out, here)
    local.wait()
    wires.close()


def call_middle(part, inputs, gains):
    vm = pl.BlockSpec(memory_space=pltpu.VMEM)
    return pl.pallas_call(
        middle_kernel,
        out_shape=(
            jax.ShapeDtypeStruct((ROWS, WIDTH), F32),
            jax.ShapeDtypeStruct((ROWS, 128), F32),
            jax.ShapeDtypeStruct((LINE, D), BF),
        ),
        in_specs=[vm] * 3,
        out_specs=(vm, vm, pl.BlockSpec(memory_space=ANY)),
        scratch_shapes=fold_scratch()
        + [
            pltpu.VMEM((ROWS, 128), F32),
            pltpu.VMEM((ROWS, 128), F32),
            pltpu.VMEM((ROWS, WIDTH), BF),
        ]
        + wire_scratch(16)
        + [pltpu.SemaphoreType.DMA((1,))],
        compiler_params=comm_params(2),
        name="line_middle",
    )(part, inputs, gains)


def norm_back(wires, values, scale, gain_row, incoming, mine, theirs, here):
    weighted = incoming * gain_row
    inner = both_cores(
        wires, mine, theirs, jnp.sum(weighted * values, axis=1, keepdims=True), here
    )
    inner = inner / D
    back = scale * (incoming * gain_row) - values * (scale * scale * scale * inner)
    return back, jnp.sum(incoming * values * scale, axis=0, keepdims=True)


def back_kernel(
    part, part_two, middle, scale, gains, cotangent, output, middle_grad, gain_out, out,
    folded, leaving, arriving, total, folded_two, leaving_two, arriving_two, total_two,
    mine, theirs, own, send_sem, recv_sem, local_sem,
):
    z, y, xl, xh, c = place()
    x = xh * 2 + xl
    here = (z, y, x, c)
    greet(line_targets(z, y, x, c))
    wires = Wires(send_sem, recv_sem)
    numbers = fold_sends(wires, part, folded, here)
    moves = fold_moves(wires, numbers, part, folded, leaving, arriving, here, total)
    numbers_two = fold_sends(wires, part_two, folded_two, here)
    moves_two = fold_moves(
        wires, numbers_two, part_two, folded_two, leaving_two, arriving_two, here, total_two
    )
    fold_finish(wires, moves, arriving, total)
    back, gain_sum = norm_back(
        wires, middle[...], scale[:, :1], gains[1:2, :], total[...], mine, theirs, here
    )
    gain_out[...] = jnp.broadcast_to(gain_sum, gain_out.shape)
    grad = cotangent[...].astype(F32) + back
    middle_grad[...] = grad
    own[...] = grad.astype(BF)
    local = pltpu.make_async_copy(own, out.at[row_span(x), col_span(c)], local_sem.at[0])
    local.start()
    sends = gather_sends(wires, own, out, here)
    fold_finish(wires, moves_two, arriving_two, total_two)
    output[...] = (middle[...] + total_two[...]).astype(BF)
    gather_relay(wires, sends, out, here)
    local.wait()
    wires.close()


def call_back(part, part_two, middle, scale, gains, cotangent):
    vm = pl.BlockSpec(memory_space=pltpu.VMEM)
    return pl.pallas_call(
        back_kernel,
        out_shape=(
            jax.ShapeDtypeStruct((ROWS, WIDTH), BF),
            jax.ShapeDtypeStruct((ROWS, WIDTH), F32),
            jax.ShapeDtypeStruct((8, WIDTH), F32),
            jax.ShapeDtypeStruct((LINE, D), BF),
        ),
        in_specs=[vm] * 6,
        out_specs=(vm, vm, vm, pl.BlockSpec(memory_space=ANY)),
        scratch_shapes=fold_scratch()
        + fold_scratch()
        + [
            pltpu.VMEM((ROWS, 128), F32),
            pltpu.VMEM((ROWS, 128), F32),
            pltpu.VMEM((ROWS, WIDTH), BF),
        ]
        + wire_scratch(24)
        + [pltpu.SemaphoreType.DMA((1,))],
        compiler_params=comm_params(3),
        name="line_back",
    )(part, part_two, middle, scale, gains, cotangent)


def last_kernel(
    part, inputs, scale, gains, middle_grad, input_grad, gain_out,
    folded, leaving, arriving, total, mine, theirs, send_sem, recv_sem,
):
    z, y, xl, xh, c = place()
    x = xh * 2 + xl
    here = (z, y, x, c)
    greet(line_targets(z, y, x, c))
    wires = Wires(send_sem, recv_sem)
    numbers = fold_sends(wires, part, folded, here)
    moves = fold_moves(wires, numbers, part, folded, leaving, arriving, here, total)
    fold_finish(wires, moves, arriving, total)
    back, gain_sum = norm_back(
        wires,
        inputs[...].astype(F32),
        scale[:, :1],
        gains[0:1, :],
        total[...],
        mine,
        theirs,
        here,
    )
    gain_out[...] = jnp.broadcast_to(gain_sum, gain_out.shape)
    input_grad[...] = middle_grad[...] + back
    wires.close()


def call_last(part, inputs, scale, gains, middle_grad):
    vm = pl.BlockSpec(memory_space=pltpu.VMEM)
    return pl.pallas_call(
        last_kernel,
        out_shape=(
            jax.ShapeDtypeStruct((ROWS, WIDTH), F32),
            jax.ShapeDtypeStruct((8, WIDTH), F32),
        ),
        in_specs=[vm] * 5,
        out_specs=(vm, vm),
        scratch_shapes=fold_scratch()
        + [pltpu.VMEM((ROWS, 128), F32), pltpu.VMEM((ROWS, 128), F32)]
        + wire_scratch(12),
        compiler_params=comm_params(4),
        name="line_last",
    )(part, inputs, scale, gains, middle_grad)


def whole_piece(ref, order, zi, yi, sub=None):
    if len(ref.shape) == 6:
        return ref.at[order, zi, yi] if sub is None else ref.at[order, zi, yi, sub]
    rows = ref.shape[2] // 2
    if sub is None:
        return ref.at[zi, yi, pl.ds(order * rows, rows)]
    return ref.at[zi, yi, pl.ds(order * rows + sub * (rows // 2), rows // 2)]


def gather_kernel(
    inputs, cotangent, gain_rows, qkv_in, gate_in, down_in, out_in,
    inputs_all, cotangent_all, gains_all, qkv_all, gate_all, down_all, out_all,
    send_sem, recv_sem, out_send, out_recv, local_sem,
):
    z, y, xl, xh, c = place()
    x = xh * 2 + xl
    here = (z, y, x, c)
    mine = xl * 2 + c
    pair = xh * 2 + 1 - xl
    spot = z * 4 + y
    every = slice(None)
    quad = [(x, 1 - c), (pair, c), (pair, 1 - c)]
    near = [(z + 1, y), (z + 3, y), (z, y + 1), (z, y + 3)]
    fixed = (
        line_targets(z, y, x, c)
        + [device(z, y, pair, 1 - c)]
        + [device(a, b, x, c) for a, b in near]
    )
    to_x, to_c = xh * 2 + z // 2, lax.rem(z, 2)
    keeps = z == mine

    barrier = pltpu.get_barrier_semaphore()
    for target in fixed:
        pl.semaphore_signal(barrier, inc=1, device_id=target, device_id_type=MESH)
    for k in range(16):
        from_y, from_x, from_c = k // 4, xh * 2 + (k // 2) % 2, k % 2

        @pl.when(jnp.logical_not(keeps & (y == from_y) & (xl == (k // 2) % 2) & (c == from_c)))
        def _():
            pl.semaphore_signal(
                barrier,
                inc=1,
                device_id=device(mine, jnp.int32(from_y), from_x, jnp.int32(from_c)),
                device_id_type=MESH,
            )

    pl.semaphore_wait(barrier, len(fixed) + 16 - keeps.astype(jnp.int32))

    wires = Wires(send_sem, recv_sem)
    locals_started = []

    def keep(src, dst):
        copy = pltpu.make_async_copy(src, dst, local_sem.at[len(locals_started)])
        copy.start()
        locals_started.append(copy)

    trio = [(qkv_in, qkv_all), (gate_in, gate_all)]
    swaps = []
    for given, whole in trio:
        swaps.append(
            [
                wires.send(
                    given.at[lax.rem(to, 2) * 2 + core],
                    whole.at[c, z, y, xl],
                    device(z, y, to, core),
                )
                for to, core in quad
            ]
        )
        keep(given.at[mine], whole.at[c, z, y, xl])
    down_swap = wires.send(
        down_in.at[1 - c], down_all.at[z, y, :, col_span(c)], device(z, y, x, 1 - c)
    )
    keep(down_in.at[c], down_all.at[z, y, :, col_span(c)])

    keep(inputs, inputs_all.at[row_span(x), col_span(c)])
    keep(cotangent, cotangent_all.at[row_span(x), col_span(c)])
    keep(gain_rows, gains_all.at[:, col_span(c)])
    gain_at = wires.send(gain_rows, gains_all.at[:, col_span(c)], device(z, y, x, 1 - c))
    input_numbers = gather_sends(wires, inputs, inputs_all, here)
    cotangent_numbers = gather_sends(wires, cotangent, cotangent_all, here)

    slot = y * 4 + mine
    out_sends = []
    out_spot = out_all.at[y, xl, :, col_span(c)]
    for k in range(16):
        copy = pltpu.make_async_remote_copy(
            src_ref=out_in,
            dst_ref=out_spot,
            send_sem=out_send.at[k],
            recv_sem=out_recv.at[slot],
            device_id=device(jnp.int32(k // 4), jnp.int32(k % 4), to_x, to_c),
            device_id_type=MESH,
        )
        to_self = keeps & (spot == k)
        out_sends.append((copy, to_self))

        @pl.when(jnp.logical_not(to_self))
        def _():
            copy.start()

        @pl.when(to_self)
        def _():
            pltpu.make_async_copy(out_in, out_spot, out_recv.at[slot]).start()

    for copy in locals_started:
        copy.wait()
    for (given, whole), numbers in zip(trio, swaps):
        for at, (from_x, from_c) in zip(numbers, quad):
            wires.landed(at, whole.at[from_c, z, y, lax.rem(from_x, 2)])
    wires.landed(down_swap, down_all.at[z, y, :, col_span(1 - c)])

    wholes = [qkv_all, gate_all, down_all]

    def step(order, by):
        return (lax.rem(z + by, 4), y) if order == 0 else (z, lax.rem(y + by, 4))

    def other_step(order, by):
        return (z, lax.rem(y + by, 4)) if order == 0 else (lax.rem(z + by, 4), y)

    def run(order, by):
        return (every, lax.rem(y + by, 4)) if order == 0 else (lax.rem(z + by, 4), every)

    first = [
        [[wires.send(whole_piece(w, o, z, y), whole_piece(w, o, z, y), device(*step(o, by), x, c)) for by in (1, 3)] for o in (0, 1)]
        for w in wholes
    ]
    second = []
    for w, numbers in zip(wholes, first):
        per_order = []
        for o in (0, 1):
            sends = []
            for sub, by in enumerate((1, 3)):
                back = 4 - by
                wires.landed(numbers[o][sub], whole_piece(w, o, *step(o, back)))
                part = whole_piece(w, o, *step(o, back), sub)
                sends.append(wires.send(part, part, device(*step(o, by), x, c)))
            per_order.append(sends)
        second.append(per_order)
    third = []
    for w, numbers in zip(wholes, second):
        per_order = []
        for o in (0, 1):
            for sub in (0, 1):
                wires.landed(numbers[o][sub], whole_piece(w, o, *step(o, 2), sub))
            line = whole_piece(w, o, *run(o, 0))
            per_order.append(
                [wires.send(line, line, device(*other_step(o, by), x, c)) for by in (1, 3)]
            )
        third.append(per_order)
    gather_relay(wires, input_numbers, inputs_all, here)
    gather_relay(wires, cotangent_numbers, cotangent_all, here)
    wires.landed(gain_at, gains_all.at[:, col_span(1 - c)])
    fourth = []
    for w, numbers in zip(wholes, third):
        per_order = []
        for o in (0, 1):
            sends = []
            for sub, by in enumerate((1, 3)):
                back = 4 - by
                wires.landed(numbers[o][sub], whole_piece(w, o, *run(o, back)))
                part = whole_piece(w, o, *run(o, back), sub)
                sends.append(wires.send(part, part, device(*other_step(o, by), x, c)))
            per_order.append(sends)
        fourth.append(per_order)
    for w, numbers in zip(wholes, fourth):
        for o in (0, 1):
            for sub in (0, 1):
                wires.landed(numbers[o][sub], whole_piece(w, o, *run(o, 2), sub))
    for k in range(16):
        spot_k = out_all.at[k // 4, (k // 2) % 2, :, pl.ds((k % 2) * WIDTH, WIDTH)]
        pltpu.make_async_copy(spot_k, spot_k, out_recv.at[k]).wait()
    for copy, to_self in out_sends:

        @pl.when(jnp.logical_not(to_self))
        def _():
            copy.wait_send()

    wires.close()


def call_gather(inputs, cotangent, gain_rows, qkv_in, gate_in, down_in, out_in):
    shapes = (
        jax.ShapeDtypeStruct((LINE, D), BF),
        jax.ShapeDtypeStruct((LINE, D), BF),
        jax.ShapeDtypeStruct((8, D), F32),
        jax.ShapeDtypeStruct((2, 4, 4, 2) + qkv_in.shape[1:], BF),
        jax.ShapeDtypeStruct((2, 4, 4, 2) + gate_in.shape[1:], BF),
        jax.ShapeDtypeStruct((4, 4, down_in.shape[1], D), BF),
        jax.ShapeDtypeStruct((4, 2, PIECE, D), BF),
    )
    hbm = pl.BlockSpec(memory_space=ANY)
    return pl.pallas_call(
        gather_kernel,
        out_shape=shapes,
        in_specs=[hbm] * 7,
        out_specs=(hbm,) * 7,
        scratch_shapes=wire_scratch(80)
        + wire_scratch(16)
        + [pltpu.SemaphoreType.DMA((8,))],
        compiler_params=comm_params(1),
        name="gather_weights",
    )(inputs, cotangent, gain_rows, qkv_in, gate_in, down_in, out_in)


def keys_kernel(own, out, send_sem, recv_sem, local_sem):
    z, y, xl, xh, c = place()
    x = xh * 2 + xl
    every = slice(None)
    greet(plane_targets(z, y, x, c))
    wires = Wires(send_sem, recv_sem)
    offsets = (2, 1, 3)
    first = [
        [wires.send(own.at[0], out.at[0, z, y], device(z + o, y, x, c)) for o in offsets],
        [wires.send(own.at[1], out.at[1, z, y], device(z, y + o, x, c)) for o in offsets],
    ]
    keeps = [pltpu.make_async_copy(own.at[s], out.at[s, z, y], local_sem.at[s]) for s in (0, 1)]
    for copy in keeps:
        copy.start()
    for copy in keeps:
        copy.wait()
    for at, o in zip(first[0], offsets):
        wires.landed(at, out.at[0, lax.rem(z + 4 - o, 4), y])
    line = out.at[0, :, y]
    low = [wires.send(line, line, device(z, y + o, x, c)) for o in offsets]
    for at, o in zip(first[1], offsets):
        wires.landed(at, out.at[1, z, lax.rem(y + 4 - o, 4)])
    line = out.at[1, z]
    high = [wires.send(line, line, device(z + o, y, x, c)) for o in offsets]
    for at, o in zip(low, offsets):
        wires.landed(at, out.at[0, :, lax.rem(y + 4 - o, 4)])
    for at, o in zip(high, offsets):
        wires.landed(at, out.at[1, lax.rem(z + 4 - o, 4)])
    wires.close()


def call_keys(own):
    hbm = pl.BlockSpec(memory_space=ANY)
    return pl.pallas_call(
        keys_kernel,
        out_shape=jax.ShapeDtypeStruct((2, 4, 4, HALF, 2 * HD), BF),
        in_specs=[hbm],
        out_specs=hbm,
        scratch_shapes=wire_scratch(12) + [pltpu.SemaphoreType.DMA((2,))],
        compiler_params=comm_params(5),
        name="gather_keys",
    )(own)


def key_grads_kernel(terms, out, rec_one, sums, rec_two, send_sem, recv_sem):
    z, y, xl, xh, c = place()
    x = xh * 2 + xl
    greet(plane_targets(z, y, x, c))
    wires = Wires(send_sem, recv_sem)
    offsets = (2, 1, 3)
    first = [[], []]
    for k, o in enumerate(offsets):
        to_y, to_z = lax.rem(y + o, 4), lax.rem(z + o, 4)
        first[0].append(
            wires.send(terms.at[0, :, to_y], rec_one.at[0, k], device(z, y + o, x, c))
        )
        first[1].append(wires.send(terms.at[1, to_z], rec_one.at[1, k], device(z + o, y, x, c)))
    second = [[], []]
    for s in (0, 1):
        for k in range(3):
            wires.landed(first[s][k], rec_one.at[s, k])
        for i in range(4):
            value = terms[0, i, y] if s == 0 else terms[1, z, i]
            value = value.astype(F32)
            for k in range(3):
                value = value + rec_one[s, k, i].astype(F32)
            sums[s, i] = value.astype(BF)
        for k, o in enumerate(offsets):
            if s == 0:
                src, target = sums.at[0, lax.rem(z + o, 4)], device(z + o, y, x, c)
            else:
                src, target = sums.at[1, lax.rem(y + o, 4)], device(z, y + o, x, c)
            second[s].append(wires.send(src, rec_two.at[s, k], target))
    for s in (0, 1):
        value = sums[s, z if s == 0 else y].astype(F32)
        for k in range(3):
            wires.landed(second[s][k], rec_two.at[s, k])
            value = value + rec_two[s, k].astype(F32)
        out[s] = value
    wires.close()


def call_key_grads(terms):
    vm = pl.BlockSpec(memory_space=pltpu.VMEM)
    return pl.pallas_call(
        key_grads_kernel,
        out_shape=jax.ShapeDtypeStruct((2, HALF, 2 * HD), F32),
        in_specs=[vm],
        out_specs=vm,
        scratch_shapes=[
            pltpu.VMEM((2, 3, 4, HALF, 2 * HD), BF),
            pltpu.VMEM((2, 4, HALF, 2 * HD), BF),
            pltpu.VMEM((2, 3, HALF, 2 * HD), BF),
        ]
        + wire_scratch(12),
        compiler_params=comm_params(6),
        name="sum_key_grads",
    )(terms)


def part_of(ref, order, zi, yi):
    return whole_piece(ref, order, zi, yi)


def grads_kernel(
    qkv, gate, down, out_grad, qkv_out, gate_out, down_out, out_out,
    qkv_rec, qkv_sum, qkv_rec_two, qkv_fin,
    gate_rec, gate_sum, gate_rec_two, gate_fin,
    down_rec, down_sum, down_rec_two, down_fin,
    out_rec, send_sem, recv_sem, out_send, out_recv, local_sem,
):
    z, y, xl, xh, c = place()
    x = xh * 2 + xl
    mine = xl * 2 + c
    pair = xh * 2 + 1 - xl
    spot = z * 4 + y
    every = slice(None)
    quad = [(x, 1 - c), (pair, c), (pair, 1 - c)]
    offsets = (2, 1, 3)
    keeps = z == mine
    from_x, from_c = xh * 2 + z // 2, lax.rem(z, 2)

    fixed = plane_targets(z, y, x, c) + [device(z, y, a, b) for a, b in quad]
    barrier = pltpu.get_barrier_semaphore()
    for target in fixed:
        pl.semaphore_signal(barrier, inc=1, device_id=target, device_id_type=MESH)
    for k in range(16):

        @pl.when(jnp.logical_not(keeps & (spot == k)))
        def _():
            pl.semaphore_signal(
                barrier,
                inc=1,
                device_id=device(jnp.int32(k // 4), jnp.int32(k % 4), from_x, from_c),
                device_id_type=MESH,
            )

    pl.semaphore_wait(barrier, len(fixed) + 16 - keeps.astype(jnp.int32))
    wires = Wires(send_sem, recv_sem)

    def second_axis(order, by):
        return device(z, y + by, x, c) if order == 0 else device(z + by, y, x, c)

    def first_axis(order, by):
        return device(z + by, y, x, c) if order == 0 else device(z, y + by, x, c)

    def run(order, by):
        return (every, lax.rem(y + by, 4)) if order == 0 else (lax.rem(z + by, 4), every)

    sets = [
        (gate, gate_rec, gate_sum, gate_rec_two, gate_fin),
        (down, down_rec, down_sum, down_rec_two, down_fin),
        (qkv, qkv_rec, qkv_sum, qkv_rec_two, qkv_fin),
    ]
    first, own = [], []
    for t, (grad, rec, total, _, _) in enumerate(sets):
        own.append([])
        first.append([])
        for o in (0, 1):
            first[t].append(
                [
                    wires.send(part_of(grad, o, *run(o, by)), rec.at[o, k], second_axis(o, by))
                    for k, by in enumerate(offsets)
                ]
            )
            copy = pltpu.make_async_copy(
                part_of(grad, o, *run(o, 0)), total.at[o], local_sem.at[t * 2 + o]
            )
            copy.start()
            own[t].append(copy)

    out_sends = []
    for k in range(16):
        to_y, to_xl, to_c = k // 4, (k // 2) % 2, k % 2
        src = out_grad.at[to_y, to_xl, :, pl.ds(to_c * WIDTH, WIDTH)]
        to_self = keeps & (y == to_y) & (xl == to_xl) & (c == to_c)
        copy = pltpu.make_async_remote_copy(
            src_ref=src,
            dst_ref=out_rec.at[spot],
            send_sem=out_send.at[k],
            recv_sem=out_recv.at[spot],
            device_id=device(mine, jnp.int32(to_y), xh * 2 + to_xl, jnp.int32(to_c)),
            device_id_type=MESH,
        )
        out_sends.append((copy, to_self))

        @pl.when(jnp.logical_not(to_self))
        def _():
            copy.start()

        @pl.when(to_self)
        def _():
            pltpu.make_async_copy(src, out_rec.at[spot], out_recv.at[spot]).start()

    second = []
    for t, (grad, rec, total, rec_two, _) in enumerate(sets):
        second.append([])
        for o in (0, 1):
            own[t][o].wait()
            for k in range(3):
                wires.landed(first[t][o][k], rec.at[o, k])

            def add(i, carry):
                value = total[o, i].astype(F32)
                for k in range(3):
                    value = value + rec[o, k, i].astype(F32)
                total[o, i] = value.astype(BF)
                return carry

            lax.fori_loop(0, 4, add, 0)
            at = z if o == 0 else y
            second[t].append(
                [
                    wires.send(
                        total.at[o, lax.rem(at + by, 4)], rec_two.at[o, k], first_axis(o, by)
                    )
                    for k, by in enumerate(offsets)
                ]
            )
    last = []
    for t, (_, _, total, rec_two, fin) in enumerate(sets):
        for o in (0, 1):
            for k in range(3):
                wires.landed(second[t][o][k], rec_two.at[o, k])
            value = total[o, z if o == 0 else y].astype(F32)
            for k in range(3):
                value = value + rec_two[o, k].astype(F32)
            fin[o] = value.astype(BF)
        if t == 1:
            to = fin.at[:, :, col_span(1 - c)]
            last.append([wires.send(to, down_out.at[c], device(z, y, x, 1 - c))])
            copy = pltpu.make_async_copy(
                fin.at[:, :, col_span(c)], down_out.at[c], local_sem.at[6]
            )
        else:
            result = gate_out if t == 0 else qkv_out
            last.append(
                [
                    wires.send(fin.at[b, lax.rem(a, 2)], result.at[mine], device(z, y, a, b))
                    for a, b in quad
                ]
            )
            copy = pltpu.make_async_copy(fin.at[c, xl], result.at[mine], local_sem.at[7 + t])
        copy.start()
        own.append(copy)
    total = None
    for k in range(16):
        pltpu.make_async_copy(out_rec.at[k], out_rec.at[k], out_recv.at[k]).wait()
        total = out_rec[k].astype(F32) if total is None else total + out_rec[k].astype(F32)
    out_out[...] = total
    for t, result in ((0, gate_out), (2, qkv_out)):
        for at, (a, b) in zip(last[t], quad):
            wires.landed(at, result.at[lax.rem(a, 2) * 2 + b])
    wires.landed(last[1][0], down_out.at[1 - c])
    for copy in own[3:]:
        copy.wait()
    for copy, to_self in out_sends:

        @pl.when(jnp.logical_not(to_self))
        def _():
            copy.wait_send()

    wires.close()


def call_grads(qkv, gate, down, out_grad):
    hbm = pl.BlockSpec(memory_space=ANY)
    vm = pl.BlockSpec(memory_space=pltpu.VMEM)

    def buffers(cols, depth):
        lead = (2, PIECE) if depth == 0 else (depth,)
        return [
            pltpu.VMEM((2, 3, 4) + lead + (cols,), BF),
            pltpu.VMEM((2, 4) + lead + (cols,), BF),
            pltpu.VMEM((2, 3) + lead + (cols,), BF),
            pltpu.VMEM((2,) + lead + (cols,), BF),
        ]

    qkv_cols, gate_cols = qkv.shape[-1], gate.shape[-1]
    return pl.pallas_call(
        grads_kernel,
        out_shape=(
            jax.ShapeDtypeStruct((4, PIECE, qkv_cols), BF),
            jax.ShapeDtypeStruct((4, PIECE, gate_cols), BF),
            jax.ShapeDtypeStruct((2, 2, PIECE, WIDTH), BF),
            jax.ShapeDtypeStruct((PIECE, WIDTH), F32),
        ),
        in_specs=[hbm] * 4,
        out_specs=(hbm, hbm, hbm, vm),
        scratch_shapes=buffers(qkv_cols, 0)
        + buffers(gate_cols, 0)
        + buffers(D, PIECE)
        + [pltpu.VMEM((16, PIECE, WIDTH), BF)]
        + wire_scratch(48)
        + wire_scratch(16)
        + [pltpu.SemaphoreType.DMA((10,))],
        compiler_params=comm_params(7),
        name="sum_weight_grads",
    )(qkv, gate, down, out_grad)


def total_kernel(terms, out, stage, rec, rec_two, rec_three, last, send_sem, recv_sem):
    z, y, xl, xh, c = place()
    x = xh * 2 + xl
    plane = [(a, b) for a in range(4) for b in range(4) if a or b]
    targets = [device(z + a, y + b, x, c) for a, b in plane] + line_targets(z, y, x, c)
    greet(targets)
    wires = Wires(send_sem, recv_sem)
    first = [
        wires.send(terms, rec.at[k], device(z + a, y + b, x, c)) for k, (a, b) in enumerate(plane)
    ]
    value = terms[...]
    for k, at in enumerate(first):
        wires.landed(at, rec.at[k])
        value = value + rec[k]
    stage[...] = value
    second = [
        wires.send(stage, rec_two.at[k], device(z, y, lax.rem(x + o, 4), c))
        for k, o in enumerate((1, 2, 3))
    ]
    for k, at in enumerate(second):
        wires.landed(at, rec_two.at[k])
        value = value + rec_two[k]
    gains = value[:16]
    square = value[16:] + jnp.sum(gains * gains)
    last[...] = square
    at = wires.send(last, rec_three, device(z, y, x, 1 - c))
    wires.landed(at, rec_three)
    out[:16] = gains
    out[16:] = square + rec_three[...]
    wires.close()


def call_total(terms):
    vm = pl.BlockSpec(memory_space=pltpu.VMEM)
    return pl.pallas_call(
        total_kernel,
        out_shape=jax.ShapeDtypeStruct((24, 128), F32),
        in_specs=[vm],
        out_specs=vm,
        scratch_shapes=[
            pltpu.VMEM((24, 128), F32),
            pltpu.VMEM((15, 24, 128), F32),
            pltpu.VMEM((3, 24, 128), F32),
            pltpu.VMEM((8, 128), F32),
            pltpu.VMEM((8, 128), F32),
        ]
        + wire_scratch(19),
        compiler_params=comm_params(8),
        name="total",
    )(terms)


def slot_of(half):
    return jnp.where(half < HALVES // 2, half, HALVES + HALVES // 2 - 1 - half)


def allowed_pairs(key_half, query_half, ends):
    keys = key_half * HALF + lax.broadcasted_iota(jnp.int32, (HALF, HALF), 0)
    queries = query_half * HALF + lax.broadcasted_iota(jnp.int32, (HALF, HALF), 1)
    same = keys <= queries
    for k in range(3):
        same = same & ((keys >= ends[k]) == (queries >= ends[k]))
    return same


def in_second(query_half, ends):
    queries = query_half * HALF + lax.broadcasted_iota(jnp.int32, (1, HALF), 1)
    return (queries >= ends[0]) & (queries < ends[1])


def forward_kernel(ends, queries, keys, out, log_out, tops, sums, mixed):
    z, y, _, _, _ = place()
    spot = z * 4 + y
    for s in (0, 1):
        half = spot if s == 0 else HALVES - 1 - spot
        tops[...] = jnp.full(tops.shape, NEVER, F32)
        sums[...] = jnp.zeros(sums.shape, F32)
        mixed[...] = jnp.zeros(mixed.shape, F32)

        def step(at, masked):
            pairs = keys[slot_of(at)]
            if masked:
                allowed = allowed_pairs(at, half, ends)
            for g in range(GROUP):
                cols = slice(g * HALF, (g + 1) * HALF)
                scores = jnp.dot(pairs, queries[s, :, cols], preferred_element_type=F32)
                if masked:
                    scores = jnp.where(allowed, scores, NEVER)
                old = tops[:, cols]
                top = jnp.maximum(old, jnp.max(scores, axis=0, keepdims=True))
                weights = jnp.exp(scores - top)
                if masked:
                    weights = jnp.where(allowed, weights, 0.0)
                shrink = jnp.exp(old - top)
                tops[:, cols] = top
                sums[:, cols] = sums[:, cols] * shrink + jnp.sum(weights, axis=0, keepdims=True)
                mixed[:, cols] = mixed[:, cols] * shrink + lax.dot_general(
                    pairs,
                    weights.astype(BF),
                    (((0,), (0,)), ((), ())),
                    preferred_element_type=F32,
                )

        def inner(at, carry):
            step(at, False)
            return carry

        lax.fori_loop(1, half, inner, 0)
        fits = in_second(half, ends)
        for g in range(GROUP):
            cols = slice(g * HALF, (g + 1) * HALF)
            tops[:, cols] = jnp.where(fits, tops[:, cols], NEVER)
            sums[:, cols] = jnp.where(fits, sums[:, cols], 0.0)
            mixed[:, cols] = jnp.where(fits, mixed[:, cols], 0.0)

        def edge(at, carry):
            step(at * half, True)
            return carry

        lax.fori_loop(0, jnp.where(half > 0, 2, 1), edge, 0)
        total = sums[...]
        out[s] = mixed[HD:, :] / total
        log_out[s] = tops[...] + jnp.log(total)


def call_forward(ends, queries, keys):
    vm = pl.BlockSpec(memory_space=pltpu.VMEM)
    cols = GROUP * HALF
    return pl.pallas_call(
        forward_kernel,
        out_shape=(
            jax.ShapeDtypeStruct((2, HD, cols), F32),
            jax.ShapeDtypeStruct((2, 1, cols), F32),
        ),
        in_specs=[pl.BlockSpec(memory_space=pltpu.SMEM), vm, vm],
        out_specs=(vm, vm),
        scratch_shapes=[
            pltpu.VMEM((1, cols), F32),
            pltpu.VMEM((1, cols), F32),
            pltpu.VMEM((2 * HD, cols), F32),
        ],
        compiler_params=pltpu.CompilerParams(vmem_limit_bytes=VMEM_LIMIT),
        name="attention",
    )(ends, queries, keys)


def backward_kernel(
    ends, queries, grads, query_rows, grad_rows, logs, delta, keys, query_back, key_back, terms, sums
):
    z, y, _, _, _ = place()
    spot = z * 4 + y
    terms[...] = jnp.zeros(terms.shape, F32)
    for s in (0, 1):
        half = spot if s == 0 else HALVES - 1 - spot
        sums[...] = jnp.zeros(sums.shape, F32)
        fits = in_second(half, ends)

        def step(at, masked):
            slot = slot_of(at)
            pairs = keys[slot]
            if masked:
                allowed = allowed_pairs(at, half, ends)
            added = None
            for g in range(GROUP):
                cols = slice(g * HALF, (g + 1) * HALF)
                scores = jnp.dot(pairs, queries[s, :, cols], preferred_element_type=F32)
                log_row = logs[s, :, cols]
                if not masked:
                    log_row = jnp.where(fits, log_row, -NEVER)
                probs = jnp.exp(scores - log_row)
                if masked:
                    probs = jnp.where(allowed, probs, 0.0)
                prob_grad = jnp.dot(pairs, grads[s, :, cols], preferred_element_type=F32)
                score_grad = (probs * (prob_grad - delta[s, :, cols])).astype(BF)
                sums[:, cols] += lax.dot_general(
                    pairs, score_grad, (((0,), (0,)), ((), ())), preferred_element_type=F32
                )
                term = jnp.dot(
                    score_grad, query_rows[s, g], preferred_element_type=F32
                ) + jnp.dot(probs.astype(BF), grad_rows[s, g], preferred_element_type=F32)
                added = term if added is None else added + term
            terms[slot] += added

        def inner(at, carry):
            step(at, False)
            return carry

        lax.fori_loop(1, half, inner, 0)

        def edge(at, carry):
            step(at * half, True)
            return carry

        lax.fori_loop(0, jnp.where(half > 0, 2, 1), edge, 0)
        query_back[s] = sums[:HD, :] * HD ** (-0.5)
    key_back[...] = terms[...].astype(BF)


def call_backward(ends, queries, grads, query_rows, grad_rows, logs, delta, keys):
    vm = pl.BlockSpec(memory_space=pltpu.VMEM)
    cols = GROUP * HALF
    return pl.pallas_call(
        backward_kernel,
        out_shape=(
            jax.ShapeDtypeStruct((2, HD, cols), F32),
            jax.ShapeDtypeStruct((HALVES, HALF, 2 * HD), BF),
        ),
        in_specs=[pl.BlockSpec(memory_space=pltpu.SMEM)] + [vm] * 7,
        out_specs=(vm, vm),
        scratch_shapes=[
            pltpu.VMEM((HALVES, HALF, 2 * HD), F32),
            pltpu.VMEM((2 * HD, cols), F32),
        ],
        compiler_params=pltpu.CompilerParams(vmem_limit_bytes=VMEM_LIMIT),
        name="attention_back",
    )(ends, queries, grads, query_rows, grad_rows, logs, delta, keys)


def rope_tables(position, head_size):
    half_size = head_size // 2
    column = jnp.arange(half_size, dtype=jnp.float32)
    inverse = jnp.exp(-(2.0 * column / head_size) * math.log(ROPE_THETA))
    wavelength = 2.0 * math.pi / inverse
    smooth = (OLD_CONTEXT / wavelength - LOW_FREQ) / (HIGH_FREQ - LOW_FREQ)
    blended = (1.0 - smooth) * inverse / ROPE_FACTOR + smooth * inverse
    inverse = jnp.where(
        wavelength < OLD_CONTEXT / HIGH_FREQ,
        inverse,
        jnp.where(wavelength > OLD_CONTEXT / LOW_FREQ, inverse / ROPE_FACTOR, blended),
    )
    angles = position.astype(jnp.float32)[:, None] * inverse[None, :]
    return (jnp.cos(angles), jnp.sin(angles))


def rotate(values, cosine, sine):
    half_size = values.shape[-1] // 2
    table_shape = (cosine.shape[0],) + (1,) * (values.ndim - 2) + (half_size,)
    cos_part = cosine.reshape(table_shape)
    sin_part = sine.reshape(table_shape)
    first_half = values[..., :half_size]
    second_half = values[..., half_size:]
    return jnp.concatenate(
        [
            first_half * cos_part - second_half * sin_part,
            second_half * cos_part + first_half * sin_part,
        ],
        axis=-1,
    )


def times(left, right, kind):
    return jnp.dot(left, right, preferred_element_type=F32).astype(kind)


def times_transpose(left, right, kind):
    return lax.dot_general(
        left, right, (((1,), (1,)), ((), ())), preferred_element_type=F32
    ).astype(kind)


def outer_rows(left, right, kind):
    return lax.dot_general(
        left, right, (((0,), (0,)), ((), ())), preferred_element_type=F32
    ).astype(kind)


def as_columns(rows):
    return rows.reshape(2, HALF, GROUP, HD).transpose(0, 3, 2, 1).reshape(2, HD, GROUP * HALF)


def as_heads(rows):
    return rows.reshape(2, HALF, GROUP, HD).transpose(0, 2, 1, 3)


def from_columns(columns):
    return columns.reshape(2, HD, GROUP, HALF).transpose(0, 3, 2, 1).reshape(LINE, GROUP * HD)


def adam(weight, moment, second, gradient, rate, decay):
    moment_next = BETA_ONE * moment + (1.0 - BETA_ONE) * gradient
    second_next = BETA_TWO * second + (1.0 - BETA_TWO) * gradient * gradient
    unbiased = moment_next / (1.0 - BETA_ONE**ADAM_STEP)
    divisor = jnp.sqrt(second_next / (1.0 - BETA_TWO**ADAM_STEP)) + ADAM_EPS
    return (weight - rate * (unbiased / divisor + decay * weight), moment_next, second_next)


def shards(
    block_input,
    out_grad,
    qkv_weight,
    qkv_moment,
    qkv_second,
    gate_up_weight,
    gate_up_moment,
    gate_up_second,
    out_weight,
    out_moment,
    out_second,
    down_weight,
    down_moment,
    down_second,
    norm_gains,
    gains_moment,
    gains_second,
    doc_lengths,
):
    z, y, xl, xh, c = place()
    x = xh * 2 + xl
    spot = z * 4 + y
    blocks = [block_of(at) for at in range(TOKENS // ROWS)]
    there = [(block, at) for at, block in enumerate(blocks)]
    home = [(at, block) for at, block in enumerate(blocks)]
    inputs = lax.ppermute(block_input, ("seq", "wide"), there)
    cotangent = lax.ppermute(out_grad, ("seq", "wide"), there)

    qkv_in = qkv_weight.astype(BF).transpose(1, 0, 2)
    gate_in = (
        gate_up_weight.astype(BF)
        .reshape(PIECE, 2, 16, 4, HD)
        .transpose(3, 0, 1, 2, 4)
        .reshape(4, PIECE, 2 * HIDDEN)
    )
    down_in = down_weight.astype(BF).reshape(2, ROWS // 2, WIDTH)
    gain_rows = jnp.concatenate([norm_gains, jnp.zeros((6, WIDTH), F32)], axis=0)
    inputs_all, cotangent_all, gains_all, qkv_whole, gate_whole, down_whole, out_whole = (
        call_gather(
            inputs, cotangent, gain_rows, qkv_in, gate_in, down_in, out_weight.astype(BF)
        )
    )
    qkv_low = qkv_whole.reshape(D, (GROUP + 2) * HD)
    gate_low = gate_whole.reshape(D, 2 * HIDDEN)
    down_low = down_whole.reshape(HIDDEN, D)
    out_low = out_whole.reshape(GROUP * HD, D)

    values = inputs_all.astype(F32)
    scale_one = lax.rsqrt(jnp.sum(values * values, axis=1, keepdims=True) / D + NORM_EPS)
    normed = (values * scale_one * gains_all[0:1, :]).astype(BF)
    projected = times(normed, qkv_low, F32)

    ends = jnp.cumsum(doc_lengths)
    local = jnp.arange(LINE, dtype=jnp.int32)
    half = jnp.where(local < HALF, spot, HALVES - 1 - spot)
    places = half * HALF + lax.rem(local, HALF)
    passed = (places[:, None] >= ends[None, :]).astype(jnp.int32)
    position = places - jnp.sum(passed * doc_lengths[None, :], axis=1)
    cosine, sine = rope_tables(position, HD)
    turned = rotate(
        projected[:, : (GROUP + 1) * HD].reshape(LINE, GROUP + 1, HD), cosine, sine
    ).astype(BF)
    queries = turned[:, :GROUP].reshape(LINE, GROUP * HD) * jnp.asarray(HD ** (-0.5), BF)
    own_keys = jnp.concatenate([turned[:, GROUP], projected[:, (GROUP + 1) * HD :].astype(BF)], axis=1)
    keys = call_keys(own_keys.reshape(2, HALF, 2 * HD)).reshape(HALVES, HALF, 2 * HD)

    blank = jnp.zeros((2, HD, GROUP * HALF), BF)
    query_columns = jnp.concatenate([as_columns(queries), blank], axis=1)
    mixed, logs = call_forward(ends, query_columns, keys)
    mixed_rows = from_columns(mixed)
    attended = mixed_rows.astype(BF)
    middle, scale_two, normed_two = call_middle(times(attended, out_low, BF), inputs, norm_gains)

    gate_up = times(normed_two, gate_low, F32)
    gate_part, up_part = gate_up[:, :HIDDEN], gate_up[:, HIDDEN:]
    sigmoid_gate = jax.nn.sigmoid(gate_part)
    hidden = (gate_part * sigmoid_gate * up_part).astype(BF)
    hidden_grad = times_transpose(cotangent_all, down_low, F32)
    gate_back = hidden_grad * up_part * sigmoid_gate * (1.0 + gate_part * (1.0 - sigmoid_gate))
    up_back = hidden_grad * gate_part * sigmoid_gate
    gate_up_back = jnp.concatenate([gate_back, up_back], axis=1).astype(BF)
    output, middle_grad, gain_two, middle_low = call_back(
        times_transpose(gate_up_back, gate_low, BF),
        times(hidden, down_low, BF),
        middle,
        scale_two,
        norm_gains,
        cotangent,
    )
    grad_down = outer_rows(hidden, cotangent_all, BF)
    grad_gate = outer_rows(normed_two, gate_up_back, BF)

    grad_out = outer_rows(attended, middle_low, BF)
    attended_grad = times_transpose(middle_low, out_low, BF)
    delta = jnp.sum(
        (attended_grad.astype(F32) * mixed_rows).reshape(LINE, GROUP, HD), axis=-1
    )
    delta = delta.reshape(2, HALF, GROUP).transpose(0, 2, 1).reshape(2, 1, GROUP * HALF)
    empty = jnp.zeros((2, GROUP, HALF, HD), BF)
    query_back, key_terms = call_backward(
        ends,
        query_columns,
        jnp.concatenate([blank, as_columns(attended_grad)], axis=1),
        jnp.concatenate([as_heads(queries), empty], axis=-1),
        jnp.concatenate([empty, as_heads(attended_grad)], axis=-1),
        logs,
        delta,
        keys,
    )
    key_grads = call_key_grads(key_terms.reshape(2, 4, 4, HALF, 2 * HD)).reshape(LINE, 2 * HD)
    turned_back = jnp.concatenate([from_columns(query_back), key_grads[:, :HD]], axis=1)
    turned_back = rotate(turned_back.reshape(LINE, GROUP + 1, HD), cosine, -sine)
    projected_back = jnp.concatenate(
        [turned_back.reshape(LINE, (GROUP + 1) * HD), key_grads[:, HD:]], axis=1
    ).astype(BF)
    grad_qkv = outer_rows(normed, projected_back, BF)
    scale_rows = lax.dynamic_slice_in_dim(scale_one, x * ROWS, ROWS, 0)
    input_grad, gain_one = call_last(
        times_transpose(projected_back, qkv_low, BF),
        inputs,
        jnp.broadcast_to(scale_rows, (ROWS, 128)),
        norm_gains,
        middle_grad,
    )
    qkv_sum, gate_sum, down_sum, out_sum = call_grads(
        grad_qkv.reshape(qkv_whole.shape),
        grad_gate.reshape(gate_whole.shape),
        grad_down.reshape(down_whole.shape),
        grad_out.reshape(out_whole.shape),
    )
    output = lax.ppermute(output, ("seq", "wide"), home)
    input_grad = lax.ppermute(input_grad, ("seq", "wide"), home)

    shares = (
        qkv_sum.transpose(1, 0, 2).astype(F32),
        gate_sum.reshape(4, PIECE, 2, 16, HD)
        .transpose(1, 2, 3, 0, 4)
        .reshape(gate_up_weight.shape)
        .astype(F32),
        out_sum,
        down_sum.reshape(down_weight.shape).astype(F32),
    )
    square = sum(
        jnp.sum(jnp.square(member.astype(F32))) for member in (qkv_sum, gate_sum, out_sum, down_sum)
    )
    terms = jnp.concatenate(
        [
            jnp.stack([gain_one[0], gain_two[0]]).reshape(16, 128),
            jnp.broadcast_to(square, (8, 128)),
        ],
        axis=0,
    )
    totals = call_total(terms)
    gains_grad = totals[:16].reshape(2, WIDTH)
    grad_norm = jnp.sqrt(totals[16, 0])
    factor = CLIP_NORM / jnp.maximum(grad_norm, CLIP_NORM)
    weights = (qkv_weight, gate_up_weight, out_weight, down_weight)
    moments = (qkv_moment, gate_up_moment, out_moment, down_moment)
    seconds = (qkv_second, gate_up_second, out_second, down_second)
    out_rate = OUTPUT_RATE * (TOKENS / (HQ * HD)) ** 0.5
    down_rate = DOWN_RATE * FF ** (-0.5)
    rates = (MATRIX_RATE, MATRIX_RATE, out_rate, down_rate)
    results = []
    for weight, moment, second, gradient, rate in zip(weights, moments, seconds, shares, rates):
        results.extend(adam(weight, moment, second, gradient * factor, rate, WEIGHT_DECAY))
    gains_new = adam(norm_gains, gains_moment, gains_second, gains_grad * factor, GAIN_RATE, 0.0)
    return (output, input_grad, grad_norm, *results, *gains_new)


def solution(mesh):
    placed = (
        P(("seq", "wide"), "narrow"),
        P(("seq", "wide"), "narrow"),
        P(("narrow", "seq"), "wide", None),
        P(("narrow", "seq"), "wide", None),
        P(("narrow", "seq"), "wide", None),
        P(("narrow", "seq"), None, "wide"),
        P(("narrow", "seq"), None, "wide"),
        P(("narrow", "seq"), None, "wide"),
        P(("wide", "seq"), "narrow"),
        P(("wide", "seq"), "narrow"),
        P(("wide", "seq"), "narrow"),
        P(("wide", "seq"), "narrow"),
        P(("wide", "seq"), "narrow"),
        P(("wide", "seq"), "narrow"),
        P(None, "narrow"),
        P(None, "narrow"),
        P(None, "narrow"),
        P(),
    )
    return jax.shard_map(
        shards,
        mesh=mesh,
        in_specs=placed,
        out_specs=(
            P(("seq", "wide"), "narrow"),
            P(("seq", "wide"), "narrow"),
            P(),
            P(("narrow", "seq"), "wide", None),
            P(("narrow", "seq"), "wide", None),
            P(("narrow", "seq"), "wide", None),
            P(("narrow", "seq"), None, "wide"),
            P(("narrow", "seq"), None, "wide"),
            P(("narrow", "seq"), None, "wide"),
            P(("wide", "seq"), "narrow"),
            P(("wide", "seq"), "narrow"),
            P(("wide", "seq"), "narrow"),
            P(("wide", "seq"), "narrow"),
            P(("wide", "seq"), "narrow"),
            P(("wide", "seq"), "narrow"),
            P(None, "narrow"),
            P(None, "narrow"),
            P(None, "narrow"),
        ),
        check_vma=False,
    )
```

time: 3610 us -> 666 us (0.18)
  waiting for transfers between devices: 3020 us -> 0.01 us
  Pallas kernels: 0 us -> 524 us
  blocking collectives: 305 us -> 0 us
  local copies, waits for them, and re-layouts: 80.3 us -> 36.9 us
  matrix products: 86.8 us -> 49.6 us
    psum x1 -> x0, waiting for transfers between devices: 1110 us -> none  [shards(): lax.psum(grad_qkv.astype(jnp.bfloat16), 'seq').astype(jnp.float32)]
    all_gather x8 -> x0, waiting for transfers between devices: 1070 us -> none  [the longest x1 356 us: shards(): lax.all_gather(gate_up_weight.astype(jnp.bfloat16), 'seq', axis=0, tiled=...]
    reduce_scatter x9 -> x0, waiting for transfers between devices: 836 us -> none  [the longest x1 706 us: shards(): lax.psum_scatter(key_terms, ('seq', 'narrow'), scatter_dimension=0, tiled...]
    pallas_call x0 -> x10, Pallas kernels: none -> 524 us  [the longest x1 136 us: call_gather(): pl.pallas_call(gather_kernel, out_shape=shapes, in_specs=[hbm] * 7, out_s...]
    psum x6 -> x0, blocking collectives: 257 us -> none  [the longest x1 153 us: shards(): gains_grad = lax.psum(jnp.stack([gain_one, gain_two]), ('seq', 'wide'))]
    all_gather x6 -> x0, blocking collectives: 48.2 us -> none  [the longest x4 39.2 us: widen(): return lax.all_gather(values, 'wide', axis=0, tiled=True)]
  transfers between devices with their start and end apart: 18 -> 4, of which waited for: 15 -> 0; matrix products, arithmetic and copies ran while one was open for 4% -> 3% of each run, Pallas kernels for 0% -> 0%
where the time goes in v1:
time: 666 us; the launch traced here: 656 us
  Pallas kernels  524 us (79%)
  matrix products  49.6 us (7%)
  local copies, waits for them, and re-layouts  36.9 us (6%)
  other arithmetic  27 us (4%)
  starting transfers between devices  12.2 us (2%)
    pallas_call x1, Pallas kernels, call_gather(): pl.pallas_call(gather_kernel, out_shape=shapes, in_specs=[hbm] * 7, out_s...  136 us
    pallas_call x1, Pallas kernels, call_grads(): pl.pallas_call(grads_kernel, out_shape=(jax.ShapeDtypeStruct((4, PIECE, q...  121 us
    pallas_call x1, Pallas kernels, call_backward(): pl.pallas_call(backward_kernel, out_shape=(jax.ShapeDtypeStruct((2, HD, c...  48.3 us
    pallas_call x1, Pallas kernels, call_back(): pl.pallas_call(back_kernel, out_shape=(jax.ShapeDtypeStruct((ROWS, WIDTH)...  45.9 us
    pallas_call x1, Pallas kernels, call_forward(): pl.pallas_call(forward_kernel, out_shape=(jax.ShapeDtypeStruct((2, HD, co...  45.4 us
    pallas_call x1, Pallas kernels, call_middle(): pl.pallas_call(middle_kernel, out_shape=(jax.ShapeDtypeStruct((ROWS, WIDT...  42.5 us
    pallas_call x1, Pallas kernels, call_keys(): pl.pallas_call(keys_kernel, out_shape=jax.ShapeDtypeStruct((2, 4, 4, HALF...  24.1 us
    pallas_call x1, Pallas kernels, call_key_grads(): pl.pallas_call(key_grads_kernel, out_shape=jax.ShapeDtypeStruct((2, HALF,...  23.3 us
  transfers between devices with their start and end apart: 4, of which 0 were waited for; matrix products, arithmetic and copies ran while one was open for 3% of the time, Pallas kernels for 0%

profile of v1, /device:TPU:1, one launch (start us, length us, event | category | flops | bytes accessed | tf_op | source)
XLA Modules:
  0.0 655.9 jit_solution(16939749388566571125)
XLA Ops:
  0.7 1.6 collective-permute-start
  2.3 1.6 collective-permute-start.1
  3.9 0.8 reduce-window.8
  4.7 0.7 select_reduce_fusion
  6.0 1.7 convert_element_type.89
  8.6 1.6 reshape.308.gate_in
  10.2 0.7 convert_element_type.90
  14.0 136.0 %gather_weights.1 = (bf16[512,2048]{1,0:T(8,128)(2,1)}, bf16[512,2048]{1,0:T(8,128)(2,1)}, f32[8,2048]{1,0:T(8,128)}, bf16[2,4,4,2,32,384]{5,4,3,2,1,0:T(8,128)(...) custom-call(bf16[128,1024]{1,0:T(8,128)(2,1)} %copy-done.1, ...), custom_call_target="tpu_custom_call" | custom-call | tf_op jit(solution)/shard_map/gather_weights/pallas_call | solution.py:570
  149.9 2.2 fusion
  152.2 0.8 slice.53
  153.0 2.6 fusion.6
  156.1 0.8 pad_maximum_fusion.8.own
  156.9 24.1 %gather_keys.1 = bf16[2,4,4,256,128]{4,3,2,1,0:T(8,128)(2,1)} custom-call(bf16[2,256,128]{2,1,0:T(8,128)(2,1)} %pad_maximum_fusion.8.own), custom_call_target="tpu_custom_call" | custom-call | tf_op jit(solution)/shard_map/gather_keys/pallas_call | solution.py:616
  181.4 0.8 concatenate.47.queries
  182.3 45.4 %attention.1 = (f32[2,64,1024]{2,1,0:T(8,128)}, f32[2,1,1024]{2,1,0:T(1,128)}) custom-call(s32[4]{0:T(128)} %bitcast.137, bf16[2,128,1024]{2,1,0:T(8,128)(2,1)} %concatenate.47.queries, bf16[32,256,128]{2,1,0:T(8,128)(2,1)} %bitcast.99), custom_call_target="tpu_custom_call" | custom-call | tf_op jit(solution)/shard_map/attention/pallas_call | solution.py:1012
  227.7 1.3 reshape.317
  230.2 2.1 convolution_convert_fusion.3.part
  232.3 42.5 %line_middle.1 = (f32[128,1024]{1,0:T(8,128)}, f32[128,128]{1,0:T(8,128)}, bf16[512,2048]{1,0:T(8,128)(2,1)}) custom-call(bf16[512,2048]{1,0:T(8,128)(2,1)} %convolution_convert_fusion.3.part, bf16[128,1024]{1,0:T(8,128)(2,1)} %copy-done.1, f32[2,1024]{1,0:T(2,128)} %gains.5), custom_call_target="tpu_custom_call" | custom-call | tf_op jit(solution)/shard_map/line_middle/pallas_call | solution.py:241
  274.8 7.7 %fusion.34 = f32[512,2048]{1,0:T(8,128)S(1)} fusion(bf16[512,2048]{1,0:T(8,128)(2,1)} %get-tuple-element.49, bf16[2048,2048]{1,0:T(8,128)(2,1)} %bitcast.140), kind=kOutput, calls=%fused_computation.92 | convolution fusion | flops 4294967296 | bytes 14680064 | tf_op jit(solution)/shard_map/dot_general | solution.py:1135
  282.6 4.1 multiply_convert_fusion.2
  286.7 7.2 %convolution_convert_fusion.5.part = bf16[512,2048]{1,0:T(8,128)(2,1)} fusion(bf16[2048,2048]{1,0:T(8,128)(2,1)S(1)} %bitcast.143, bf16[512,1024]{1,0:T(8,128)(2,1)} %get-tuple-element.136, bf16[512,1024]{1,0:T(8,128)(2,1)S(1)} %get-tuple-element.135), kind=kOutput, calls=%fused_computation.10 | convolution fusion | flops 4300210176 | bytes 12582912 | tf_op jit(solution)/shard_map/dot_general | solution.py:1139
  293.9 8.4 %convolution_convert_fusion = bf16[2048,2048]{1,0:T(8,128)(2,1)} fusion(bf16[512,2048]{1,0:T(8,128)(2,1)S(1)} %copy-done.35, bf16[512,1024]{1,0:T(8,128)(2,1)} %get-tuple-element.136, bf16[512,1024]{1,0:T(8,128)(2,1)S(1)} %get-tuple-element.135), kind=kOutput, calls=%fused_computation | convolution fusion | flops 4303355904 | bytes 12582912 | tf_op jit(solution)/shard_map/dot_general | solution.py:1145
  302.3 3.7 convolution_convert_fusion.2.part_two
  306.0 4.4 convolution_convert_fusion.1
  310.4 45.9 %line_back.1 = (bf16[128,1024]{1,0:T(8,128)(2,1)}, f32[128,1024]{1,0:T(8,128)}, f32[8,1024]{1,0:T(8,128)}, bf16[512,2048]{1,0:T(8,128)(2,1)}) custom-call(bf16[512,2048]{1,0:T(8,128)(2,1)} %convolution_convert_fusion.5.part, bf16[512,2048]{1,0:T(8,128)(2,1)} %convolution_convert_fusion.2.part_two, f32[128,1024]{1,0:T(8,128)} %get-tuple-element.51.middle, ...), custom_call_target="tpu_custom_call" | custom-call | tf_op jit(solution)/shard_map/line_back/pallas_call | solution.py:309
  356.4 3.4 convolution_convert_fusion.7
  359.8 0.8 bitcast_reduce_fusion
  361.2 0.9 copy.78
  362.2 1.1 reshape.321
  363.3 0.8 concatenate.52.grads
  364.1 1.0 concatenate.54.grad_rows
  365.8 0.9 concatenate.53.query_rows
  366.7 48.3 %attention_back.1 = (f32[2,64,1024]{2,1,0:T(8,128)}, bf16[32,256,128]{2,1,0:T(8,128)(2,1)}) custom-call(s32[4]{0:T(128)} %bitcast.138, bf16[2,128,1024]{2,1,0:T(8,128)(2,1)} %concatenate.47.queries, bf16[2,128,1024]{2,1,0:T(8,128)(2,1)} %concatenate.52.grads, bf16[2,4,256,128]{3,2,1,0:T(8,128)(2,1)} %concatenate.53.query_rows, ...), custom_call_target="tpu_custom_call" | custom-call | tf_op jit(solution)/shard_map/attention_back/pallas_call | solution.py:1085
  414.9 1.3 reshape.326
  416.7 23.3 %sum_key_grads.1 = f32[2,256,128]{2,1,0:T(8,128)} custom-call(bf16[2,4,4,256,128]{4,3,2,1,0:T(8,128)(2,1)} %bitcast.112), custom_call_target="tpu_custom_call" | custom-call | tf_op jit(solution)/shard_map/sum_key_grads/pallas_call | solution.py:667
  440.0 1.1 slice.81
  441.1 1.1 copy.92
  442.5 2.6 convolution_convert_fusion.6
  445.1 2.6 convolution_convert_fusion.4.part
  447.7 120.8 %sum_weight_grads.1 = (bf16[4,32,384]{2,1,0:T(8,128)(2,1)}, bf16[4,32,2048]{2,1,0:T(8,128)(2,1)}, bf16[2,2,32,1024]{3,2,1,0:T(8,128)(2,1)}, f32[32,1024]{1,0:T(8,128)}) custom-call(bf16[2,4,4,2,32,384]{5,4,3,2,1,0:T(8,128)(2,1)} %bitcast.121, bf16[2,4,4,2,32,2048]{5,4,3,2,1,0:T(8,128)(2,1)} %bitcast.101, bf16[4,4,64,2048]{3,2,1,0:T(8,128)(2,1)} %bitcast.104, ...), custom_call_target="tpu_custom_call" | custom-call | tf_op jit(solution)/shard_map/sum_weight_grads/pallas_call | solution.py:862
  568.6 1.6 fusion.14
  570.2 1.9 fusion.3
  572.1 1.5 multiply_reduce_fusion
  573.6 1.7 fusion.8
  576.2 22.2 %line_last.1 = (f32[128,1024]{1,0:T(8,128)}, f32[8,1024]{1,0:T(8,128)}) custom-call(bf16[512,2048]{1,0:T(8,128)(2,1)} %convolution_convert_fusion.4.part, bf16[128,1024]{1,0:T(8,128)(2,1)} %copy-done.1, f32[128,128]{1,0:T(8,128)} %broadcast_in_dim.12.scale, f32[2,1024]{1,0:T(2,128)} %gains.5, f32[128,1024]{1,0:T(8,128)} %get-tuple-element.58.middle_grad), custom_call_target="tpu_custom_call" | custom-call | tf_op jit(solution)/shard_map/line_last/pallas_call | solution.py:362
  598.4 0.8 slice.66
  599.2 0.8 slice.67
  603.2 15.3 %total.1 = f32[24,128]{1,0:T(8,128)} custom-call(f32[24,128]{1,0:T(8,128)} %concatenate.58.terms), custom_call_target="tpu_custom_call" | custom-call | tf_op jit(solution)/shard_map/total/pallas_call | solution.py:918
  618.4 1.2 slice.68
  620.4 0.8 convert_multiply_fusion.4
  621.3 0.8 mul.468
  622.2 3.1 copy.88
  625.3 3.3 mul.470
  628.6 5.4 collective-permute-start.3
  634.0 3.6 collective-permute-start.2
  637.6 1.2 multiply_subtract_fusion.2
  638.8 2.6 multiply_subtract_fusion.1
  641.6 5.2 multiply_subtract_fusion
  647.4 0.8 copy.89
  648.2 0.8 copy.90
  649.0 0.8 copy.91
  649.9 0.8 multiply_subtract_fusion.3
  650.7 1.7 copy.116
  652.4 1.9 copy.117
  (124 shorter events, 10.9 us)
Async XLA Ops:
  0.7 12.5 %collective-permute-start = (bf16[128,1024]{1,0:T(8,128)(2,1)}, bf16[128,1024]{1,0:T(8,128)(2,1)S(1)}, u32[]{:S(2)}, u32[]{:S(2)}) collective-permute-start(bf16[128,1024]{1,0:T(8,128)(2,1)} %param.18), channel_id=1, source_target_pairs={{0,0},{124,1},{1,4},{125,5},{4,8},{120,9},{5,12},{121,13},{8,16},{... | collective-permute-start | bytes 786440 | tf_op jit(solution)/shard_map/ppermute | solution.py:1196
  2.3 10.9 %collective-permute-start.1 = (bf16[128,1024]{1,0:T(8,128)(2,1)}, bf16[128,1024]{1,0:T(8,128)(2,1)S(1)}, u32[]{:S(2)}, u32[]{:S(2)}) collective-permute-start(bf16[128,1024]{1,0:T(8,128)(2,1)} %param.19), channel_id=1, source_target_pairs={{0,0},{124,1},{1,4},{125,5},{4,8},{120,9},{5,12},{121,13},{8,16},{... | collective-permute-start | bytes 786440 | tf_op jit(solution)/shard_map/ppermute | solution.py:1197
  4.7 3.9 copy-start.28
  8.3 1.9 copy-start.3
  8.3 2.6 copy-start.14
  8.3 3.2 copy-start.17
  8.3 3.9 copy-start.21
  8.6 4.3 copy-start.31
  13.2 0.7 copy-start.1
  13.2 0.8 copy-start.11
  149.9 3.1 copy-start.6
  152.2 3.4 copy-start.29
  229.0 1.2 copy-start.13
  274.8 7.7 %copy-start.32 = (bf16[4,4,64,2048]{3,2,1,0:T(8,128)(2,1)S(1)}, bf16[4,4,64,2048]{3,2,1,0:T(8,128)(2,1)}, u32[]{:S(2)}) copy-start(bf16[4,4,64,2048]{3,2,1,0:T(8,128)(2,1)} %get-tuple-element.43) | copy-start | bytes 12582916
  274.8 7.7 %copy-start.34 = (bf16[512,2048]{1,0:T(8,128)(2,1)S(1)}, bf16[512,2048]{1,0:T(8,128)(2,1)}, u32[]{:S(2)}) copy-start(bf16[512,2048]{1,0:T(8,128)(2,1)} %get-tuple-element.42) | copy-start | bytes 6291460
  274.8 11.9 %slice-start = ((s8[8388608]{0:T(1024)(128)(4,1)}), s8[4194304]{0:T(1024)(128)(4,1)S(1)}, s32[]{:S(2)}) async-start(s8[8388608]{0:T(1024)(128)(4,1)} %bitcast.141), calls=%async_computation | async-start | bytes 8388608
  282.6 4.1 slice-start.1
  286.7 7.2 %copy-start.35 = (bf16[512,2048]{1,0:T(8,128)(2,1)S(1)}, bf16[512,2048]{1,0:T(8,128)(2,1)}, u32[]{:S(2)}) copy-start(bf16[512,2048]{1,0:T(8,128)(2,1)} %get-tuple-element.49) | copy-start | bytes 6291460
  293.9 8.4 %copy-start.33 = (bf16[4,4,64,2048]{3,2,1,0:T(8,128)(2,1)S(1)}, bf16[4,4,64,2048]{3,2,1,0:T(8,128)(2,1)}, u32[]{:S(2)}) copy-start(bf16[4,4,64,2048]{3,2,1,0:T(8,128)(2,1)} %get-tuple-element.43) | copy-start | bytes 12582916
  356.4 3.4 copy-start.2
  440.0 2.4 copy-start.30
  442.5 2.6 copy-start.8
  568.6 51.8 %copy-start.12 = (bf16[2,2,32,1024]{3,2,1,0:T(8,128)(2,1)S(1)}, bf16[2,2,32,1024]{3,2,1,0:T(8,128)(2,1)}, u32[]{:S(2)}) copy-start(bf16[2,2,32,1024]{3,2,1,0:T(8,128)(2,1)} %get-tuple-element.65) | copy-start | bytes 786436
  573.6 47.6 %copy-start.7 = (bf16[4,32,2048]{2,1,0:T(8,128)(2,1)S(1)}, bf16[4,32,2048]{2,1,0:T(8,128)(2,1)}, u32[]{:S(2)}) copy-start(bf16[4,32,2048]{2,1,0:T(8,128)(2,1)} %get-tuple-element.63) | copy-start | bytes 1572868
  625.3 12.3 %copy-start.15 = (f32[32,4,384]{2,1,0:T(4,128)S(1)}, f32[32,4,384]{2,1,0:T(4,128)}, u32[]{:S(2)}) copy-start(f32[32,4,384]{2,1,0:T(4,128)} %param.20) | copy-start | bytes 589828
  625.3 12.3 %copy-start.20 = (bf16[4,32,384]{2,1,0:T(8,128)(2,1)S(1)}, bf16[4,32,384]{2,1,0:T(8,128)(2,1)}, u32[]{:S(2)}) copy-start(bf16[4,32,384]{2,1,0:T(8,128)(2,1)} %get-tuple-element.62) | copy-start | bytes 294916
  625.3 13.5 %copy-start.4 = (f32[128,1024]{1,0:T(8,128)S(1)}, f32[128,1024]{1,0:T(8,128)}, u32[]{:S(2)}) copy-start(f32[128,1024]{1,0:T(8,128)} %param.29) | copy-start | bytes 1572868
  625.3 13.5 %copy-start.5 = (f32[2,2,32,1024]{3,2,1,0:T(8,128)S(1)}, f32[2,2,32,1024]{3,2,1,0:T(8,128)}, u32[]{:S(2)}) copy-start(f32[2,2,32,1024]{3,2,1,0:T(8,128)} %convert_multiply_fusion.4) | copy-start | bytes 1572868
  625.3 13.5 %copy-start.16 = (f32[128,1024]{1,0:T(8,128)S(1)}, f32[128,1024]{1,0:T(8,128)}, u32[]{:S(2)}) copy-start(f32[128,1024]{1,0:T(8,128)} %param.30) | copy-start | bytes 1572868
  628.6 22.1 %collective-permute-start.3 = (f32[128,1024]{1,0:T(8,128)}, f32[128,1024]{1,0:T(8,128)}, u32[]{:S(2)}, u32[]{:S(2)}) collective-permute-start(f32[128,1024]{1,0:T(8,128)} %get-tuple-element.59), channel_id=1, source_target_pairs={{0,0},{1,124},{4,1},{5,125},{8,4},{9,120},{12,5},{13,121},{16,8},{... | collective-permute-start | bytes 1572872 | tf_op jit(solution)/shard_map/ppermute | solution.py:1302
  634.0 16.7 %collective-permute-start.2 = (bf16[128,1024]{1,0:T(8,128)(2,1)}, bf16[128,1024]{1,0:T(8,128)(2,1)}, u32[]{:S(2)}, u32[]{:S(2)}) collective-permute-start(bf16[128,1024]{1,0:T(8,128)(2,1)} %get-tuple-element.53), channel_id=1, source_target_pairs={{0,0},{1,124},{4,1},{5,125},{8,4},{9,120},{12,5},{13,121},{16,8},{... | collective-permute-start | bytes 786440 | tf_op jit(solution)/shard_map/ppermute | solution.py:1301
  638.8 2.7 copy-start
  638.8 2.6 copy-start.9
  638.8 2.6 copy-start.10
  641.5 5.3 copy-start.25
  641.5 5.3 copy-start.22
  641.5 5.3 copy-start.26
  641.5 5.3 copy-start.27
  641.5 8.3 %copy-start.18 = (f32[32,1024]{1,0:T(8,128)S(1)}, f32[32,1024]{1,0:T(8,128)}, u32[]{:S(2)}) copy-start(f32[32,1024]{1,0:T(8,128)} %param.26) | copy-start | bytes 393220
  641.5 8.3 %copy-start.19 = (f32[32,1024]{1,0:T(8,128)S(1)}, f32[32,1024]{1,0:T(8,128)}, u32[]{:S(2)}) copy-start(f32[32,1024]{1,0:T(8,128)} %get-tuple-element.64) | copy-start | bytes 393220
  641.5 8.3 %copy-start.23 = (f32[32,1024]{1,0:T(8,128)S(1)}, f32[32,1024]{1,0:T(8,128)}, u32[]{:S(2)}) copy-start(f32[32,1024]{1,0:T(8,128)} %param.27) | copy-start | bytes 393220
  641.5 8.3 %copy-start.24 = (f32[32,1024]{1,0:T(8,128)S(1)}, f32[32,1024]{1,0:T(8,128)}, u32[]{:S(2)}) copy-start(f32[32,1024]{1,0:T(8,128)} %param.28) | copy-start | bytes 393220

commit v2 on v1

v2 whole, which is shorter than its diff:
```python
import functools
import math

import jax
import jax.numpy as jnp
from jax import lax
from jax.experimental import pallas as pl
from jax.experimental.pallas import tpu as pltpu
from jax.sharding import PartitionSpec as P

D = 2048
HQ = 32
HD = 64
FF = 8192
ADAM_STEP = 10


NORM_EPS = 1e-05
ADAM_EPS = 1e-08
BETA_ONE = 0.9
BETA_TWO = 0.95
WEIGHT_DECAY = 0.1
MATRIX_RATE = 0.01
OUTPUT_RATE = 0.9
DOWN_RATE = 3.0
GAIN_RATE = 2.5
CLIP_NORM = 1.0
ROPE_THETA = 500000.0
ROPE_FACTOR = 32.0
LOW_FREQ = 1.0
HIGH_FREQ = 4.0
OLD_CONTEXT = 8192.0

TOKENS = 8192
HALF = 256
HALVES = TOKENS // HALF
ROWS = 128
LINE = 512
WIDTH = 1024
GROUP = 4
PIECE = 32
HIDDEN = 1024
MESH = pl.DeviceIdType.MESH
ANY = pl.ANY
BF = jnp.bfloat16
F32 = jnp.float32
VMEM_LIMIT = 56 * 1024 * 1024
NEVER = -1e30


def place():
    seq = lax.axis_index("seq")
    return (
        seq // 8,
        lax.rem(seq // 2, 4),
        lax.rem(seq, 2),
        lax.axis_index("wide"),
        lax.axis_index("narrow"),
    )


def device(z, y, x, c):
    return (lax.rem(z, 4) * 8 + lax.rem(y, 4) * 2 + lax.rem(x, 2), c, x // 2)


class Wires:
    def __init__(self, send_sem, recv_sem):
        self.send_sem, self.recv_sem, self.used, self.sent = send_sem, recv_sem, 0, []

    def send(self, src, dst, target, start=True):
        at = self.used
        self.used += 1
        copy = pltpu.make_async_remote_copy(
            src_ref=src,
            dst_ref=dst,
            send_sem=self.send_sem.at[at],
            recv_sem=self.recv_sem.at[at],
            device_id=target,
            device_id_type=MESH,
        )
        if start:
            copy.start()
        self.sent.append(copy)
        return at

    def landed(self, at, region):
        pltpu.make_async_copy(region, region, self.recv_sem.at[at]).wait()

    def close(self):
        for copy in self.sent:
            copy.wait_send()


def greet(targets):
    barrier = pltpu.get_barrier_semaphore()
    for target in targets:
        pl.semaphore_signal(barrier, inc=1, device_id=target, device_id_type=MESH)
    pl.semaphore_wait(barrier, len(targets))


def line_targets(z, y, x, c):
    return [device(z, y, lax.rem(x + o, 4), c) for o in (1, 2, 3)] + [device(z, y, x, 1 - c)]


def plane_targets(z, y, x, c):
    return [device(z + o, y, x, c) for o in (1, 2, 3)] + [device(z, y + o, x, c) for o in (1, 2, 3)]


def wire_scratch(count):
    return [pltpu.SemaphoreType.DMA((count,)), pltpu.SemaphoreType.DMA((count,))]


def comm_params(number):
    return pltpu.CompilerParams(
        collective_id=number, has_side_effects=True, vmem_limit_bytes=VMEM_LIMIT
    )


def row_span(at):
    return pl.ds(pl.multiple_of(at * ROWS, ROWS), ROWS)


def col_span(c):
    return pl.ds(pl.multiple_of(c * WIDTH, WIDTH), WIDTH)


def gather_sends(wires, own, out, here):
    z, y, x, c = here
    spot = out.at[row_span(x), col_span(c)]
    across = {o: wires.send(own, spot, device(z, y, lax.rem(x + o, 4), c)) for o in (2, 1, 3)}
    return across, wires.send(own, spot, device(z, y, x, 1 - c))


def gather_relay(wires, numbers, out, here):
    z, y, x, c = here
    across, direct = numbers
    relays = []
    for o in (1, 3, 2):
        rows = row_span(lax.rem(x + 4 - o, 4))
        spot = out.at[rows, col_span(c)]
        wires.landed(across[o], spot)
        relays.append((wires.send(spot, spot, device(z, y, x, 1 - c)), rows))
    wires.landed(direct, out.at[row_span(x), col_span(1 - c)])
    for at, rows in relays:
        wires.landed(at, out.at[rows, col_span(1 - c)])


FOLD_ORDER = (2, 1, 3, 0)


def fold_sends(wires, part, folded, here):
    z, y, x, c = here
    return [
        wires.send(
            part.at[row_span(lax.rem(x + o, 4)), col_span(1 - c)],
            folded.at[k],
            device(z, y, x, 1 - c),
        )
        for k, o in enumerate(FOLD_ORDER)
    ]


def fold_moves(wires, numbers, part, folded, leaving, arriving, here, total):
    z, y, x, c = here
    moves = []
    for k, o in enumerate(FOLD_ORDER):
        wires.landed(numbers[k], folded.at[k])
        both = part[row_span(lax.rem(x + o, 4)), col_span(c)].astype(F32) + folded[k].astype(F32)
        if o:
            leaving[k] = both.astype(BF)
            moves.append(
                wires.send(leaving.at[k], arriving.at[k], device(z, y, lax.rem(x + o, 4), c))
            )
        else:
            total[...] = both
    return moves


def fold_finish(wires, moves, arriving, total):
    for k, at in enumerate(moves):
        wires.landed(at, arriving.at[k])
    total[...] = (
        total[...]
        + arriving[0].astype(F32)
        + arriving[1].astype(F32)
        + arriving[2].astype(F32)
    )


def fold_scratch():
    return [
        pltpu.VMEM((4, ROWS, WIDTH), BF),
        pltpu.VMEM((3, ROWS, WIDTH), BF),
        pltpu.VMEM((3, ROWS, WIDTH), BF),
        pltpu.VMEM((ROWS, WIDTH), F32),
    ]


def both_cores(wires, mine, theirs, value, here):
    z, y, x, c = here
    mine[...] = jnp.broadcast_to(value, mine.shape)
    at = wires.send(mine, theirs, device(z, y, x, 1 - c))
    wires.landed(at, theirs)
    return value + theirs[:, :1]


EVERY = slice(None)


def first_device(here, order, by):
    z, y, x, c = here
    return device(z + by, y, x, c) if order == 0 else device(z, y + by, x, c)


def second_device(here, order, by):
    z, y, x, c = here
    return device(z, y + by, x, c) if order == 0 else device(z + by, y, x, c)


def first_at(here, order, by=0):
    return lax.rem((here[0] if order == 0 else here[1]) + by, 4)


def run_of(ref, here, order, by, sub=None):
    z, y, _, _ = here
    zi, yi = (EVERY, lax.rem(y + by, 4)) if order == 0 else (lax.rem(z + by, 4), EVERY)
    if len(ref.shape) == 6:
        return ref.at[order, zi, yi] if sub is None else ref.at[order, zi, yi, sub]
    rows = ref.shape[2] // 2
    if sub is None:
        return ref.at[zi, yi, pl.ds(order * rows, rows)]
    return ref.at[zi, yi, pl.ds(order * rows + sub * (rows // 2), rows // 2)]


def spot_of(line, order, at, sub=None):
    if sub is None:
        return line.at[order, at]
    if len(line.shape) == 5:
        return line.at[order, at, sub]
    rows = line.shape[2] // 2
    return line.at[order, at, pl.ds(sub * rows, rows)]


class LineGather:
    def __init__(self, wires, line, here):
        self.wires, self.line, self.here = wires, line, here

    def start(self):
        self.numbers = []
        for o in (0, 1):
            spot = spot_of(self.line, o, first_at(self.here, o))
            self.numbers.append(
                [self.wires.send(spot, spot, first_device(self.here, o, by)) for by in (1, 3)]
            )

    def relay(self):
        relays = []
        for o in (0, 1):
            sends = []
            for sub, by in enumerate((1, 3)):
                at = first_at(self.here, o, 4 - by)
                self.wires.landed(self.numbers[o][sub], spot_of(self.line, o, at))
                spot = spot_of(self.line, o, at, sub)
                sends.append(self.wires.send(spot, spot, first_device(self.here, o, by)))
            relays.append(sends)
        self.numbers = relays

    def finish(self):
        for o in (0, 1):
            for sub in (0, 1):
                at = first_at(self.here, o, 2)
                self.wires.landed(self.numbers[o][sub], spot_of(self.line, o, at, sub))


class PlaneGather:
    def __init__(self, wires, line, whole, here, local_sem, at):
        self.wires, self.line, self.whole, self.here = wires, line, whole, here
        self.kept = [
            pltpu.make_async_copy(line.at[o], run_of(whole, here, o, 0), local_sem.at[at + o])
            for o in (0, 1)
        ]

    def start(self):
        self.numbers = []
        for o in (0, 1):
            spot = run_of(self.whole, self.here, o, 0)
            self.numbers.append(
                [
                    self.wires.send(self.line.at[o], spot, second_device(self.here, o, by))
                    for by in (1, 3)
                ]
            )
        for copy in self.kept:
            copy.start()

    def relay(self):
        relays = []
        for o in (0, 1):
            sends = []
            for sub, by in enumerate((1, 3)):
                self.wires.landed(self.numbers[o][sub], run_of(self.whole, self.here, o, 4 - by))
                spot = run_of(self.whole, self.here, o, 4 - by, sub)
                sends.append(self.wires.send(spot, spot, second_device(self.here, o, by)))
            relays.append(sends)
        self.numbers = relays

    def finish(self):
        for o in (0, 1):
            for sub in (0, 1):
                self.wires.landed(
                    self.numbers[o][sub], run_of(self.whole, self.here, o, 2, sub)
                )
        for copy in self.kept:
            copy.wait()


OFFSETS = (2, 1, 3)


class PlaneSum:
    def __init__(self, wires, terms, buffers, here, local_sem, at):
        self.wires, self.terms, self.here = wires, terms, here
        self.rec, self.total, self.rec_two, self.fin = buffers
        self.kept = [
            pltpu.make_async_copy(
                run_of(terms, here, o, 0), self.total.at[o], local_sem.at[at + o]
            )
            for o in (0, 1)
        ]

    def start(self):
        self.numbers = []
        for o in (0, 1):
            self.numbers.append(
                [
                    self.wires.send(
                        run_of(self.terms, self.here, o, by),
                        self.rec.at[o, k],
                        second_device(self.here, o, by),
                    )
                    for k, by in enumerate(OFFSETS)
                ]
            )
        for copy in self.kept:
            copy.start()

    def middle(self):
        moves = []
        for o in (0, 1):
            self.kept[o].wait()
            for k in range(3):
                self.wires.landed(self.numbers[o][k], self.rec.at[o, k])

            def add(i, carry):
                value = self.total[o, i].astype(F32)
                for k in range(3):
                    value = value + self.rec[o, k, i].astype(F32)
                self.total[o, i] = value.astype(BF)
                return carry

            lax.fori_loop(0, 4, add, 0)
            moves.append(
                [
                    self.wires.send(
                        self.total.at[o, first_at(self.here, o, by)],
                        self.rec_two.at[o, k],
                        first_device(self.here, o, by),
                    )
                    for k, by in enumerate(OFFSETS)
                ]
            )
        self.numbers = moves

    def finish(self):
        for o in (0, 1):
            for k in range(3):
                self.wires.landed(self.numbers[o][k], self.rec_two.at[o, k])
            value = self.total[o, first_at(self.here, o)].astype(F32)
            for k in range(3):
                value = value + self.rec_two[o, k].astype(F32)
            self.fin[o] = value.astype(self.fin.dtype)


def sum_buffers(piece, kind):
    return [
        pltpu.VMEM((2, 3, 4) + piece, BF),
        pltpu.VMEM((2, 4) + piece, BF),
        pltpu.VMEM((2, 3) + piece, BF),
        pltpu.VMEM((2,) + piece, kind),
    ]


def worked_at(p, x):
    block = p * 4 + lax.rem(x, 2) * 2 + x // 2
    half = block // 2
    low = half < HALVES // 2
    return jnp.where(low, half, HALVES - 1 - half), lax.rem(block, 2) + jnp.where(low, 0, 2)


def lives_at(p, x):
    block = jnp.where(x < 2, 2 * p + x, 2 * (HALVES - 1 - p) + x - 2)
    rest = lax.rem(block, 4)
    return block // 4, lax.rem(rest, 2) * 2 + rest // 2


class Posting:
    def __init__(self, here, to, come, send_sem, recv_sem):
        z, y, x, c = here
        self.here, self.c = here, c
        self.target = device(to[0] // 4, lax.rem(to[0], 4), to[1], c)
        self.source = device(come[0] // 4, lax.rem(come[0], 4), come[1], c)
        self.same = (to[0] == z * 4 + y) & (to[1] == x)
        self.send_sem, self.recv_sem, self.sent = send_sem, recv_sem, []

    def greet(self, barrier):
        @pl.when(jnp.logical_not(self.same))
        def _():
            pl.semaphore_signal(barrier, inc=1, device_id=self.source, device_id_type=MESH)

        return 1 - self.same.astype(jnp.int32)

    def send(self, src, dst):
        at = len(self.sent)
        copy = pltpu.make_async_remote_copy(
            src_ref=src,
            dst_ref=dst,
            send_sem=self.send_sem.at[at],
            recv_sem=self.recv_sem.at[at],
            device_id=self.target,
            device_id_type=MESH,
        )
        self.sent.append(copy)

        @pl.when(jnp.logical_not(self.same))
        def _():
            copy.start()

        @pl.when(self.same)
        def _():
            pltpu.make_async_copy(src, dst, self.recv_sem.at[at]).start()

        return at

    def landed(self, at, region):
        pltpu.make_async_copy(region, region, self.recv_sem.at[at]).wait()

    def close(self):
        @pl.when(jnp.logical_not(self.same))
        def _():
            for copy in self.sent:
                copy.wait_send()


def quad_of(xl, xh, x, c):
    pair = xh * 2 + 1 - xl
    return [(x, 1 - c), (pair, c), (pair, 1 - c)]


def start_kernel(
    block_input, out_grad, gain_rows, qkv_in, gate_in, down_in,
    inputs, cotangent, inputs_all, gains_all, qkv_all, qkv_line, gate_line, down_line,
    send_sem, recv_sem, post_send, post_recv, local_sem,
):
    z, y, xl, xh, c = place()
    x = xh * 2 + xl
    here = (z, y, x, c)
    mine = xl * 2 + c
    quad = quad_of(xl, xh, x, c)
    fixed = line_targets(z, y, x, c) + [device(z, y, *quad[2])]
    fixed += [first_device(here, o, by) for o in (0, 1) for by in (1, 3)]
    barrier = pltpu.get_barrier_semaphore()
    post = Posting(here, worked_at(z * 4 + y, x), lives_at(z * 4 + y, x), post_send, post_recv)
    for target in fixed:
        pl.semaphore_signal(barrier, inc=1, device_id=target, device_id_type=MESH)
    extra = post.greet(barrier)
    pl.semaphore_wait(barrier, len(fixed) + extra)
    wires = Wires(send_sem, recv_sem)
    kept = []

    def keep(src, dst):
        copy = pltpu.make_async_copy(src, dst, local_sem.at[len(kept)])
        copy.start()
        kept.append(copy)

    input_at = post.send(block_input, inputs)
    cotangent_at = post.send(out_grad, cotangent)

    at_here = jnp.where(c == 0, z, y)
    swaps = []
    for given, line in ((qkv_in, qkv_line), (gate_in, gate_line)):
        swaps.append(
            [
                wires.send(
                    given.at[lax.rem(to, 2) * 2 + core],
                    line.at[c, at_here, xl],
                    device(z, y, to, core),
                )
                for to, core in quad
            ]
        )
        keep(given.at[mine], line.at[c, at_here, xl])
    down_swap = [
        wires.send(
            down_in.at[1 - c, pl.ds(o * PIECE, PIECE)],
            down_line.at[o, first_at(here, o), :, col_span(c)],
            device(z, y, x, 1 - c),
        )
        for o in (0, 1)
    ]
    for o in (0, 1):
        keep(
            down_in.at[c, pl.ds(o * PIECE, PIECE)],
            down_line.at[o, first_at(here, o), :, col_span(c)],
        )
    keep(gain_rows, gains_all.at[:, col_span(c)])
    gain_at = wires.send(gain_rows, gains_all.at[:, col_span(c)], device(z, y, x, 1 - c))

    post.landed(input_at, inputs)
    keep(inputs, inputs_all.at[row_span(x), col_span(c)])
    input_numbers = gather_sends(wires, inputs, inputs_all, here)

    def swapped(line, numbers):
        for at, (from_x, from_c) in zip(numbers, quad):
            spot = line.at[from_c, jnp.where(from_c == 0, z, y), lax.rem(from_x, 2)]
            wires.landed(at, spot)

    for copy in kept:
        copy.wait()
    swapped(qkv_line, swaps[0])
    qkv = LineGather(wires, qkv_line, here)
    qkv.start()
    swapped(gate_line, swaps[1])
    gate = LineGather(wires, gate_line, here)
    gate.start()
    for o in (0, 1):
        wires.landed(
            down_swap[o], down_line.at[o, first_at(here, o), :, col_span(1 - c)]
        )
    down = LineGather(wires, down_line, here)
    down.start()
    qkv.relay()
    qkv.finish()
    qkv_plane = PlaneGather(wires, qkv_line, qkv_all, here, local_sem, 8)
    qkv_plane.start()
    gate.relay()
    down.relay()
    qkv_plane.relay()
    gather_relay(wires, input_numbers, inputs_all, here)
    wires.landed(gain_at, gains_all.at[:, col_span(1 - c)])
    qkv_plane.finish()
    gate.finish()
    down.finish()
    post.landed(cotangent_at, cotangent)
    post.close()
    wires.close()


def call_start(block_input, out_grad, gain_rows, qkv_in, gate_in, down_in):
    qkv_cols, gate_cols = qkv_in.shape[2], gate_in.shape[2]
    shapes = (
        jax.ShapeDtypeStruct((ROWS, WIDTH), BF),
        jax.ShapeDtypeStruct((ROWS, WIDTH), BF),
        jax.ShapeDtypeStruct((LINE, D), BF),
        jax.ShapeDtypeStruct((8, D), F32),
        jax.ShapeDtypeStruct((2, 4, 4, 2, PIECE, qkv_cols), BF),
        jax.ShapeDtypeStruct((2, 4, 2, PIECE, qkv_cols), BF),
        jax.ShapeDtypeStruct((2, 4, 2, PIECE, gate_cols), BF),
        jax.ShapeDtypeStruct((2, 4, PIECE, D), BF),
    )
    hbm = pl.BlockSpec(memory_space=ANY)
    return pl.pallas_call(
        start_kernel,
        out_shape=shapes,
        in_specs=[hbm] * 6,
        out_specs=(hbm,) * len(shapes),
        scratch_shapes=wire_scratch(64) + wire_scratch(2) + [pltpu.SemaphoreType.DMA((10,))],
        compiler_params=comm_params(1),
        name="start",
    )(block_input, out_grad, gain_rows, qkv_in, gate_in, down_in)


def middle_kernel(
    part, inputs, gains, down_line, middle_out, scale_out, out, down_all,
    folded, leaving, arriving, total, mine, theirs, own, send_sem, recv_sem, local_sem,
):
    z, y, xl, xh, c = place()
    x = xh * 2 + xl
    here = (z, y, x, c)
    greet(
        line_targets(z, y, x, c)
        + [second_device(here, o, by) for o in (0, 1) for by in (1, 3)]
    )
    wires = Wires(send_sem, recv_sem)
    numbers = fold_sends(wires, part, folded, here)
    down = PlaneGather(wires, down_line, down_all, here, local_sem, 1)
    down.start()
    moves = fold_moves(wires, numbers, part, folded, leaving, arriving, here, total)
    fold_finish(wires, moves, arriving, total)
    middle = total[...] + inputs[...].astype(F32)
    middle_out[...] = middle
    square = both_cores(
        wires, mine, theirs, jnp.sum(middle * middle, axis=1, keepdims=True), here
    )
    scale = lax.rsqrt(square / D + NORM_EPS)
    scale_out[...] = jnp.broadcast_to(scale, scale_out.shape)
    own[...] = (middle_out[...] * scale * gains[1:2, :]).astype(BF)
    local = pltpu.make_async_copy(own, out.at[row_span(x), col_span(c)], local_sem.at[0])
    local.start()
    sends = gather_sends(wires, own, out, here)
    down.relay()
    gather_relay(wires, sends, out, here)
    down.finish()
    local.wait()
    wires.close()


def call_middle(part, inputs, gains, down_line):
    vm = pl.BlockSpec(memory_space=pltpu.VMEM)
    hbm = pl.BlockSpec(memory_space=ANY)
    return pl.pallas_call(
        middle_kernel,
        out_shape=(
            jax.ShapeDtypeStruct((ROWS, WIDTH), F32),
            jax.ShapeDtypeStruct((ROWS, 128), F32),
            jax.ShapeDtypeStruct((LINE, D), BF),
            jax.ShapeDtypeStruct((4, 4, 2 * PIECE, D), BF),
        ),
        in_specs=[vm] * 3 + [hbm],
        out_specs=(vm, vm, hbm, hbm),
        scratch_shapes=fold_scratch()
        + [
            pltpu.VMEM((ROWS, 128), F32),
            pltpu.VMEM((ROWS, 128), F32),
            pltpu.VMEM((ROWS, WIDTH), BF),
        ]
        + wire_scratch(24)
        + [pltpu.SemaphoreType.DMA((3,))],
        compiler_params=comm_params(2),
        name="line_middle",
    )(part, inputs, gains, down_line)


def norm_back(wires, values, scale, gain_row, incoming, mine, theirs, here):
    weighted = incoming * gain_row
    inner = both_cores(
        wires, mine, theirs, jnp.sum(weighted * values, axis=1, keepdims=True), here
    )
    inner = inner / D
    back = scale * (incoming * gain_row) - values * (scale * scale * scale * inner)
    return back, jnp.sum(incoming * values * scale, axis=0, keepdims=True)


def back_kernel(
    part, part_two, middle, scale, gains, cotangent, grad_down,
    output, middle_grad, gain_out, out, down_out,
    folded, leaving, arriving, total, folded_two, leaving_two, arriving_two, total_two,
    mine, theirs, own, rec, rec_sum, rec_two, fin, send_sem, recv_sem, local_sem,
):
    z, y, xl, xh, c = place()
    x = xh * 2 + xl
    here = (z, y, x, c)
    greet(line_targets(z, y, x, c) + plane_targets(z, y, x, c))
    wires = Wires(send_sem, recv_sem)
    numbers = fold_sends(wires, part, folded, here)
    down = PlaneSum(wires, grad_down, (rec, rec_sum, rec_two, fin), here, local_sem, 1)
    down.start()
    moves = fold_moves(wires, numbers, part, folded, leaving, arriving, here, total)
    numbers_two = fold_sends(wires, part_two, folded_two, here)
    moves_two = fold_moves(
        wires, numbers_two, part_two, folded_two, leaving_two, arriving_two, here, total_two
    )
    fold_finish(wires, moves, arriving, total)
    back, gain_sum = norm_back(
        wires, middle[...], scale[:, :1], gains[1:2, :], total[...], mine, theirs, here
    )
    gain_out[...] = jnp.broadcast_to(gain_sum, gain_out.shape)
    grad = cotangent[...].astype(F32) + back
    middle_grad[...] = grad
    own[...] = grad.astype(BF)
    local = pltpu.make_async_copy(own, out.at[row_span(x), col_span(c)], local_sem.at[0])
    local.start()
    sends = gather_sends(wires, own, out, here)
    fold_finish(wires, moves_two, arriving_two, total_two)
    output[...] = (middle[...] + total_two[...]).astype(BF)
    down.middle()
    gather_relay(wires, sends, out, here)
    down.finish()
    swap = wires.send(fin.at[:, :, col_span(1 - c)], down_out.at[c], device(z, y, x, 1 - c))
    kept = pltpu.make_async_copy(fin.at[:, :, col_span(c)], down_out.at[c], local_sem.at[3])
    kept.start()
    wires.landed(swap, down_out.at[1 - c])
    kept.wait()
    local.wait()
    wires.close()


def call_back(part, part_two, middle, scale, gains, cotangent, grad_down):
    vm = pl.BlockSpec(memory_space=pltpu.VMEM)
    hbm = pl.BlockSpec(memory_space=ANY)
    return pl.pallas_call(
        back_kernel,
        out_shape=(
            jax.ShapeDtypeStruct((ROWS, WIDTH), BF),
            jax.ShapeDtypeStruct((ROWS, WIDTH), F32),
            jax.ShapeDtypeStruct((8, WIDTH), F32),
            jax.ShapeDtypeStruct((LINE, D), BF),
            jax.ShapeDtypeStruct((2, 2, PIECE, WIDTH), BF),
        ),
        in_specs=[vm] * 6 + [hbm],
        out_specs=(vm, vm, vm, hbm, hbm),
        scratch_shapes=fold_scratch()
        + fold_scratch()
        + [
            pltpu.VMEM((ROWS, 128), F32),
            pltpu.VMEM((ROWS, 128), F32),
            pltpu.VMEM((ROWS, WIDTH), BF),
        ]
        + sum_buffers((PIECE, D), BF)
        + wire_scratch(40)
        + [pltpu.SemaphoreType.DMA((4,))],
        compiler_params=comm_params(3),
        name="line_back",
    )(part, part_two, middle, scale, gains, cotangent, grad_down)


def last_kernel(
    part, inputs, scale, gains, middle_grad, output, grad_qkv,
    input_home, output_home, gain_out, qkv_out,
    folded, leaving, arriving, total, mine, theirs, rec, rec_sum, rec_two, fin,
    send_sem, recv_sem, post_send, post_recv, local_sem,
):
    z, y, xl, xh, c = place()
    x = xh * 2 + xl
    here = (z, y, x, c)
    quad = quad_of(xl, xh, x, c)
    fixed = line_targets(z, y, x, c) + plane_targets(z, y, x, c) + [device(z, y, *quad[2])]
    barrier = pltpu.get_barrier_semaphore()
    post = Posting(here, lives_at(z * 4 + y, x), worked_at(z * 4 + y, x), post_send, post_recv)
    for target in fixed:
        pl.semaphore_signal(barrier, inc=1, device_id=target, device_id_type=MESH)
    extra = post.greet(barrier)
    pl.semaphore_wait(barrier, len(fixed) + extra)
    wires = Wires(send_sem, recv_sem)
    numbers = fold_sends(wires, part, folded, here)
    qkv = PlaneSum(wires, grad_qkv, (rec, rec_sum, rec_two, fin), here, local_sem, 0)
    qkv.start()
    output_at = post.send(output, output_home)
    moves = fold_moves(wires, numbers, part, folded, leaving, arriving, here, total)
    qkv.middle()
    fold_finish(wires, moves, arriving, total)
    back, gain_sum = norm_back(
        wires,
        inputs[...].astype(F32),
        scale[:, :1],
        gains[0:1, :],
        total[...],
        mine,
        theirs,
        here,
    )
    gain_out[...] = jnp.broadcast_to(gain_sum, gain_out.shape)
    total[...] = middle_grad[...] + back
    input_at = post.send(total, input_home)
    qkv.finish()
    at_mine = xl * 2 + c
    swaps = [
        wires.send(fin.at[b, lax.rem(a, 2)], qkv_out.at[at_mine], device(z, y, a, b))
        for a, b in quad
    ]
    kept = pltpu.make_async_copy(fin.at[c, xl], qkv_out.at[at_mine], local_sem.at[2])
    kept.start()
    for at, (a, b) in zip(swaps, quad):
        wires.landed(at, qkv_out.at[lax.rem(a, 2) * 2 + b])
    kept.wait()
    post.landed(output_at, output_home)
    post.landed(input_at, input_home)
    post.close()
    wires.close()


def call_last(part, inputs, scale, gains, middle_grad, output, grad_qkv):
    vm = pl.BlockSpec(memory_space=pltpu.VMEM)
    hbm = pl.BlockSpec(memory_space=ANY)
    cols = grad_qkv.shape[-1]
    return pl.pallas_call(
        last_kernel,
        out_shape=(
            jax.ShapeDtypeStruct((ROWS, WIDTH), F32),
            jax.ShapeDtypeStruct((ROWS, WIDTH), BF),
            jax.ShapeDtypeStruct((8, WIDTH), F32),
            jax.ShapeDtypeStruct((4, PIECE, cols), BF),
        ),
        in_specs=[vm] * 5 + [hbm, hbm],
        out_specs=(hbm, hbm, vm, hbm),
        scratch_shapes=fold_scratch()
        + [pltpu.VMEM((ROWS, 128), F32), pltpu.VMEM((ROWS, 128), F32)]
        + sum_buffers((2, PIECE, cols), BF)
        + wire_scratch(32)
        + wire_scratch(2)
        + [pltpu.SemaphoreType.DMA((3,))],
        compiler_params=comm_params(4),
        name="line_last",
    )(part, inputs, scale, gains, middle_grad, output, grad_qkv)


def key_at(half):
    low = half < HALVES // 2
    at = jnp.where(low, half, HALVES - 1 - half)
    return jnp.where(low, 0, 1), at // 4, lax.rem(at, 4)


def allowed_pairs(key_half, query_half, ends):
    keys = key_half * HALF + lax.broadcasted_iota(jnp.int32, (HALF, HALF), 0)
    queries = query_half * HALF + lax.broadcasted_iota(jnp.int32, (HALF, HALF), 1)
    same = keys <= queries
    for k in range(3):
        same = same & ((keys >= ends[k]) == (queries >= ends[k]))
    return same


def in_second(query_half, ends):
    queries = query_half * HALF + lax.broadcasted_iota(jnp.int32, (1, HALF), 1)
    return (queries >= ends[0]) & (queries < ends[1])


class Tour:
    def __init__(self, spot):
        self.spot = spot
        self.low = jnp.maximum(spot - 1, 0)
        self.count = self.low + HALVES - 2 - spot

    def half(self, s):
        return jnp.where(s == 0, self.spot, HALVES - 1 - self.spot)

    def inner(self, step, start, stop):
        def body(at, carry):
            s = jnp.where(at >= self.low, 1, 0)
            step(s, 1 + at - s * self.low, False)
            return carry

        lax.fori_loop(start, stop, body, 0)

    def edges(self, step):
        for s in (0, 1):
            half = self.half(s)

            def body(at, carry):
                step(s, at * half, True)
                return carry

            lax.fori_loop(0, jnp.where(half > 0, 2, 1), body, 0)


def head_cols(g):
    return slice(g * HALF, (g + 1) * HALF)


def out_partner(z, y, xl, xh, c):
    return xl * 2 + c, xh * 2 + z // 2, lax.rem(z, 2)


def attention_kernel(
    ends, queries, own_keys, cotangent, gate_line, out_in,
    out, log_out, keys_out, cotangent_all, gate_all, out_all,
    keys, tops, sums, mixed, send_sem, recv_sem, out_send, out_recv, local_sem,
):
    z, y, xl, xh, c = place()
    x = xh * 2 + xl
    here = (z, y, x, c)
    spot = z * 4 + y
    mine, to_x, to_c = out_partner(z, y, xl, xh, c)
    keeps = z == mine
    fixed = plane_targets(z, y, x, c) + line_targets(z, y, x, c)
    barrier = pltpu.get_barrier_semaphore()
    for target in fixed:
        pl.semaphore_signal(barrier, inc=1, device_id=target, device_id_type=MESH)
    for k in range(16):
        from_y, from_xl, from_c = k // 4, (k // 2) % 2, k % 2

        @pl.when(jnp.logical_not(keeps & (y == from_y) & (xl == from_xl) & (c == from_c)))
        def _():
            pl.semaphore_signal(
                barrier,
                inc=1,
                device_id=device(mine, jnp.int32(from_y), xh * 2 + from_xl, jnp.int32(from_c)),
                device_id_type=MESH,
            )

    pl.semaphore_wait(barrier, len(fixed) + 16 - keeps.astype(jnp.int32))
    wires = Wires(send_sem, recv_sem)

    first = [
        [
            wires.send(own_keys.at[s], keys.at[s, z, y], first_device(here, s, by))
            for by in OFFSETS
        ]
        for s in (0, 1)
    ]
    kept = [
        pltpu.make_async_copy(own_keys.at[s], keys.at[s, z, y], local_sem.at[s]) for s in (0, 1)
    ]
    for copy in kept:
        copy.start()
    cotangent_kept = pltpu.make_async_copy(
        cotangent, cotangent_all.at[row_span(x), col_span(c)], local_sem.at[2]
    )
    cotangent_kept.start()
    cotangent_numbers = gather_sends(wires, cotangent, cotangent_all, here)
    for copy in kept:
        copy.wait()
    second = []
    for s in (0, 1):
        for at, by in zip(first[s], OFFSETS):
            back = first_at(here, s, 4 - by)
            wires.landed(at, keys.at[s, back, y] if s == 0 else keys.at[s, z, back])
        line = keys.at[0, :, y] if s == 0 else keys.at[1, z]
        second.append([wires.send(line, line, second_device(here, s, by)) for by in OFFSETS])
    for s in (0, 1):
        for at, by in zip(second[s], OFFSETS):
            if s == 0:
                wires.landed(at, keys.at[0, :, lax.rem(y + 4 - by, 4)])
            else:
                wires.landed(at, keys.at[1, lax.rem(z + 4 - by, 4)])
    keys_kept = pltpu.make_async_copy(keys, keys_out, local_sem.at[3])
    keys_kept.start()

    gate = PlaneGather(wires, gate_line, gate_all, here, local_sem, 4)
    gate.start()
    slot = y * 4 + mine
    out_spot = out_all.at[y, xl, :, col_span(c)]
    out_sends = []
    for k in range(16):
        copy = pltpu.make_async_remote_copy(
            src_ref=out_in,
            dst_ref=out_spot,
            send_sem=out_send.at[k],
            recv_sem=out_recv.at[slot],
            device_id=device(jnp.int32(k // 4), jnp.int32(k % 4), to_x, to_c),
            device_id_type=MESH,
        )
        to_self = keeps & (spot == k)
        out_sends.append((copy, to_self))

        @pl.when(jnp.logical_not(to_self))
        def _():
            copy.start()

        @pl.when(to_self)
        def _():
            pltpu.make_async_copy(out_in, out_spot, out_recv.at[slot]).start()

    tour = Tour(spot)
    tops[...] = jnp.full(tops.shape, NEVER, F32)
    sums[...] = jnp.zeros(sums.shape, F32)
    mixed[...] = jnp.zeros(mixed.shape, F32)

    def step(s, at, masked):
        pairs = keys[key_at(at)]
        if masked:
            allowed = allowed_pairs(at, tour.half(s), ends)
        for g in range(GROUP):
            cols = head_cols(g)
            scores = jnp.dot(pairs, queries[s, :, cols], preferred_element_type=F32)
            if masked:
                scores = jnp.where(allowed, scores, NEVER)
            old = tops[s, :, cols]
            top = jnp.maximum(old, jnp.max(scores, axis=0, keepdims=True))
            weights = jnp.exp(scores - top)
            if masked:
                weights = jnp.where(allowed, weights, 0.0)
            shrink = jnp.exp(old - top)
            tops[s, :, cols] = top
            sums[s, :, cols] = sums[s, :, cols] * shrink + jnp.sum(
                weights, axis=0, keepdims=True
            )
            mixed[s, :, cols] = mixed[s, :, cols] * shrink + lax.dot_general(
                pairs, weights.astype(BF), (((0,), (0,)), ((), ())), preferred_element_type=F32
            )

    tour.inner(step, 0, 10)
    gather_relay(wires, cotangent_numbers, cotangent_all, here)
    tour.inner(step, 10, 22)
    gate.relay()
    tour.inner(step, 22, tour.count)
    for s in (0, 1):
        fits = in_second(tour.half(s), ends)
        for g in range(GROUP):
            cols = head_cols(g)
            tops[s, :, cols] = jnp.where(fits, tops[s, :, cols], NEVER)
            sums[s, :, cols] = jnp.where(fits, sums[s, :, cols], 0.0)
            mixed[s, :, cols] = jnp.where(fits, mixed[s, :, cols], 0.0)
    tour.edges(step)
    for s in (0, 1):
        out[s] = mixed[s, HD:, :] / sums[s]
        log_out[s] = tops[s] + jnp.log(sums[s])
    for k in range(16):
        spot_k = out_all.at[k // 4, (k // 2) % 2, :, pl.ds((k % 2) * WIDTH, WIDTH)]
        pltpu.make_async_copy(spot_k, spot_k, out_recv.at[k]).wait()
    gate.finish()
    cotangent_kept.wait()
    keys_kept.wait()
    for copy, to_self in out_sends:

        @pl.when(jnp.logical_not(to_self))
        def _():
            copy.wait_send()

    wires.close()


def call_attention(ends, queries, own_keys, cotangent, gate_line, out_in):
    vm = pl.BlockSpec(memory_space=pltpu.VMEM)
    hbm = pl.BlockSpec(memory_space=ANY)
    cols = GROUP * HALF
    return pl.pallas_call(
        attention_kernel,
        out_shape=(
            jax.ShapeDtypeStruct((2, HD, cols), F32),
            jax.ShapeDtypeStruct((2, 1, cols), F32),
            jax.ShapeDtypeStruct((2, 4, 4, HALF, 2 * HD), BF),
            jax.ShapeDtypeStruct((LINE, D), BF),
            jax.ShapeDtypeStruct((2, 4, 4, 2, PIECE, gate_line.shape[-1]), BF),
            jax.ShapeDtypeStruct((4, 2, PIECE, D), BF),
        ),
        in_specs=[pl.BlockSpec(memory_space=pltpu.SMEM), vm] + [hbm] * 4,
        out_specs=(vm, vm, hbm, hbm, hbm, hbm),
        scratch_shapes=[
            pltpu.VMEM((2, 4, 4, HALF, 2 * HD), BF),
            pltpu.VMEM((2, 1, cols), F32),
            pltpu.VMEM((2, 1, cols), F32),
            pltpu.VMEM((2, 2 * HD, cols), F32),
        ]
        + wire_scratch(32)
        + wire_scratch(16)
        + [pltpu.SemaphoreType.DMA((6,))],
        compiler_params=comm_params(5),
        name="attention",
    )(ends, queries, own_keys, cotangent, gate_line, out_in)


def attention_back_kernel(
    ends, queries, grads, query_rows, grad_rows, logs, delta, keys, grad_gate, grad_out,
    query_back, key_back, gate_out, out_out,
    terms, sums, rounded, rec, rec_sum, rec_two, fin, key_rec, key_sums, key_rec_two, out_rec,
    send_sem, recv_sem, out_send, out_recv, local_sem,
):
    z, y, xl, xh, c = place()
    x = xh * 2 + xl
    here = (z, y, x, c)
    spot = z * 4 + y
    mine, from_x, from_c = out_partner(z, y, xl, xh, c)
    keeps = z == mine
    quad = quad_of(xl, xh, x, c)
    fixed = plane_targets(z, y, x, c) + [device(z, y, a, b) for a, b in quad]
    barrier = pltpu.get_barrier_semaphore()
    for target in fixed:
        pl.semaphore_signal(barrier, inc=1, device_id=target, device_id_type=MESH)
    for k in range(16):

        @pl.when(jnp.logical_not(keeps & (spot == k)))
        def _():
            pl.semaphore_signal(
                barrier,
                inc=1,
                device_id=device(jnp.int32(k // 4), jnp.int32(k % 4), from_x, from_c),
                device_id_type=MESH,
            )

    pl.semaphore_wait(barrier, len(fixed) + 16 - keeps.astype(jnp.int32))
    wires = Wires(send_sem, recv_sem)
    gate = PlaneSum(wires, grad_gate, (rec, rec_sum, rec_two, fin), here, local_sem, 0)
    gate.start()
    out_sends = []
    for k in range(16):
        to_y, to_xl, to_c = k // 4, (k // 2) % 2, k % 2
        src = grad_out.at[to_y, to_xl, :, pl.ds(to_c * WIDTH, WIDTH)]
        to_self = keeps & (y == to_y) & (xl == to_xl) & (c == to_c)
        copy = pltpu.make_async_remote_copy(
            src_ref=src,
            dst_ref=out_rec.at[spot],
            send_sem=out_send.at[k],
            recv_sem=out_recv.at[spot],
            device_id=device(mine, jnp.int32(to_y), xh * 2 + to_xl, jnp.int32(to_c)),
            device_id_type=MESH,
        )
        out_sends.append((copy, to_self))

        @pl.when(jnp.logical_not(to_self))
        def _():
            copy.start()

        @pl.when(to_self)
        def _():
            pltpu.make_async_copy(src, out_rec.at[spot], out_recv.at[spot]).start()

    tour = Tour(spot)
    terms[...] = jnp.zeros(terms.shape, F32)
    sums[...] = jnp.zeros(sums.shape, F32)

    def step(s, at, masked):
        slot = key_at(at)
        pairs = keys[slot]
        if masked:
            allowed = allowed_pairs(at, tour.half(s), ends)
        else:
            fits = in_second(tour.half(s), ends)
        added = None
        for g in range(GROUP):
            cols = head_cols(g)
            scores = jnp.dot(pairs, queries[s, :, cols], preferred_element_type=F32)
            log_row = logs[s, :, cols]
            if not masked:
                log_row = jnp.where(fits, log_row, -NEVER)
            probs = jnp.exp(scores - log_row)
            if masked:
                probs = jnp.where(allowed, probs, 0.0)
            prob_grad = jnp.dot(pairs, grads[s, :, cols], preferred_element_type=F32)
            score_grad = (probs * (prob_grad - delta[s, :, cols])).astype(BF)
            sums[s, :, cols] += lax.dot_general(
                pairs, score_grad, (((0,), (0,)), ((), ())), preferred_element_type=F32
            )
            term = jnp.dot(score_grad, query_rows[s, g], preferred_element_type=F32) + jnp.dot(
                probs.astype(BF), grad_rows[s, g], preferred_element_type=F32
            )
            added = term if added is None else added + term
        terms[slot] += added

    tour.inner(step, 0, tour.count)
    tour.edges(step)

    for s in (0, 1):
        for i in range(4):
            rounded[s, i] = terms[s, i].astype(BF)
    first = [[], []]
    for k, by in enumerate(OFFSETS):
        first[0].append(
            wires.send(
                rounded.at[0, :, lax.rem(y + by, 4)], key_rec.at[0, k], second_device(here, 0, by)
            )
        )
        first[1].append(
            wires.send(
                rounded.at[1, lax.rem(z + by, 4)], key_rec.at[1, k], second_device(here, 1, by)
            )
        )
    for s in (0, 1):
        query_back[s] = sums[s, :HD, :] * HD ** (-0.5)
    gate.middle()
    second = [[], []]
    for s in (0, 1):
        for k in range(3):
            wires.landed(first[s][k], key_rec.at[s, k])
        for i in range(4):
            value = terms[0, i, y] if s == 0 else terms[1, z, i]
            for k in range(3):
                value = value + key_rec[s, k, i].astype(F32)
            key_sums[s, i] = value.astype(BF)
        for k, by in enumerate(OFFSETS):
            second[s].append(
                wires.send(
                    key_sums.at[s, first_at(here, s, by)],
                    key_rec_two.at[s, k],
                    first_device(here, s, by),
                )
            )
    gate.finish()
    swaps = [
        wires.send(fin.at[b, lax.rem(a, 2)], gate_out.at[mine], device(z, y, a, b))
        for a, b in quad
    ]
    kept = pltpu.make_async_copy(fin.at[c, xl], gate_out.at[mine], local_sem.at[2])
    kept.start()
    total = None
    for k in range(16):
        pltpu.make_async_copy(out_rec.at[k], out_rec.at[k], out_recv.at[k]).wait()
        total = out_rec[k].astype(F32) if total is None else total + out_rec[k].astype(F32)
    out_out[...] = total
    for s in (0, 1):
        value = key_sums[s, first_at(here, s)].astype(F32)
        for k in range(3):
            wires.landed(second[s][k], key_rec_two.at[s, k])
            value = value + key_rec_two[s, k].astype(F32)
        key_back[s] = value
    for at, (a, b) in zip(swaps, quad):
        wires.landed(at, gate_out.at[lax.rem(a, 2) * 2 + b])
    kept.wait()
    for copy, to_self in out_sends:

        @pl.when(jnp.logical_not(to_self))
        def _():
            copy.wait_send()

    wires.close()


def call_attention_back(
    ends, queries, grads, query_rows, grad_rows, logs, delta, keys, grad_gate, grad_out
):
    vm = pl.BlockSpec(memory_space=pltpu.VMEM)
    hbm = pl.BlockSpec(memory_space=ANY)
    cols = GROUP * HALF
    gate_cols = grad_gate.shape[-1]
    return pl.pallas_call(
        attention_back_kernel,
        out_shape=(
            jax.ShapeDtypeStruct((2, HD, cols), F32),
            jax.ShapeDtypeStruct((2, HALF, 2 * HD), F32),
            jax.ShapeDtypeStruct((4, PIECE, gate_cols), BF),
            jax.ShapeDtypeStruct((PIECE, WIDTH), F32),
        ),
        in_specs=[pl.BlockSpec(memory_space=pltpu.SMEM)] + [vm] * 7 + [hbm, hbm],
        out_specs=(vm, vm, hbm, vm),
        scratch_shapes=[
            pltpu.VMEM((2, 4, 4, HALF, 2 * HD), F32),
            pltpu.VMEM((2, 2 * HD, cols), F32),
            pltpu.VMEM((2, 4, 4, HALF, 2 * HD), BF),
        ]
        + sum_buffers((2, PIECE, gate_cols), BF)
        + [
            pltpu.VMEM((2, 3, 4, HALF, 2 * HD), BF),
            pltpu.VMEM((2, 4, HALF, 2 * HD), BF),
            pltpu.VMEM((2, 3, HALF, 2 * HD), BF),
            pltpu.VMEM((16, PIECE, WIDTH), BF),
        ]
        + wire_scratch(40)
        + wire_scratch(16)
        + [pltpu.SemaphoreType.DMA((3,))],
        compiler_params=comm_params(6),
        name="attention_back",
    )(ends, queries, grads, query_rows, grad_rows, logs, delta, keys, grad_gate, grad_out)


def total_kernel(terms, out, stage, rec, rec_two, rec_three, last, send_sem, recv_sem):
    z, y, xl, xh, c = place()
    x = xh * 2 + xl
    plane = [(a, b) for a in range(4) for b in range(4) if a or b]
    targets = [device(z + a, y + b, x, c) for a, b in plane] + line_targets(z, y, x, c)
    greet(targets)
    wires = Wires(send_sem, recv_sem)
    first = [
        wires.send(terms, rec.at[k], device(z + a, y + b, x, c)) for k, (a, b) in enumerate(plane)
    ]
    value = terms[...]
    for k, at in enumerate(first):
        wires.landed(at, rec.at[k])
        value = value + rec[k]
    stage[...] = value
    second = [
        wires.send(stage, rec_two.at[k], device(z, y, lax.rem(x + o, 4), c))
        for k, o in enumerate((1, 2, 3))
    ]
    for k, at in enumerate(second):
        wires.landed(at, rec_two.at[k])
        value = value + rec_two[k]
    gains = value[:16]
    square = value[16:] + jnp.sum(gains * gains)
    last[...] = square
    at = wires.send(last, rec_three, device(z, y, x, 1 - c))
    wires.landed(at, rec_three)
    out[:16] = gains
    out[16:] = square + rec_three[...]
    wires.close()


def call_total(terms):
    vm = pl.BlockSpec(memory_space=pltpu.VMEM)
    return pl.pallas_call(
        total_kernel,
        out_shape=jax.ShapeDtypeStruct((24, 128), F32),
        in_specs=[vm],
        out_specs=vm,
        scratch_shapes=[
            pltpu.VMEM((24, 128), F32),
            pltpu.VMEM((15, 24, 128), F32),
            pltpu.VMEM((3, 24, 128), F32),
            pltpu.VMEM((8, 128), F32),
            pltpu.VMEM((8, 128), F32),
        ]
        + wire_scratch(19),
        compiler_params=comm_params(8),
        name="total",
    )(terms)


def rope_tables(position, head_size):
    half_size = head_size // 2
    column = jnp.arange(half_size, dtype=jnp.float32)
    inverse = jnp.exp(-(2.0 * column / head_size) * math.log(ROPE_THETA))
    wavelength = 2.0 * math.pi / inverse
    smooth = (OLD_CONTEXT / wavelength - LOW_FREQ) / (HIGH_FREQ - LOW_FREQ)
    blended = (1.0 - smooth) * inverse / ROPE_FACTOR + smooth * inverse
    inverse = jnp.where(
        wavelength < OLD_CONTEXT / HIGH_FREQ,
        inverse,
        jnp.where(wavelength > OLD_CONTEXT / LOW_FREQ, inverse / ROPE_FACTOR, blended),
    )
    angles = position.astype(jnp.float32)[:, None] * inverse[None, :]
    return (jnp.cos(angles), jnp.sin(angles))


def rotate(values, cosine, sine):
    half_size = values.shape[-1] // 2
    table_shape = (cosine.shape[0],) + (1,) * (values.ndim - 2) + (half_size,)
    cos_part = cosine.reshape(table_shape)
    sin_part = sine.reshape(table_shape)
    first_half = values[..., :half_size]
    second_half = values[..., half_size:]
    return jnp.concatenate(
        [
            first_half * cos_part - second_half * sin_part,
            second_half * cos_part + first_half * sin_part,
        ],
        axis=-1,
    )


def times(left, right, kind):
    return jnp.dot(left, right, preferred_element_type=F32).astype(kind)


def times_transpose(left, right, kind):
    return lax.dot_general(
        left, right, (((1,), (1,)), ((), ())), preferred_element_type=F32
    ).astype(kind)


def outer_rows(left, right, kind):
    return lax.dot_general(
        left, right, (((0,), (0,)), ((), ())), preferred_element_type=F32
    ).astype(kind)


def as_columns(rows):
    return rows.reshape(2, HALF, GROUP, HD).transpose(0, 3, 2, 1).reshape(2, HD, GROUP * HALF)


def as_heads(rows):
    return rows.reshape(2, HALF, GROUP, HD).transpose(0, 2, 1, 3)


def from_columns(columns):
    return columns.reshape(2, HD, GROUP, HALF).transpose(0, 3, 2, 1).reshape(LINE, GROUP * HD)


def adam(weight, moment, second, gradient, rate, decay):
    moment_next = BETA_ONE * moment + (1.0 - BETA_ONE) * gradient
    second_next = BETA_TWO * second + (1.0 - BETA_TWO) * gradient * gradient
    unbiased = moment_next / (1.0 - BETA_ONE**ADAM_STEP)
    divisor = jnp.sqrt(second_next / (1.0 - BETA_TWO**ADAM_STEP)) + ADAM_EPS
    return (weight - rate * (unbiased / divisor + decay * weight), moment_next, second_next)


def shards(
    block_input,
    out_grad,
    qkv_weight,
    qkv_moment,
    qkv_second,
    gate_up_weight,
    gate_up_moment,
    gate_up_second,
    out_weight,
    out_moment,
    out_second,
    down_weight,
    down_moment,
    down_second,
    norm_gains,
    gains_moment,
    gains_second,
    doc_lengths,
):
    z, y, xl, xh, c = place()
    x = xh * 2 + xl
    spot = z * 4 + y

    qkv_in = qkv_weight.astype(BF).transpose(1, 0, 2)
    gate_in = (
        gate_up_weight.astype(BF)
        .reshape(PIECE, 2, 16, 4, HD)
        .transpose(3, 0, 1, 2, 4)
        .reshape(4, PIECE, 2 * HIDDEN)
    )
    down_in = down_weight.astype(BF).reshape(2, ROWS // 2, WIDTH)
    gain_rows = jnp.concatenate([norm_gains, jnp.zeros((6, WIDTH), F32)], axis=0)
    inputs, cotangent, inputs_all, gains_all, qkv_whole, _, gate_line, down_line = call_start(
        block_input, out_grad, gain_rows, qkv_in, gate_in, down_in
    )
    qkv_low = qkv_whole.reshape(D, (GROUP + 2) * HD)

    values = inputs_all.astype(F32)
    scale_one = lax.rsqrt(jnp.sum(values * values, axis=1, keepdims=True) / D + NORM_EPS)
    normed = (values * scale_one * gains_all[0:1, :]).astype(BF)
    projected = times(normed, qkv_low, F32)

    ends = jnp.cumsum(doc_lengths)
    local = jnp.arange(LINE, dtype=jnp.int32)
    half = jnp.where(local < HALF, spot, HALVES - 1 - spot)
    places = half * HALF + lax.rem(local, HALF)
    passed = (places[:, None] >= ends[None, :]).astype(jnp.int32)
    position = places - jnp.sum(passed * doc_lengths[None, :], axis=1)
    cosine, sine = rope_tables(position, HD)
    turned = rotate(
        projected[:, : (GROUP + 1) * HD].reshape(LINE, GROUP + 1, HD), cosine, sine
    ).astype(BF)
    queries = turned[:, :GROUP].reshape(LINE, GROUP * HD) * jnp.asarray(HD ** (-0.5), BF)
    own_keys = jnp.concatenate([turned[:, GROUP], projected[:, (GROUP + 1) * HD :].astype(BF)], axis=1)

    blank = jnp.zeros((2, HD, GROUP * HALF), BF)
    query_columns = jnp.concatenate([as_columns(queries), blank], axis=1)
    mixed, logs, keys, cotangent_all, gate_whole, out_whole = call_attention(
        ends,
        query_columns,
        own_keys.reshape(2, HALF, 2 * HD),
        cotangent,
        gate_line,
        out_weight.astype(BF),
    )
    gate_low = gate_whole.reshape(D, 2 * HIDDEN)
    out_low = out_whole.reshape(GROUP * HD, D)
    mixed_rows = from_columns(mixed)
    attended = mixed_rows.astype(BF)
    middle, scale_two, normed_two, down_whole = call_middle(
        times(attended, out_low, BF), inputs, norm_gains, down_line
    )
    down_low = down_whole.reshape(HIDDEN, D)

    gate_up = times(normed_two, gate_low, F32)
    gate_part, up_part = gate_up[:, :HIDDEN], gate_up[:, HIDDEN:]
    sigmoid_gate = jax.nn.sigmoid(gate_part)
    hidden = (gate_part * sigmoid_gate * up_part).astype(BF)
    hidden_grad = times_transpose(cotangent_all, down_low, F32)
    gate_back = hidden_grad * up_part * sigmoid_gate * (1.0 + gate_part * (1.0 - sigmoid_gate))
    up_back = hidden_grad * gate_part * sigmoid_gate
    gate_up_back = jnp.concatenate([gate_back, up_back], axis=1).astype(BF)
    grad_down = outer_rows(hidden, cotangent_all, BF)
    output, middle_grad, gain_two, middle_low, down_sum = call_back(
        times_transpose(gate_up_back, gate_low, BF),
        times(hidden, down_low, BF),
        middle,
        scale_two,
        norm_gains,
        cotangent,
        grad_down.reshape(down_whole.shape),
    )
    grad_gate = outer_rows(normed_two, gate_up_back, BF)

    grad_out = outer_rows(attended, middle_low, BF)
    attended_grad = times_transpose(middle_low, out_low, BF)
    delta = jnp.sum(
        (attended_grad.astype(F32) * mixed_rows).reshape(LINE, GROUP, HD), axis=-1
    )
    delta = delta.reshape(2, HALF, GROUP).transpose(0, 2, 1).reshape(2, 1, GROUP * HALF)
    empty = jnp.zeros((2, GROUP, HALF, HD), BF)
    query_back, key_grads, gate_sum, out_sum = call_attention_back(
        ends,
        query_columns,
        jnp.concatenate([blank, as_columns(attended_grad)], axis=1),
        jnp.concatenate([as_heads(queries), empty], axis=-1),
        jnp.concatenate([empty, as_heads(attended_grad)], axis=-1),
        logs,
        delta,
        keys,
        grad_gate.reshape(gate_whole.shape),
        grad_out.reshape(out_whole.shape),
    )
    key_grads = key_grads.reshape(LINE, 2 * HD)
    turned_back = jnp.concatenate([from_columns(query_back), key_grads[:, :HD]], axis=1)
    turned_back = rotate(turned_back.reshape(LINE, GROUP + 1, HD), cosine, -sine)
    projected_back = jnp.concatenate(
        [turned_back.reshape(LINE, (GROUP + 1) * HD), key_grads[:, HD:]], axis=1
    ).astype(BF)
    grad_qkv = outer_rows(normed, projected_back, BF)
    scale_rows = lax.dynamic_slice_in_dim(scale_one, x * ROWS, ROWS, 0)
    input_grad, output, gain_one, qkv_sum = call_last(
        times_transpose(projected_back, qkv_low, BF),
        inputs,
        jnp.broadcast_to(scale_rows, (ROWS, 128)),
        norm_gains,
        middle_grad,
        output,
        grad_qkv.reshape(qkv_whole.shape),
    )

    shares = (
        qkv_sum.transpose(1, 0, 2).astype(F32),
        gate_sum.reshape(4, PIECE, 2, 16, HD)
        .transpose(1, 2, 3, 0, 4)
        .reshape(gate_up_weight.shape)
        .astype(F32),
        out_sum,
        down_sum.reshape(down_weight.shape).astype(F32),
    )
    square = sum(
        jnp.sum(jnp.square(member.astype(F32))) for member in (qkv_sum, gate_sum, out_sum, down_sum)
    )
    terms = jnp.concatenate(
        [
            jnp.stack([gain_one[0], gain_two[0]]).reshape(16, 128),
            jnp.broadcast_to(square, (8, 128)),
        ],
        axis=0,
    )
    totals = call_total(terms)
    gains_grad = totals[:16].reshape(2, WIDTH)
    grad_norm = jnp.sqrt(totals[16, 0])
    factor = CLIP_NORM / jnp.maximum(grad_norm, CLIP_NORM)
    weights = (qkv_weight, gate_up_weight, out_weight, down_weight)
    moments = (qkv_moment, gate_up_moment, out_moment, down_moment)
    seconds = (qkv_second, gate_up_second, out_second, down_second)
    out_rate = OUTPUT_RATE * (TOKENS / (HQ * HD)) ** 0.5
    down_rate = DOWN_RATE * FF ** (-0.5)
    rates = (MATRIX_RATE, MATRIX_RATE, out_rate, down_rate)
    results = []
    for weight, moment, second, gradient, rate in zip(weights, moments, seconds, shares, rates):
        results.extend(adam(weight, moment, second, gradient * factor, rate, WEIGHT_DECAY))
    gains_new = adam(norm_gains, gains_moment, gains_second, gains_grad * factor, GAIN_RATE, 0.0)
    return (output, input_grad, grad_norm, *results, *gains_new)


def solution(mesh):
    placed = (
        P(("seq", "wide"), "narrow"),
        P(("seq", "wide"), "narrow"),
        P(("narrow", "seq"), "wide", None),
        P(("narrow", "seq"), "wide", None),
        P(("narrow", "seq"), "wide", None),
        P(("narrow", "seq"), None, "wide"),
        P(("narrow", "seq"), None, "wide"),
        P(("narrow", "seq"), None, "wide"),
        P(("wide", "seq"), "narrow"),
        P(("wide", "seq"), "narrow"),
        P(("wide", "seq"), "narrow"),
        P(("wide", "seq"), "narrow"),
        P(("wide", "seq"), "narrow"),
        P(("wide", "seq"), "narrow"),
        P(None, "narrow"),
        P(None, "narrow"),
        P(None, "narrow"),
        P(),
    )
    return jax.shard_map(
        shards,
        mesh=mesh,
        in_specs=placed,
        out_specs=(
            P(("seq", "wide"), "narrow"),
            P(("seq", "wide"), "narrow"),
            P(),
            P(("narrow", "seq"), "wide", None),
            P(("narrow", "seq"), "wide", None),
            P(("narrow", "seq"), "wide", None),
            P(("narrow", "seq"), None, "wide"),
            P(("narrow", "seq"), None, "wide"),
            P(("narrow", "seq"), None, "wide"),
            P(("wide", "seq"), "narrow"),
            P(("wide", "seq"), "narrow"),
            P(("wide", "seq"), "narrow"),
            P(("wide", "seq"), "narrow"),
            P(("wide", "seq"), "narrow"),
            P(("wide", "seq"), "narrow"),
            P(None, "narrow"),
            P(None, "narrow"),
            P(None, "narrow"),
        ),
        check_vma=False,
    )
```

time: 666 us -> 520 us (0.78)
  Pallas kernels: 524 us -> 404 us
  starting transfers between devices: 12.2 us -> 0 us
    pallas_call x6 -> x3, Pallas kernels: 398 us -> 253 us  [the longest x1 98.2 us: call_attention_back(): pl.pallas_call(attention_back_kernel, out_shape=(jax.ShapeDtypeStruct((2,...]
    pallas_call x1, Pallas kernels: 15.3 us -> 28.1 us  [call_total(): pl.pallas_call(total_kernel, out_shape=jax.ShapeDtypeStruct((24, 128), F3...]
    ppermute x4 -> x0, starting transfers between devices: 12.2 us -> none  [the longest x1 5.37 us: shards(): input_grad = lax.ppermute(input_grad, ('seq', 'wide'), home)]
    pallas_call x1, Pallas kernels: 22.2 us -> 33.8 us  [call_last(): pl.pallas_call(last_kernel, out_shape=(jax.ShapeDtypeStruct((ROWS, WIDTH)...]
  transfers between devices with their start and end apart: 4 -> 0, of which waited for: 0 -> 0; matrix products, arithmetic and copies ran while one was open for 3% -> 0% of each run, Pallas kernels for 0% -> 0%
where the time goes in v2:
time: 520 us; the launch traced here: 512 us
  Pallas kernels  404 us (78%)
  matrix products  46 us (9%)
  local copies, waits for them, and re-layouts  32.5 us (6%)
  other arithmetic  23.5 us (5%)
  between operations  6.01 us (1%)
    pallas_call x1, Pallas kernels, call_attention_back(): pl.pallas_call(attention_back_kernel, out_shape=(jax.ShapeDtypeStruct((2,...  98.2 us
    pallas_call x1, Pallas kernels, call_attention(): pl.pallas_call(attention_kernel, out_shape=(jax.ShapeDtypeStruct((2, HD,...  90 us
    pallas_call x1, Pallas kernels, call_start(): pl.pallas_call(start_kernel, out_shape=shapes, in_specs=[hbm] * 6, out_sp...  64.9 us
    pallas_call x1, Pallas kernels, call_back(): pl.pallas_call(back_kernel, out_shape=(jax.ShapeDtypeStruct((ROWS, WIDTH)...  48.2 us
    pallas_call x1, Pallas kernels, call_middle(): pl.pallas_call(middle_kernel, out_shape=(jax.ShapeDtypeStruct((ROWS, WIDT...  41 us
    pallas_call x1, Pallas kernels, call_last(): pl.pallas_call(last_kernel, out_shape=(jax.ShapeDtypeStruct((ROWS, WIDTH)...  33.8 us
    pallas_call x1, Pallas kernels, call_total(): pl.pallas_call(total_kernel, out_shape=jax.ShapeDtypeStruct((24, 128), F3...  28.1 us
    dot_general x4, matrix products, times(): return jnp.dot(left, right, preferred_element_type=F32).astype(kind)  16.3 us

profile of v2, /device:TPU:1, one launch (start us, length us, event | category | flops | bytes accessed | tf_op | source)
XLA Modules:
  0.0 512.2 jit_solution(7211397744412176130)
XLA Ops:
  0.7 0.8 reduce-window.8
  1.5 0.7 select_reduce_fusion
  2.3 1.0 fusion.21
  3.3 1.7 convert_element_type.89
  4.9 0.7 reshape.303
  5.8 1.6 reshape.304.gate_in
  7.4 0.7 convert_element_type.90
  8.2 0.7 copy.113
  8.8 0.6 concatenate.45.gain_rows
  9.4 64.9 %start.1 = (bf16[128,1024]{1,0:T(8,128)(2,1)}, bf16[128,1024]{1,0:T(8,128)(2,1)}, bf16[512,2048]{1,0:T(8,128)(2,1)}, f32[8,2048]{1,0:T(8,128)}, bf16[2,4,4,2,32,...) custom-call(bf16[128,1024]{1,0:T(8,128)(2,1)} %block_input.1, ...), custom_call_target="tpu_custom_call" | custom-call | tf_op jit(solution)/shard_map/start/pallas_call | solution.py:571
  74.4 2.2 fusion
  76.6 0.9 slice.53
  77.5 2.6 fusion.6
  80.5 0.8 pad_maximum_fusion.8.own_keys
  81.8 0.8 concatenate.47.queries
  82.7 0.6 convert_element_type.94.out_in
  83.3 90.0 %attention.1 = (f32[2,64,1024]{2,1,0:T(8,128)}, f32[2,1,1024]{2,1,0:T(1,128)}, bf16[2,4,4,256,128]{4,3,2,1,0:T(8,128)(2,1)}, bf16[512,2048]{1,0:T(8,128)(2,1)}, ...) custom-call(s32[4]{0:T(128)} %bitcast.132, bf16[2,128,1024]{2,1,0:T(8,128)(2,1)} %concatenate.47.queries, ...), custom_call_target="tpu_custom_call" | custom-call | tf_op jit(solution)/shard_map/attention/pallas_call | solution.py:1015
  173.3 1.4 reshape.309
  175.2 2.1 convolution_convert_fusion.3.part
  177.3 41.0 %line_middle.1 = (f32[128,1024]{1,0:T(8,128)}, f32[128,128]{1,0:T(8,128)}, bf16[512,2048]{1,0:T(8,128)(2,1)}, bf16[4,4,64,2048]{3,2,1,0:T(8,128)(2,1)}) custom-call(bf16[512,2048]{1,0:T(8,128)(2,1)} %convolution_convert_fusion.3.part, bf16[128,1024]{1,0:T(8,128)(2,1)} %get-tuple-element.56.inputs, f32[2,1024]{1,0:T(2,128)} %gains.5, ...), custom_call_target="tpu_custom_call" | custom-call | tf_op jit(solution)/shard_map/line_middle/pallas_call | solution.py:620
  218.3 7.9 %fusion.34 = f32[512,2048]{1,0:T(8,128)S(1)} fusion(bf16[512,2048]{1,0:T(8,128)(2,1)} %get-tuple-element.59, bf16[2048,2048]{1,0:T(8,128)(2,1)} %bitcast.135), kind=kOutput, calls=%fused_computation.92 | convolution fusion | flops 4294967296 | bytes 14680064 | tf_op jit(solution)/shard_map/dot_general | solution.py:1318
  226.2 4.5 multiply_convert_fusion.2
  230.7 4.4 convolution_convert_fusion.1
  235.1 3.7 convolution_convert_fusion.2.part_two
  238.8 5.8 %convolution_convert_fusion.5.part = bf16[512,2048]{1,0:T(8,128)(2,1)} fusion(bf16[2048,2048]{1,0:T(8,128)(2,1)S(1)} %bitcast.138, bf16[512,1024]{1,0:T(8,128)(2,1)S(1)} %copy-done.33, bf16[512,1024]{1,0:T(8,128)(2,1)S(1)} %copy-done.32), kind=kOutput, calls=%fused_computation.10 | convolution fusion | flops 4300210176 | bytes 12582912 | tf_op jit(solution)/shard_map/dot_general | solution.py:1322
  244.5 48.2 %line_back.1 = (bf16[128,1024]{1,0:T(8,128)(2,1)}, f32[128,1024]{1,0:T(8,128)}, f32[8,1024]{1,0:T(8,128)}, bf16[512,2048]{1,0:T(8,128)(2,1)}, bf16[2,2,32,1024]{3,2,1,0:T(8,128)(2,1)}) custom-call(bf16[512,2048]{1,0:T(8,128)(2,1)} %convolution_convert_fusion.5.part, bf16[512,2048]{1,0:T(8,128)(2,1)} %convolution_convert_fusion.2.part_two, ...), custom_call_target="tpu_custom_call" | custom-call | tf_op jit(solution)/shard_map/line_back/pallas_call | solution.py:700
  293.2 1.1 copy-done.1
  294.3 1.7 convolution_convert_fusion.7
  296.0 7.3 %convolution_convert_fusion = bf16[2048,2048]{1,0:T(8,128)(2,1)} fusion(bf16[512,2048]{1,0:T(8,128)(2,1)S(1)} %copy-done.30, bf16[512,1024]{1,0:T(8,128)(2,1)S(1)} %copy-done.33, bf16[512,1024]{1,0:T(8,128)(2,1)S(1)} %copy-done.32), kind=kOutput, calls=%fused_computation | convolution fusion | flops 4303355904 | bytes 12582912 | tf_op jit(solution)/shard_map/dot_general | solution.py:1328
  303.2 0.9 bitcast_reduce_fusion
  304.6 0.8 concatenate.52.grads
  305.8 1.0 concatenate.54.grad_rows
  306.8 0.6 reshape.319.delta
  307.7 0.9 concatenate.53.query_rows
  308.6 98.2 %attention_back.1 = (f32[2,64,1024]{2,1,0:T(8,128)}, f32[2,256,128]{2,1,0:T(8,128)}, bf16[4,32,2048]{2,1,0:T(8,128)(2,1)}, f32[32,1024]{1,0:T(8,128)}) custom-call(s32[4]{0:T(128)} %bitcast.133, bf16[2,128,1024]{2,1,0:T(8,128)(2,1)} %concatenate.47.queries, bf16[2,128,1024]{2,1,0:T(8,128)(2,1)} %concatenate.52.grads, ...), custom_call_target="tpu_custom_call" | custom-call | tf_op jit(solution)/shard_map/attention_back/pallas_call | solution.py:1203
  406.8 1.3 reshape.322
  408.6 1.2 copy.92
  409.8 1.0 subtract_convert_fusion
  411.1 2.6 convolution_convert_fusion.6
  413.7 2.7 convolution_convert_fusion.4.part
  416.4 0.7 broadcast_in_dim.12.scale
  417.2 33.8 %line_last.1 = (f32[128,1024]{1,0:T(8,128)}, bf16[128,1024]{1,0:T(8,128)(2,1)}, f32[8,1024]{1,0:T(8,128)}, bf16[4,32,384]{2,1,0:T(8,128)(2,1)}) custom-call(bf16[512,2048]{1,0:T(8,128)(2,1)} %convolution_convert_fusion.4.part, bf16[128,1024]{1,0:T(8,128)(2,1)} %get-tuple-element.56.inputs, f32[128,128]{1,0:T(8,128)} %broadcast_in_dim.12.scale, ...), custom_call_target="tpu_custom_call" | custom-call | tf_op jit(solution)/shard_map/line_last/pallas_call | solution.py:785
  451.0 1.6 fusion.14
  452.7 0.9 fusion.3
  454.8 0.6 multiply_reduce_fusion
  456.1 0.7 fusion.8
  457.5 0.8 slice.66
  458.3 0.8 slice.67
  459.1 0.6 concatenate.58.terms
  459.7 28.1 %total.1 = f32[24,128]{1,0:T(8,128)} custom-call(f32[24,128]{1,0:T(8,128)} %concatenate.58.terms), custom_call_target="tpu_custom_call" | custom-call | tf_op jit(solution)/shard_map/total/pallas_call | solution.py:1267
  487.8 1.2 slice.68
  489.7 0.7 slice_multiply_fusion
  490.4 0.6 multiply_subtract_fusion.4
  491.2 1.4 multiply_subtract_fusion.1
  492.6 0.8 multiply_subtract_fusion.3
  493.5 0.8 mul.468
  494.4 3.1 copy.88
  497.5 3.3 mul.470
  500.8 5.9 %multiply_subtract_fusion = (f32[32,2,4096]{2,1,0:T(2,128)}, f32[32,2,4096]{2,1,0:T(2,128)}, f32[32,2,4096]{2,1,0:T(2,128)}) fusion(f32[32,2,4096]{2,1,0:T(2,128)S(1)} %copy-done, f32[32,2,4096]{2,1,0:T(2,128)S(1)} %mul.470, f32[32,2,4096]{2,1,0:T(2,128)S(1)} %copy-done.7, f32[32,2,4096]{2,1,0:T(2,128)} %param.25), kind=kLoop, calls=%fused_computation.25 | loop fusion | flops 3932160 | bytes 7340032 | tf_op jit(solution)/shard_map/sub | solution.py:1350
  507.0 0.8 copy.89
  507.8 0.8 copy.90
  508.6 0.8 copy.91
  509.4 0.7 copy.116
  510.1 0.8 copy.117
  (109 shorter events, 4.3 us)
Async XLA Ops:
  1.5 4.3 copy-start.28
  5.6 1.8 copy-start.2
  5.6 2.6 copy-start.10
  5.6 3.2 copy-start.20
  74.4 3.1 copy-start.3
  80.2 2.4 copy-start.14
  173.3 1.8 copy-start.9
  218.3 7.9 %copy-start.29 = (bf16[4,4,64,2048]{3,2,1,0:T(8,128)(2,1)S(1)}, bf16[4,4,64,2048]{3,2,1,0:T(8,128)(2,1)}, u32[]{:S(2)}) copy-start(bf16[4,4,64,2048]{3,2,1,0:T(8,128)(2,1)} %get-tuple-element.58) | copy-start | bytes 12582916
  218.3 7.9 %copy-start.31 = (bf16[512,2048]{1,0:T(8,128)(2,1)S(1)}, bf16[512,2048]{1,0:T(8,128)(2,1)}, u32[]{:S(2)}) copy-start(bf16[512,2048]{1,0:T(8,128)(2,1)} %get-tuple-element.53) | copy-start | bytes 6291460
  230.7 8.1 %slice-start = ((s8[8388608]{0:T(1024)(128)(4,1)}), s8[4194304]{0:T(1024)(128)(4,1)S(1)}, s32[]{:S(2)}) async-start(s8[8388608]{0:T(1024)(128)(4,1)} %bitcast.136), calls=%async_computation | async-start | bytes 8388608
  235.1 3.7 slice-start.1
  235.1 3.7 copy-start.32
  235.1 3.7 copy-start.33
  292.7 1.6 copy-start.1
  293.2 2.8 copy-start.30
  408.5 2.5 copy-start.4
  409.8 1.1 copy-start.11
  411.1 2.6 copy-start.6
  417.1 35.5 %copy-start.5 = (bf16[4,32,2048]{2,1,0:T(8,128)(2,1)S(1)}, bf16[4,32,2048]{2,1,0:T(8,128)(2,1)}, u32[]{:S(2)}) copy-start(bf16[4,32,2048]{2,1,0:T(8,128)(2,1)} %get-tuple-element.75) | copy-start | bytes 1572868
  417.1 37.7 %copy-start.16 = (f32[32,1024]{1,0:T(8,128)S(1)}, f32[32,1024]{1,0:T(8,128)}, u32[]{:S(2)}) copy-start(f32[32,1024]{1,0:T(8,128)} %get-tuple-element.76) | copy-start | bytes 393220
  417.1 39.0 %copy-start.8 = (bf16[2,2,32,1024]{3,2,1,0:T(8,128)(2,1)S(1)}, bf16[2,2,32,1024]{3,2,1,0:T(8,128)(2,1)}, u32[]{:S(2)}) copy-start(bf16[2,2,32,1024]{3,2,1,0:T(8,128)(2,1)} %get-tuple-element.77) | copy-start | bytes 786436
  417.1 73.3 %copy-start.21 = (f32[2,1024]{1,0:T(2,128)S(1)}, f32[2,1024]{1,0:T(2,128)}, u32[]{:S(2)}) copy-start(f32[2,1024]{1,0:T(2,128)} %gains.5) | copy-start | bytes 24580
  417.1 73.3 %copy-start.26 = (f32[2,1024]{1,0:T(2,128)S(1)}, f32[2,1024]{1,0:T(2,128)}, u32[]{:S(2)}) copy-start(f32[2,1024]{1,0:T(2,128)} %param.33) | copy-start | bytes 24580
  417.1 73.3 %copy-start.27 = (f32[2,1024]{1,0:T(2,128)S(1)}, f32[2,1024]{1,0:T(2,128)}, u32[]{:S(2)}) copy-start(f32[2,1024]{1,0:T(2,128)} %param.34) | copy-start | bytes 24580
  451.0 40.1 %copy-start.12 = (f32[128,1024]{1,0:T(8,128)S(1)}, f32[128,1024]{1,0:T(8,128)}, u32[]{:S(2)}) copy-start(f32[128,1024]{1,0:T(8,128)} %param.30) | copy-start | bytes 1572868
  451.0 40.1 %copy-start.13 = (f32[128,1024]{1,0:T(8,128)S(1)}, f32[128,1024]{1,0:T(8,128)}, u32[]{:S(2)}) copy-start(f32[128,1024]{1,0:T(8,128)} %param.31) | copy-start | bytes 1572868
  491.1 1.5 copy-start.15
  491.1 1.5 copy-start.24
  491.1 1.5 copy-start.25
  497.5 3.3 copy-start
  497.5 3.3 copy-start.7
  500.8 6.0 %copy-start.18 = (bf16[4,32,384]{2,1,0:T(8,128)(2,1)S(1)}, bf16[4,32,384]{2,1,0:T(8,128)(2,1)}, u32[]{:S(2)}) copy-start(bf16[4,32,384]{2,1,0:T(8,128)(2,1)} %get-tuple-element.74) | copy-start | bytes 294916
  500.8 6.0 %copy-start.22 = (f32[32,4,384]{2,1,0:T(4,128)S(1)}, f32[32,4,384]{2,1,0:T(4,128)}, u32[]{:S(2)}) copy-start(f32[32,4,384]{2,1,0:T(4,128)} %param.21) | copy-start | bytes 589828
  500.8 5.9 %copy-start.23 = (f32[32,4,384]{2,1,0:T(4,128)S(1)}, f32[32,4,384]{2,1,0:T(4,128)}, u32[]{:S(2)}) copy-start(f32[32,4,384]{2,1,0:T(4,128)} %param.22) | copy-start | bytes 589828
  506.8 2.6 copy-start.19
  506.8 3.3 copy-start.17

commit v3 on v2

v3 whole, which is shorter than its diff:
```python
import functools
import math

import jax
import jax.numpy as jnp
from jax import lax
from jax.experimental import pallas as pl
from jax.experimental.pallas import tpu as pltpu
from jax.sharding import PartitionSpec as P

D = 2048
HQ = 32
HD = 64
FF = 8192
ADAM_STEP = 10


NORM_EPS = 1e-05
ADAM_EPS = 1e-08
BETA_ONE = 0.9
BETA_TWO = 0.95
WEIGHT_DECAY = 0.1
MATRIX_RATE = 0.01
OUTPUT_RATE = 0.9
DOWN_RATE = 3.0
GAIN_RATE = 2.5
CLIP_NORM = 1.0
ROPE_THETA = 500000.0
ROPE_FACTOR = 32.0
LOW_FREQ = 1.0
HIGH_FREQ = 4.0
OLD_CONTEXT = 8192.0

TOKENS = 8192
HALF = 256
HALVES = TOKENS // HALF
ROWS = 128
LINE = 512
WIDTH = 1024
GROUP = 4
PIECE = 32
HIDDEN = 1024
MESH = pl.DeviceIdType.MESH
ANY = pl.ANY
BF = jnp.bfloat16
F32 = jnp.float32
VMEM_LIMIT = 56 * 1024 * 1024
NEVER = -1e30


def place():
    seq = lax.axis_index("seq")
    return (
        seq // 8,
        lax.rem(seq // 2, 4),
        lax.rem(seq, 2),
        lax.axis_index("wide"),
        lax.axis_index("narrow"),
    )


def device(z, y, x, c):
    return (lax.rem(z, 4) * 8 + lax.rem(y, 4) * 2 + lax.rem(x, 2), c, x // 2)


class Wires:
    def __init__(self, send_sem, recv_sem):
        self.send_sem, self.recv_sem, self.used, self.sent = send_sem, recv_sem, 0, []

    def send(self, src, dst, target, start=True):
        at = self.used
        self.used += 1
        copy = pltpu.make_async_remote_copy(
            src_ref=src,
            dst_ref=dst,
            send_sem=self.send_sem.at[at],
            recv_sem=self.recv_sem.at[at],
            device_id=target,
            device_id_type=MESH,
        )
        if start:
            copy.start()
        self.sent.append(copy)
        return at

    def landed(self, at, region):
        pltpu.make_async_copy(region, region, self.recv_sem.at[at]).wait()

    def close(self):
        for copy in self.sent:
            copy.wait_send()


def greet(targets):
    barrier = pltpu.get_barrier_semaphore()
    for target in targets:
        pl.semaphore_signal(barrier, inc=1, device_id=target, device_id_type=MESH)
    pl.semaphore_wait(barrier, len(targets))


def line_targets(z, y, x, c):
    return [device(z, y, lax.rem(x + o, 4), c) for o in (1, 2, 3)] + [device(z, y, x, 1 - c)]


def plane_targets(z, y, x, c):
    return [device(z + o, y, x, c) for o in (1, 2, 3)] + [device(z, y + o, x, c) for o in (1, 2, 3)]


def wire_scratch(count):
    return [pltpu.SemaphoreType.DMA((count,)), pltpu.SemaphoreType.DMA((count,))]


def comm_params(number):
    return pltpu.CompilerParams(
        collective_id=number, has_side_effects=True, vmem_limit_bytes=VMEM_LIMIT
    )


def rows_of(x):
    return lax.rem(x, 2) * 2 + x // 2


def row_span(x):
    return pl.ds(pl.multiple_of(rows_of(x) * ROWS, ROWS), ROWS)


def col_span(c):
    return pl.ds(pl.multiple_of(c * WIDTH, WIDTH), WIDTH)


def gather_sends(wires, own, out, here):
    z, y, x, c = here
    spot = out.at[row_span(x), col_span(c)]
    across = {o: wires.send(own, spot, device(z, y, lax.rem(x + o, 4), c)) for o in (2, 1, 3)}
    return across, wires.send(own, spot, device(z, y, x, 1 - c))


def gather_relay(wires, numbers, out, here):
    z, y, x, c = here
    across, direct = numbers
    relays = []
    for o in (1, 3, 2):
        rows = row_span(lax.rem(x + 4 - o, 4))
        spot = out.at[rows, col_span(c)]
        wires.landed(across[o], spot)
        relays.append((wires.send(spot, spot, device(z, y, x, 1 - c)), rows))
    wires.landed(direct, out.at[row_span(x), col_span(1 - c)])
    for at, rows in relays:
        wires.landed(at, out.at[rows, col_span(1 - c)])


FOLD_ORDER = (2, 1, 3, 0)


def fold_sends(wires, part, folded, here):
    z, y, x, c = here
    return [
        wires.send(
            part.at[row_span(lax.rem(x + o, 4)), col_span(1 - c)],
            folded.at[k],
            device(z, y, x, 1 - c),
        )
        for k, o in enumerate(FOLD_ORDER)
    ]


def fold_moves(wires, numbers, part, folded, leaving, arriving, here, total):
    z, y, x, c = here
    moves = []
    for k, o in enumerate(FOLD_ORDER):
        wires.landed(numbers[k], folded.at[k])
        both = part[row_span(lax.rem(x + o, 4)), col_span(c)].astype(F32) + folded[k].astype(F32)
        if o:
            leaving[k] = both.astype(BF)
            moves.append(
                wires.send(leaving.at[k], arriving.at[k], device(z, y, lax.rem(x + o, 4), c))
            )
        else:
            total[...] = both
    return moves


def fold_finish(wires, moves, arriving, total):
    for k, at in enumerate(moves):
        wires.landed(at, arriving.at[k])
    total[...] = (
        total[...]
        + arriving[0].astype(F32)
        + arriving[1].astype(F32)
        + arriving[2].astype(F32)
    )


def fold_scratch():
    return [
        pltpu.VMEM((4, ROWS, WIDTH), BF),
        pltpu.VMEM((3, ROWS, WIDTH), BF),
        pltpu.VMEM((3, ROWS, WIDTH), BF),
        pltpu.VMEM((ROWS, WIDTH), F32),
    ]


def both_cores(wires, mine, theirs, value, here):
    z, y, x, c = here
    mine[...] = jnp.broadcast_to(value, mine.shape)
    at = wires.send(mine, theirs, device(z, y, x, 1 - c))
    wires.landed(at, theirs)
    return value + theirs[:, :1]


EVERY = slice(None)


def first_device(here, order, by):
    z, y, x, c = here
    return device(z + by, y, x, c) if order == 0 else device(z, y + by, x, c)


def second_device(here, order, by):
    z, y, x, c = here
    return device(z, y + by, x, c) if order == 0 else device(z + by, y, x, c)


def first_at(here, order, by=0):
    return lax.rem((here[0] if order == 0 else here[1]) + by, 4)


def run_of(ref, here, order, by, sub=None):
    z, y, _, _ = here
    zi, yi = (EVERY, lax.rem(y + by, 4)) if order == 0 else (lax.rem(z + by, 4), EVERY)
    if len(ref.shape) == 6:
        return ref.at[order, zi, yi] if sub is None else ref.at[order, zi, yi, sub]
    rows = ref.shape[2] // 2
    if sub is None:
        return ref.at[zi, yi, pl.ds(order * rows, rows)]
    return ref.at[zi, yi, pl.ds(order * rows + sub * (rows // 2), rows // 2)]


def spot_of(ref, here, order, at, sub=None):
    z, y, _, _ = here
    zi, yi = (at, y) if order == 0 else (z, at)
    if len(ref.shape) == 6:
        return ref.at[order, zi, yi] if sub is None else ref.at[order, zi, yi, sub]
    rows = ref.shape[2] // 2
    if sub is None:
        return ref.at[zi, yi, pl.ds(order * rows, rows)]
    return ref.at[zi, yi, pl.ds(order * rows + sub * (rows // 2), rows // 2)]


class PlaneGather:
    def __init__(self, wires, whole, here):
        self.wires, self.whole, self.here = wires, whole, here

    def start(self):
        self.numbers = []
        for o in (0, 1):
            spot = spot_of(self.whole, self.here, o, first_at(self.here, o))
            self.numbers.append(
                [self.wires.send(spot, spot, first_device(self.here, o, by)) for by in (1, 3)]
            )

    def relay(self):
        relays = []
        for o in (0, 1):
            sends = []
            for sub, by in enumerate((1, 3)):
                at = first_at(self.here, o, 4 - by)
                self.wires.landed(self.numbers[o][sub], spot_of(self.whole, self.here, o, at))
                spot = spot_of(self.whole, self.here, o, at, sub)
                sends.append(self.wires.send(spot, spot, first_device(self.here, o, by)))
            relays.append(sends)
        self.numbers = relays

    def turn(self):
        lines = []
        for o in (0, 1):
            for sub in (0, 1):
                at = first_at(self.here, o, 2)
                self.wires.landed(
                    self.numbers[o][sub], spot_of(self.whole, self.here, o, at, sub)
                )
            spot = run_of(self.whole, self.here, o, 0)
            lines.append(
                [self.wires.send(spot, spot, second_device(self.here, o, by)) for by in (1, 3)]
            )
        self.numbers = lines

    def relay_two(self):
        relays = []
        for o in (0, 1):
            sends = []
            for sub, by in enumerate((1, 3)):
                self.wires.landed(self.numbers[o][sub], run_of(self.whole, self.here, o, 4 - by))
                spot = run_of(self.whole, self.here, o, 4 - by, sub)
                sends.append(self.wires.send(spot, spot, second_device(self.here, o, by)))
            relays.append(sends)
        self.numbers = relays

    def finish(self):
        for o in (0, 1):
            for sub in (0, 1):
                self.wires.landed(
                    self.numbers[o][sub], run_of(self.whole, self.here, o, 2, sub)
                )


OFFSETS = (2, 1, 3)


class PlaneSum:
    def __init__(self, wires, terms, buffers, here, local_sem, at):
        self.wires, self.terms, self.here = wires, terms, here
        self.far, self.joined, self.rec, self.total, self.rec_two, self.fin = buffers
        self.kept, self.added = [], []
        for o in (0, 1):
            self.kept.append(
                pltpu.make_async_copy(
                    run_of(terms, here, o, 0), self.total.at[o], local_sem.at[at + 3 * o]
                )
            )
            self.added.append(
                [
                    pltpu.make_async_copy(
                        run_of(terms, here, o, by, sub),
                        self.joined.at[o, sub],
                        local_sem.at[at + 3 * o + 1 + sub],
                    )
                    for sub, by in enumerate((1, 3))
                ]
            )

    def start(self):
        self.numbers = []
        for o in (0, 1):
            self.numbers.append(
                [
                    self.wires.send(
                        run_of(self.terms, self.here, o, 2, sub),
                        self.far.at[o, sub],
                        second_device(self.here, o, by),
                    )
                    for sub, by in enumerate((1, 3))
                ]
            )
        for o in (0, 1):
            for copy in self.added[o]:
                copy.start()
        self.direct = []
        for o in (0, 1):
            self.direct.append(
                [
                    self.wires.send(
                        run_of(self.terms, self.here, o, by, 1 - sub),
                        half_of(self.rec.at[o, sub], 1 - sub),
                        second_device(self.here, o, by),
                    )
                    for sub, by in enumerate((1, 3))
                ]
            )
        for copy in self.kept:
            copy.start()

    def relay(self):
        self.passed = []
        for o in (0, 1):
            moves = []
            for sub, by in enumerate((1, 3)):
                self.added[o][sub].wait()
                self.wires.landed(self.numbers[o][sub], self.far.at[o, sub])

                def add(i, carry):
                    value = self.joined[o, sub, i].astype(F32) + self.far[o, sub, i].astype(F32)
                    self.joined[o, sub, i] = value.astype(BF)
                    return carry

                lax.fori_loop(0, 4, add, 0)
                moves.append(
                    self.wires.send(
                        self.joined.at[o, sub],
                        half_of(self.rec.at[o, sub], sub),
                        second_device(self.here, o, by),
                    )
                )
            self.passed.append(moves)

    def middle(self):
        self.moves = []
        for o in (0, 1):
            self.kept[o].wait()
            for sub in (0, 1):
                self.wires.landed(self.direct[o][sub], half_of(self.rec.at[o, sub], 1 - sub))
                self.wires.landed(self.passed[o][sub], half_of(self.rec.at[o, sub], sub))

            def add(i, carry):
                value = self.total[o, i].astype(F32)
                for sub in (0, 1):
                    value = value + self.rec[o, sub, i].astype(F32)
                self.total[o, i] = value.astype(BF)
                return carry

            lax.fori_loop(0, 4, add, 0)
            self.moves.append(
                [
                    self.wires.send(
                        self.total.at[o, first_at(self.here, o, by)],
                        self.rec_two.at[o, k],
                        first_device(self.here, o, by),
                    )
                    for k, by in enumerate(OFFSETS)
                ]
            )

    def finish(self):
        for o in (0, 1):
            for k in range(3):
                self.wires.landed(self.moves[o][k], self.rec_two.at[o, k])
            value = self.total[o, first_at(self.here, o)].astype(F32)
            for k in range(3):
                value = value + self.rec_two[o, k].astype(F32)
            self.fin[o] = value.astype(self.fin.dtype)


def half_of(line, sub):
    if len(line.shape) == 4:
        return line.at[:, sub]
    rows = line.shape[1] // 2
    return line.at[:, pl.ds(sub * rows, rows)]


def sum_buffers(piece, kind):
    half = piece[1:] if len(piece) == 3 else (piece[0] // 2,) + piece[1:]
    return [
        pltpu.VMEM((2, 2, 4) + half, BF),
        pltpu.VMEM((2, 2, 4) + half, BF),
        pltpu.VMEM((2, 2, 4) + piece, BF),
        pltpu.VMEM((2, 4) + piece, BF),
        pltpu.VMEM((2, 3) + piece, BF),
        pltpu.VMEM((2,) + piece, kind),
    ]


class OutGather:
    def __init__(self, wires, stage, whole, here, mine, send_sem, recv_sem, local_sem, at):
        z, y, x, c = here
        self.wires, self.stage, self.whole, self.here = wires, stage, whole, here
        self.off = lax.rem(z - mine + 4, 4)
        self.recv_sem = recv_sem
        spot = whole.at[y]
        self.kept = pltpu.make_async_copy(stage, spot, local_sem.at[at])

        def copy(k, src, dst, by):
            return pltpu.make_async_remote_copy(
                src_ref=src,
                dst_ref=dst,
                send_sem=send_sem.at[k],
                recv_sem=recv_sem.at[k],
                device_id=device(z + by, y, x, c),
                device_id_type=MESH,
            )

        self.first = [copy(0, stage, spot, 1), copy(1, stage, spot, 3)]
        self.onward = [
            copy(2, spot.at[0], spot.at[0], 1),
            copy(3, spot.at[1], spot.at[1], 3),
        ]

    def landed(self, k, region):
        pltpu.make_async_copy(region, region, self.recv_sem.at[k]).wait()

    def start(self):
        @pl.when(self.off == 0)
        def _():
            self.kept.start()
            for copy in self.first:
                copy.start()

    def relay(self):
        spot = self.whole.at[self.here[1]]
        for k, off in ((0, 1), (1, 3)):

            @pl.when(self.off == off)
            def _():
                self.landed(k, spot)
                self.onward[k].start()

    def turn(self):
        z, y, x, c = self.here
        spot = self.whole.at[y]

        @pl.when(self.off == 0)
        def _():
            self.kept.wait()

        @pl.when(self.off == 2)
        def _():
            self.landed(2, spot.at[0])
            self.landed(3, spot.at[1])

        self.numbers = [self.wires.send(spot, spot, device(z, y + by, x, c)) for by in (1, 3)]

    def relay_two(self):
        z, y, x, c = self.here
        relays = []
        for sub, by in enumerate((1, 3)):
            spot = self.whole.at[lax.rem(y + 4 - by, 4)]
            self.wires.landed(self.numbers[sub], spot)
            relays.append(
                self.wires.send(spot.at[sub], spot.at[sub], device(z, y + by, x, c))
            )
        self.numbers = relays

    def finish(self):
        spot = self.whole.at[lax.rem(self.here[1] + 2, 4)]
        for sub in (0, 1):
            self.wires.landed(self.numbers[sub], spot.at[sub])

        @pl.when(self.off == 0)
        def _():
            for copy in self.first:
                copy.wait_send()

        for k, off in ((0, 1), (1, 3)):

            @pl.when(self.off == off)
            def _():
                self.onward[k].wait_send()


class OutSum:
    def __init__(self, wires, terms, buffers, piece, here, mine, quad, sems, local_sem, at):
        self.wires, self.terms, self.here, self.mine, self.quad = wires, terms, here, mine, quad
        self.rec, self.total, self.rec_two = buffers
        self.piece, self.local_sem, self.at = piece, local_sem, at
        self.send_sem, self.recv_sem = sems
        self.off = lax.rem(here[0] - mine + 4, 4)
        self.kept = pltpu.make_async_copy(
            terms.at[here[1]], self.total, local_sem.at[at]
        )

    def start(self):
        z, y, x, c = self.here
        self.kept.start()
        self.numbers = [
            self.wires.send(
                self.terms.at[lax.rem(y + by, 4)], self.rec.at[k], device(z, y + by, x, c)
            )
            for k, by in enumerate(OFFSETS)
        ]

    def copy(self, k, src, dst, target):
        return pltpu.make_async_remote_copy(
            src_ref=src,
            dst_ref=dst,
            send_sem=self.send_sem.at[k],
            recv_sem=self.recv_sem.at[k],
            device_id=target,
            device_id_type=MESH,
        )

    def middle(self):
        z, y, x, c = self.here
        self.kept.wait()
        value = self.total[...].astype(F32)
        for k in range(3):
            self.wires.landed(self.numbers[k], self.rec.at[k])
            value = value + self.rec[k].astype(F32)
        self.total[...] = value.astype(BF)
        self.moves = []
        for off in (1, 2, 3):
            move = self.copy(
                off - 1, self.total, self.rec_two.at[off - 1], device(self.mine, y, x, c)
            )
            self.moves.append(move)

            @pl.when(self.off == off)
            def _():
                move.start()

    def deal(self):
        z, y, x, c = self.here
        self.deals = []
        xl = lax.rem(x, 2)
        for k, (a, b) in enumerate(self.quad):
            self.deals.append(
                self.copy(
                    3 + k, self.total.at[lax.rem(a, 2), :, col_span(b)], self.piece, device(z, y, a, b)
                )
            )

        @pl.when(self.off == 0)
        def _():
            value = self.total[...].astype(F32)
            for k in range(3):
                region = self.rec_two.at[k]
                pltpu.make_async_copy(region, region, self.recv_sem.at[k]).wait()
                value = value + self.rec_two[k].astype(F32)
            self.total[...] = value.astype(BF)
            for copy in self.deals:
                copy.start()
            own = pltpu.make_async_copy(
                self.total.at[xl, :, col_span(c)], self.piece, self.local_sem.at[self.at]
            )
            own.start()
            own.wait()

    def finish(self):
        z, y, x, c = self.here
        xl = lax.rem(x, 2)
        holder_xl, holder_c = z // 2, lax.rem(z, 2)
        for k, (dx, dc) in enumerate(((0, 1), (1, 0), (1, 1))):

            @pl.when(
                (holder_xl == lax.rem(xl + dx, 2)) & (holder_c == lax.rem(c + dc, 2))
            )
            def _():
                pltpu.make_async_copy(self.piece, self.piece, self.recv_sem.at[3 + k]).wait()

        for off in (1, 2, 3):

            @pl.when(self.off == off)
            def _():
                self.moves[off - 1].wait_send()

        @pl.when(self.off == 0)
        def _():
            for copy in self.deals:
                copy.wait_send()


class Posting:
    def __init__(self, here, send_sem, recv_sem):
        z, y, x, c = here
        self.target = device(3 - z, 3 - y, x, c)
        self.away = lax.rem(x, 2) == 1
        self.send_sem, self.recv_sem, self.sent = send_sem, recv_sem, []

    def greet(self, barrier):
        @pl.when(self.away)
        def _():
            pl.semaphore_signal(barrier, inc=1, device_id=self.target, device_id_type=MESH)

        return self.away.astype(jnp.int32)

    def send(self, src, dst):
        at = len(self.sent)
        copy = pltpu.make_async_remote_copy(
            src_ref=src,
            dst_ref=dst,
            send_sem=self.send_sem.at[at],
            recv_sem=self.recv_sem.at[at],
            device_id=self.target,
            device_id_type=MESH,
        )
        self.sent.append(copy)

        @pl.when(self.away)
        def _():
            copy.start()

        @pl.when(jnp.logical_not(self.away))
        def _():
            pltpu.make_async_copy(src, dst, self.recv_sem.at[at]).start()

        return at

    def landed(self, at, region):
        pltpu.make_async_copy(region, region, self.recv_sem.at[at]).wait()

    def close(self):
        @pl.when(self.away)
        def _():
            for copy in self.sent:
                copy.wait_send()


def quad_of(xl, xh, x, c):
    pair = xh * 2 + 1 - xl
    return [(x, 1 - c), (pair, c), (pair, 1 - c)]


def norm_back(wires, values, scale, gain_row, incoming, mine, theirs, here):
    weighted = incoming * gain_row
    inner = both_cores(
        wires, mine, theirs, jnp.sum(weighted * values, axis=1, keepdims=True), here
    )
    inner = inner / D
    back = scale * (incoming * gain_row) - values * (scale * scale * scale * inner)
    return back, jnp.sum(incoming * values * scale, axis=0, keepdims=True)


def back_kernel(
    part, middle, scale, gains, cotangent, grad_down, grad_up,
    middle_grad, gain_out, out, down_out, up_out,
    folded, leaving, arriving, total, mine, theirs, own, *rest,
):
    down_buffers, up_buffers, (send_sem, recv_sem, local_sem) = rest[:6], rest[6:12], rest[12:]
    z, y, xl, xh, c = place()
    x = xh * 2 + xl
    here = (z, y, x, c)
    greet(line_targets(z, y, x, c) + plane_targets(z, y, x, c))
    wires = Wires(send_sem, recv_sem)
    numbers = fold_sends(wires, part, folded, here)
    down = PlaneSum(wires, grad_down, down_buffers, here, local_sem, 0)
    up = PlaneSum(wires, grad_up, up_buffers, here, local_sem, 6)
    down.start()
    up.start()
    moves = fold_moves(wires, numbers, part, folded, leaving, arriving, here, total)
    down.relay()
    up.relay()
    fold_finish(wires, moves, arriving, total)
    back, gain_sum = norm_back(
        wires, middle[...], scale[:, :1], gains[1:2, :], total[...], mine, theirs, here
    )
    gain_out[...] = jnp.broadcast_to(gain_sum, gain_out.shape)
    grad = cotangent[...].astype(F32) + back
    middle_grad[...] = grad
    own[...] = grad.astype(BF)
    local = pltpu.make_async_copy(own, out.at[row_span(x), col_span(c)], local_sem.at[12])
    local.start()
    sends = gather_sends(wires, own, out, here)
    down.middle()
    gather_relay(wires, sends, out, here)
    up.middle()
    down.finish()
    up.finish()
    kept = [
        pltpu.make_async_copy(down_buffers[5], down_out, local_sem.at[13]),
        pltpu.make_async_copy(up_buffers[5], up_out, local_sem.at[14]),
        local,
    ]
    for copy in kept[:2]:
        copy.start()
    for copy in kept:
        copy.wait()
    wires.close()


def call_back(part, middle, scale, gains, cotangent, grad_down, grad_up):
    vm = pl.BlockSpec(memory_space=pltpu.VMEM)
    hbm = pl.BlockSpec(memory_space=ANY)
    return pl.pallas_call(
        back_kernel,
        out_shape=(
            jax.ShapeDtypeStruct((ROWS, WIDTH), F32),
            jax.ShapeDtypeStruct((8, WIDTH), F32),
            jax.ShapeDtypeStruct((LINE, D), BF),
            jax.ShapeDtypeStruct((2, PIECE, D), BF),
            jax.ShapeDtypeStruct((2, 2, PIECE, HIDDEN), BF),
        ),
        in_specs=[vm] * 5 + [hbm] * 2,
        out_specs=(vm, vm, hbm, hbm, hbm),
        scratch_shapes=fold_scratch()
        + [
            pltpu.VMEM((ROWS, 128), F32),
            pltpu.VMEM((ROWS, 128), F32),
            pltpu.VMEM((ROWS, WIDTH), BF),
        ]
        + sum_buffers((PIECE, D), BF)
        + sum_buffers((2, PIECE, HIDDEN), BF)
        + wire_scratch(56)
        + [pltpu.SemaphoreType.DMA((15,))],
        compiler_params=comm_params(3),
        name="line_back",
    )(part, middle, scale, gains, cotangent, grad_down, grad_up)


PLANE = [(a, b) for a in range(4) for b in range(4) if a or b]


def last_kernel(
    part, inputs, scale, gains, middle_grad, gain_two, squares, output, grad_qkv,
    input_home, output_home, qkv_out, totals,
    folded, leaving, arriving, total, mine, theirs, *rest,
):
    buffers, rest = rest[:6], rest[6:]
    landing, terms, stage, rec_one, rec_two = rest[:5]
    send_sem, recv_sem, post_send, post_recv, local_sem = rest[5:]
    fin = buffers[5]
    z, y, xl, xh, c = place()
    x = xh * 2 + xl
    here = (z, y, x, c)
    quad = quad_of(xl, xh, x, c)
    line = [(o, b) for b in (0, 1) for o in range(4) if o or b]
    fixed = [device(z + a, y + b, x, c) for a, b in PLANE]
    fixed += [device(z, y, lax.rem(x + o, 4), lax.rem(c + b, 2)) for o, b in line]
    barrier = pltpu.get_barrier_semaphore()
    post = Posting(here, post_send, post_recv)
    for target in fixed:
        pl.semaphore_signal(barrier, inc=1, device_id=target, device_id_type=MESH)
    extra = post.greet(barrier)
    pl.semaphore_wait(barrier, len(fixed) + extra)
    wires = Wires(send_sem, recv_sem)
    numbers = fold_sends(wires, part, folded, here)
    qkv = PlaneSum(wires, grad_qkv, buffers, here, local_sem, 0)
    qkv.start()
    output_at = post.send(output, output_home)
    moves = fold_moves(wires, numbers, part, folded, leaving, arriving, here, total)
    qkv.relay()
    qkv.middle()
    fold_finish(wires, moves, arriving, total)
    back, gain_one = norm_back(
        wires,
        inputs[...].astype(F32),
        scale[:, :1],
        gains[0:1, :],
        total[...],
        mine,
        theirs,
        here,
    )
    total[...] = middle_grad[...] + back
    input_at = post.send(total, input_home)
    qkv.finish()
    at_mine = xl * 2 + c
    swaps = [
        wires.send(fin.at[b, lax.rem(a, 2)], landing.at[at_mine], device(z, y, a, b))
        for a, b in quad
    ]
    landing[at_mine] = fin[c, xl]
    for at, (a, b) in zip(swaps, quad):
        wires.landed(at, landing.at[lax.rem(a, 2) * 2 + b])
    square = squares[...]
    for k in range(4):
        value = landing[k].astype(F32)
        square = square + jnp.sum(value * value)
    qkv_out[...] = landing[...]

    for k in range(8):
        cols = slice(k * 128, (k + 1) * 128)
        terms[k : k + 1] = gain_one[:, cols]
        terms[8 + k : 9 + k] = gain_two[0:1, cols]
    terms[16:] = square
    first = [
        wires.send(terms, rec_one.at[k], device(z + a, y + b, x, c))
        for k, (a, b) in enumerate(PLANE)
    ]
    value = terms[...]
    for k, at in enumerate(first):
        wires.landed(at, rec_one.at[k])
        value = value + rec_one[k]
    stage[...] = value
    second = [
        wires.send(stage, rec_two.at[k], device(z, y, lax.rem(x + o, 4), lax.rem(c + b, 2)))
        for k, (o, b) in enumerate(line)
    ]
    both = [value, None]
    for k, (o, b) in enumerate(line):
        wires.landed(second[k], rec_two.at[k])
        both[b] = rec_two[k] if both[b] is None else both[b] + rec_two[k]
    totals[:16] = both[0][:16]
    totals[16:] = (
        both[0][16:]
        + both[1][16:]
        + jnp.sum(both[0][:16] * both[0][:16])
        + jnp.sum(both[1][:16] * both[1][:16])
    )
    post.landed(output_at, output_home)
    post.landed(input_at, input_home)
    post.close()
    wires.close()


def call_last(part, inputs, scale, gains, middle_grad, gain_two, squares, output, grad_qkv):
    vm = pl.BlockSpec(memory_space=pltpu.VMEM)
    hbm = pl.BlockSpec(memory_space=ANY)
    cols = grad_qkv.shape[-1]
    return pl.pallas_call(
        last_kernel,
        out_shape=(
            jax.ShapeDtypeStruct((ROWS, WIDTH), F32),
            jax.ShapeDtypeStruct((ROWS, WIDTH), BF),
            jax.ShapeDtypeStruct((4, PIECE, cols), BF),
            jax.ShapeDtypeStruct((24, 128), F32),
        ),
        in_specs=[vm] * 7 + [hbm, hbm],
        out_specs=(hbm, hbm, vm, vm),
        scratch_shapes=fold_scratch()
        + [pltpu.VMEM((ROWS, 128), F32), pltpu.VMEM((ROWS, 128), F32)]
        + sum_buffers((2, PIECE, cols), BF)
        + [
            pltpu.VMEM((4, PIECE, cols), BF),
            pltpu.VMEM((24, 128), F32),
            pltpu.VMEM((24, 128), F32),
            pltpu.VMEM((15, 24, 128), F32),
            pltpu.VMEM((7, 24, 128), F32),
        ]
        + wire_scratch(64)
        + wire_scratch(2)
        + [pltpu.SemaphoreType.DMA((6,))],
        compiler_params=comm_params(4),
        name="line_last",
    )(part, inputs, scale, gains, middle_grad, gain_two, squares, output, grad_qkv)


def key_at(half):
    odd = lax.rem(half, 2)
    at = jnp.where(odd == 1, HALVES - 1 - half, half) // 2
    return odd, at // 4, lax.rem(at, 4)


def allowed_pairs(key_half, query_half, ends):
    keys = key_half * HALF + lax.broadcasted_iota(jnp.int32, (HALF, HALF), 0)
    queries = query_half * HALF + lax.broadcasted_iota(jnp.int32, (HALF, HALF), 1)
    same = keys <= queries
    for k in range(3):
        same = same & ((keys >= ends[k]) == (queries >= ends[k]))
    return same


def in_second(query_half, ends):
    queries = query_half * HALF + lax.broadcasted_iota(jnp.int32, (1, HALF), 1)
    return (queries >= ends[0]) & (queries < ends[1])


class Tour:
    def __init__(self, spot):
        self.spot = spot
        self.low = jnp.maximum(2 * spot - 1, 0)
        self.count = self.low + HALVES - 2 - 2 * spot

    def half(self, s):
        return jnp.where(s == 0, 2 * self.spot, HALVES - 1 - 2 * self.spot)

    def inner(self, step, start, stop):
        def body(at, carry):
            s = jnp.where(at >= self.low, 1, 0)
            step(s, 1 + at - s * self.low, False)
            return carry

        lax.fori_loop(start, stop, body, 0)

    def edges(self, step):
        for s in (0, 1):
            half = self.half(s)

            def body(at, carry):
                step(s, at * half, True)
                return carry

            lax.fori_loop(0, jnp.where(half > 0, 2, 1), body, 0)


def head_cols(g):
    return slice(g * HALF, (g + 1) * HALF)


def rope(columns, at, cosine, sine):
    first = columns[at : at + HD // 2]
    second = columns[at + HD // 2 : at + HD]
    return first * cosine - second * sine, second * cosine + first * sine


def forward_kernel(
    ends, cosine, sine, block_input, out_grad, gain_rows, qkv_in, gate_in, up_in, down_in, out_in,
    inputs, scale_one, normed_out, qkv_out, queries, mixed_out, log_out, attended, keys_out,
    cotangent, cotangent_all, out_out, gate_all, up_all, down_all, middle_out, scale_two, out,
    inputs_all, gains_all, qkv_all, normed, columns, own_keys, keys, tops, sums, mixed,
    out_stage, out_all, part, folded, leaving, arriving, total, mine_row, their_row, own,
    send_sem, recv_sem, post_send, post_recv, stage_send, stage_recv, out_send, out_recv, local_sem,
):
    z, y, xl, xh, c = place()
    x = xh * 2 + xl
    here = (z, y, x, c)
    mine = xl * 2 + c
    quad = quad_of(xl, xh, x, c)
    fixed = line_targets(z, y, x, c) + [device(z, y, *quad[2])] + plane_targets(z, y, x, c)
    barrier = pltpu.get_barrier_semaphore()
    post = Posting(here, post_send, post_recv)
    for target in fixed:
        pl.semaphore_signal(barrier, inc=1, device_id=target, device_id_type=MESH)
    extra = post.greet(barrier)
    pl.semaphore_wait(barrier, len(fixed) + extra)
    wires = Wires(send_sem, recv_sem)
    kept = {}

    def keep(name, src, dst):
        copy = pltpu.make_async_copy(src, dst, local_sem.at[len(kept)])
        copy.start()
        kept[name] = copy

    def swap(given, whole):
        numbers = [
            wires.send(
                given.at[lax.rem(to, 2) * 2 + core], whole.at[c, z, y, xl], device(z, y, to, core)
            )
            for to, core in quad
        ]
        return numbers

    def swapped(numbers, whole):
        for at, (from_x, from_c) in zip(numbers, quad):
            wires.landed(at, whole.at[from_c, z, y, lax.rem(from_x, 2)])

    input_at = post.send(block_input, inputs)
    keep("qkv", qkv_in.at[mine], qkv_all.at[c, z, y, xl])
    qkv_swap = swap(qkv_in, qkv_all)
    keep("gains", gain_rows, gains_all.at[:, col_span(c)])
    gain_at = wires.send(gain_rows, gains_all.at[:, col_span(c)], device(z, y, x, 1 - c))
    keep("gate", gate_in.at[mine], gate_all.at[c, z, y, xl])
    keep("up", up_in.at[mine], up_all.at[c, z, y, xl])
    keep("down", down_in.at[c], down_all.at[z, y, :, col_span(c)])
    down_swap = wires.send(
        down_in.at[1 - c], down_all.at[z, y, :, col_span(c)], device(z, y, x, 1 - c)
    )
    holds = z == mine
    stage_spot = out_stage.at[xl, :, col_span(c)]
    stage_copy = pltpu.make_async_remote_copy(
        src_ref=out_in,
        dst_ref=stage_spot,
        send_sem=stage_send.at[0],
        recv_sem=stage_recv.at[mine],
        device_id=device(z, y, xh * 2 + z // 2, lax.rem(z, 2)),
        device_id_type=MESH,
    )

    @pl.when(jnp.logical_not(holds))
    def _():
        stage_copy.start()

    @pl.when(holds)
    def _():
        pltpu.make_async_copy(out_in, stage_spot, stage_recv.at[mine]).start()

    qkv = PlaneGather(wires, qkv_all, here)
    gate = PlaneGather(wires, gate_all, here)
    up = PlaneGather(wires, up_all, here)
    down = PlaneGather(wires, down_all, here)
    out_gather = OutGather(
        wires, out_stage, out_all, here, mine, out_send, out_recv, local_sem, 12
    )

    kept["qkv"].wait()
    swapped(qkv_swap, qkv_all)
    qkv.start()
    post.landed(input_at, inputs)
    keep("inputs", inputs, inputs_all.at[row_span(x), col_span(c)])
    input_numbers = gather_sends(wires, inputs, inputs_all, here)
    gate_swap = swap(gate_in, gate_all)
    up_swap = swap(up_in, up_all)
    cotangent_at = post.send(out_grad, cotangent)
    qkv.relay()
    qkv.turn()
    gather_relay(wires, input_numbers, inputs_all, here)
    qkv.relay_two()
    kept["inputs"].wait()
    kept["gains"].wait()
    wires.landed(gain_at, gains_all.at[:, col_span(1 - c)])
    gain_one = gains_all[0:1, :]

    def norm_rows(i, carry):
        rows = pl.ds(pl.multiple_of(i * ROWS, ROWS), ROWS)
        values = inputs_all[rows, :].astype(F32)
        scale = lax.rsqrt(jnp.sum(values * values, axis=1, keepdims=True) / D + NORM_EPS)
        normed[rows, :] = (values * scale * gain_one).astype(BF)

        @pl.when(i == rows_of(x))
        def _():
            scale_one[...] = jnp.broadcast_to(scale, scale_one.shape)

        return carry

    lax.fori_loop(0, 4, norm_rows, 0)
    keep("normed", normed, normed_out)
    swapped(gate_swap, gate_all)
    kept["gate"].wait()
    gate.start()
    swapped(up_swap, up_all)
    kept["up"].wait()
    up.start()
    qkv.finish()
    keep("qkv_out", qkv_all, qkv_out)
    weight = qkv_all[...].reshape(D, columns.shape[0])

    def project_rows(i, carry):
        rows = pl.ds(pl.multiple_of(i * ROWS, ROWS), ROWS)
        product = jnp.dot(normed[rows, :], weight, preferred_element_type=F32)
        columns[:, rows] = product.T
        return carry

    lax.fori_loop(0, 4, project_rows, 0)
    queries[:, HD:, :] = jnp.zeros((2, HD, GROUP * HALF), BF)
    for g in range(GROUP):
        first, second = rope(columns, g * HD, cosine[...], sine[...])
        for s in (0, 1):
            tokens = slice(s * HALF, (s + 1) * HALF)
            queries[s, : HD // 2, head_cols(g)] = (first[:, tokens] * HD ** (-0.5)).astype(BF)
            queries[s, HD // 2 : HD, head_cols(g)] = (second[:, tokens] * HD ** (-0.5)).astype(BF)
    first, second = rope(columns, GROUP * HD, cosine[...], sine[...])
    pair_columns = jnp.concatenate([first, second, columns[(GROUP + 1) * HD :]], axis=0)
    for s in (0, 1):
        own_keys[s] = pair_columns[:, s * HALF : (s + 1) * HALF].T.astype(BF)

    numbers = [
        [
            wires.send(own_keys.at[s], keys.at[s, z, y], first_device(here, s, by))
            for by in OFFSETS
        ]
        for s in (0, 1)
    ]
    for s in (0, 1):
        keys[s, z, y] = own_keys[s]
    second_numbers = []
    for s in (0, 1):
        for at, by in zip(numbers[s], OFFSETS):
            back = first_at(here, s, 4 - by)
            wires.landed(at, keys.at[s, back, y] if s == 0 else keys.at[s, z, back])
        line = keys.at[0, :, y] if s == 0 else keys.at[1, z]
        second_numbers.append(
            [wires.send(line, line, second_device(here, s, by)) for by in OFFSETS]
        )

    @pl.when(holds)
    def _():
        for k in range(4):
            spot = out_stage.at[k // 2, :, pl.ds((k % 2) * WIDTH, WIDTH)]
            pltpu.make_async_copy(spot, spot, stage_recv.at[k]).wait()

    out_gather.start()
    gate.relay()
    up.relay()
    post.landed(cotangent_at, cotangent)
    keep("cotangent", cotangent, cotangent_all.at[row_span(x), col_span(c)])
    cotangent_numbers = gather_sends(wires, cotangent, cotangent_all, here)
    for s in (0, 1):
        for at, by in zip(second_numbers[s], OFFSETS):
            if s == 0:
                wires.landed(at, keys.at[0, :, lax.rem(y + 4 - by, 4)])
            else:
                wires.landed(at, keys.at[1, lax.rem(z + 4 - by, 4)])
    keep("keys", keys, keys_out)
    out_gather.relay()
    gate.turn()
    up.turn()

    tour = Tour(spot=z * 4 + y)
    tops[...] = jnp.full(tops.shape, NEVER, F32)
    sums[...] = jnp.zeros(sums.shape, F32)
    mixed[...] = jnp.zeros(mixed.shape, F32)
    heads = range(GROUP)

    def step(s, at, masked):
        pairs = keys[key_at(at)]
        old = [tops[s, :, head_cols(g)] for g in heads]
        old_sums = [sums[s, :, head_cols(g)] for g in heads]
        scores = [
            jnp.dot(pairs, queries[s, :, head_cols(g)], preferred_element_type=F32) for g in heads
        ]
        if masked:
            allowed = allowed_pairs(at, tour.half(s), ends)
            scores = [jnp.where(allowed, value, NEVER) for value in scores]
        top = [jnp.maximum(old[g], jnp.max(scores[g], axis=0, keepdims=True)) for g in heads]
        weights = [jnp.exp(scores[g] - top[g]) for g in heads]
        if masked:
            weights = [jnp.where(allowed, value, 0.0) for value in weights]
        shrink = [jnp.exp(old[g] - top[g]) for g in heads]
        new_sums = [
            old_sums[g] * shrink[g] + jnp.sum(weights[g], axis=0, keepdims=True) for g in heads
        ]
        new = [
            lax.dot_general(
                pairs, weights[g].astype(BF), (((0,), (0,)), ((), ())), preferred_element_type=F32
            )
            for g in heads
        ]
        for g in heads:
            cols = head_cols(g)
            tops[s, :, cols] = top[g]
            sums[s, :, cols] = new_sums[g]
            mixed[s, :, cols] = mixed[s, :, cols] * shrink[g] + new[g]

    tour.inner(step, 0, 6)
    out_gather.turn()
    gather_relay(wires, cotangent_numbers, cotangent_all, here)
    kept["down"].wait()
    wires.landed(down_swap, down_all.at[z, y, :, col_span(1 - c)])
    down.start()
    tour.inner(step, 6, 20)
    out_gather.relay_two()
    down.relay()
    tour.inner(step, 20, tour.count)
    for s in (0, 1):
        fits = in_second(tour.half(s), ends)
        for g in heads:
            cols = head_cols(g)
            tops[s, :, cols] = jnp.where(fits, tops[s, :, cols], NEVER)
            sums[s, :, cols] = jnp.where(fits, sums[s, :, cols], 0.0)
            mixed[s, :, cols] = jnp.where(fits, mixed[s, :, cols], 0.0)
    tour.edges(step)
    gate.relay_two()
    up.relay_two()
    down.turn()
    for s in (0, 1):
        tokens = slice(s * HALF, (s + 1) * HALF)
        log_out[s] = tops[s] + jnp.log(sums[s])
        mixed_out[s] = mixed[s, HD:, :] / sums[s]
        for g in range(0, GROUP, 2):
            two = jnp.concatenate(
                [mixed_out[s, :, head_cols(g)], mixed_out[s, :, head_cols(g + 1)]], axis=0
            )
            attended[tokens, g * HD : (g + 2) * HD] = two.T.astype(BF)

    out_gather.finish()
    keep("out", out_all, out_out)
    out_low = out_all[...].reshape(GROUP * HD, D)
    fold_numbers = []
    for k, o in enumerate(FOLD_ORDER):
        rows = row_span(lax.rem(x + o, 4))
        part[rows, :] = jnp.dot(
            attended[rows, :], out_low, preferred_element_type=F32
        ).astype(BF)
        fold_numbers.append(
            wires.send(part.at[rows, col_span(1 - c)], folded.at[k], device(z, y, x, 1 - c))
        )
    moves = fold_moves(wires, fold_numbers, part, folded, leaving, arriving, here, total)
    fold_finish(wires, moves, arriving, total)
    middle = total[...] + inputs[...].astype(F32)
    middle_out[...] = middle
    square = both_cores(
        wires, mine_row, their_row, jnp.sum(middle * middle, axis=1, keepdims=True), here
    )
    scale = lax.rsqrt(square / D + NORM_EPS)
    scale_two[...] = jnp.broadcast_to(scale, scale_two.shape)
    own[...] = (
        middle_out[...] * scale * gains_all[1:2, col_span(c)]
    ).astype(BF)
    keep("own", own, out.at[row_span(x), col_span(c)])
    sends = gather_sends(wires, own, out, here)
    down.relay_two()
    gather_relay(wires, sends, out, here)
    gate.finish()
    up.finish()
    down.finish()
    for name in ("normed", "qkv_out", "cotangent", "keys", "out", "own"):
        kept[name].wait()

    @pl.when(jnp.logical_not(holds))
    def _():
        stage_copy.wait_send()

    post.close()
    wires.close()


def call_forward(ends, cosine, sine, block_input, out_grad, gain_rows, qkv_in, gate_in, up_in, down_in, out_in):
    vm = pl.BlockSpec(memory_space=pltpu.VMEM)
    hbm = pl.BlockSpec(memory_space=ANY)
    cols = GROUP * HALF
    qkv_cols = qkv_in.shape[2]
    share = (ROWS, WIDTH)
    whole = (2, 4, 4, 2, PIECE)
    outs = [
        (share, BF, vm),
        ((ROWS, 128), F32, vm),
        ((LINE, D), BF, hbm),
        (whole + (qkv_cols,), BF, hbm),
        ((2, 2 * HD, cols), BF, vm),
        ((2, HD, cols), F32, vm),
        ((2, 1, cols), F32, vm),
        ((LINE, GROUP * HD), BF, vm),
        ((2, 4, 4, HALF, 2 * HD), BF, hbm),
        (share, BF, hbm),
        ((LINE, D), BF, hbm),
        ((4, 2, PIECE, D), BF, hbm),
        (whole + (HIDDEN,), BF, hbm),
        (whole + (HIDDEN,), BF, hbm),
        ((4, 4, 2 * PIECE, D), BF, hbm),
        (share, F32, vm),
        ((ROWS, 128), F32, vm),
        ((LINE, D), BF, hbm),
    ]
    return pl.pallas_call(
        forward_kernel,
        out_shape=tuple(jax.ShapeDtypeStruct(shape, kind) for shape, kind, _ in outs),
        in_specs=[pl.BlockSpec(memory_space=pltpu.SMEM), vm, vm] + [hbm] * 8,
        out_specs=tuple(spec for _, _, spec in outs),
        scratch_shapes=[
            pltpu.VMEM((LINE, D), BF),
            pltpu.VMEM((8, D), F32),
            pltpu.VMEM(whole + (qkv_cols,), BF),
            pltpu.VMEM((LINE, D), BF),
            pltpu.VMEM((qkv_cols, LINE), F32),
            pltpu.VMEM((2, HALF, 2 * HD), BF),
            pltpu.VMEM((2, 4, 4, HALF, 2 * HD), BF),
            pltpu.VMEM((2, 1, cols), F32),
            pltpu.VMEM((2, 1, cols), F32),
            pltpu.VMEM((2, 2 * HD, cols), F32),
            pltpu.VMEM((2, PIECE, D), BF),
            pltpu.VMEM((4, 2, PIECE, D), BF),
            pltpu.VMEM((LINE, D), BF),
        ]
        + fold_scratch()
        + [
            pltpu.VMEM((ROWS, 128), F32),
            pltpu.VMEM((ROWS, 128), F32),
            pltpu.VMEM((ROWS, WIDTH), BF),
        ]
        + wire_scratch(128)
        + wire_scratch(2)
        + wire_scratch(4)
        + wire_scratch(4)
        + [pltpu.SemaphoreType.DMA((13,))],
        compiler_params=comm_params(1),
        name="forward",
    )(ends, cosine, sine, block_input, out_grad, gain_rows, qkv_in, gate_in, up_in, down_in, out_in)


def attention_back_kernel(
    ends, queries, grads, query_rows, grad_rows, logs, delta, keys, output_part, middle,
    grad_gate, grad_out, down_fin, up_fin,
    query_back, key_back, output, gate_out, up_out, down_out, out_out,
    terms, sums, rounded, folded, leaving, arriving, total, *rest,
):
    buffers, key_buffers, out_buffers = rest[:6], rest[6:9], rest[9:12]
    send_sem, recv_sem, out_send, out_recv, local_sem = rest[12:]
    key_rec, key_sums, key_rec_two = key_buffers
    fin = buffers[5]
    z, y, xl, xh, c = place()
    x = xh * 2 + xl
    here = (z, y, x, c)
    mine = xl * 2 + c
    quad = quad_of(xl, xh, x, c)
    greet(plane_targets(z, y, x, c) + line_targets(z, y, x, c) + [device(z, y, *quad[2])])
    wires = Wires(send_sem, recv_sem)
    gate = PlaneSum(wires, grad_gate, buffers, here, local_sem, 0)
    out_sum = OutSum(
        wires, grad_out, out_buffers, out_out, here, mine, quad, (out_send, out_recv), local_sem, 6
    )
    numbers = fold_sends(wires, output_part, folded, here)
    gate.start()
    out_sum.start()
    up_swaps = [
        wires.send(up_fin.at[b, lax.rem(a, 2)], up_out.at[mine], device(z, y, a, b))
        for a, b in quad
    ]
    down_swap = wires.send(
        down_fin.at[:, :, col_span(1 - c)], down_out.at[c], device(z, y, x, 1 - c)
    )
    kept = [
        pltpu.make_async_copy(up_fin.at[c, xl], up_out.at[mine], local_sem.at[7]),
        pltpu.make_async_copy(down_fin.at[:, :, col_span(c)], down_out.at[c], local_sem.at[8]),
    ]
    for copy in kept:
        copy.start()

    tour = Tour(z * 4 + y)
    terms[...] = jnp.zeros(terms.shape, F32)
    sums[...] = jnp.zeros(sums.shape, F32)
    heads = range(GROUP)

    def step(s, at, masked):
        slot = key_at(at)
        pairs = keys[slot]
        columns = [queries[s, :, head_cols(g)] for g in heads]
        grad_columns = [grads[s, :, head_cols(g)] for g in heads]
        log_rows = [logs[s, :, head_cols(g)] for g in heads]
        deltas = [delta[s, :, head_cols(g)] for g in heads]
        rows = [query_rows[s, g] for g in heads]
        outer = [grad_rows[s, g] for g in heads]
        if not masked:
            fits = in_second(tour.half(s), ends)
            log_rows = [jnp.where(fits, value, -NEVER) for value in log_rows]
        scores = [jnp.dot(pairs, value, preferred_element_type=F32) for value in columns]
        prob_grads = [jnp.dot(pairs, value, preferred_element_type=F32) for value in grad_columns]
        probs = [jnp.exp(scores[g] - log_rows[g]) for g in heads]
        if masked:
            allowed = allowed_pairs(at, tour.half(s), ends)
            probs = [jnp.where(allowed, value, 0.0) for value in probs]
        score_grads = [(probs[g] * (prob_grads[g] - deltas[g])).astype(BF) for g in heads]
        probs_low = [value.astype(BF) for value in probs]
        back = [
            lax.dot_general(
                pairs, value, (((0,), (0,)), ((), ())), preferred_element_type=F32
            )
            for value in score_grads
        ]
        added = [
            jnp.dot(score_grads[g], rows[g], preferred_element_type=F32)
            + jnp.dot(probs_low[g], outer[g], preferred_element_type=F32)
            for g in heads
        ]
        terms[slot] += (added[0] + added[1]) + (added[2] + added[3])
        for g in heads:
            sums[s, :, head_cols(g)] += back[g]

    tour.inner(step, 0, 8)
    gate.relay()
    moves = fold_moves(wires, numbers, output_part, folded, leaving, arriving, here, total)
    out_sum.middle()
    tour.inner(step, 8, 20)
    fold_finish(wires, moves, arriving, total)
    output[...] = (middle[...] + total[...]).astype(BF)
    out_sum.deal()
    gate.middle()
    tour.inner(step, 20, tour.count)
    tour.edges(step)

    for s in (0, 1):
        for i in range(4):
            rounded[s, i] = terms[s, i].astype(BF)
    first = [[], []]
    for k, by in enumerate(OFFSETS):
        first[0].append(
            wires.send(
                rounded.at[0, :, lax.rem(y + by, 4)], key_rec.at[0, k], second_device(here, 0, by)
            )
        )
        first[1].append(
            wires.send(
                rounded.at[1, lax.rem(z + by, 4)], key_rec.at[1, k], second_device(here, 1, by)
            )
        )
    for s in (0, 1):
        query_back[s] = sums[s, :HD, :] * HD ** (-0.5)
    gate.finish()
    swaps = [
        wires.send(fin.at[b, lax.rem(a, 2)], gate_out.at[mine], device(z, y, a, b))
        for a, b in quad
    ]
    kept.append(pltpu.make_async_copy(fin.at[c, xl], gate_out.at[mine], local_sem.at[9]))
    kept[-1].start()
    second = [[], []]
    for s in (0, 1):
        for k in range(3):
            wires.landed(first[s][k], key_rec.at[s, k])
        for i in range(4):
            value = terms[0, i, y] if s == 0 else terms[1, z, i]
            for k in range(3):
                value = value + key_rec[s, k, i].astype(F32)
            key_sums[s, i] = value.astype(BF)
        for k, by in enumerate(OFFSETS):
            second[s].append(
                wires.send(
                    key_sums.at[s, first_at(here, s, by)],
                    key_rec_two.at[s, k],
                    first_device(here, s, by),
                )
            )
    out_sum.finish()
    for s in (0, 1):
        value = key_sums[s, first_at(here, s)].astype(F32)
        for k in range(3):
            wires.landed(second[s][k], key_rec_two.at[s, k])
            value = value + key_rec_two[s, k].astype(F32)
        key_back[s] = value
    for at, (a, b) in zip(up_swaps, quad):
        wires.landed(at, up_out.at[lax.rem(a, 2) * 2 + b])
    wires.landed(down_swap, down_out.at[1 - c])
    for at, (a, b) in zip(swaps, quad):
        wires.landed(at, gate_out.at[lax.rem(a, 2) * 2 + b])
    for copy in kept:
        copy.wait()
    wires.close()


def call_attention_back(
    ends, queries, grads, query_rows, grad_rows, logs, delta, keys, output_part, middle,
    grad_gate, grad_out, down_fin, up_fin,
):
    vm = pl.BlockSpec(memory_space=pltpu.VMEM)
    hbm = pl.BlockSpec(memory_space=ANY)
    cols = GROUP * HALF
    return pl.pallas_call(
        attention_back_kernel,
        out_shape=(
            jax.ShapeDtypeStruct((2, HD, cols), F32),
            jax.ShapeDtypeStruct((2, HALF, 2 * HD), F32),
            jax.ShapeDtypeStruct((ROWS, WIDTH), BF),
            jax.ShapeDtypeStruct((4, PIECE, HIDDEN), BF),
            jax.ShapeDtypeStruct((4, PIECE, HIDDEN), BF),
            jax.ShapeDtypeStruct((2, 2, PIECE, WIDTH), BF),
            jax.ShapeDtypeStruct((PIECE, WIDTH), BF),
        ),
        in_specs=[pl.BlockSpec(memory_space=pltpu.SMEM)] + [vm] * 9 + [hbm] * 4,
        out_specs=(vm, vm, vm, hbm, hbm, hbm, hbm),
        scratch_shapes=[
            pltpu.VMEM((2, 4, 4, HALF, 2 * HD), F32),
            pltpu.VMEM((2, 2 * HD, cols), F32),
            pltpu.VMEM((2, 4, 4, HALF, 2 * HD), BF),
        ]
        + fold_scratch()
        + sum_buffers((2, PIECE, HIDDEN), BF)
        + [
            pltpu.VMEM((2, 3, 4, HALF, 2 * HD), BF),
            pltpu.VMEM((2, 4, HALF, 2 * HD), BF),
            pltpu.VMEM((2, 3, HALF, 2 * HD), BF),
            pltpu.VMEM((3, 2, PIECE, D), BF),
            pltpu.VMEM((2, PIECE, D), BF),
            pltpu.VMEM((3, 2, PIECE, D), BF),
        ]
        + wire_scratch(56)
        + wire_scratch(6)
        + [pltpu.SemaphoreType.DMA((10,))],
        compiler_params=comm_params(6),
        name="attention_back",
    )(
        ends, queries, grads, query_rows, grad_rows, logs, delta, keys, output_part, middle,
        grad_gate, grad_out, down_fin, up_fin,
    )


def rope_tables(position, head_size):
    half_size = head_size // 2
    column = jnp.arange(half_size, dtype=jnp.float32)
    inverse = jnp.exp(-(2.0 * column / head_size) * math.log(ROPE_THETA))
    wavelength = 2.0 * math.pi / inverse
    smooth = (OLD_CONTEXT / wavelength - LOW_FREQ) / (HIGH_FREQ - LOW_FREQ)
    blended = (1.0 - smooth) * inverse / ROPE_FACTOR + smooth * inverse
    inverse = jnp.where(
        wavelength < OLD_CONTEXT / HIGH_FREQ,
        inverse,
        jnp.where(wavelength > OLD_CONTEXT / LOW_FREQ, inverse / ROPE_FACTOR, blended),
    )
    angles = position.astype(jnp.float32)[:, None] * inverse[None, :]
    return (jnp.cos(angles), jnp.sin(angles))


def rotate(values, cosine, sine):
    half_size = values.shape[-1] // 2
    table_shape = (cosine.shape[0],) + (1,) * (values.ndim - 2) + (half_size,)
    cos_part = cosine.reshape(table_shape)
    sin_part = sine.reshape(table_shape)
    first_half = values[..., :half_size]
    second_half = values[..., half_size:]
    return jnp.concatenate(
        [
            first_half * cos_part - second_half * sin_part,
            second_half * cos_part + first_half * sin_part,
        ],
        axis=-1,
    )


def times(left, right, kind):
    return jnp.dot(left, right, preferred_element_type=F32).astype(kind)


def times_transpose(left, right, kind):
    return lax.dot_general(
        left, right, (((1,), (1,)), ((), ())), preferred_element_type=F32
    ).astype(kind)


def outer_rows(left, right, kind):
    return lax.dot_general(
        left, right, (((0,), (0,)), ((), ())), preferred_element_type=F32
    ).astype(kind)


def as_columns(rows):
    return rows.reshape(2, HALF, GROUP, HD).transpose(0, 3, 2, 1).reshape(2, HD, GROUP * HALF)


def as_heads(rows):
    return rows.reshape(2, HALF, GROUP, HD).transpose(0, 2, 1, 3)


def from_columns(columns):
    return columns.reshape(2, HD, GROUP, HALF).transpose(0, 3, 2, 1).reshape(LINE, GROUP * HD)


def adam(weight, moment, second, gradient, rate, decay):
    moment_next = BETA_ONE * moment + (1.0 - BETA_ONE) * gradient
    second_next = BETA_TWO * second + (1.0 - BETA_TWO) * gradient * gradient
    unbiased = moment_next / (1.0 - BETA_ONE**ADAM_STEP)
    divisor = jnp.sqrt(second_next / (1.0 - BETA_TWO**ADAM_STEP)) + ADAM_EPS
    return (weight - rate * (unbiased / divisor + decay * weight), moment_next, second_next)


def shards(
    block_input,
    out_grad,
    qkv_weight,
    qkv_moment,
    qkv_second,
    gate_up_weight,
    gate_up_moment,
    gate_up_second,
    out_weight,
    out_moment,
    out_second,
    down_weight,
    down_moment,
    down_second,
    norm_gains,
    gains_moment,
    gains_second,
    doc_lengths,
):
    z, y, xl, xh, c = place()
    x = xh * 2 + xl
    spot = z * 4 + y

    ends = jnp.cumsum(doc_lengths)
    local = jnp.arange(LINE, dtype=jnp.int32)
    half = jnp.where(local < HALF, 2 * spot, HALVES - 1 - 2 * spot)
    places = half * HALF + lax.rem(local, HALF)
    passed = (places[:, None] >= ends[None, :]).astype(jnp.int32)
    position = places - jnp.sum(passed * doc_lengths[None, :], axis=1)
    cosine, sine = rope_tables(position, HD)

    def dealt(half_weight):
        return (
            half_weight.astype(BF)
            .reshape(PIECE, 16, 4, HD)
            .transpose(2, 0, 1, 3)
            .reshape(4, PIECE, HIDDEN)
        )

    (
        inputs,
        scale_one,
        normed,
        qkv_whole,
        query_columns,
        mixed,
        logs,
        attended,
        keys,
        cotangent,
        cotangent_all,
        out_whole,
        gate_whole,
        up_whole,
        down_whole,
        middle,
        scale_two,
        normed_two,
    ) = call_forward(
        ends,
        cosine.T,
        sine.T,
        block_input,
        out_grad,
        jnp.concatenate([norm_gains, jnp.zeros((6, WIDTH), F32)], axis=0),
        qkv_weight.astype(BF).transpose(1, 0, 2),
        dealt(gate_up_weight[:, 0]),
        dealt(gate_up_weight[:, 1]),
        down_weight.astype(BF).reshape(2, ROWS // 2, WIDTH),
        out_weight.astype(BF),
    )
    qkv_low = qkv_whole.reshape(D, (GROUP + 2) * HD)
    gate_low = gate_whole.reshape(D, HIDDEN)
    up_low = up_whole.reshape(D, HIDDEN)
    down_low = down_whole.reshape(HIDDEN, D)
    out_low = out_whole.reshape(GROUP * HD, D)

    gate_part = times(normed_two, gate_low, F32)
    up_part = times(normed_two, up_low, F32)
    sigmoid_gate = jax.nn.sigmoid(gate_part)
    hidden = (gate_part * sigmoid_gate * up_part).astype(BF)
    hidden_grad = times_transpose(cotangent_all, down_low, F32)
    gate_back = hidden_grad * up_part * sigmoid_gate * (1.0 + gate_part * (1.0 - sigmoid_gate))
    up_back = hidden_grad * gate_part * sigmoid_gate
    gate_back, up_back = gate_back.astype(BF), up_back.astype(BF)
    grad_down = outer_rows(hidden, cotangent_all, BF)
    grad_up = outer_rows(normed_two, up_back, BF)
    half_shape = gate_whole.shape
    middle_grad, gain_two, middle_low, down_fin, up_fin = call_back(
        (
            times_transpose(gate_back, gate_low, F32) + times_transpose(up_back, up_low, F32)
        ).astype(BF),
        middle,
        scale_two,
        norm_gains,
        cotangent,
        grad_down.reshape(down_whole.shape),
        grad_up.reshape(half_shape),
    )
    output_part = times(hidden, down_low, BF)
    grad_gate = outer_rows(normed_two, gate_back, BF)

    grad_out = outer_rows(attended, middle_low, BF)
    attended_grad = times_transpose(middle_low, out_low, BF)
    delta = jnp.sum(
        (attended_grad.astype(F32) * from_columns(mixed)).reshape(LINE, GROUP, HD), axis=-1
    )
    delta = delta.reshape(2, HALF, GROUP).transpose(0, 2, 1).reshape(2, 1, GROUP * HALF)
    blank = jnp.zeros((2, HD, GROUP * HALF), BF)
    empty = jnp.zeros((2, GROUP, HALF, HD), BF)
    query_back, key_grads, output, gate_sum, up_sum, down_sum, out_sum = call_attention_back(
        ends,
        query_columns,
        jnp.concatenate([blank, as_columns(attended_grad)], axis=1),
        query_columns.reshape(2, 2 * HD, GROUP, HALF).transpose(0, 2, 3, 1),
        jnp.concatenate([empty, as_heads(attended_grad)], axis=-1),
        logs,
        delta,
        keys,
        output_part,
        middle,
        grad_gate.reshape(half_shape),
        grad_out.reshape(out_whole.shape),
        down_fin,
        up_fin,
    )
    key_grads = key_grads.reshape(LINE, 2 * HD)
    turned_back = jnp.concatenate([from_columns(query_back), key_grads[:, :HD]], axis=1)
    turned_back = rotate(turned_back.reshape(LINE, GROUP + 1, HD), cosine, -sine)
    projected_back = jnp.concatenate(
        [turned_back.reshape(LINE, (GROUP + 1) * HD), key_grads[:, HD:]], axis=1
    ).astype(BF)
    grad_qkv = outer_rows(normed, projected_back, BF)
    square = sum(
        jnp.sum(jnp.square(member.astype(F32))) for member in (gate_sum, up_sum, out_sum, down_sum)
    )
    input_grad, output, qkv_sum, totals = call_last(
        times_transpose(projected_back, qkv_low, BF),
        inputs,
        scale_one,
        norm_gains,
        middle_grad,
        gain_two,
        jnp.broadcast_to(square, (8, 128)),
        output,
        grad_qkv.reshape(qkv_whole.shape),
    )
    gate_both = jnp.stack([gate_sum, up_sum], axis=2).reshape(4, PIECE, 2, 16, HD)
    shares = (
        qkv_sum.transpose(1, 0, 2).astype(F32),
        gate_both.transpose(1, 2, 3, 0, 4).reshape(gate_up_weight.shape).astype(F32),
        out_sum.astype(F32),
        down_sum.reshape(down_weight.shape).astype(F32),
    )
    gains_grad = totals[:16].reshape(2, WIDTH)
    grad_norm = jnp.sqrt(totals[16, 0])
    factor = CLIP_NORM / jnp.maximum(grad_norm, CLIP_NORM)
    weights = (qkv_weight, gate_up_weight, out_weight, down_weight)
    moments = (qkv_moment, gate_up_moment, out_moment, down_moment)
    seconds = (qkv_second, gate_up_second, out_second, down_second)
    out_rate = OUTPUT_RATE * (TOKENS / (HQ * HD)) ** 0.5
    down_rate = DOWN_RATE * FF ** (-0.5)
    rates = (MATRIX_RATE, MATRIX_RATE, out_rate, down_rate)
    results = []
    for weight, moment, second, gradient, rate in zip(weights, moments, seconds, shares, rates):
        results.extend(adam(weight, moment, second, gradient * factor, rate, WEIGHT_DECAY))
    gains_new = adam(norm_gains, gains_moment, gains_second, gains_grad * factor, GAIN_RATE, 0.0)
    return (output, input_grad, grad_norm, *results, *gains_new)


def solution(mesh):
    placed = (
        P(("seq", "wide"), "narrow"),
        P(("seq", "wide"), "narrow"),
        P(("narrow", "seq"), "wide", None),
        P(("narrow", "seq"), "wide", None),
        P(("narrow", "seq"), "wide", None),
        P(("narrow", "seq"), None, "wide"),
        P(("narrow", "seq"), None, "wide"),
        P(("narrow", "seq"), None, "wide"),
        P(("wide", "seq"), "narrow"),
        P(("wide", "seq"), "narrow"),
        P(("wide", "seq"), "narrow"),
        P(("wide", "seq"), "narrow"),
        P(("wide", "seq"), "narrow"),
        P(("wide", "seq"), "narrow"),
        P(None, "narrow"),
        P(None, "narrow"),
        P(None, "narrow"),
        P(),
    )
    return jax.shard_map(
        shards,
        mesh=mesh,
        in_specs=placed,
        out_specs=(
            P(("seq", "wide"), "narrow"),
            P(("seq", "wide"), "narrow"),
            P(),
            P(("narrow", "seq"), "wide", None),
            P(("narrow", "seq"), "wide", None),
            P(("narrow", "seq"), "wide", None),
            P(("narrow", "seq"), None, "wide"),
            P(("narrow", "seq"), None, "wide"),
            P(("narrow", "seq"), None, "wide"),
            P(("wide", "seq"), "narrow"),
            P(("wide", "seq"), "narrow"),
            P(("wide", "seq"), "narrow"),
            P(("wide", "seq"), "narrow"),
            P(("wide", "seq"), "narrow"),
            P(("wide", "seq"), "narrow"),
            P(None, "narrow"),
            P(None, "narrow"),
            P(None, "narrow"),
        ),
        check_vma=False,
    )
```

time: 520 us -> 425 us (0.82)
  Pallas kernels: 404 us -> 318 us
    pallas_call x4 -> x1, Pallas kernels: 224 us -> 142 us  [call_forward(): pl.pallas_call(forward_kernel, out_shape=tuple((jax.ShapeDtypeStruct(shap...]
    pallas_call x1, Pallas kernels: 98.2 us -> 74.9 us  [call_attention_back(): pl.pallas_call(attention_back_kernel, out_shape=(jax.ShapeDtypeStruct((2,...]
    pallas_call x1, Pallas kernels: 33.8 us -> 44.9 us  [call_last(): pl.pallas_call(last_kernel, out_shape=(jax.ShapeDtypeStruct((ROWS, WIDTH)...]
    pallas_call x1, Pallas kernels: 48.2 us -> 55.3 us  [call_back(): pl.pallas_call(back_kernel, out_shape=(jax.ShapeDtypeStruct((ROWS, WIDTH)...]
    dot_general x4 -> x3, matrix products: 16.3 us -> 14.1 us  [times(): return jnp.dot(left, right, preferred_element_type=F32).astype(kind)]
    dot_general x4 -> x5, matrix products: 15.9 us -> 17.3 us  [outer_rows(): lax.dot_general(left, right, (((0,), (0,)), ((), ())), preferred_element_...]
    dot_general x4 -> x5, matrix products: 13.8 us -> 13.9 us  [times_transpose(): lax.dot_general(left, right, (((1,), (1,)), ((), ())), preferred_element_...]
where the time goes in v3:
time: 425 us; the launch traced here: 417 us
  Pallas kernels  318 us (75%)
  matrix products  45.2 us (11%)
  local copies, waits for them, and re-layouts  28.9 us (7%)
  other arithmetic  18.7 us (4%)
  between operations  6.21 us (1%)
    pallas_call x1, Pallas kernels, call_forward(): pl.pallas_call(forward_kernel, out_shape=tuple((jax.ShapeDtypeStruct(shap...  142 us
    pallas_call x1, Pallas kernels, call_attention_back(): pl.pallas_call(attention_back_kernel, out_shape=(jax.ShapeDtypeStruct((2,...  74.9 us
    pallas_call x1, Pallas kernels, call_back(): pl.pallas_call(back_kernel, out_shape=(jax.ShapeDtypeStruct((ROWS, WIDTH)...  55.3 us
    pallas_call x1, Pallas kernels, call_last(): pl.pallas_call(last_kernel, out_shape=(jax.ShapeDtypeStruct((ROWS, WIDTH)...  44.9 us
    dot_general x5, matrix products, outer_rows(): lax.dot_general(left, right, (((0,), (0,)), ((), ())), preferred_element_...  17.3 us
    dot_general x3, matrix products, times(): return jnp.dot(left, right, preferred_element_type=F32).astype(kind)  14.1 us
    dot_general x5, matrix products, times_transpose(): lax.dot_general(left, right, (((1,), (1,)), ((), ())), preferred_element_...  13.9 us
    sub x5, other arithmetic, adam(): weight - rate * (unbiased / divisor + decay * weight)  10.2 us

profile of v3, /device:TPU:1, one launch (start us, length us, event | category | flops | bytes accessed | tf_op | source)
XLA Modules:
  0.0 416.6 jit_solution(6200347469767560019)
XLA Ops:
  0.7 0.8 reduce-window.8
  1.5 0.7 select_reduce_fusion
  2.3 1.0 multiply_sine_fusion.1
  3.3 1.3 concatenate.21.gain_rows
  4.6 1.6 copy.102
  6.2 1.7 convert.16
  7.8 2.2 slice_reduce_fusion
  10.0 0.5 convert_element_type.93
  10.6 1.1 reshape.252.gate_in
  11.7 0.5 convert_element_type.94
  12.3 1.1 reshape.253.up_in
  13.4 0.7 convert_element_type.95
  14.1 0.6 convert_element_type.96.out_in
  14.7 142.5 %forward.1 = (bf16[128,1024]{1,0:T(8,128)(2,1)}, f32[128,128]{1,0:T(8,128)}, bf16[512,2048]{1,0:T(8,128)(2,1)}, bf16[2,4,4,2,32,384]{5,4,3,2,1,0:T(8,128)(2,1)},...) custom-call(s32[4]{0:T(128)} %bitcast.116, ...), custom_call_target="tpu_custom_call" | custom-call | tf_op jit(solution)/shard_map/forward/pallas_call | solution.py:1271
  157.2 1.4 reshape.264
  158.7 0.4 copy.74
  159.1 4.7 %fusion.24 = f32[512,1024]{1,0:T(8,128)S(1)} fusion(bf16[512,2048]{1,0:T(8,128)(2,1)S(1)} %copy-done.30, bf16[2048,1024]{1,0:T(8,128)(2,1)} %bitcast.123), kind=kOutput, calls=%fused_computation.74 | convolution fusion | flops 2147483648 | bytes 8388608 | tf_op jit(solution)/shard_map/dot_general | solution.py:1534
  163.8 2.4 fusion.23
  166.2 3.2 multiply_convert_fusion
  169.4 2.4 fusion.25
  171.8 4.1 add_convert_fusion.part
  176.0 4.4 %convolution_convert_fusion.2 = bf16[1024,2048]{1,0:T(8,128)(2,1)} fusion(bf16[512,1024]{1,0:T(8,128)(2,1)S(1)} %get-tuple-element.157, bf16[512,2048]{1,0:T(8,128)(2,1)S(1)} %copy-done.31), kind=kOutput, calls=%fused_computation.3 | convolution fusion | flops 2149580800 | bytes 7340032 | tf_op jit(solution)/shard_map/dot_general | solution.py:1544
  180.4 4.4 %convolution_convert_fusion.1 = bf16[2048,1024]{1,0:T(8,128)(2,1)} fusion(bf16[512,2048]{1,0:T(8,128)(2,1)S(1)} %copy-done.30, bf16[512,1024]{1,0:T(8,128)(2,1)S(1)} %get-tuple-element.159), kind=kOutput, calls=%fused_computation.2 | convolution fusion | flops 2149580800 | bytes 7340032 | tf_op jit(solution)/shard_map/dot_general | solution.py:1544
  184.8 55.3 %line_back.1 = (f32[128,1024]{1,0:T(8,128)}, f32[8,1024]{1,0:T(8,128)}, bf16[512,2048]{1,0:T(8,128)(2,1)}, bf16[2,32,2048]{2,1,0:T(8,128)(2,1)}, bf16[2,2,32,1024]{3,2,1,0:T(8,128)(2,1)}) custom-call(bf16[512,2048]{1,0:T(8,128)(2,1)} %add_convert_fusion.part, f32[128,1024]{1,0:T(8,128)} %get-tuple-element.58.middle, f32[128,128]{1,0:T(8,128)} %get-tuple-element.59.scale, ...), custom_call_target="tpu_custom_call" | custom-call | tf_op jit(solution)/shard_map/line_back/pallas_call | solution.py:741
  240.1 2.4 bitcast_reduce_fusion
  242.5 0.2 copy.71
  242.9 0.8 concatenate.22.grads
  243.8 1.0 copy.72
  244.8 0.3 copy.73
  245.1 1.0 concatenate.23.grad_rows
  246.1 0.6 reshape.268.delta
  246.7 6.3 %convolution_convert_fusion.3.output_part = bf16[512,2048]{1,0:T(8,128)(2,1)} fusion(bf16[512,1024]{1,0:T(8,128)(2,1)} %copy-done.35, bf16[1024,2048]{1,0:T(8,128)(2,1)} %bitcast.119), kind=kOutput, calls=%fused_computation.4 | convolution fusion | flops 2148532224 | bytes 7340032 | tf_op jit(solution)/shard_map/dot_general | solution.py:1534
  253.0 4.3 %convolution_convert_fusion = bf16[2048,1024]{1,0:T(8,128)(2,1)} fusion(bf16[512,2048]{1,0:T(8,128)(2,1)S(1)} %copy-done.30, bf16[512,1024]{1,0:T(8,128)(2,1)S(1)} %copy-done.34), kind=kOutput, calls=%fused_computation.1 | convolution fusion | flops 2149580800 | bytes 7340032 | tf_op jit(solution)/shard_map/dot_general | solution.py:1544
  257.3 1.7 convolution_convert_fusion.6
  259.0 74.9 %attention_back.1 = (f32[2,64,1024]{2,1,0:T(8,128)}, f32[2,256,128]{2,1,0:T(8,128)}, bf16[128,1024]{1,0:T(8,128)(2,1)}, bf16[4,32,1024]{2,1,0:T(8,128)(2,1)}, bf...) custom-call(s32[4]{0:T(128)} %bitcast.117, ...), custom_call_target="tpu_custom_call" | custom-call | tf_op jit(solution)/shard_map/attention_back/pallas_call | solution.py:1462
  333.9 1.0 slice.40
  335.1 1.1 copy.86
  336.1 1.3 reshape.271
  337.4 0.4 copy.75
  337.9 0.3 multiply_cosine_fusion
  338.4 0.8 copy-done.4
  339.3 2.6 convolution_convert_fusion.4.part
  341.9 0.8 multiply_reduce_fusion
  344.0 0.6 fusion.8
  345.3 0.7 fusion.1
  346.6 0.6 broadcast_in_dim.12.squares
  347.2 2.4 convolution_convert_fusion.5
  349.7 44.9 %line_last.1 = (f32[128,1024]{1,0:T(8,128)}, bf16[128,1024]{1,0:T(8,128)(2,1)}, bf16[4,32,384]{2,1,0:T(8,128)(2,1)}, f32[24,128]{1,0:T(8,128)}) custom-call(bf16[512,2048]{1,0:T(8,128)(2,1)} %convolution_convert_fusion.4.part, bf16[128,1024]{1,0:T(8,128)(2,1)} %get-tuple-element.72.inputs, f32[128,128]{1,0:T(8,128)} %get-tuple-element.73.scale, ...), custom_call_target="tpu_custom_call" | custom-call | tf_op jit(solution)/shard_map/line_last/pallas_call | solution.py:867
  394.6 1.2 slice.33
  396.6 1.1 multiply_subtract_fusion.2
  397.6 0.8 copy.83
  398.4 0.8 copy.84
  399.2 0.8 copy.85
  400.0 0.3 stack.10
  400.4 0.3 stack.9
  400.7 0.2 multiply_bitcast_fusion
  401.0 1.4 copy.82
  402.3 1.8 mul.406
  404.2 6.3 %multiply_subtract_fusion = (f32[32,2,4096]{2,1,0:T(2,128)}, f32[32,2,4096]{2,1,0:T(2,128)}, f32[32,2,4096]{2,1,0:T(2,128)}) fusion(f32[32,2,4096]{2,1,0:T(2,128)} %param.23, f32[32,2,4096]{2,1,0:T(2,128)S(1)} %mul.406, f32[32,2,4096]{2,1,0:T(2,128)} %param.24, f32[32,2,4096]{2,1,0:T(2,128)} %param.25), kind=kLoop, calls=%fused_computation.16 | loop fusion | flops 3932160 | bytes 7340032 | tf_op jit(solution)/shard_map/sub | solution.py:1566
  410.5 0.8 multiply_subtract_fusion.3
  411.4 1.4 multiply_subtract_fusion.1
  412.9 0.6 multiply_subtract_fusion.4
  413.5 0.7 copy.105
  414.3 0.8 copy.106
  (87 shorter events, 1.0 us)
Async XLA Ops:
  1.5 9.1 %copy-start.25 = (s32[4,1]{0,1:T(1,128)}, s32[4,1]{0,1:T(1,128)S(1)}, u32[]{:S(2)}) copy-start(s32[4,1]{0,1:T(1,128)S(1)} %reduce-window.8) | copy-start | bytes 52
  10.5 2.8 copy-start
  10.6 3.5 copy-start.12
  157.2 1.9 copy-start.30
  159.1 4.7 %copy-start.26 = (bf16[4,4,64,2048]{3,2,1,0:T(8,128)(2,1)S(1)}, bf16[4,4,64,2048]{3,2,1,0:T(8,128)(2,1)}, u32[]{:S(2)}) copy-start(bf16[4,4,64,2048]{3,2,1,0:T(8,128)(2,1)} %get-tuple-element.54) | copy-start | bytes 12582916
  159.1 4.7 %copy-start.31 = (bf16[512,2048]{1,0:T(8,128)(2,1)S(1)}, bf16[512,2048]{1,0:T(8,128)(2,1)}, u32[]{:S(2)}) copy-start(bf16[512,2048]{1,0:T(8,128)(2,1)} %get-tuple-element.53) | copy-start | bytes 6291460
  163.8 2.4 copy-start.27
  166.2 3.2 copy-start.28
  169.4 2.4 copy-start.33
  169.4 6.5 %copy-start.35 = (bf16[512,1024]{1,0:T(8,128)(2,1)}, bf16[512,1024]{1,0:T(8,128)(2,1)S(1)}, u32[]{:S(2)}) copy-start(bf16[512,1024]{1,0:T(8,128)(2,1)S(1)} %get-tuple-element.157) | copy-start | bytes 3145732
  184.7 55.3 %copy-start.32 = (bf16[4,2,32,2048]{3,2,1,0:T(8,128)(2,1)S(1)}, bf16[4,2,32,2048]{3,2,1,0:T(8,128)(2,1)}, u32[]{:S(2)}) copy-start(bf16[4,2,32,2048]{3,2,1,0:T(8,128)(2,1)} %get-tuple-element.62) | copy-start | bytes 3145732
  242.5 1.3 copy-start.2
  246.7 6.3 %copy-start.34 = (bf16[512,1024]{1,0:T(8,128)(2,1)S(1)}, bf16[512,1024]{1,0:T(8,128)(2,1)}, u32[]{:S(2)}) copy-start(bf16[512,1024]{1,0:T(8,128)(2,1)} %copy-done.33) | copy-start | bytes 3145732
  253.0 4.3 %copy-start.3 = (bf16[512,2048]{1,0:T(8,128)(2,1)S(1)}, bf16[512,2048]{1,0:T(8,128)(2,1)}, u32[]{:S(2)}) copy-start(bf16[512,2048]{1,0:T(8,128)(2,1)} %get-tuple-element.61) | copy-start | bytes 6291460
  253.0 4.3 %copy-start.16 = (bf16[512,256]{1,0:T(8,128)(2,1)S(1)}, bf16[512,256]{1,0:T(8,128)(2,1)}, u32[]{:S(2)}) copy-start(bf16[512,256]{1,0:T(8,128)(2,1)} %get-tuple-element.66) | copy-start | bytes 786436
  337.8 1.4 copy-start.4
  338.4 3.5 copy-start.5
  338.4 3.5 copy-start.6
  339.2 4.7 %copy-start.13 = (bf16[32,1024]{1,0:T(8,128)(2,1)S(1)}, bf16[32,1024]{1,0:T(8,128)(2,1)}, u32[]{:S(2)}) copy-start(bf16[32,1024]{1,0:T(8,128)(2,1)} %get-tuple-element.78) | copy-start | bytes 196612
  339.2 6.0 %copy-start.7 = (bf16[2,2,32,1024]{3,2,1,0:T(8,128)(2,1)S(1)}, bf16[2,2,32,1024]{3,2,1,0:T(8,128)(2,1)}, u32[]{:S(2)}) copy-start(bf16[2,2,32,1024]{3,2,1,0:T(8,128)(2,1)} %get-tuple-element.79) | copy-start | bytes 786436
  339.3 8.0 %copy-start.29 = (bf16[512,2048]{1,0:T(8,128)(2,1)S(1)}, bf16[512,2048]{1,0:T(8,128)(2,1)}, u32[]{:S(2)}) copy-start(bf16[512,2048]{1,0:T(8,128)(2,1)} %get-tuple-element.81) | copy-start | bytes 6291460
  349.7 46.8 %copy-start.8 = (f32[32,4,384]{2,1,0:T(4,128)S(1)}, f32[32,4,384]{2,1,0:T(4,128)}, u32[]{:S(2)}) copy-start(f32[32,4,384]{2,1,0:T(4,128)} %param.20) | copy-start | bytes 589828
  349.7 46.8 %copy-start.17 = (f32[32,4,384]{2,1,0:T(4,128)S(1)}, f32[32,4,384]{2,1,0:T(4,128)}, u32[]{:S(2)}) copy-start(f32[32,4,384]{2,1,0:T(4,128)} %param.21) | copy-start | bytes 589828
  349.7 46.9 %copy-start.18 = (f32[32,4,384]{2,1,0:T(4,128)S(1)}, f32[32,4,384]{2,1,0:T(4,128)}, u32[]{:S(2)}) copy-start(f32[32,4,384]{2,1,0:T(4,128)} %param.22) | copy-start | bytes 589828
  404.1 6.4 %copy-start.14 = (bf16[32,1024]{1,0:T(8,128)(2,1)S(1)}, bf16[32,1024]{1,0:T(8,128)(2,1)}, u32[]{:S(2)}) copy-start(bf16[32,1024]{1,0:T(8,128)(2,1)} %get-tuple-element.78) | copy-start | bytes 196612
  404.1 6.4 %copy-start.20 = (f32[32,1024]{1,0:T(8,128)S(1)}, f32[32,1024]{1,0:T(8,128)}, u32[]{:S(2)}) copy-start(f32[32,1024]{1,0:T(8,128)} %param.27) | copy-start | bytes 393220
  404.1 6.4 %copy-start.21 = (f32[32,1024]{1,0:T(8,128)S(1)}, f32[32,1024]{1,0:T(8,128)}, u32[]{:S(2)}) copy-start(f32[32,1024]{1,0:T(8,128)} %param.28) | copy-start | bytes 393220
  404.2 7.2 %copy-start.1 = (f32[128,1024]{1,0:T(8,128)S(1)}, f32[128,1024]{1,0:T(8,128)}, u32[]{:S(2)}) copy-start(f32[128,1024]{1,0:T(8,128)} %param.29) | copy-start | bytes 1572868
  404.2 7.2 %copy-start.9 = (f32[128,1024]{1,0:T(8,128)S(1)}, f32[128,1024]{1,0:T(8,128)}, u32[]{:S(2)}) copy-start(f32[128,1024]{1,0:T(8,128)} %param.30) | copy-start | bytes 1572868
  404.2 7.2 %copy-start.10 = (f32[128,1024]{1,0:T(8,128)S(1)}, f32[128,1024]{1,0:T(8,128)}, u32[]{:S(2)}) copy-start(f32[128,1024]{1,0:T(8,128)} %param.31) | copy-start | bytes 1572868
  411.3 1.5 copy-start.24
  411.3 1.6 copy-start.19
  411.3 1.6 copy-start.22
  411.3 1.6 copy-start.23
  411.3 2.2 copy-start.15
  411.4 2.8 copy-start.11

commit v4 on v3

--- a/solution.py
+++ b/solution.py
@@ -44,7 +44,7 @@
 ANY = pl.ANY
 BF = jnp.bfloat16
 F32 = jnp.float32
-VMEM_LIMIT = 56 * 1024 * 1024
+VMEM_LIMIT = 60 * 1024 * 1024
 NEVER = -1e30
 
 
@@ -66,6 +66,7 @@
 class Wires:
     def __init__(self, send_sem, recv_sem):
         self.send_sem, self.recv_sem, self.used, self.sent = send_sem, recv_sem, 0, []
+        self.settled = set()
 
     def send(self, src, dst, target, start=True):
         at = self.used
@@ -86,9 +87,13 @@
     def landed(self, at, region):
         pltpu.make_async_copy(region, region, self.recv_sem.at[at]).wait()
 
+    def settle(self, numbers):
+        for at in numbers:
+            self.sent[at].wait_send()
+            self.settled.add(at)
+
     def close(self):
-        for copy in self.sent:
-            copy.wait_send()
+        self.settle([at for at in range(self.used) if at not in self.settled])
 
 
 def greet(targets):
@@ -147,9 +152,11 @@
     wires.landed(direct, out.at[row_span(x), col_span(1 - c)])
     for at, rows in relays:
         wires.landed(at, out.at[rows, col_span(1 - c)])
+    return [at for at, _ in relays]
 
 
 FOLD_ORDER = (2, 1, 3, 0)
+EVERY = slice(None)
 
 
 def fold_sends(wires, part, folded, here):
@@ -164,12 +171,12 @@
     ]
 
 
-def fold_moves(wires, numbers, part, folded, leaving, arriving, here, total):
+def fold_moves(wires, numbers, part, folded, leaving, arriving, here, total, cols=EVERY):
     z, y, x, c = here
     moves = []
     for k, o in enumerate(FOLD_ORDER):
         wires.landed(numbers[k], folded.at[k])
-        both = part[row_span(lax.rem(x + o, 4)), col_span(c)].astype(F32) + folded[k].astype(F32)
+        both = part[row_span(lax.rem(x + o, 4)), cols].astype(F32) + folded[k].astype(F32)
         if o:
             leaving[k] = both.astype(BF)
             moves.append(
@@ -206,9 +213,6 @@
     at = wires.send(mine, theirs, device(z, y, x, 1 - c))
     wires.landed(at, theirs)
     return value + theirs[:, :1]
-
-
-EVERY = slice(None)
 
 
 def first_device(here, order, by):
@@ -688,208 +692,7 @@
     return back, jnp.sum(incoming * values * scale, axis=0, keepdims=True)
 
 
-def back_kernel(
-    part, middle, scale, gains, cotangent, grad_down, grad_up,
-    middle_grad, gain_out, out, down_out, up_out,
-    folded, leaving, arriving, total, mine, theirs, own, *rest,
-):
-    down_buffers, up_buffers, (send_sem, recv_sem, local_sem) = rest[:6], rest[6:12], rest[12:]
-    z, y, xl, xh, c = place()
-    x = xh * 2 + xl
-    here = (z, y, x, c)
-    greet(line_targets(z, y, x, c) + plane_targets(z, y, x, c))
-    wires = Wires(send_sem, recv_sem)
-    numbers = fold_sends(wires, part, folded, here)
-    down = PlaneSum(wires, grad_down, down_buffers, here, local_sem, 0)
-    up = PlaneSum(wires, grad_up, up_buffers, here, local_sem, 6)
-    down.start()
-    up.start()
-    moves = fold_moves(wires, numbers, part, folded, leaving, arriving, here, total)
-    down.relay()
-    up.relay()
-    fold_finish(wires, moves, arriving, total)
-    back, gain_sum = norm_back(
-        wires, middle[...], scale[:, :1], gains[1:2, :], total[...], mine, theirs, here
-    )
-    gain_out[...] = jnp.broadcast_to(gain_sum, gain_out.shape)
-    grad = cotangent[...].astype(F32) + back
-    middle_grad[...] = grad
-    own[...] = grad.astype(BF)
-    local = pltpu.make_async_copy(own, out.at[row_span(x), col_span(c)], local_sem.at[12])
-    local.start()
-    sends = gather_sends(wires, own, out, here)
-    down.middle()
-    gather_relay(wires, sends, out, here)
-    up.middle()
-    down.finish()
-    up.finish()
-    kept = [
-        pltpu.make_async_copy(down_buffers[5], down_out, local_sem.at[13]),
-        pltpu.make_async_copy(up_buffers[5], up_out, local_sem.at[14]),
-        local,
-    ]
-    for copy in kept[:2]:
-        copy.start()
-    for copy in kept:
-        copy.wait()
-    wires.close()
-
-
-def call_back(part, middle, scale, gains, cotangent, grad_down, grad_up):
-    vm = pl.BlockSpec(memory_space=pltpu.VMEM)
-    hbm = pl.BlockSpec(memory_space=ANY)
-    return pl.pallas_call(
-        back_kernel,
-        out_shape=(
-            jax.ShapeDtypeStruct((ROWS, WIDTH), F32),
-            jax.ShapeDtypeStruct((8, WIDTH), F32),
-            jax.ShapeDtypeStruct((LINE, D), BF),
-            jax.ShapeDtypeStruct((2, PIECE, D), BF),
-            jax.ShapeDtypeStruct((2, 2, PIECE, HIDDEN), BF),
-        ),
-        in_specs=[vm] * 5 + [hbm] * 2,
-        out_specs=(vm, vm, hbm, hbm, hbm),
-        scratch_shapes=fold_scratch()
-        + [
-            pltpu.VMEM((ROWS, 128), F32),
-            pltpu.VMEM((ROWS, 128), F32),
-            pltpu.VMEM((ROWS, WIDTH), BF),
-        ]
-        + sum_buffers((PIECE, D), BF)
-        + sum_buffers((2, PIECE, HIDDEN), BF)
-        + wire_scratch(56)
-        + [pltpu.SemaphoreType.DMA((15,))],
-        compiler_params=comm_params(3),
-        name="line_back",
-    )(part, middle, scale, gains, cotangent, grad_down, grad_up)
-
-
 PLANE = [(a, b) for a in range(4) for b in range(4) if a or b]
-
-
-def last_kernel(
-    part, inputs, scale, gains, middle_grad, gain_two, squares, output, grad_qkv,
-    input_home, output_home, qkv_out, totals,
-    folded, leaving, arriving, total, mine, theirs, *rest,
-):
-    buffers, rest = rest[:6], rest[6:]
-    landing, terms, stage, rec_one, rec_two = rest[:5]
-    send_sem, recv_sem, post_send, post_recv, local_sem = rest[5:]
-    fin = buffers[5]
-    z, y, xl, xh, c = place()
-    x = xh * 2 + xl
-    here = (z, y, x, c)
-    quad = quad_of(xl, xh, x, c)
-    line = [(o, b) for b in (0, 1) for o in range(4) if o or b]
-    fixed = [device(z + a, y + b, x, c) for a, b in PLANE]
-    fixed += [device(z, y, lax.rem(x + o, 4), lax.rem(c + b, 2)) for o, b in line]
-    barrier = pltpu.get_barrier_semaphore()
-    post = Posting(here, post_send, post_recv)
-    for target in fixed:
-        pl.semaphore_signal(barrier, inc=1, device_id=target, device_id_type=MESH)
-    extra = post.greet(barrier)
-    pl.semaphore_wait(barrier, len(fixed) + extra)
-    wires = Wires(send_sem, recv_sem)
-    numbers = fold_sends(wires, part, folded, here)
-    qkv = PlaneSum(wires, grad_qkv, buffers, here, local_sem, 0)
-    qkv.start()
-    output_at = post.send(output, output_home)
-    moves = fold_moves(wires, numbers, part, folded, leaving, arriving, here, total)
-    qkv.relay()
-    qkv.middle()
-    fold_finish(wires, moves, arriving, total)
-    back, gain_one = norm_back(
-        wires,
-        inputs[...].astype(F32),
-        scale[:, :1],
-        gains[0:1, :],
-        total[...],
-        mine,
-        theirs,
-        here,
-    )
-    total[...] = middle_grad[...] + back
-    input_at = post.send(total, input_home)
-    qkv.finish()
-    at_mine = xl * 2 + c
-    swaps = [
-        wires.send(fin.at[b, lax.rem(a, 2)], landing.at[at_mine], device(z, y, a, b))
-        for a, b in quad
-    ]
-    landing[at_mine] = fin[c, xl]
-    for at, (a, b) in zip(swaps, quad):
-        wires.landed(at, landing.at[lax.rem(a, 2) * 2 + b])
-    square = squares[...]
-    for k in range(4):
-        value = landing[k].astype(F32)
-        square = square + jnp.sum(value * value)
-    qkv_out[...] = landing[...]
-
-    for k in range(8):
-        cols = slice(k * 128, (k + 1) * 128)
-        terms[k : k + 1] = gain_one[:, cols]
-        terms[8 + k : 9 + k] = gain_two[0:1, cols]
-    terms[16:] = square
-    first = [
-        wires.send(terms, rec_one.at[k], device(z + a, y + b, x, c))
-        for k, (a, b) in enumerate(PLANE)
-    ]
-    value = terms[...]
-    for k, at in enumerate(first):
-        wires.landed(at, rec_one.at[k])
-        value = value + rec_one[k]
-    stage[...] = value
-    second = [
-        wires.send(stage, rec_two.at[k], device(z, y, lax.rem(x + o, 4), lax.rem(c + b, 2)))
-        for k, (o, b) in enumerate(line)
-    ]
-    both = [value, None]
-    for k, (o, b) in enumerate(line):
-        wires.landed(second[k], rec_two.at[k])
-        both[b] = rec_two[k] if both[b] is None else both[b] + rec_two[k]
-    totals[:16] = both[0][:16]
-    totals[16:] = (
-        both[0][16:]
-        + both[1][16:]
-        + jnp.sum(both[0][:16] * both[0][:16])
-        + jnp.sum(both[1][:16] * both[1][:16])
-    )
-    post.landed(output_at, output_home)
-    post.landed(input_at, input_home)
-    post.close()
-    wires.close()
-
-
-def call_last(part, inputs, scale, gains, middle_grad, gain_two, squares, output, grad_qkv):
-    vm = pl.BlockSpec(memory_space=pltpu.VMEM)
-    hbm = pl.BlockSpec(memory_space=ANY)
-    cols = grad_qkv.shape[-1]
-    return pl.pallas_call(
-        last_kernel,
-        out_shape=(
-            jax.ShapeDtypeStruct((ROWS, WIDTH), F32),
-            jax.ShapeDtypeStruct((ROWS, WIDTH), BF),
-            jax.ShapeDtypeStruct((4, PIECE, cols), BF),
-            jax.ShapeDtypeStruct((24, 128), F32),
-        ),
-        in_specs=[vm] * 7 + [hbm, hbm],
-        out_specs=(hbm, hbm, vm, vm),
-        scratch_shapes=fold_scratch()
-        + [pltpu.VMEM((ROWS, 128), F32), pltpu.VMEM((ROWS, 128), F32)]
-        + sum_buffers((2, PIECE, cols), BF)
-        + [
-            pltpu.VMEM((4, PIECE, cols), BF),
-            pltpu.VMEM((24, 128), F32),
-            pltpu.VMEM((24, 128), F32),
-            pltpu.VMEM((15, 24, 128), F32),
-            pltpu.VMEM((7, 24, 128), F32),
-        ]
-        + wire_scratch(64)
-        + wire_scratch(2)
-        + [pltpu.SemaphoreType.DMA((6,))],
-        compiler_params=comm_params(4),
-        name="line_last",
-    )(part, inputs, scale, gains, middle_grad, gain_two, squares, output, grad_qkv)
 
 
 def key_at(half):
@@ -952,10 +755,10 @@
 
 def forward_kernel(
     ends, cosine, sine, block_input, out_grad, gain_rows, qkv_in, gate_in, up_in, down_in, out_in,
-    inputs, scale_one, normed_out, qkv_out, queries, mixed_out, log_out, attended, keys_out,
+    inputs, scale_one, normed_out, qkv_out, queries, mixed_out, log_out, attended_out, keys_out,
     cotangent, cotangent_all, out_out, gate_all, up_all, down_all, middle_out, scale_two, out,
     inputs_all, gains_all, qkv_all, normed, columns, own_keys, keys, tops, sums, mixed,
-    out_stage, out_all, part, folded, leaving, arriving, total, mine_row, their_row, own,
+    attended, out_stage, out_all, part, folded, leaving, arriving, total, mine_row, their_row, own,
     send_sem, recv_sem, post_send, post_recv, stage_send, stage_recv, out_send, out_recv, local_sem,
 ):
     z, y, xl, xh, c = place()
@@ -1197,6 +1000,7 @@
             two = jnp.concatenate(
                 [mixed_out[s, :, head_cols(g)], mixed_out[s, :, head_cols(g + 1)]], axis=0
             )
+            attended_out[g * HD : (g + 2) * HD, tokens] = two.astype(BF)
             attended[tokens, g * HD : (g + 2) * HD] = two.T.astype(BF)
 
     out_gather.finish()
@@ -1211,7 +1015,9 @@
         fold_numbers.append(
             wires.send(part.at[rows, col_span(1 - c)], folded.at[k], device(z, y, x, 1 - c))
         )
-    moves = fold_moves(wires, fold_numbers, part, folded, leaving, arriving, here, total)
+    moves = fold_moves(
+        wires, fold_numbers, part, folded, leaving, arriving, here, total, col_span(c)
+    )
     fold_finish(wires, moves, arriving, total)
     middle = total[...] + inputs[...].astype(F32)
     middle_out[...] = middle
@@ -1256,7 +1062,7 @@
         ((2, 2 * HD, cols), BF, vm),
         ((2, HD, cols), F32, vm),
         ((2, 1, cols), F32, vm),
-        ((LINE, GROUP * HD), BF, vm),
+        ((GROUP * HD, LINE), BF, vm),
         ((2, 4, 4, HALF, 2 * HD), BF, hbm),
         (share, BF, hbm),
         ((LINE, D), BF, hbm),
@@ -1284,6 +1090,7 @@
             pltpu.VMEM((2, 1, cols), F32),
             pltpu.VMEM((2, 1, cols), F32),
             pltpu.VMEM((2, 2 * HD, cols), F32),
+            pltpu.VMEM((LINE, GROUP * HD), BF),
             pltpu.VMEM((2, PIECE, D), BF),
             pltpu.VMEM((4, 2, PIECE, D), BF),
             pltpu.VMEM((LINE, D), BF),
@@ -1304,53 +1111,142 @@
     )(ends, cosine, sine, block_input, out_grad, gain_rows, qkv_in, gate_in, up_in, down_in, out_in)
 
 
-def attention_back_kernel(
-    ends, queries, grads, query_rows, grad_rows, logs, delta, keys, output_part, middle,
-    grad_gate, grad_out, down_fin, up_fin,
-    query_back, key_back, output, gate_out, up_out, down_out, out_out,
-    terms, sums, rounded, folded, leaving, arriving, total, *rest,
+def backward_kernel(
+    ends, cosine, sine, part, output_part, middle, scale_two, scale_one, gains, inputs, cotangent,
+    queries, mixed, logs, attended, keys, out_low, qkv_low, normed, grad_down, grad_up, grad_gate,
+    input_home, output_home, qkv_out, gate_out, up_out, down_out, out_out, totals,
+    middle_grad, middle_all, grads, delta, query_rows, grad_rows, out_terms, output,
+    terms, sums, rounded, columns, rows_back, qkv_terms, key_rec, key_sums, key_rec_two,
+    *rest,
 ):
-    buffers, key_buffers, out_buffers = rest[:6], rest[6:9], rest[9:12]
-    send_sem, recv_sem, out_send, out_recv, local_sem = rest[12:]
-    key_rec, key_sums, key_rec_two = key_buffers
-    fin = buffers[5]
+    rest = list(rest)
+
+    def take(count):
+        taken = rest[:count]
+        del rest[:count]
+        return taken
+
+    first_fold, output_fold, (part_own, output_own) = take(4), take(4), take(2)
+    last_fold = first_fold
+    first_rows, last_rows, (own,) = take(2), take(2), take(1)
+    down_buffers, up_buffers, gate_buffers, qkv_buffers = take(6), take(6), take(6), take(6)
+    out_buffers, (total_terms, stage, rec_one, rec_two) = take(3), take(4)
+    send_sem, recv_sem, post_send, post_recv, out_send, out_recv, local_sem = rest
     z, y, xl, xh, c = place()
     x = xh * 2 + xl
     here = (z, y, x, c)
     mine = xl * 2 + c
     quad = quad_of(xl, xh, x, c)
-    greet(plane_targets(z, y, x, c) + line_targets(z, y, x, c) + [device(z, y, *quad[2])])
+    line = [(o, b) for b in (0, 1) for o in range(4) if o or b]
+    fixed = [device(z + a, y + b, x, c) for a, b in PLANE]
+    fixed += [device(z, y, lax.rem(x + o, 4), lax.rem(c + b, 2)) for o, b in line]
+    barrier = pltpu.get_barrier_semaphore()
+    post = Posting(here, post_send, post_recv)
+    for target in fixed:
+        pl.semaphore_signal(barrier, inc=1, device_id=target, device_id_type=MESH)
+    extra = post.greet(barrier)
+    pl.semaphore_wait(barrier, len(fixed) + extra)
     wires = Wires(send_sem, recv_sem)
-    gate = PlaneSum(wires, grad_gate, buffers, here, local_sem, 0)
+    kept = []
+
+    def keep(src, dst):
+        copy = pltpu.make_async_copy(src, dst, local_sem.at[25 + len(kept)])
+        copy.start()
+        kept.append(copy)
+
+    def deal(fin, result):
+        keep(fin.at[c, xl], result.at[mine])
+        return [
+            wires.send(fin.at[b, lax.rem(a, 2)], result.at[mine], device(z, y, a, b))
+            for a, b in quad
+        ]
+
+    def dealt(numbers, result):
+        for at, (a, b) in zip(numbers, quad):
+            wires.landed(at, result.at[lax.rem(a, 2) * 2 + b])
+
+    numbers = fold_sends(wires, part, first_fold[0], here)
+    own_parts = [
+        pltpu.make_async_copy(part.at[:, col_span(c)], part_own, local_sem.at[36]),
+        pltpu.make_async_copy(output_part.at[:, col_span(c)], output_own, local_sem.at[37]),
+        pltpu.make_async_copy(out_low, out_terms, local_sem.at[38]),
+        pltpu.make_async_copy(qkv_low, qkv_terms, local_sem.at[39]),
+    ]
+    for copy in own_parts:
+        copy.start()
+    down = PlaneSum(wires, grad_down, down_buffers, here, local_sem, 0)
+    up = PlaneSum(wires, grad_up, up_buffers, here, local_sem, 6)
+    gate = PlaneSum(wires, grad_gate, gate_buffers, here, local_sem, 12)
+    qkv = PlaneSum(wires, qkv_terms, qkv_buffers, here, local_sem, 18)
     out_sum = OutSum(
-        wires, grad_out, out_buffers, out_out, here, mine, quad, (out_send, out_recv), local_sem, 6
-    )
-    numbers = fold_sends(wires, output_part, folded, here)
+        wires, out_terms, out_buffers, out_out, here, mine, quad, (out_send, out_recv), local_sem, 24
+    )
+    down.start()
+    up.start()
+    own_parts[0].wait()
+    moves = fold_moves(wires, numbers, part_own, *first_fold[:3], here, first_fold[3])
+    down.relay()
+    up.relay()
     gate.start()
-    out_sum.start()
-    up_swaps = [
-        wires.send(up_fin.at[b, lax.rem(a, 2)], up_out.at[mine], device(z, y, a, b))
-        for a, b in quad
-    ]
-    down_swap = wires.send(
-        down_fin.at[:, :, col_span(1 - c)], down_out.at[c], device(z, y, x, 1 - c)
-    )
-    kept = [
-        pltpu.make_async_copy(up_fin.at[c, xl], up_out.at[mine], local_sem.at[7]),
-        pltpu.make_async_copy(down_fin.at[:, :, col_span(c)], down_out.at[c], local_sem.at[8]),
-    ]
-    for copy in kept:
-        copy.start()
-
-    tour = Tour(z * 4 + y)
+    fold_finish(wires, moves, first_fold[2], first_fold[3])
+    back, gain_two = norm_back(
+        wires, middle[...], scale_two[:, :1], gains[1:2, :], first_fold[3][...], *first_rows, here
+    )
+    grad = cotangent[...].astype(F32) + back
+    middle_grad[...] = grad
+    own[...] = grad.astype(BF)
+    keep(own, middle_all.at[row_span(x), col_span(c)])
+    sends = gather_sends(wires, own, middle_all, here)
+    for s in (0, 1):
+        for g in range(GROUP):
+            query_rows[s, g] = queries[s, :, head_cols(g)].astype(F32).T.astype(BF)
+    grads[:, :HD, :] = jnp.zeros((2, HD, GROUP * HALF), BF)
     terms[...] = jnp.zeros(terms.shape, F32)
     sums[...] = jnp.zeros(sums.shape, F32)
+    down.middle()
+    relayed = gather_relay(wires, sends, middle_all, here)
+    kept[0].wait()
+
+    own_parts[2].wait()
+    shared = out_terms[...].reshape(GROUP * HD, D)
+
+    def attended_rows(i, carry):
+        rows = pl.ds(pl.multiple_of(i * ROWS, ROWS), ROWS)
+        value = lax.dot_general(
+            middle_all[rows, :], shared, (((1,), (1,)), ((), ())), preferred_element_type=F32
+        )
+        columns[: GROUP * HD, rows] = value.astype(BF).astype(F32).T
+        return carry
+
+    lax.fori_loop(0, 4, attended_rows, 0)
+    for s in (0, 1):
+        for g in range(GROUP):
+            cols = head_cols(g)
+            value = columns[g * HD : (g + 1) * HD, s * HALF : (s + 1) * HALF]
+            grads[s, HD:, cols] = value.astype(BF)
+            delta[s, :, cols] = jnp.sum(value * mixed[s, :, cols], axis=0, keepdims=True)
+            grad_rows[s, g] = (
+                jnp.concatenate([jnp.zeros_like(value), value], axis=0).T.astype(BF)
+            )
+
+    def out_columns(i, carry):
+        cols = pl.ds(pl.multiple_of(i * HALF, HALF), HALF)
+        value = jnp.dot(attended[...], middle_all[:, cols], preferred_element_type=F32)
+        out_terms[:, :, :, cols] = value.astype(BF).reshape(4, 2, PIECE, HALF)
+        return carry
+
+    lax.fori_loop(0, D // HALF, out_columns, 0)
+    out_sum.start()
+    gate.relay()
+    output_numbers = fold_sends(wires, output_part, output_fold[0], here)
+
+    tour = Tour(z * 4 + y)
     heads = range(GROUP)
 
     def step(s, at, masked):
         slot = key_at(at)
         pairs = keys[slot]
-        columns = [queries[s, :, head_cols(g)] for g in heads]
+        query_columns = [queries[s, :, head_cols(g)] for g in heads]
         grad_columns = [grads[s, :, head_cols(g)] for g in heads]
         log_rows = [logs[s, :, head_cols(g)] for g in heads]
         deltas = [delta[s, :, head_cols(g)] for g in heads]
@@ -1359,7 +1255,7 @@
         if not masked:
             fits = in_second(tour.half(s), ends)
             log_rows = [jnp.where(fits, value, -NEVER) for value in log_rows]
-        scores = [jnp.dot(pairs, value, preferred_element_type=F32) for value in columns]
+        scores = [jnp.dot(pairs, value, preferred_element_type=F32) for value in query_columns]
         prob_grads = [jnp.dot(pairs, value, preferred_element_type=F32) for value in grad_columns]
         probs = [jnp.exp(scores[g] - log_rows[g]) for g in heads]
         if masked:
@@ -1368,9 +1264,7 @@
         score_grads = [(probs[g] * (prob_grads[g] - deltas[g])).astype(BF) for g in heads]
         probs_low = [value.astype(BF) for value in probs]
         back = [
-            lax.dot_general(
-                pairs, value, (((0,), (0,)), ((), ())), preferred_element_type=F32
-            )
+            lax.dot_general(pairs, value, (((0,), (0,)), ((), ())), preferred_element_type=F32)
             for value in score_grads
         ]
         added = [
@@ -1383,13 +1277,29 @@
             sums[s, :, head_cols(g)] += back[g]
 
     tour.inner(step, 0, 8)
-    gate.relay()
-    moves = fold_moves(wires, numbers, output_part, folded, leaving, arriving, here, total)
+    own_parts[1].wait()
+    output_moves = fold_moves(
+        wires, output_numbers, output_own, *output_fold[:3], here, output_fold[3]
+    )
     out_sum.middle()
+    up.middle()
     tour.inner(step, 8, 20)
-    fold_finish(wires, moves, arriving, total)
-    output[...] = (middle[...] + total[...]).astype(BF)
+    fold_finish(wires, output_moves, output_fold[2], output_fold[3])
+    output[...] = (middle[...] + output_fold[3][...]).astype(BF)
+    output_at = post.send(output, output_home)
+    normed_parts = [
+        pltpu.make_async_copy(normed.at[:, pl.ds(n * WIDTH, WIDTH)], value, local_sem.at[40 + n])
+        for n, value in enumerate((part_own, output_own))
+    ]
+    for copy in normed_parts:
+        copy.start()
     out_sum.deal()
+    down.finish()
+    down_fin = down_buffers[5]
+    down_swap = wires.send(
+        down_fin.at[:, :, col_span(1 - c)], down_out.at[c], device(z, y, x, 1 - c)
+    )
+    keep(down_fin.at[:, :, col_span(c)], down_out.at[c])
     gate.middle()
     tour.inner(step, 20, tour.count)
     tour.edges(step)
@@ -1410,14 +1320,18 @@
             )
         )
     for s in (0, 1):
-        query_back[s] = sums[s, :HD, :] * HD ** (-0.5)
+        tokens = slice(s * HALF, (s + 1) * HALF)
+        for g in range(GROUP):
+            turned = rope(
+                sums.at[s, :, head_cols(g)], 0, cosine[:, tokens], -sine[:, tokens]
+            )
+            for i, value in enumerate(turned):
+                at = g * HD + i * (HD // 2)
+                columns[at : at + HD // 2, tokens] = value * HD ** (-0.5)
+    up.finish()
+    up_swap = deal(up_buffers[5], up_out)
     gate.finish()
-    swaps = [
-        wires.send(fin.at[b, lax.rem(a, 2)], gate_out.at[mine], device(z, y, a, b))
-        for a, b in quad
-    ]
-    kept.append(pltpu.make_async_copy(fin.at[c, xl], gate_out.at[mine], local_sem.at[9]))
-    kept[-1].start()
+    gate_swap = deal(gate_buffers[5], gate_out)
     second = [[], []]
     for s in (0, 1):
         for k in range(3):
@@ -1435,67 +1349,185 @@
                     first_device(here, s, by),
                 )
             )
-    out_sum.finish()
     for s in (0, 1):
+        tokens = slice(s * HALF, (s + 1) * HALF)
         value = key_sums[s, first_at(here, s)].astype(F32)
         for k in range(3):
             wires.landed(second[s][k], key_rec_two.at[s, k])
             value = value + key_rec_two[s, k].astype(F32)
-        key_back[s] = value
-    for at, (a, b) in zip(up_swaps, quad):
-        wires.landed(at, up_out.at[lax.rem(a, 2) * 2 + b])
+        pair_columns = value.T
+        turned = rope(pair_columns, 0, cosine[:, tokens], -sine[:, tokens])
+        for i, value in enumerate(turned):
+            at = GROUP * HD + i * (HD // 2)
+            columns[at : at + HD // 2, tokens] = value
+        columns[(GROUP + 1) * HD :, tokens] = pair_columns[HD:]
+
+    own_parts[3].wait()
+    wires.settle(relayed)
+    weight = qkv_terms[...].reshape(D, columns.shape[0])
+    last_numbers = []
+    for k, o in enumerate(FOLD_ORDER):
+        rows = row_span(lax.rem(x + o, 4))
+        back_rows = columns[:, rows].T.astype(BF)
+        rows_back[rows, :] = back_rows
+        middle_all[rows, :] = lax.dot_general(
+            back_rows, weight, (((1,), (1,)), ((), ())), preferred_element_type=F32
+        ).astype(BF)
+        last_numbers.append(
+            wires.send(
+                middle_all.at[rows, col_span(1 - c)], last_fold[0].at[k], device(z, y, x, 1 - c)
+            )
+        )
+    wires.settle(moves)
+    back_all = rows_back[...]
+    for n, half in enumerate((part_own, output_own)):
+        normed_parts[n].wait()
+
+        def outer_rows_of(i, carry):
+            cols = pl.ds(pl.multiple_of(i * 256, 256), 256)
+            value = lax.dot_general(
+                half[:, cols], back_all, (((0,), (0,)), ((), ())), preferred_element_type=F32
+            )
+            qkv_terms[n, i] = value.astype(BF).reshape(qkv_terms.shape[2:])
+            return carry
+
+        lax.fori_loop(0, 4, outer_rows_of, 0)
+    qkv.start()
+    last_moves = fold_moves(
+        wires, last_numbers, middle_all, *last_fold[:3], here, last_fold[3], col_span(c)
+    )
+    qkv.relay()
+    qkv.middle()
+    fold_finish(wires, last_moves, last_fold[2], last_fold[3])
+    back, gain_one = norm_back(
+        wires,
+        inputs[...].astype(F32),
+        scale_one[:, :1],
+        gains[0:1, :],
+        last_fold[3][...],
+        *last_rows,
+        here,
+    )
+    middle_grad[...] = middle_grad[...] + back
+    input_at = post.send(middle_grad, input_home)
+    qkv.finish()
+    qkv_swap = deal(qkv_buffers[5], qkv_out)
+    out_sum.finish()
     wires.landed(down_swap, down_out.at[1 - c])
-    for at, (a, b) in zip(swaps, quad):
-        wires.landed(at, gate_out.at[lax.rem(a, 2) * 2 + b])
-    for copy in kept:
+    dealt(up_swap, up_out)
+    dealt(gate_swap, gate_out)
+    for copy in kept[1:]:
         copy.wait()
+    squares = jnp.zeros((), F32)
+    for result in (gate_out, up_out, down_out):
+        for k in range(result.shape[0]):
+            value = result[k].astype(F32)
+            squares = squares + jnp.sum(value * value)
+    value = out_out[...].astype(F32)
+    squares = squares + jnp.sum(value * value)
+    dealt(qkv_swap, qkv_out)
+    for k in range(4):
+        value = qkv_out[k].astype(F32)
+        squares = squares + jnp.sum(value * value)
+
+    for k in range(8):
+        cols = slice(k * 128, (k + 1) * 128)
+        total_terms[k : k + 1] = gain_one[:, cols]
+        total_terms[8 + k : 9 + k] = gain_two[:, cols]
+    total_terms[16:] = jnp.broadcast_to(squares, (8, 128))
+    first = [
+        wires.send(total_terms, rec_one.at[k], device(z + a, y + b, x, c))
+        for k, (a, b) in enumerate(PLANE)
+    ]
+    value = total_terms[...]
+    for k, at in enumerate(first):
+        wires.landed(at, rec_one.at[k])
+        value = value + rec_one[k]
+    stage[...] = value
+    second = [
+        wires.send(stage, rec_two.at[k], device(z, y, lax.rem(x + o, 4), lax.rem(c + b, 2)))
+        for k, (o, b) in enumerate(line)
+    ]
+    both = [value, None]
+    for k, (o, b) in enumerate(line):
+        wires.landed(second[k], rec_two.at[k])
+        both[b] = rec_two[k] if both[b] is None else both[b] + rec_two[k]
+    totals[:16] = both[0][:16]
+    totals[16:] = (
+        both[0][16:]
+        + both[1][16:]
+        + jnp.sum(both[0][:16] * both[0][:16])
+        + jnp.sum(both[1][:16] * both[1][:16])
+    )
+    post.landed(output_at, output_home)
+    post.landed(input_at, input_home)
+    post.close()
     wires.close()
 
 
-def call_attention_back(
-    ends, queries, grads, query_rows, grad_rows, logs, delta, keys, output_part, middle,
-    grad_gate, grad_out, down_fin, up_fin,
-):
+def call_backward(*operands):
     vm = pl.BlockSpec(memory_space=pltpu.VMEM)
     hbm = pl.BlockSpec(memory_space=ANY)
     cols = GROUP * HALF
+    qkv_cols = (GROUP + 2) * HD
+    share = (ROWS, WIDTH)
+    outs = [
+        (share, F32, hbm),
+        (share, BF, hbm),
+        ((4, PIECE, qkv_cols), BF, vm),
+        ((4, PIECE, HIDDEN), BF, vm),
+        ((4, PIECE, HIDDEN), BF, vm),
+        ((2, 2, PIECE, WIDTH), BF, vm),
+        ((PIECE, WIDTH), BF, vm),
+        ((24, 128), F32, vm),
+    ]
     return pl.pallas_call(
-        attention_back_kernel,
-        out_shape=(
-            jax.ShapeDtypeStruct((2, HD, cols), F32),
-            jax.ShapeDtypeStruct((2, HALF, 2 * HD), F32),
-            jax.ShapeDtypeStruct((ROWS, WIDTH), BF),
-            jax.ShapeDtypeStruct((4, PIECE, HIDDEN), BF),
-            jax.ShapeDtypeStruct((4, PIECE, HIDDEN), BF),
-            jax.ShapeDtypeStruct((2, 2, PIECE, WIDTH), BF),
-            jax.ShapeDtypeStruct((PIECE, WIDTH), BF),
-        ),
-        in_specs=[pl.BlockSpec(memory_space=pltpu.SMEM)] + [vm] * 9 + [hbm] * 4,
-        out_specs=(vm, vm, vm, hbm, hbm, hbm, hbm),
+        backward_kernel,
+        out_shape=tuple(jax.ShapeDtypeStruct(shape, kind) for shape, kind, _ in outs),
+        in_specs=[pl.BlockSpec(memory_space=pltpu.SMEM)] + [vm] * 2 + [hbm] * 2 + [vm] * 11 + [hbm] * 6,
+        out_specs=tuple(spec for _, _, spec in outs),
         scratch_shapes=[
+            pltpu.VMEM(share, F32),
+            pltpu.VMEM((LINE, D), BF),
+            pltpu.VMEM((2, 2 * HD, cols), BF),
+            pltpu.VMEM((2, 1, cols), F32),
+            pltpu.VMEM((2, GROUP, HALF, 2 * HD), BF),
+            pltpu.VMEM((2, GROUP, HALF, 2 * HD), BF),
+            pltpu.VMEM((4, 2, PIECE, D), BF),
+            pltpu.VMEM(share, BF),
             pltpu.VMEM((2, 4, 4, HALF, 2 * HD), F32),
             pltpu.VMEM((2, 2 * HD, cols), F32),
             pltpu.VMEM((2, 4, 4, HALF, 2 * HD), BF),
-        ]
-        + fold_scratch()
-        + sum_buffers((2, PIECE, HIDDEN), BF)
-        + [
+            pltpu.VMEM((qkv_cols, LINE), F32),
+            pltpu.VMEM((LINE, qkv_cols), BF),
+            pltpu.VMEM((2, 4, 4, 2, PIECE, qkv_cols), BF),
             pltpu.VMEM((2, 3, 4, HALF, 2 * HD), BF),
             pltpu.VMEM((2, 4, HALF, 2 * HD), BF),
             pltpu.VMEM((2, 3, HALF, 2 * HD), BF),
+        ]
+        + fold_scratch() * 2
+        + [pltpu.VMEM((LINE, WIDTH), BF)] * 2
+        + [pltpu.VMEM((ROWS, 128), F32)] * 4
+        + [pltpu.VMEM(share, BF)]
+        + sum_buffers((PIECE, D), BF)
+        + sum_buffers((2, PIECE, HIDDEN), BF) * 2
+        + sum_buffers((2, PIECE, qkv_cols), BF)
+        + [
             pltpu.VMEM((3, 2, PIECE, D), BF),
             pltpu.VMEM((2, PIECE, D), BF),
             pltpu.VMEM((3, 2, PIECE, D), BF),
+            pltpu.VMEM((24, 128), F32),
+            pltpu.VMEM((24, 128), F32),
+            pltpu.VMEM((15, 24, 128), F32),
+            pltpu.VMEM((7, 24, 128), F32),
         ]
-        + wire_scratch(56)
+        + wire_scratch(160)
+        + wire_scratch(2)
         + wire_scratch(6)
-        + [pltpu.SemaphoreType.DMA((10,))],
-        compiler_params=comm_params(6),
-        name="attention_back",
-    )(
-        ends, queries, grads, query_rows, grad_rows, logs, delta, keys, output_part, middle,
-        grad_gate, grad_out, down_fin, up_fin,
-    )
+        + [pltpu.SemaphoreType.DMA((42,))],
+        compiler_params=comm_params(2),
+        name="backward",
+    )(*operands)
 
 
 def rope_tables(position, head_size):
@@ -1514,22 +1546,6 @@
     return (jnp.cos(angles), jnp.sin(angles))
 
 
-def rotate(values, cosine, sine):
-    half_size = values.shape[-1] // 2
-    table_shape = (cosine.shape[0],) + (1,) * (values.ndim - 2) + (half_size,)
-    cos_part = cosine.reshape(table_shape)
-    sin_part = sine.reshape(table_shape)
-    first_half = values[..., :half_size]
-    second_half = values[..., half_size:]
-    return jnp.concatenate(
-        [
-            first_half * cos_part - second_half * sin_part,
-            second_half * cos_part + first_half * sin_part,
-        ],
-        axis=-1,
-    )
-
-
 def times(left, right, kind):
     return jnp.dot(left, right, preferred_element_type=F32).astype(kind)
 
@@ -1544,18 +1560,6 @@
     return lax.dot_general(
         left, right, (((0,), (0,)), ((), ())), preferred_element_type=F32
     ).astype(kind)
-
-
-def as_columns(rows):
-    return rows.reshape(2, HALF, GROUP, HD).transpose(0, 3, 2, 1).reshape(2, HD, GROUP * HALF)
-
-
-def as_heads(rows):
-    return rows.reshape(2, HALF, GROUP, HD).transpose(0, 2, 1, 3)
-
-
-def from_columns(columns):
-    return columns.reshape(2, HD, GROUP, HALF).transpose(0, 3, 2, 1).reshape(LINE, GROUP * HD)
 
 
 def adam(weight, moment, second, gradient, rate, decay):
@@ -1597,6 +1601,7 @@
     passed = (places[:, None] >= ends[None, :]).astype(jnp.int32)
     position = places - jnp.sum(passed * doc_lengths[None, :], axis=1)
     cosine, sine = rope_tables(position, HD)
+    cosine, sine = cosine.T, sine.T
 
     def dealt(half_weight):
         return (
@@ -1627,8 +1632,8 @@
         normed_two,
     ) = call_forward(
         ends,
-        cosine.T,
-        sine.T,
+        cosine,
+        sine,
         block_input,
         out_grad,
         jnp.concatenate([norm_gains, jnp.zeros((6, WIDTH), F32)], axis=0),
@@ -1638,11 +1643,9 @@
         down_weight.astype(BF).reshape(2, ROWS // 2, WIDTH),
         out_weight.astype(BF),
     )
-    qkv_low = qkv_whole.reshape(D, (GROUP + 2) * HD)
     gate_low = gate_whole.reshape(D, HIDDEN)
     up_low = up_whole.reshape(D, HIDDEN)
     down_low = down_whole.reshape(HIDDEN, D)
-    out_low = out_whole.reshape(GROUP * HD, D)
 
     gate_part = times(normed_two, gate_low, F32)
     up_part = times(normed_two, up_low, F32)
@@ -1654,65 +1657,31 @@
     gate_back, up_back = gate_back.astype(BF), up_back.astype(BF)
     grad_down = outer_rows(hidden, cotangent_all, BF)
     grad_up = outer_rows(normed_two, up_back, BF)
-    half_shape = gate_whole.shape
-    middle_grad, gain_two, middle_low, down_fin, up_fin = call_back(
-        (
-            times_transpose(gate_back, gate_low, F32) + times_transpose(up_back, up_low, F32)
-        ).astype(BF),
+    grad_gate = outer_rows(normed_two, gate_back, BF)
+    part = times_transpose(gate_back, gate_low, F32) + times_transpose(up_back, up_low, F32)
+    input_grad, output, qkv_sum, gate_sum, up_sum, down_sum, out_sum, totals = call_backward(
+        ends,
+        cosine,
+        sine,
+        part.astype(BF),
+        times(hidden, down_low, BF),
         middle,
         scale_two,
-        norm_gains,
-        cotangent,
-        grad_down.reshape(down_whole.shape),
-        grad_up.reshape(half_shape),
-    )
-    output_part = times(hidden, down_low, BF)
-    grad_gate = outer_rows(normed_two, gate_back, BF)
-
-    grad_out = outer_rows(attended, middle_low, BF)
-    attended_grad = times_transpose(middle_low, out_low, BF)
-    delta = jnp.sum(
-        (attended_grad.astype(F32) * from_columns(mixed)).reshape(LINE, GROUP, HD), axis=-1
-    )
-    delta = delta.reshape(2, HALF, GROUP).transpose(0, 2, 1).reshape(2, 1, GROUP * HALF)
-    blank = jnp.zeros((2, HD, GROUP * HALF), BF)
-    empty = jnp.zeros((2, GROUP, HALF, HD), BF)
-    query_back, key_grads, output, gate_sum, up_sum, down_sum, out_sum = call_attention_back(
-        ends,
-        query_columns,
-        jnp.concatenate([blank, as_columns(attended_grad)], axis=1),
-        query_columns.reshape(2, 2 * HD, GROUP, HALF).transpose(0, 2, 3, 1),
-        jnp.concatenate([empty, as_heads(attended_grad)], axis=-1),
-        logs,
-        delta,
-        keys,
-        output_part,
-        middle,
-        grad_gate.reshape(half_shape),
-        grad_out.reshape(out_whole.shape),
-        down_fin,
-        up_fin,
-    )
-    key_grads = key_grads.reshape(LINE, 2 * HD)
-    turned_back = jnp.concatenate([from_columns(query_back), key_grads[:, :HD]], axis=1)
-    turned_back = rotate(turned_back.reshape(LINE, GROUP + 1, HD), cosine, -sine)
-    projected_back = jnp.concatenate(
-        [turned_back.reshape(LINE, (GROUP + 1) * HD), key_grads[:, HD:]], axis=1
-    ).astype(BF)
-    grad_qkv = outer_rows(normed, projected_back, BF)
-    square = sum(
-        jnp.sum(jnp.square(member.astype(F32))) for member in (gate_sum, up_sum, out_sum, down_sum)
-    )
-    input_grad, output, qkv_sum, totals = call_last(
-        times_transpose(projected_back, qkv_low, BF),
-        inputs,
         scale_one,
         norm_gains,
-        middle_grad,
-        gain_two,
-        jnp.broadcast_to(square, (8, 128)),
-        output,
-        grad_qkv.reshape(qkv_whole.shape),
+        inputs,
+        cotangent,
+        query_columns,
+        mixed,
+        logs,
+        attended,
+        keys,
+        out_whole,
+        qkv_whole,
+        normed,
+        grad_down.reshape(down_whole.shape),
+        grad_up.reshape(up_whole.shape),
+        grad_gate.reshape(gate_whole.shape),
     )
     gate_both = jnp.stack([gate_sum, up_sum], axis=2).reshape(4, PIECE, 2, 16, HD)
     shares = (

time: 425 us -> 387 us (0.911)
  Pallas kernels: 318 us -> 304 us
  matrix products: 45.2 us -> 34.1 us
  local copies, waits for them, and re-layouts: 28.9 us -> 19.5 us
    pallas_call x3 -> x1, Pallas kernels: 175 us -> 161 us  [call_backward(): pl.pallas_call(backward_kernel, out_shape=tuple((jax.ShapeDtypeStruct(sha...]
    dot_general x3, matrix products: 14.1 us -> 9.28 us  [times(): return jnp.dot(left, right, preferred_element_type=F32).astype(kind)]
    reshape x7 -> x0, local copies, waits for them, and re-layouts: 4.26 us -> none  [the longest x3 3.11 us: from_columns(): columns.reshape(2, HD, GROUP, HALF).transpose(0, 3, 2, 1)]
    dot_general x5 -> x3, matrix products: 17.3 us -> 13.2 us  [outer_rows(): lax.dot_general(left, right, (((0,), (0,)), ((), ())), preferred_element_...]
    dot_general x5 -> x3, matrix products: 13.9 us -> 11.6 us  [times_transpose(): lax.dot_general(left, right, (((1,), (1,)), ((), ())), preferred_element_...]
where the time goes in v4:
time: 387 us; the launch traced here: 379 us
  Pallas kernels  304 us (79%)
  matrix products  34.1 us (9%)
  local copies, waits for them, and re-layouts  19.5 us (5%)
  other arithmetic  18.6 us (5%)
    pallas_call x1, Pallas kernels, call_backward(): pl.pallas_call(backward_kernel, out_shape=tuple((jax.ShapeDtypeStruct(sha...  161 us
    pallas_call x1, Pallas kernels, call_forward(): pl.pallas_call(forward_kernel, out_shape=tuple((jax.ShapeDtypeStruct(shap...  143 us
    dot_general x3, matrix products, outer_rows(): lax.dot_general(left, right, (((0,), (0,)), ((), ())), preferred_element_...  13.2 us
    dot_general x3, matrix products, times_transpose(): lax.dot_general(left, right, (((1,), (1,)), ((), ())), preferred_element_...  11.6 us
    sub x5, other arithmetic, adam(): weight - rate * (unbiased / divisor + decay * weight)  10.5 us
    dot_general x3, matrix products, times(): return jnp.dot(left, right, preferred_element_type=F32).astype(kind)  9.28 us

profile of v4, /device:TPU:1, one launch (start us, length us, event | category | flops | bytes accessed | tf_op | source)
XLA Modules:
  0.0 379.3 jit_solution(17658925479893871686)
XLA Ops:
  0.7 0.0 copy-start
  0.7 0.9 reduce-window.8
  1.6 0.7 select_reduce_fusion
  2.4 1.3 concatenate.4.gain_rows
  3.7 1.5 convert_element_type.72.out_in
  5.3 1.6 copy.81
  6.8 1.0 multiply_sine_fusion
  7.8 1.8 convert_element_type.71
  9.6 0.0 copy-done
  9.6 0.4 convert.4
  10.0 2.2 slice_reduce_fusion
  12.2 0.0 copy-done.17
  12.2 0.5 convert_element_type.70
  12.7 0.1 copy.60
  12.8 1.1 reshape.150.up_in
  13.9 0.5 convert_element_type.69
  14.4 0.1 copy.59
  14.5 1.1 reshape.149.gate_in
  15.6 142.7 %forward.1 = (bf16[128,1024]{1,0:T(8,128)(2,1)}, f32[128,128]{1,0:T(8,128)}, bf16[512,2048]{1,0:T(8,128)(2,1)}, bf16[2,4,4,2,32,384]{5,4,3,2,1,0:T(8,128)(2,1)},...) custom-call(s32[4]{0:T(128)} %bitcast.61, ...), custom_call_target="tpu_custom_call" | custom-call | tf_op jit(solution)/shard_map/forward/pallas_call | solution.py:1077
  158.3 0.0 copy-start.19
  158.3 0.0 copy-start.21
  158.3 5.3 %fusion.15 = f32[512,1024]{1,0:T(8,128)S(1)} fusion(bf16[512,2048]{1,0:T(8,128)(2,1)} %get-tuple-element.44, bf16[1024,2048]{1,0:T(8,128)(2,1)} %bitcast.68), kind=kOutput, calls=%fused_computation.50 | convolution fusion | flops 2147483648 | bytes 8388608 | tf_op jit(solution)/shard_map/dot_general | solution.py:1554
  163.6 0.0 copy-done.19
  163.6 0.0 copy-done.21
  163.6 0.0 copy-start.18
  163.6 2.3 fusion.16
  166.0 0.0 copy-done.18
  166.0 3.1 multiply_convert_fusion
  169.2 3.8 %convolution_convert_fusion.3.output_part = bf16[512,2048]{1,0:T(8,128)(2,1)} fusion(bf16[512,1024]{1,0:T(8,128)(2,1)S(1)} %get-tuple-element.141, bf16[1024,2048]{1,0:T(8,128)(2,1)S(1)} %bitcast.69), kind=kOutput, calls=%fused_computation.4 | convolution fusion | flops 2148532224 | bytes 7340032 | tf_op jit(solution)/shard_map/dot_general | solution.py:1550
  173.0 2.6 fusion.17
  175.5 0.0 copy-start.22
  175.5 3.7 add_convert_fusion.part
  179.3 4.4 %convolution_convert_fusion.2 = bf16[1024,2048]{1,0:T(8,128)(2,1)} fusion(bf16[512,1024]{1,0:T(8,128)(2,1)S(1)} %get-tuple-element.141, bf16[512,2048]{1,0:T(8,128)(2,1)S(1)} %copy-done.22), kind=kOutput, calls=%fused_computation.3 | convolution fusion | flops 2149580800 | bytes 7340032 | tf_op jit(solution)/shard_map/dot_general | solution.py:1560
  183.6 4.4 %convolution_convert_fusion.1 = bf16[2048,1024]{1,0:T(8,128)(2,1)} fusion(bf16[512,2048]{1,0:T(8,128)(2,1)S(1)} %copy-done.21, bf16[512,1024]{1,0:T(8,128)(2,1)S(1)} %get-tuple-element.143), kind=kOutput, calls=%fused_computation.2 | convolution fusion | flops 2149580800 | bytes 7340032 | tf_op jit(solution)/shard_map/dot_general | solution.py:1560
  188.0 4.4 %convolution_convert_fusion = bf16[2048,1024]{1,0:T(8,128)(2,1)} fusion(bf16[512,2048]{1,0:T(8,128)(2,1)S(1)} %copy-done.21, bf16[512,1024]{1,0:T(8,128)(2,1)S(1)} %get-tuple-element.142), kind=kOutput, calls=%fused_computation.1 | convolution fusion | flops 2149580800 | bytes 7340032 | tf_op jit(solution)/shard_map/dot_general | solution.py:1560
  192.5 0.0 copy-start.11
  192.5 0.0 copy-start.12
  192.5 161.1 %backward.1 = (f32[128,1024]{1,0:T(8,128)}, bf16[128,1024]{1,0:T(8,128)(2,1)}, bf16[4,32,384]{2,1,0:T(8,128)(2,1)}, bf16[4,32,1024]{2,1,0:T(8,128)(2,1)}, bf16[4...) custom-call(s32[4]{0:T(128)} %bitcast.62, ...), custom_call_target="tpu_custom_call" | custom-call | tf_op jit(solution)/shard_map/backward/pallas_call | solution.py:1484
  353.6 0.0 copy-start.4
  353.6 0.0 copy-start.9
  353.6 0.0 copy-start.10
  353.7 1.3 slice.16
  355.6 0.7 slice_multiply_fusion
  356.4 0.6 multiply_subtract_fusion.4
  357.0 1.6 multiply_subtract_fusion.3
  358.7 1.3 stack.9
  360.0 1.3 stack.10
  361.4 0.8 convert_multiply_fusion
  362.2 0.0 copy-done.13
  362.2 0.2 multiply_subtract_fusion.2
  362.4 0.8 copy.66
  363.2 0.8 copy.67
  364.0 0.8 copy.68
  364.8 0.2 multiply_bitcast_fusion
  365.0 1.4 copy.65
  366.4 1.8 mul.346
  368.2 0.0 copy-start.1
  368.2 0.0 copy-start.2
  368.2 0.0 copy-start.3
  368.2 3.1 multiply_subtract_fusion.1
  371.4 4.9 %multiply_subtract_fusion = (f32[32,2,4096]{2,1,0:T(2,128)}, f32[32,2,4096]{2,1,0:T(2,128)}, f32[32,2,4096]{2,1,0:T(2,128)}) fusion(f32[32,2,4096]{2,1,0:T(2,128)S(1)} %copy-done.1, f32[32,2,4096]{2,1,0:T(2,128)S(1)} %mul.346, f32[32,2,4096]{2,1,0:T(2,128)S(1)} %copy-done.2, f32[32,2,4096]{2,1,0:T(2,128)S(1)} %copy-done.3), kind=kLoop, calls=%fused_computation.12 | loop fusion | flops 3932160 | bytes 7340032 | tf_op jit(solution)/shard_map/sub | solution.py:1570
  376.3 0.7 copy.84
  377.0 0.0 copy-done.5
  377.0 0.8 copy.85
  (30 shorter events, 0.1 us)
Async XLA Ops:
  0.7 8.9 %copy-start = (f32[32,2,4096]{2,1,0:T(2,128)S(1)}, f32[32,2,4096]{2,1,0:T(2,128)}, u32[]{:S(2)}) copy-start(f32[32,2,4096]{2,1,0:T(2,128)} %param.23) | copy-start | bytes 3145732
  1.6 10.6 %copy-start.17 = (s32[4,1]{0,1:T(1,128)}, s32[4,1]{0,1:T(1,128)S(1)}, u32[]{:S(2)}) copy-start(s32[4,1]{0,1:T(1,128)S(1)} %reduce-window.8) | copy-start | bytes 52
  158.3 5.4 %copy-start.19 = (bf16[2,4,4,2,32,1024]{5,4,3,2,1,0:T(8,128)(2,1)S(1)}, bf16[2,4,4,2,32,1024]{5,4,3,2,1,0:T(8,128)(2,1)}, u32[]{:S(2)}) copy-start(bf16[2,4,4,2,32,1024]{5,4,3,2,1,0:T(8,128)(2,1)} %get-tuple-element.48) | copy-start | bytes 12582916
  158.3 5.4 %copy-start.21 = (bf16[512,2048]{1,0:T(8,128)(2,1)S(1)}, bf16[512,2048]{1,0:T(8,128)(2,1)}, u32[]{:S(2)}) copy-start(bf16[512,2048]{1,0:T(8,128)(2,1)} %get-tuple-element.46) | copy-start | bytes 6291460
  163.6 2.4 copy-start.18
  166.0 3.1 copy-start.20
  175.5 3.7 copy-start.22
  192.5 163.9 %copy-start.14 = (f32[2,1024]{1,0:T(2,128)S(1)}, f32[2,1024]{1,0:T(2,128)}, u32[]{:S(2)}) copy-start(f32[2,1024]{1,0:T(2,128)} %gains.1) | copy-start | bytes 24580
  192.5 163.9 %copy-start.15 = (f32[2,1024]{1,0:T(2,128)S(1)}, f32[2,1024]{1,0:T(2,128)}, u32[]{:S(2)}) copy-start(f32[2,1024]{1,0:T(2,128)} %param.33) | copy-start | bytes 24580
  192.5 163.9 %copy-start.16 = (f32[2,1024]{1,0:T(2,128)S(1)}, f32[2,1024]{1,0:T(2,128)}, u32[]{:S(2)}) copy-start(f32[2,1024]{1,0:T(2,128)} %param.34) | copy-start | bytes 24580
  192.5 164.5 %copy-start.6 = (f32[32,1024]{1,0:T(8,128)S(1)}, f32[32,1024]{1,0:T(8,128)}, u32[]{:S(2)}) copy-start(f32[32,1024]{1,0:T(8,128)} %param.26) | copy-start | bytes 393220
  192.5 164.5 %copy-start.11 = (f32[32,1024]{1,0:T(8,128)S(1)}, f32[32,1024]{1,0:T(8,128)}, u32[]{:S(2)}) copy-start(f32[32,1024]{1,0:T(8,128)} %param.27) | copy-start | bytes 393220
  192.5 164.5 %copy-start.12 = (f32[32,1024]{1,0:T(8,128)S(1)}, f32[32,1024]{1,0:T(8,128)}, u32[]{:S(2)}) copy-start(f32[32,1024]{1,0:T(8,128)} %param.28) | copy-start | bytes 393220
  353.6 7.8 %copy-start.8 = (bf16[2,2,32,1024]{3,2,1,0:T(8,128)(2,1)S(1)}, bf16[2,2,32,1024]{3,2,1,0:T(8,128)(2,1)}, u32[]{:S(2)}) copy-start(bf16[2,2,32,1024]{3,2,1,0:T(8,128)(2,1)} %get-tuple-element.69) | copy-start | bytes 786436
  353.6 8.6 %copy-start.4 = (f32[32,4,384]{2,1,0:T(4,128)S(1)}, f32[32,4,384]{2,1,0:T(4,128)}, u32[]{:S(2)}) copy-start(f32[32,4,384]{2,1,0:T(4,128)} %param.20) | copy-start | bytes 589828
  353.6 8.6 %copy-start.9 = (f32[32,4,384]{2,1,0:T(4,128)S(1)}, f32[32,4,384]{2,1,0:T(4,128)}, u32[]{:S(2)}) copy-start(f32[32,4,384]{2,1,0:T(4,128)} %param.21) | copy-start | bytes 589828
  353.6 8.6 %copy-start.10 = (f32[32,4,384]{2,1,0:T(4,128)S(1)}, f32[32,4,384]{2,1,0:T(4,128)}, u32[]{:S(2)}) copy-start(f32[32,4,384]{2,1,0:T(4,128)} %param.22) | copy-start | bytes 589828
  353.6 8.6 %copy-start.13 = (bf16[4,32,384]{2,1,0:T(8,128)(2,1)S(1)}, bf16[4,32,384]{2,1,0:T(8,128)(2,1)}, u32[]{:S(2)}) copy-start(bf16[4,32,384]{2,1,0:T(8,128)(2,1)} %get-tuple-element.65) | copy-start | bytes 294916
  368.2 3.1 copy-start.1
  368.2 3.1 copy-start.2
  368.2 3.1 copy-start.3
  371.3 4.9 %copy-start.7 = (bf16[128,1024]{1,0:T(8,128)(2,1)S(1)}, bf16[128,1024]{1,0:T(8,128)(2,1)}, u32[]{:S(2)}) copy-start(bf16[128,1024]{1,0:T(8,128)(2,1)} %get-tuple-element.164) | copy-start | bytes 786436
  371.3 5.6 %copy-start.5 = (f32[128,1024]{1,0:T(8,128)S(1)}, f32[128,1024]{1,0:T(8,128)}, u32[]{:S(2)}) copy-start(f32[128,1024]{1,0:T(8,128)} %get-tuple-element.165) | copy-start | bytes 1572868

commit v5 on v4

v5 whole, which is shorter than its diff:
```python
import functools
import math

import jax
import jax.numpy as jnp
import numpy as np
from jax import lax
from jax.experimental import pallas as pl
from jax.experimental.pallas import tpu as pltpu
from jax.sharding import PartitionSpec as P

D = 2048
HQ = 32
HD = 64
FF = 8192
ADAM_STEP = 10


NORM_EPS = 1e-05
ADAM_EPS = 1e-08
BETA_ONE = 0.9
BETA_TWO = 0.95
WEIGHT_DECAY = 0.1
MATRIX_RATE = 0.01
OUTPUT_RATE = 0.9
DOWN_RATE = 3.0
GAIN_RATE = 2.5
CLIP_NORM = 1.0
ROPE_THETA = 500000.0
ROPE_FACTOR = 32.0
LOW_FREQ = 1.0
HIGH_FREQ = 4.0
OLD_CONTEXT = 8192.0

TOKENS = 8192
HALF = 256
HALVES = TOKENS // HALF
ROWS = 128
LINE = 512
WIDTH = 1024
GROUP = 4
PIECE = 32
HIDDEN = 1024
MESH = pl.DeviceIdType.MESH
ANY = pl.ANY
BF = jnp.bfloat16
F32 = jnp.float32
VMEM_LIMIT = 60 * 1024 * 1024
NEVER = -1e30


def place():
    seq = lax.axis_index("seq")
    return (
        seq // 8,
        lax.rem(seq // 2, 4),
        lax.rem(seq, 2),
        lax.axis_index("wide"),
        lax.axis_index("narrow"),
    )


def device(z, y, x, c):
    return (lax.rem(z, 4) * 8 + lax.rem(y, 4) * 2 + lax.rem(x, 2), c, x // 2)


class Wires:
    def __init__(self, send_sem, recv_sem):
        self.send_sem, self.recv_sem, self.used, self.sent = send_sem, recv_sem, 0, []
        self.settled = set()

    def reserve(self):
        self.used += 1
        self.sent.append(None)
        return self.used - 1

    def send(self, src, dst, target, start=True, at=None):
        held = at is None
        if held:
            at = self.reserve()
        copy = pltpu.make_async_remote_copy(
            src_ref=src,
            dst_ref=dst,
            send_sem=self.send_sem.at[at],
            recv_sem=self.recv_sem.at[at],
            device_id=target,
            device_id_type=MESH,
        )
        if start:
            copy.start()
        if held:
            self.sent[at] = copy
        return at

    def left(self, at, region):
        pltpu.make_async_copy(region, region, self.send_sem.at[at]).wait()

    def landed(self, at, region):
        pltpu.make_async_copy(region, region, self.recv_sem.at[at]).wait()

    def settle(self, numbers):
        for at in numbers:
            self.sent[at].wait_send()
            self.settled.add(at)

    def close(self):
        held = [at for at in range(self.used) if self.sent[at] is not None]
        self.settle([at for at in held if at not in self.settled])


def greet(targets):
    barrier = pltpu.get_barrier_semaphore()
    for target in targets:
        pl.semaphore_signal(barrier, inc=1, device_id=target, device_id_type=MESH)
    pl.semaphore_wait(barrier, len(targets))


def line_targets(z, y, x, c):
    return [device(z, y, lax.rem(x + o, 4), c) for o in (1, 2, 3)] + [device(z, y, x, 1 - c)]


def plane_targets(z, y, x, c):
    return [device(z + o, y, x, c) for o in (1, 2, 3)] + [device(z, y + o, x, c) for o in (1, 2, 3)]


def wire_scratch(count):
    return [pltpu.SemaphoreType.DMA((count,)), pltpu.SemaphoreType.DMA((count,))]


def comm_params(number):
    return pltpu.CompilerParams(
        collective_id=number, has_side_effects=True, vmem_limit_bytes=VMEM_LIMIT
    )


def rows_of(x):
    return lax.rem(x, 2) * 2 + x // 2


def row_span(x):
    return pl.ds(pl.multiple_of(rows_of(x) * ROWS, ROWS), ROWS)


def col_span(c):
    return pl.ds(pl.multiple_of(c * WIDTH, WIDTH), WIDTH)


def half_span(x, half):
    return pl.ds(pl.multiple_of(rows_of(x) * ROWS + half * (ROWS // 2), ROWS // 2), ROWS // 2)


def chip(x, by):
    return lax.rem(x + by, 4)


def gather_sends(wires, own, out, here):
    z, y, x, c = here
    numbers = {}
    for first in (0, 1):
        for by, half in ((1, first), (3, 1 - first)):
            src = own.at[pl.ds(half * (ROWS // 2), ROWS // 2)]
            spot = out.at[half_span(x, half), col_span(c)]
            numbers[by, half] = wires.send(src, spot, device(z, y, chip(x, by), c))
    spot = out.at[row_span(x), col_span(c)]
    numbers["core"] = wires.send(own, spot, device(z, y, x, 1 - c))
    return numbers


def gather_hand(wires, numbers, out, here):
    z, y, x, c = here
    for by, half in ((1, 0), (3, 1)):
        spot = out.at[half_span(chip(x, 4 - by), half), col_span(c)]
        wires.landed(numbers[by, half], spot)
        numbers["far", half] = wires.send(spot, spot, device(z, y, chip(x, by), c))
    relays = []
    for by, half in ((1, 1), (3, 0)):
        from_x = chip(x, 4 - by)
        wires.landed(numbers[by, half], out.at[half_span(from_x, half), col_span(c)])
        spot = out.at[row_span(from_x), col_span(c)]
        relays.append((wires.send(spot, spot, device(z, y, x, 1 - c)), from_x))
    return relays


def gather_take(wires, numbers, relays, out, here):
    z, y, x, c = here
    far = chip(x, 2)
    for half in (0, 1):
        wires.landed(numbers["far", half], out.at[half_span(far, half), col_span(c)])
    spot = out.at[row_span(far), col_span(c)]
    relays = relays + [(wires.send(spot, spot, device(z, y, x, 1 - c)), far)]
    wires.landed(numbers["core"], out.at[row_span(x), col_span(1 - c)])
    for at, from_x in relays:
        wires.landed(at, out.at[row_span(from_x), col_span(1 - c)])
    return [at for at, _ in relays] + [numbers["far", 0], numbers["far", 1]]


def gather_relay(wires, numbers, out, here):
    relays = gather_hand(wires, numbers, out, here)
    return gather_take(wires, numbers, relays, out, here)


FOLD_ORDER = (2, 1, 3, 0)
EVERY = slice(None)


def fold_sends(wires, part, folded, here):
    z, y, x, c = here
    return [
        wires.send(
            part.at[row_span(lax.rem(x + o, 4)), col_span(1 - c)],
            folded.at[k],
            device(z, y, x, 1 - c),
        )
        for k, o in enumerate(FOLD_ORDER)
    ]


def fold_moves(wires, numbers, part, folded, leaving, arriving, here, total, cols=EVERY):
    z, y, x, c = here
    halves = [pl.ds(half * (ROWS // 2), ROWS // 2) for half in (0, 1)]
    near = [device(z, y, chip(x, by), c) for by in (1, 3)]
    far, direct, passed = [], [], []
    for k, o in enumerate(FOLD_ORDER):
        wires.landed(numbers[k], folded.at[k])
        both = part[row_span(chip(x, o)), cols].astype(F32) + folded[k].astype(F32)
        if o == 0:
            total[...] = both
            continue
        leaving[k] = both.astype(BF)
        if o == 2:
            for half in (0, 1):
                src = leaving.at[k, halves[half]]
                far.append(wires.send(src, arriving.at[2, halves[half]], near[half]))
        else:
            side = k - 1
            spot = halves[1 - side]
            direct.append(wires.send(leaving.at[k, spot], arriving.at[side, spot], near[side]))
    for side in (0, 1):
        spot = halves[side]
        wires.landed(far[side], arriving.at[2, spot])
        both = leaving[side + 1, spot].astype(F32) + arriving[2, spot].astype(F32)
        leaving[side + 1, spot] = both.astype(BF)
        passed.append(wires.send(leaving.at[side + 1, spot], arriving.at[side, spot], near[side]))
    return direct + passed + far


def fold_finish(wires, moves, arriving, total):
    for side in (0, 1):
        for at, half in ((moves[side], 1 - side), (moves[2 + side], side)):
            wires.landed(at, arriving.at[side, pl.ds(half * (ROWS // 2), ROWS // 2)])
    total[...] = total[...] + arriving[0].astype(F32) + arriving[1].astype(F32)


def fold_scratch():
    return [
        pltpu.VMEM((4, ROWS, WIDTH), BF),
        pltpu.VMEM((3, ROWS, WIDTH), BF),
        pltpu.VMEM((3, ROWS, WIDTH), BF),
        pltpu.VMEM((ROWS, WIDTH), F32),
    ]


def both_cores(wires, mine, theirs, value, here):
    z, y, x, c = here
    mine[...] = jnp.broadcast_to(value, mine.shape)
    at = wires.send(mine, theirs, device(z, y, x, 1 - c))
    wires.landed(at, theirs)
    return value + theirs[:, :1]


def first_device(here, order, by):
    z, y, x, c = here
    return device(z + by, y, x, c) if order == 0 else device(z, y + by, x, c)


def second_device(here, order, by):
    z, y, x, c = here
    return device(z, y + by, x, c) if order == 0 else device(z + by, y, x, c)


def first_at(here, order, by=0):
    return lax.rem((here[0] if order == 0 else here[1]) + by, 4)


def run_of(ref, here, order, by, sub=None):
    z, y, _, _ = here
    zi, yi = (EVERY, lax.rem(y + by, 4)) if order == 0 else (lax.rem(z + by, 4), EVERY)
    if len(ref.shape) > 4:
        return ref.at[order, zi, yi] if sub is None else ref.at[order, zi, yi, sub]
    rows = ref.shape[2] // 2
    if sub is None:
        return ref.at[zi, yi, pl.ds(order * rows, rows)]
    return ref.at[zi, yi, pl.ds(order * rows + sub * (rows // 2), rows // 2)]


def spot_of(ref, here, order, at, sub=None):
    z, y, _, _ = here
    zi, yi = (at, y) if order == 0 else (z, at)
    if len(ref.shape) > 4:
        return ref.at[order, zi, yi] if sub is None else ref.at[order, zi, yi, sub]
    rows = ref.shape[2] // 2
    if sub is None:
        return ref.at[zi, yi, pl.ds(order * rows, rows)]
    return ref.at[zi, yi, pl.ds(order * rows + sub * (rows // 2), rows // 2)]


class PlaneGather:
    def __init__(self, wires, whole, here):
        self.wires, self.whole, self.here, self.numbers = wires, whole, here, {}

    def send(self, key, spot, target):
        if key not in self.numbers:
            self.numbers[key] = self.wires.reserve()
        self.wires.send(spot, spot, target, at=self.numbers[key])

    def start(self, o):
        spot = spot_of(self.whole, self.here, o, first_at(self.here, o))
        for by in (1, 3):
            self.send(("first", o, by), spot, first_device(self.here, o, by))

    def relay(self, o):
        for sub, by in enumerate((1, 3)):
            at = first_at(self.here, o, 4 - by)
            self.wires.landed(self.numbers["first", o, by], spot_of(self.whole, self.here, o, at))
            spot = spot_of(self.whole, self.here, o, at, sub)
            self.send(("onward", o, by), spot, first_device(self.here, o, by))

    def turn(self, o):
        at = first_at(self.here, o, 2)
        for sub, by in enumerate((1, 3)):
            spot = spot_of(self.whole, self.here, o, at, sub)
            self.wires.landed(self.numbers["onward", o, by], spot)
        spot = run_of(self.whole, self.here, o, 0)
        for by in (1, 3):
            self.send(("second", o, by), spot, second_device(self.here, o, by))

    def relay_two(self, o):
        for sub, by in enumerate((1, 3)):
            spot = run_of(self.whole, self.here, o, 4 - by)
            self.wires.landed(self.numbers["second", o, by], spot)
            spot = run_of(self.whole, self.here, o, 4 - by, sub)
            self.send(("last", o, by), spot, second_device(self.here, o, by))

    def finish(self, o):
        for sub, by in enumerate((1, 3)):
            spot = run_of(self.whole, self.here, o, 2, sub)
            self.wires.landed(self.numbers["last", o, by], spot)

    def leave(self):
        for o in (0, 1):
            spot = spot_of(self.whole, self.here, o, first_at(self.here, o))
            half = spot_of(self.whole, self.here, o, first_at(self.here, o), 0)
            for by in (1, 3):
                self.wires.left(self.numbers["first", o, by], spot)
                self.wires.left(self.numbers["onward", o, by], half)
                self.wires.left(self.numbers["second", o, by], run_of(self.whole, self.here, o, 0))
                self.wires.left(self.numbers["last", o, by], run_of(self.whole, self.here, o, 0, 0))


def in_turn(c, members, first):
    def run(*steps):
        for core in (0, 1):

            @pl.when(c == core)
            def _():
                for step in steps:
                    for member in members:
                        getattr(member, step)(core if first else 1 - core)

    return run


OFFSETS = (2, 1, 3)


class DirectGather:
    def __init__(self, wires, whole, here):
        self.wires, self.whole, self.here = wires, whole, here

    def start(self):
        self.numbers = []
        for o in (0, 1):
            spot = spot_of(self.whole, self.here, o, first_at(self.here, o))
            self.numbers.append(
                [self.wires.send(spot, spot, first_device(self.here, o, by)) for by in OFFSETS]
            )

    def turn(self):
        lines = []
        for o in (0, 1):
            for at, by in zip(self.numbers[o], OFFSETS):
                back = first_at(self.here, o, 4 - by)
                self.wires.landed(at, spot_of(self.whole, self.here, o, back))
            spot = run_of(self.whole, self.here, o, 0)
            lines.append(
                [self.wires.send(spot, spot, second_device(self.here, o, by)) for by in OFFSETS]
            )
        self.numbers = lines

    def finish(self):
        for o in (0, 1):
            for at, by in zip(self.numbers[o], OFFSETS):
                self.wires.landed(at, run_of(self.whole, self.here, o, 4 - by))


class PlaneSum:
    def __init__(self, wires, terms, buffers, here, local_sem, at):
        self.wires, self.terms, self.here, self.numbers = wires, terms, here, {}
        self.far, self.joined, self.rec, self.total, self.rec_two, self.fin = buffers
        self.kept, self.added = [], []
        for o in (0, 1):
            self.kept.append(
                pltpu.make_async_copy(
                    run_of(terms, here, o, 0), self.total.at[o], local_sem.at[at + 3 * o]
                )
            )
            self.added.append(
                [
                    pltpu.make_async_copy(
                        run_of(terms, here, o, by, sub),
                        self.joined.at[o, sub],
                        local_sem.at[at + 3 * o + 1 + sub],
                    )
                    for sub, by in enumerate((1, 3))
                ]
            )

    def send(self, key, src, dst, target):
        if key not in self.numbers:
            self.numbers[key] = self.wires.reserve()
        self.wires.send(src, dst, target, at=self.numbers[key])

    def start(self, o):
        for sub, by in enumerate((1, 3)):
            self.send(
                ("far", o, sub),
                run_of(self.terms, self.here, o, 2, sub),
                self.far.at[o, sub],
                second_device(self.here, o, by),
            )
        for copy in self.added[o]:
            copy.start()
        self.kept[o].start()

    def direct(self, o):
        for sub, by in enumerate((1, 3)):
            self.send(
                ("direct", o, sub),
                run_of(self.terms, self.here, o, by, 1 - sub),
                half_of(self.rec.at[o, sub], 1 - sub),
                second_device(self.here, o, by),
            )

    def relay(self, o):
        for sub, by in enumerate((1, 3)):
            self.added[o][sub].wait()
            self.wires.landed(self.numbers["far", o, sub], self.far.at[o, sub])

            def add(i, carry):
                value = self.joined[o, sub, i].astype(F32) + self.far[o, sub, i].astype(F32)
                self.joined[o, sub, i] = value.astype(BF)
                return carry

            lax.fori_loop(0, 4, add, 0)
            self.send(
                ("passed", o, sub),
                self.joined.at[o, sub],
                half_of(self.rec.at[o, sub], sub),
                second_device(self.here, o, by),
            )

    def middle(self, o):
        self.kept[o].wait()
        for sub in (0, 1):
            rec = self.rec.at[o, sub]
            self.wires.landed(self.numbers["direct", o, sub], half_of(rec, 1 - sub))
            self.wires.landed(self.numbers["passed", o, sub], half_of(rec, sub))

        def add(i, carry):
            value = self.total[o, i].astype(F32)
            for sub in (0, 1):
                value = value + self.rec[o, sub, i].astype(F32)
            self.total[o, i] = value.astype(BF)
            return carry

        lax.fori_loop(0, 4, add, 0)
        for k, by in enumerate(OFFSETS):
            self.send(
                ("last", o, k),
                self.total.at[o, first_at(self.here, o, by)],
                self.rec_two.at[o, k],
                first_device(self.here, o, by),
            )

    def finish(self, o):
        value = self.total[o, first_at(self.here, o)].astype(F32)
        for k in range(3):
            self.wires.landed(self.numbers["last", o, k], self.rec_two.at[o, k])
            value = value + self.rec_two[o, k].astype(F32)
        self.fin[o] = value.astype(self.fin.dtype)

    def leave(self):
        for o in (0, 1):
            for sub in (0, 1):
                self.wires.left(self.numbers["far", o, sub], self.far.at[o, sub])
                self.wires.left(self.numbers["passed", o, sub], self.joined.at[o, sub])
                half = half_of(self.rec.at[o, sub], 1 - sub)
                self.wires.left(self.numbers["direct", o, sub], half)
            for k in range(3):
                self.wires.left(self.numbers["last", o, k], self.rec_two.at[o, k])


def run_bulk(members, steps):
    for step in steps:
        for o in (0, 1):
            for member in members:
                getattr(member, step)(o)


def half_of(line, sub):
    if len(line.shape) == 4:
        return line.at[:, sub]
    rows = line.shape[1] // 2
    return line.at[:, pl.ds(sub * rows, rows)]


def sum_buffers(piece, kind):
    half = piece[1:] if len(piece) == 3 else (piece[0] // 2,) + piece[1:]
    return [
        pltpu.VMEM((2, 2, 4) + half, BF),
        pltpu.VMEM((2, 2, 4) + half, BF),
        pltpu.VMEM((2, 2, 4) + piece, BF),
        pltpu.VMEM((2, 4) + piece, BF),
        pltpu.VMEM((2, 3) + piece, BF),
        pltpu.VMEM((2,) + piece, kind),
    ]


class OutGather:
    def __init__(self, wires, stage, whole, here, mine, send_sem, recv_sem, local_sem, at):
        z, y, x, c = here
        self.wires, self.stage, self.whole, self.here = wires, stage, whole, here
        self.off = lax.rem(z - mine + 4, 4)
        self.recv_sem = recv_sem
        spot = whole.at[y]
        self.kept = pltpu.make_async_copy(stage, spot, local_sem.at[at])

        def copy(k, src, dst, by):
            return pltpu.make_async_remote_copy(
                src_ref=src,
                dst_ref=dst,
                send_sem=send_sem.at[k],
                recv_sem=recv_sem.at[k],
                device_id=device(z + by, y, x, c),
                device_id_type=MESH,
            )

        self.first = [copy(0, stage, spot, 1), copy(1, stage, spot, 3)]
        self.onward = [
            copy(2, spot.at[0], spot.at[0], 1),
            copy(3, spot.at[1], spot.at[1], 3),
        ]

    def landed(self, k, region):
        pltpu.make_async_copy(region, region, self.recv_sem.at[k]).wait()

    def start(self):
        @pl.when(self.off == 0)
        def _():
            self.kept.start()
            for copy in self.first:
                copy.start()

    def relay(self):
        spot = self.whole.at[self.here[1]]
        for k, off in ((0, 1), (1, 3)):

            @pl.when(self.off == off)
            def _():
                self.landed(k, spot)
                self.onward[k].start()

    def turn(self):
        z, y, x, c = self.here
        spot = self.whole.at[y]

        @pl.when(self.off == 0)
        def _():
            self.kept.wait()

        @pl.when(self.off == 2)
        def _():
            self.landed(2, spot.at[0])
            self.landed(3, spot.at[1])

        self.numbers = [self.wires.send(spot, spot, device(z, y + by, x, c)) for by in (1, 3)]

    def relay_two(self):
        z, y, x, c = self.here
        relays = []
        for sub, by in enumerate((1, 3)):
            spot = self.whole.at[lax.rem(y + 4 - by, 4)]
            self.wires.landed(self.numbers[sub], spot)
            relays.append(
                self.wires.send(spot.at[sub], spot.at[sub], device(z, y + by, x, c))
            )
        self.numbers = relays

    def finish(self):
        spot = self.whole.at[lax.rem(self.here[1] + 2, 4)]
        for sub in (0, 1):
            self.wires.landed(self.numbers[sub], spot.at[sub])

        @pl.when(self.off == 0)
        def _():
            for copy in self.first:
                copy.wait_send()

        for k, off in ((0, 1), (1, 3)):

            @pl.when(self.off == off)
            def _():
                self.onward[k].wait_send()


class OutSum:
    def __init__(self, wires, terms, buffers, piece, here, mine, quad, sems, local_sem, at):
        self.wires, self.terms, self.here, self.mine, self.quad = wires, terms, here, mine, quad
        self.rec, self.total, self.rec_two = buffers
        self.piece, self.local_sem, self.at = piece, local_sem, at
        self.send_sem, self.recv_sem = sems
        self.off = lax.rem(here[0] - mine + 4, 4)
        self.kept = pltpu.make_async_copy(
            terms.at[here[1]], self.total, local_sem.at[at]
        )

    def start(self):
        z, y, x, c = self.here
        self.kept.start()
        self.numbers = [
            self.wires.send(
                self.terms.at[lax.rem(y + by, 4)], self.rec.at[k], device(z, y + by, x, c)
            )
            for k, by in enumerate(OFFSETS)
        ]

    def copy(self, k, src, dst, target):
        return pltpu.make_async_remote_copy(
            src_ref=src,
            dst_ref=dst,
            send_sem=self.send_sem.at[k],
            recv_sem=self.recv_sem.at[k],
            device_id=target,
            device_id_type=MESH,
        )

    def middle(self):
        z, y, x, c = self.here
        self.kept.wait()
        value = self.total[...].astype(F32)
        for k in range(3):
            self.wires.landed(self.numbers[k], self.rec.at[k])
            value = value + self.rec[k].astype(F32)
        self.total[...] = value.astype(BF)
        self.moves = []
        for off in (1, 2, 3):
            move = self.copy(
                off - 1, self.total, self.rec_two.at[off - 1], device(self.mine, y, x, c)
            )
            self.moves.append(move)

            @pl.when(self.off == off)
            def _():
                move.start()

    def deal(self):
        z, y, x, c = self.here
        self.deals = []
        xl = lax.rem(x, 2)
        for k, (a, b) in enumerate(self.quad):
            self.deals.append(
                self.copy(
                    3 + k, self.total.at[lax.rem(a, 2), :, col_span(b)], self.piece, device(z, y, a, b)
                )
            )

        @pl.when(self.off == 0)
        def _():
            value = self.total[...].astype(F32)
            for k in range(3):
                region = self.rec_two.at[k]
                pltpu.make_async_copy(region, region, self.recv_sem.at[k]).wait()
                value = value + self.rec_two[k].astype(F32)
            self.total[...] = value.astype(BF)
            for copy in self.deals:
                copy.start()
            own = pltpu.make_async_copy(
                self.total.at[xl, :, col_span(c)], self.piece, self.local_sem.at[self.at]
            )
            own.start()
            own.wait()

    def finish(self):
        z, y, x, c = self.here
        xl = lax.rem(x, 2)
        holder_xl, holder_c = z // 2, lax.rem(z, 2)
        for k, (dx, dc) in enumerate(((0, 1), (1, 0), (1, 1))):

            @pl.when(
                (holder_xl == lax.rem(xl + dx, 2)) & (holder_c == lax.rem(c + dc, 2))
            )
            def _():
                pltpu.make_async_copy(self.piece, self.piece, self.recv_sem.at[3 + k]).wait()

        for off in (1, 2, 3):

            @pl.when(self.off == off)
            def _():
                self.moves[off - 1].wait_send()

        @pl.when(self.off == 0)
        def _():
            for copy in self.deals:
                copy.wait_send()


def quad_of(xl, xh, x, c):
    pair = xh * 2 + 1 - xl
    return [(x, 1 - c), (pair, c), (pair, 1 - c)]


def norm_back(wires, values, scale, gain_row, incoming, mine, theirs, here):
    weighted = incoming * gain_row
    inner = both_cores(
        wires, mine, theirs, jnp.sum(weighted * values, axis=1, keepdims=True), here
    )
    inner = inner / D
    back = scale * (incoming * gain_row) - values * (scale * scale * scale * inner)
    return back, jnp.sum(incoming * values * scale, axis=0, keepdims=True)


PLANE = [(a, b) for a in range(4) for b in range(4) if a or b]


def key_at(half):
    at = half // 2
    return lax.rem(half, 2), at // 4, lax.rem(at, 4)


def ends_of(lengths):
    ends = [lengths[0]]
    for k in range(1, 4):
        ends.append(ends[-1] + lengths[k])
    return ends


def allowed_pairs(key_half, query_half, ends):
    keys = key_half * HALF + lax.broadcasted_iota(jnp.int32, (HALF, HALF), 0)
    queries = query_half * HALF + lax.broadcasted_iota(jnp.int32, (HALF, HALF), 1)
    same = keys <= queries
    for k in range(3):
        same = same & ((keys >= ends[k]) == (queries >= ends[k]))
    return same


def in_second(query_half, ends):
    queries = query_half * HALF + lax.broadcasted_iota(jnp.int32, (1, HALF), 1)
    return (queries >= ends[0]) & (queries < ends[1])


class Tour:
    def __init__(self, spot, order):
        self.spot, self.order = spot, order
        halves = [2 * spot, HALVES - 1 - 2 * spot]
        self.first, self.last = halves[order[0]], halves[order[1]]
        self.turn = self.first + 1

    def half(self, s):
        return jnp.where(s == 0, 2 * self.spot, HALVES - 1 - 2 * self.spot)

    def run(self, step, between, start, stop):
        def body(t, carry):
            late = t >= self.turn

            @pl.when(t == self.turn)
            def _():
                between()

            half = jnp.where(late, self.last, self.first)
            s = jnp.where(late, self.order[1], self.order[0])
            u = t - jnp.where(late, self.turn, 0)
            inner = jnp.maximum(half - 1, 0)

            @pl.when(u < inner)
            def _():
                step(s, 1 + u, False)

            @pl.when(u >= inner)
            def _():
                step(s, (u - inner) * half, True)

            return carry

        lax.fori_loop(start, stop, body, 0)


def head_cols(g):
    return slice(g * HALF, (g + 1) * HALF)


def rope(columns, at, cosine, sine):
    first = columns[at : at + HD // 2]
    second = columns[at + HD // 2 : at + HD]
    return first * cosine - second * sine, second * cosine + first * sine


def forward_kernel(
    lengths, inverse, block_input, qkv_weight, gate_up_weight, down_weight, out_weight, gains, out_grad,
    cosine, sine, scale_one, normed_out, qkv_out, queries, mixed_out, log_out, attended_out, keys_out,
    cotangent_all, out_out, gate_all, up_all, down_all, middle_out, scale_two, out,
    qkv_in, gate_in, up_in, down_in, out_in, gain_rows,
    inputs_all, gains_all, qkv_all, normed, columns, across_queries, attended_here, across,
    keys, tops, sums, mixed,
    attended, out_stage, out_all, part, folded, leaving, arriving, total, mine_row, their_row, own,
    send_sem, recv_sem, stage_send, stage_recv, out_send, out_recv, local_sem,
):
    z, y, xl, xh, c = place()
    x = xh * 2 + xl
    here = (z, y, x, c)
    mine = xl * 2 + c
    quad = quad_of(xl, xh, x, c)
    opposite = device(3 - z, 3 - y, x, c)
    greet(
        line_targets(z, y, x, c)
        + [device(z, y, *quad[2]), opposite]
        + plane_targets(z, y, x, c)
    )
    wires = Wires(send_sem, recv_sem)
    kept = {}

    def keep(name, src, dst):
        copy = pltpu.make_async_copy(src, dst, local_sem.at[len(kept)])
        copy.start()
        kept[name] = copy

    def swap(given, whole):
        numbers = [
            wires.send(
                given.at[lax.rem(to, 2) * 2 + core], whole.at[c, z, y, xl], device(z, y, to, core)
            )
            for to, core in quad
        ]
        return numbers

    def swapped(numbers, whole):
        for at, (from_x, from_c) in zip(numbers, quad):
            wires.landed(at, whole.at[from_c, z, y, lax.rem(from_x, 2)])

    keep("inputs", block_input, inputs_all.at[row_span(x), col_span(c)])
    input_numbers = gather_sends(wires, block_input, inputs_all, here)
    for k in range(4):
        qkv_in[k] = qkv_weight[:, k, :].astype(BF)
    qkv_swap = swap(qkv_in, qkv_all)
    qkv_all[c, z, y, xl] = qkv_in[mine]
    gain_rows[...] = jnp.zeros(gain_rows.shape, F32)
    gain_rows[0:2, :] = gains[...]
    gains_all[:, col_span(c)] = gain_rows[...]
    gain_at = wires.send(gain_rows, gains_all.at[:, col_span(c)], device(z, y, x, 1 - c))
    for k in (0, 1):
        down_in[k] = down_weight[k * 2 * PIECE : (k + 1) * 2 * PIECE, :].astype(BF)
    keep("down", down_in.at[c], down_all.at[z, y, :, col_span(c)])
    down_swap = wires.send(
        down_in.at[1 - c], down_all.at[z, y, :, col_span(c)], device(z, y, x, 1 - c)
    )
    out_in[...] = out_weight[...].astype(BF)
    holds = z == mine
    stage_spot = out_stage.at[xl, :, col_span(c)]
    stage_copy = pltpu.make_async_remote_copy(
        src_ref=out_in,
        dst_ref=stage_spot,
        send_sem=stage_send.at[0],
        recv_sem=stage_recv.at[mine],
        device_id=device(z, y, xh * 2 + z // 2, lax.rem(z, 2)),
        device_id_type=MESH,
    )

    @pl.when(jnp.logical_not(holds))
    def _():
        stage_copy.start()

    @pl.when(holds)
    def _():
        pltpu.make_async_copy(out_in, stage_spot, stage_recv.at[mine]).start()

    qkv = DirectGather(wires, qkv_all, here)
    pairs_gather = DirectGather(wires, keys, here)
    gate = PlaneGather(wires, gate_all, here)
    up = PlaneGather(wires, up_all, here)
    down = PlaneGather(wires, down_all, here)
    bulk = (gate, up, down)
    out_gather = OutGather(
        wires, out_stage, out_all, here, mine, out_send, out_recv, local_sem, 12
    )

    def down_ready():
        wires.landed(down_swap, down_all.at[z, y, :, col_span(1 - c)])
        kept["down"].wait()

    swapped(qkv_swap, qkv_all)
    qkv.start()
    down_ready()
    run_bulk((down,), ('start',))
    left = lax.broadcasted_iota(jnp.int32, (PIECE, 2 * HD), 1) < HD
    for u, dealt in enumerate((gate_in, up_in)):
        for side in (0, 1):
            for j in range(HIDDEN // (2 * HD)):
                cols = slice(j * 2 * HD, (j + 1) * 2 * HD)
                even, odd = (
                    gate_up_weight[:, u, ((2 * j + i) * 2 + side) * 2 * HD :][:, : 2 * HD]
                    for i in (0, 1)
                )
                dealt[side * 2, :, cols] = jnp.where(left, even, pltpu.roll(odd, HD, 1)).astype(BF)
                dealt[side * 2 + 1, :, cols] = jnp.where(
                    left, pltpu.roll(even, HD, 1), odd
                ).astype(BF)
    keep("gate", gate_in.at[mine], gate_all.at[c, z, y, xl])
    keep("up", up_in.at[mine], up_all.at[c, z, y, xl])
    gate_swap = swap(gate_in, gate_all)
    up_swap = swap(up_in, up_all)
    ends = ends_of(lengths)
    tokens = (z * 4 + y) * LINE + lax.broadcasted_iota(jnp.int32, (HD // 2, LINE), 1)
    position = tokens
    for k in range(4):
        position = position - jnp.where(tokens >= ends[k], lengths[k], 0)
    angles = position.astype(F32) * inverse[:, :1]
    cosine[...] = jnp.cos(angles)
    sine[...] = jnp.sin(angles)
    input_relays = gather_hand(wires, input_numbers, inputs_all, here)
    qkv.turn()
    run_bulk((down,), ('relay',))
    gather_take(wires, input_numbers, input_relays, inputs_all, here)
    kept["inputs"].wait()
    wires.landed(gain_at, gains_all.at[:, col_span(1 - c)])
    gain_one = gains_all[0:1, :]

    def norm_rows(i, carry):
        rows = pl.ds(pl.multiple_of(i * ROWS, ROWS), ROWS)
        values = inputs_all[rows, :].astype(F32)
        scale = lax.rsqrt(jnp.sum(values * values, axis=1, keepdims=True) / D + NORM_EPS)
        normed[rows, :] = (values * scale * gain_one).astype(BF)

        @pl.when(i == rows_of(x))
        def _():
            scale_one[...] = jnp.broadcast_to(scale, scale_one.shape)

        return carry

    lax.fori_loop(0, 4, norm_rows, 0)
    keep("normed", normed, normed_out)
    swapped(gate_swap, gate_all)
    swapped(up_swap, up_all)
    for name in ("gate", "up"):
        kept[name].wait()
    run_bulk((gate, up), ('start',))
    qkv.finish()
    keep("qkv_out", qkv_all, qkv_out)
    weight = qkv_all[...].reshape(D, columns.shape[0])

    def project(cols):
        def body(i, carry):
            rows = pl.ds(pl.multiple_of(i * ROWS, ROWS), ROWS)
            product = jnp.dot(normed[rows, :], weight[:, cols], preferred_element_type=F32)
            columns[cols, rows] = product.T
            return carry

        lax.fori_loop(0, 4, body, 0)

    project(slice(GROUP * HD, (GROUP + 2) * HD))
    first, second = rope(columns, GROUP * HD, cosine[...], sine[...])
    pair_columns = jnp.concatenate([first, second, columns[(GROUP + 1) * HD :]], axis=0)
    for s in (0, 1):
        keys[s, z, y] = pair_columns[:, s * HALF : (s + 1) * HALF].T.astype(BF)

    pairs_gather.start()
    project(slice(0, GROUP * HD))
    queries[:, HD:, :] = jnp.zeros((2, HD, GROUP * HALF), BF)
    for g in range(GROUP):
        turned = rope(columns, g * HD, cosine[...], sine[...])
        for i, value in enumerate(turned):
            rows = slice(i * (HD // 2), (i + 1) * (HD // 2))
            value = (value * HD ** (-0.5)).astype(BF)
            queries[0, rows, head_cols(g)] = value[:, :HALF]
            across_queries[rows, head_cols(g)] = value[:, HALF:]
    query_at = wires.send(across_queries, queries.at[1, pl.ds(0, HD)], opposite)
    pairs_gather.turn()
    run_bulk((gate, up), ('relay',))

    @pl.when(holds)
    def _():
        for k in range(4):
            spot = out_stage.at[k // 2, :, pl.ds((k % 2) * WIDTH, WIDTH)]
            pltpu.make_async_copy(spot, spot, stage_recv.at[k]).wait()

    out_gather.start()
    keep("cotangent", out_grad, cotangent_all.at[row_span(x), col_span(c)])
    cotangent_numbers = gather_sends(wires, out_grad, cotangent_all, here)
    pairs_gather.finish()
    keep("keys", keys, keys_out)
    out_gather.relay()
    run_bulk((gate,), ('turn',))

    wires.landed(query_at, queries.at[1, pl.ds(0, HD)])
    tour = Tour(z * 4 + y, (1, 0))
    tops[...] = jnp.full(tops.shape, NEVER, F32)
    sums[...] = jnp.zeros(sums.shape, F32)
    mixed[...] = jnp.zeros(mixed.shape, F32)
    heads = range(GROUP)

    def step(s, at, masked):
        pairs = keys[key_at(at)]
        old = [tops[s, :, head_cols(g)] for g in heads]
        old_sums = [sums[s, :, head_cols(g)] for g in heads]
        scores = [
            jnp.dot(pairs, queries[s, :, head_cols(g)], preferred_element_type=F32) for g in heads
        ]
        if masked:
            counts = in_second(tour.half(s), ends) | (at > 0)
            old = [jnp.where(counts, value, NEVER) for value in old]
            old_sums = [jnp.where(counts, value, 0.0) for value in old_sums]
            allowed = allowed_pairs(at, tour.half(s), ends)
            scores = [jnp.where(allowed, value, NEVER) for value in scores]
        top = [jnp.maximum(old[g], jnp.max(scores[g], axis=0, keepdims=True)) for g in heads]
        weights = [jnp.exp(scores[g] - top[g]) for g in heads]
        if masked:
            weights = [jnp.where(allowed, value, 0.0) for value in weights]
        shrink = [jnp.exp(old[g] - top[g]) for g in heads]
        if masked:
            shrink = [jnp.where(counts, value, 0.0) for value in shrink]
        new_sums = [
            old_sums[g] * shrink[g] + jnp.sum(weights[g], axis=0, keepdims=True) for g in heads
        ]
        new = [
            lax.dot_general(
                pairs, weights[g].astype(BF), (((0,), (0,)), ((), ())), preferred_element_type=F32
            )
            for g in heads
        ]
        for g in heads:
            cols = head_cols(g)
            tops[s, :, cols] = top[g]
            sums[s, :, cols] = new_sums[g]
            mixed[s, :, cols] = mixed[s, :, cols] * shrink[g] + new[g]

    def settle(s, rows):
        log_out[s] = tops[s] + jnp.log(sums[s])
        mixed_out[s] = mixed[s, HD:, :] / sums[s]
        for g in heads:
            rows[g * HD : (g + 1) * HD, :] = mixed_out[s, :, head_cols(g)].astype(BF)

    across_at = wires.send(attended_here, across, opposite, start=False)

    def between():
        settle(1, attended_here)
        wires.sent[across_at].start()

    tour.run(step, between, 0, 5)
    out_gather.turn()
    tour.run(step, between, 5, 9)
    gather_relay(wires, cotangent_numbers, cotangent_all, here)
    run_bulk((up,), ('turn',))
    tour.run(step, between, 9, 17)
    out_gather.relay_two()
    run_bulk((gate,), ('relay_two',))
    tour.run(step, between, 17, 21)
    tour.run(step, between, 21, 27)
    run_bulk((down,), ('turn',))
    tour.run(step, between, 27, 33)
    run_bulk((up,), ('relay_two',))
    settle(0, attended_out.at[:, pl.ds(0, HALF)])
    wires.landed(across_at, across)
    attended_out[:, HALF:] = across[...]
    for g in range(0, GROUP, 2):
        rows = slice(g * HD, (g + 2) * HD)
        attended[:, rows] = attended_out[rows, :].astype(F32).T.astype(BF)

    out_gather.finish()
    keep("out", out_all, out_out)
    out_low = out_all[...].reshape(GROUP * HD, D)
    fold_numbers = []
    for k, o in enumerate(FOLD_ORDER):
        rows = row_span(lax.rem(x + o, 4))
        part[rows, :] = jnp.dot(
            attended[rows, :], out_low, preferred_element_type=F32
        ).astype(BF)
        fold_numbers.append(
            wires.send(part.at[rows, col_span(1 - c)], folded.at[k], device(z, y, x, 1 - c))
        )
    moves = fold_moves(
        wires, fold_numbers, part, folded, leaving, arriving, here, total, col_span(c)
    )
    fold_finish(wires, moves, arriving, total)
    run_bulk((down,), ('relay_two',))
    middle = total[...] + block_input[...].astype(F32)
    middle_out[...] = middle
    square = both_cores(
        wires, mine_row, their_row, jnp.sum(middle * middle, axis=1, keepdims=True), here
    )
    scale = lax.rsqrt(square / D + NORM_EPS)
    scale_two[...] = jnp.broadcast_to(scale, scale_two.shape)
    own[...] = (
        middle_out[...] * scale * gains_all[1:2, col_span(c)]
    ).astype(BF)
    keep("own", own, out.at[row_span(x), col_span(c)])
    sends = gather_sends(wires, own, out, here)
    gather_relay(wires, sends, out, here)
    run_bulk(bulk, ('finish',))
    for member in bulk:
        member.leave()
    for name in ("normed", "qkv_out", "cotangent", "keys", "out", "own"):
        kept[name].wait()

    @pl.when(jnp.logical_not(holds))
    def _():
        stage_copy.wait_send()

    wires.close()


def call_forward(*operands):
    vm = pl.BlockSpec(memory_space=pltpu.VMEM)
    hbm = pl.BlockSpec(memory_space=ANY)
    cols = GROUP * HALF
    qkv_cols = (GROUP + 2) * HD
    share = (ROWS, WIDTH)
    whole = (2, 4, 4, 2, PIECE)
    outs = [
        ((HD // 2, LINE), F32, vm),
        ((HD // 2, LINE), F32, vm),
        ((ROWS, 128), F32, vm),
        ((LINE, D), BF, hbm),
        (whole + (qkv_cols,), BF, hbm),
        ((2, 2 * HD, cols), BF, vm),
        ((2, HD, cols), F32, vm),
        ((2, 1, cols), F32, vm),
        ((GROUP * HD, LINE), BF, vm),
        ((2, 4, 4, HALF, 2 * HD), BF, hbm),
        ((LINE, D), BF, hbm),
        ((4, 2, PIECE, D), BF, hbm),
        (whole + (HIDDEN,), BF, hbm),
        (whole + (HIDDEN,), BF, hbm),
        ((4, 4, 2 * PIECE, D), BF, hbm),
        (share, F32, vm),
        ((ROWS, 128), F32, vm),
        ((LINE, D), BF, hbm),
    ]
    return pl.pallas_call(
        forward_kernel,
        out_shape=tuple(jax.ShapeDtypeStruct(shape, kind) for shape, kind, _ in outs),
        in_specs=[pl.BlockSpec(memory_space=pltpu.SMEM)] + [vm] * 7 + [hbm],
        out_specs=tuple(spec for _, _, spec in outs),
        scratch_shapes=[
            pltpu.VMEM((4, PIECE, qkv_cols), BF),
            pltpu.VMEM((4, PIECE, HIDDEN), BF),
            pltpu.VMEM((4, PIECE, HIDDEN), BF),
            pltpu.VMEM((2, ROWS // 2, WIDTH), BF),
            pltpu.VMEM((PIECE, WIDTH), BF),
            pltpu.VMEM((8, WIDTH), F32),
            pltpu.VMEM((LINE, D), BF),
            pltpu.VMEM((8, D), F32),
            pltpu.VMEM(whole + (qkv_cols,), BF),
            pltpu.VMEM((LINE, D), BF),
            pltpu.VMEM((qkv_cols, LINE), F32),
            pltpu.VMEM((HD, cols), BF),
            pltpu.VMEM((GROUP * HD, HALF), BF),
            pltpu.VMEM((GROUP * HD, HALF), BF),
            pltpu.VMEM((2, 4, 4, HALF, 2 * HD), BF),
            pltpu.VMEM((2, 1, cols), F32),
            pltpu.VMEM((2, 1, cols), F32),
            pltpu.VMEM((2, 2 * HD, cols), F32),
            pltpu.VMEM((LINE, GROUP * HD), BF),
            pltpu.VMEM((2, PIECE, D), BF),
            pltpu.VMEM((4, 2, PIECE, D), BF),
            pltpu.VMEM((LINE, D), BF),
        ]
        + fold_scratch()
        + [
            pltpu.VMEM((ROWS, 128), F32),
            pltpu.VMEM((ROWS, 128), F32),
            pltpu.VMEM((ROWS, WIDTH), BF),
        ]
        + wire_scratch(144)
        + wire_scratch(4)
        + wire_scratch(4)
        + [pltpu.SemaphoreType.DMA((13,))],
        compiler_params=comm_params(1),
        name="forward",
    )(*operands)


def backward_kernel(
    lengths, cosine, sine, part, output_part, middle, scale_two, scale_one, gains, inputs, cotangent,
    queries, mixed, logs, attended, keys, out_low, qkv_low, normed, grad_down, grad_up, grad_gate,
    input_grad, output, qkv_grad, gate_up_grad, down_grad, out_grad, totals,
    q_out, kv_out, gate_out, up_out, down_out, out_out, across_grads, across_back, across,
    middle_all, grads, delta, query_rows, grad_rows, out_terms,
    terms, sums, rounded, columns, rows_back, q_terms, kv_terms, key_rec, key_sums, key_rec_two,
    *rest,
):
    rest = list(rest)

    def take(count):
        taken = rest[:count]
        del rest[:count]
        return taken

    first_fold, output_fold, (part_own, output_own) = take(4), take(4), take(2)
    last_fold = first_fold
    first_rows, last_rows, (own,) = take(2), take(2), take(1)
    down_buffers, up_buffers, gate_buffers = take(6), take(6), take(6)
    q_buffers, kv_buffers = take(6), take(6)
    out_buffers, (total_terms, stage, rec_one, rec_two) = take(3), take(4)
    send_sem, recv_sem, out_send, out_recv, local_sem = rest
    z, y, xl, xh, c = place()
    x = xh * 2 + xl
    here = (z, y, x, c)
    mine = xl * 2 + c
    quad = quad_of(xl, xh, x, c)
    line = [(o, b) for b in (0, 1) for o in range(4) if o or b]
    fixed = [device(z + a, y + b, x, c) for a, b in PLANE]
    fixed += [device(z, y, lax.rem(x + o, 4), lax.rem(c + b, 2)) for o, b in line]
    opposite = device(3 - z, 3 - y, x, c)
    greet(fixed)
    wires = Wires(send_sem, recv_sem)
    kept = []

    def keep(src, dst):
        copy = pltpu.make_async_copy(src, dst, local_sem.at[31 + len(kept)])
        copy.start()
        kept.append(copy)

    def deal(fin, result):
        keep(fin.at[c, xl], result.at[mine])
        return [
            wires.send(fin.at[b, lax.rem(a, 2)], result.at[mine], device(z, y, a, b))
            for a, b in quad
        ]

    def dealt(numbers, result):
        for at, (a, b) in zip(numbers, quad):
            wires.landed(at, result.at[lax.rem(a, 2) * 2 + b])

    numbers = fold_sends(wires, part, first_fold[0], here)
    own_parts = [
        pltpu.make_async_copy(part.at[:, col_span(c)], part_own, local_sem.at[42]),
        pltpu.make_async_copy(output_part.at[:, col_span(c)], output_own, local_sem.at[43]),
        pltpu.make_async_copy(out_low, out_terms, local_sem.at[44]),
        pltpu.make_async_copy(
            qkv_low.at[:, :, :, :, :, pl.ds(0, GROUP * HD)], q_terms, local_sem.at[45]
        ),
        pltpu.make_async_copy(
            qkv_low.at[:, :, :, :, :, pl.ds(GROUP * HD, 2 * HD)], kv_terms, local_sem.at[48]
        ),
    ]
    for copy in own_parts:
        copy.start()
    down = PlaneSum(wires, grad_down, down_buffers, here, local_sem, 0)
    up = PlaneSum(wires, grad_up, up_buffers, here, local_sem, 6)
    gate = PlaneSum(wires, grad_gate, gate_buffers, here, local_sem, 12)
    q_sum = PlaneSum(wires, q_terms, q_buffers, here, local_sem, 18)
    kv_sum = PlaneSum(wires, kv_terms, kv_buffers, here, local_sem, 24)
    out_sum = OutSum(
        wires, out_terms, out_buffers, out_out, here, mine, quad, (out_send, out_recv), local_sem, 30
    )
    bulk = (down, up, gate)
    in_turn(c, bulk, True)(*('start', 'direct'))
    own_parts[0].wait()
    moves = fold_moves(wires, numbers, part_own, *first_fold[:3], here, first_fold[3])
    in_turn(c, bulk, True)(*('relay',))
    fold_finish(wires, moves, first_fold[2], first_fold[3])
    back, gain_two = norm_back(
        wires, middle[...], scale_two[:, :1], gains[1:2, :], first_fold[3][...], *first_rows, here
    )
    grad = cotangent[...].astype(F32) + back
    input_grad[...] = grad
    own[...] = grad.astype(BF)
    keep(own, middle_all.at[row_span(x), col_span(c)])
    sends = gather_sends(wires, own, middle_all, here)
    for s in (0, 1):
        for g in range(GROUP):
            query_rows[s, g] = queries[s, :, head_cols(g)].astype(F32).T.astype(BF)
    grads[:, :HD, :] = jnp.zeros((2, HD, GROUP * HALF), BF)
    terms[...] = jnp.zeros(terms.shape, F32)
    sums[...] = jnp.zeros(sums.shape, F32)
    in_turn(c, bulk, True)(*('middle',))
    in_turn(c, bulk, False)(*('start', 'direct'))
    relayed = gather_relay(wires, sends, middle_all, here)
    kept[0].wait()

    own_parts[2].wait()
    shared = out_terms[...].reshape(GROUP * HD, D)

    def attended_rows(i, carry):
        rows = pl.ds(pl.multiple_of(i * ROWS, ROWS), ROWS)
        value = lax.dot_general(
            middle_all[rows, :], shared, (((1,), (1,)), ((), ())), preferred_element_type=F32
        )
        columns[: GROUP * HD, rows] = value.astype(BF).astype(F32).T
        return carry

    lax.fori_loop(0, 4, attended_rows, 0)
    for g in range(GROUP):
        rows = slice(g * HD, (g + 1) * HD)
        grads[0, HD:, head_cols(g)] = columns[rows, :HALF].astype(BF)
        across_grads[:, head_cols(g)] = columns[rows, HALF:].astype(BF)
    grad_at = wires.send(across_grads, grads.at[1, pl.ds(HD, HD)], opposite)

    def prepare(s):
        for g in range(GROUP):
            cols = head_cols(g)
            value = grads[s, :, cols].astype(F32)
            delta[s, :, cols] = jnp.sum(value[HD:] * mixed[s, :, cols], axis=0, keepdims=True)
            grad_rows[s, g] = value.T.astype(BF)

    prepare(0)

    def out_columns(i, carry):
        cols = pl.ds(pl.multiple_of(i * HALF, HALF), HALF)
        value = jnp.dot(attended[...], middle_all[:, cols], preferred_element_type=F32)
        out_terms[:, :, :, cols] = value.astype(BF).reshape(4, 2, PIECE, HALF)
        return carry

    lax.fori_loop(0, D // HALF, out_columns, 0)
    out_sum.start()
    in_turn(c, bulk, False)(*('relay',))
    output_numbers = fold_sends(wires, output_part, output_fold[0], here)

    ends = ends_of(lengths)
    tour = Tour(z * 4 + y, (0, 1))
    heads = range(GROUP)

    def step(s, at, masked):
        slot = key_at(at)
        pairs = keys[slot]
        query_columns = [queries[s, :, head_cols(g)] for g in heads]
        grad_columns = [grads[s, :, head_cols(g)] for g in heads]
        log_rows = [logs[s, :, head_cols(g)] for g in heads]
        deltas = [delta[s, :, head_cols(g)] for g in heads]
        rows = [query_rows[s, g] for g in heads]
        outer = [grad_rows[s, g] for g in heads]
        if not masked:
            fits = in_second(tour.half(s), ends)
            log_rows = [jnp.where(fits, value, -NEVER) for value in log_rows]
        scores = [jnp.dot(pairs, value, preferred_element_type=F32) for value in query_columns]
        prob_grads = [jnp.dot(pairs, value, preferred_element_type=F32) for value in grad_columns]
        probs = [jnp.exp(scores[g] - log_rows[g]) for g in heads]
        if masked:
            allowed = allowed_pairs(at, tour.half(s), ends)
            probs = [jnp.where(allowed, value, 0.0) for value in probs]
        score_grads = [(probs[g] * (prob_grads[g] - deltas[g])).astype(BF) for g in heads]
        probs_low = [value.astype(BF) for value in probs]
        back = [
            lax.dot_general(pairs, value, (((0,), (0,)), ((), ())), preferred_element_type=F32)
            for value in score_grads
        ]
        added = [
            jnp.dot(score_grads[g], rows[g], preferred_element_type=F32)
            + jnp.dot(probs_low[g], outer[g], preferred_element_type=F32)
            for g in heads
        ]
        terms[slot] += (added[0] + added[1]) + (added[2] + added[3])
        for g in heads:
            sums[s, :, head_cols(g)] += back[g]

    def between():
        wires.landed(grad_at, grads.at[1, pl.ds(HD, HD)])
        prepare(1)

    tour.run(step, between, 0, 4)
    tour.run(step, between, 4, 8)
    own_parts[1].wait()
    output_moves = fold_moves(
        wires, output_numbers, output_own, *output_fold[:3], here, output_fold[3]
    )
    out_sum.middle()
    tour.run(step, between, 8, 14)
    tour.run(step, between, 14, 20)
    fold_finish(wires, output_moves, output_fold[2], output_fold[3])
    output[...] = (middle[...] + output_fold[3][...]).astype(BF)
    normed_parts = [
        pltpu.make_async_copy(normed.at[:, pl.ds(n * WIDTH, WIDTH)], value, local_sem.at[46 + n])
        for n, value in enumerate((part_own, output_own))
    ]
    for copy in normed_parts:
        copy.start()
    out_sum.deal()
    in_turn(c, bulk, True)(*('finish',))
    in_turn(c, bulk, False)(*('middle',))
    tour.run(step, between, 20, 26)
    tour.run(step, between, 26, 33)

    for s in (0, 1):
        for i in range(4):
            rounded[s, i] = terms[s, i].astype(BF)
    first = [[], []]
    for k, by in enumerate(OFFSETS):
        first[0].append(
            wires.send(
                rounded.at[0, :, lax.rem(y + by, 4)], key_rec.at[0, k], second_device(here, 0, by)
            )
        )
        first[1].append(
            wires.send(
                rounded.at[1, lax.rem(z + by, 4)], key_rec.at[1, k], second_device(here, 1, by)
            )
        )
    across_back[...] = (sums[1, :HD, :] * HD ** (-0.5)).astype(BF)
    back_at = wires.send(across_back, across, opposite)
    in_turn(c, bulk, False)(*('finish',))
    down_fin = down_buffers[5]
    down_swap = wires.send(
        down_fin.at[:, :, col_span(1 - c)], down_out.at[c], device(z, y, x, 1 - c)
    )
    keep(down_fin.at[:, :, col_span(c)], down_out.at[c])
    up_swap = deal(up_buffers[5], up_out)
    gate_swap = deal(gate_buffers[5], gate_out)

    def turn_back(values, tokens, scale):
        for g in range(GROUP):
            turned = rope(values.at[:, head_cols(g)], 0, cosine[:, tokens], -sine[:, tokens])
            for i, value in enumerate(turned):
                at = g * HD + i * (HD // 2)
                columns[at : at + HD // 2, tokens] = value * scale

    turn_back(sums.at[0], slice(0, HALF), HD ** (-0.5))
    wires.landed(back_at, across)
    turn_back(across, slice(HALF, LINE), 1.0)

    def take_rows(cols):
        for r in range(4):
            rows = slice(r * ROWS, (r + 1) * ROWS)
            rows_back[rows, cols] = columns[cols, rows].T.astype(BF)

    def weight_terms(cols, result):
        back_part = rows_back[:, cols]
        for n, half in enumerate((part_own, output_own)):

            def body(i, carry):
                at = pl.ds(pl.multiple_of(i * 256, 256), 256)
                value = lax.dot_general(
                    half[:, at], back_part, (((0,), (0,)), ((), ())), preferred_element_type=F32
                )
                result[n, i] = value.astype(BF).reshape(result.shape[2:])
                return carry

            lax.fori_loop(0, 4, body, 0)

    q_cols, kv_cols = slice(0, GROUP * HD), slice(GROUP * HD, (GROUP + 2) * HD)
    take_rows(q_cols)
    own_parts[3].wait()
    wires.settle(relayed)
    weight = q_terms[...].reshape(D, GROUP * HD)
    for r in range(4):
        rows = slice(r * ROWS, (r + 1) * ROWS)
        middle_all[rows, :] = lax.dot_general(
            rows_back[rows, q_cols], weight, (((1,), (1,)), ((), ())), preferred_element_type=F32
        ).astype(BF)
    for copy in normed_parts:
        copy.wait()
    weight_terms(q_cols, q_terms)
    run_bulk((q_sum,), ('start', 'direct'))
    second = [[], []]
    for s in (0, 1):
        for k in range(3):
            wires.landed(first[s][k], key_rec.at[s, k])
        for i in range(4):
            value = terms[0, i, y] if s == 0 else terms[1, z, i]
            for k in range(3):
                value = value + key_rec[s, k, i].astype(F32)
            key_sums[s, i] = value.astype(BF)
        for k, by in enumerate(OFFSETS):
            second[s].append(
                wires.send(
                    key_sums.at[s, first_at(here, s, by)],
                    key_rec_two.at[s, k],
                    first_device(here, s, by),
                )
            )
    run_bulk((q_sum,), ('relay',))
    for s in (0, 1):
        tokens = slice(s * HALF, (s + 1) * HALF)
        value = key_sums[s, first_at(here, s)].astype(F32)
        for k in range(3):
            wires.landed(second[s][k], key_rec_two.at[s, k])
            value = value + key_rec_two[s, k].astype(F32)
        pair_columns = value.T
        turned = rope(pair_columns, 0, cosine[:, tokens], -sine[:, tokens])
        for i, value in enumerate(turned):
            at = GROUP * HD + i * (HD // 2)
            columns[at : at + HD // 2, tokens] = value
        columns[(GROUP + 1) * HD :, tokens] = pair_columns[HD:]

    take_rows(kv_cols)
    own_parts[4].wait()
    weight = kv_terms[...].reshape(D, 2 * HD)
    last_numbers = []
    for k, o in enumerate(FOLD_ORDER):
        rows = row_span(lax.rem(x + o, 4))
        value = lax.dot_general(
            rows_back[rows, kv_cols], weight, (((1,), (1,)), ((), ())), preferred_element_type=F32
        )
        middle_all[rows, :] = (middle_all[rows, :].astype(F32) + value).astype(BF)
        last_numbers.append(
            wires.send(
                middle_all.at[rows, col_span(1 - c)], last_fold[0].at[k], device(z, y, x, 1 - c)
            )
        )
    weight_terms(kv_cols, kv_terms)
    run_bulk((kv_sum,), ('start', 'direct'))
    wires.settle(moves)
    last_moves = fold_moves(
        wires, last_numbers, middle_all, *last_fold[:3], here, last_fold[3], col_span(c)
    )

    run_bulk((kv_sum,), ('relay',))
    run_bulk((q_sum,), ('middle',))
    out_sum.finish()
    wires.landed(down_swap, down_out.at[1 - c])
    dealt(up_swap, up_out)
    dealt(gate_swap, gate_out)
    for copy in kept[1:]:
        copy.wait()
    left = lax.broadcasted_iota(jnp.int32, (PIECE, 2 * HD), 1) < HD
    squares = jnp.zeros((PIECE, 2 * HD), F32)
    for u, result in enumerate((gate_out, up_out)):
        for side in (0, 1):
            for j in range(HIDDEN // (2 * HD)):
                cols = slice(j * 2 * HD, (j + 1) * 2 * HD)
                one = result[side * 2, :, cols].astype(F32)
                two = result[side * 2 + 1, :, cols].astype(F32)
                squares = squares + one * one + two * two
                even = jnp.where(left, one, pltpu.roll(two, HD, 1))
                odd = jnp.where(left, pltpu.roll(one, HD, 1), two)
                for i, value in enumerate((even, odd)):
                    at = ((2 * j + i) * 2 + side) * 2 * HD
                    gate_up_grad[:, u, at : at + 2 * HD] = value
    square = jnp.sum(squares)
    for k in range(2):
        for o in range(2):
            value = down_out[k, o].astype(F32)
            down_grad[(2 * k + o) * PIECE : (2 * k + o + 1) * PIECE, :] = value
            square = square + jnp.sum(value * value)
    value = out_out[...].astype(F32)
    out_grad[...] = value
    square = square + jnp.sum(value * value)
    run_bulk((kv_sum,), ('middle',))
    run_bulk((q_sum,), ('finish',))
    q_swap = deal(q_buffers[5], q_out)
    fold_finish(wires, last_moves, last_fold[2], last_fold[3])
    back, gain_one = norm_back(
        wires,
        inputs[...].astype(F32),
        scale_one[:, :1],
        gains[0:1, :],
        last_fold[3][...],
        *last_rows,
        here,
    )
    input_grad[...] = input_grad[...] + back
    run_bulk((kv_sum,), ('finish',))
    kv_swap = deal(kv_buffers[5], kv_out)
    dealt(q_swap, q_out)
    dealt(kv_swap, kv_out)
    for copy in kept[-2:]:
        copy.wait()
    for k in range(4):
        for result, at in ((q_out, 0), (kv_out, GROUP * HD)):
            value = result[k].astype(F32)
            qkv_grad[:, k, at : at + value.shape[1]] = value
            square = square + jnp.sum(value * value)

    for k in range(8):
        cols = slice(k * 128, (k + 1) * 128)
        total_terms[k : k + 1] = gain_one[:, cols]
        total_terms[8 + k : 9 + k] = gain_two[:, cols]
    total_terms[16:] = jnp.broadcast_to(square, (8, 128))
    first = [
        wires.send(total_terms, rec_one.at[k], device(z + a, y + b, x, c))
        for k, (a, b) in enumerate(PLANE)
    ]
    value = total_terms[...]
    for k, at in enumerate(first):
        wires.landed(at, rec_one.at[k])
        value = value + rec_one[k]
    stage[...] = value
    second = [
        wires.send(stage, rec_two.at[k], device(z, y, lax.rem(x + o, 4), lax.rem(c + b, 2)))
        for k, (o, b) in enumerate(line)
    ]
    both = [value, None]
    for k, (o, b) in enumerate(line):
        wires.landed(second[k], rec_two.at[k])
        both[b] = rec_two[k] if both[b] is None else both[b] + rec_two[k]
    totals[:16] = both[0][:16]
    totals[16:] = (
        both[0][16:]
        + both[1][16:]
        + jnp.sum(both[0][:16] * both[0][:16])
        + jnp.sum(both[1][:16] * both[1][:16])
    )
    for member in bulk + (q_sum, kv_sum):
        member.leave()
    wires.close()


def call_backward(*operands):
    vm = pl.BlockSpec(memory_space=pltpu.VMEM)
    hbm = pl.BlockSpec(memory_space=ANY)
    cols = GROUP * HALF
    qkv_cols = (GROUP + 2) * HD
    share = (ROWS, WIDTH)
    outs = [
        (share, F32, vm),
        (share, BF, vm),
        ((PIECE, 4, qkv_cols), F32, vm),
        ((PIECE, 2, 4 * HIDDEN), F32, vm),
        (share, F32, vm),
        ((PIECE, WIDTH), F32, vm),
        ((24, 128), F32, vm),
    ]
    return pl.pallas_call(
        backward_kernel,
        out_shape=tuple(jax.ShapeDtypeStruct(shape, kind) for shape, kind, _ in outs),
        in_specs=[pl.BlockSpec(memory_space=pltpu.SMEM)] + [vm] * 2 + [hbm] * 2 + [vm] * 11 + [hbm] * 6,
        out_specs=tuple(spec for _, _, spec in outs),
        scratch_shapes=[
            pltpu.VMEM((4, PIECE, GROUP * HD), BF),
            pltpu.VMEM((4, PIECE, 2 * HD), BF),
            pltpu.VMEM((4, PIECE, HIDDEN), BF),
            pltpu.VMEM((4, PIECE, HIDDEN), BF),
            pltpu.VMEM((2, 2, PIECE, WIDTH), BF),
            pltpu.VMEM((PIECE, WIDTH), BF),
            pltpu.VMEM((HD, cols), BF),
            pltpu.VMEM((HD, cols), BF),
            pltpu.VMEM((HD, cols), BF),
            pltpu.VMEM((LINE, D), BF),
            pltpu.VMEM((2, 2 * HD, cols), BF),
            pltpu.VMEM((2, 1, cols), F32),
            pltpu.VMEM((2, GROUP, HALF, 2 * HD), BF),
            pltpu.VMEM((2, GROUP, HALF, 2 * HD), BF),
            pltpu.VMEM((4, 2, PIECE, D), BF),
            pltpu.VMEM((2, 4, 4, HALF, 2 * HD), F32),
            pltpu.VMEM((2, 2 * HD, cols), F32),
            pltpu.VMEM((2, 4, 4, HALF, 2 * HD), BF),
            pltpu.VMEM((qkv_cols, LINE), F32),
            pltpu.VMEM((LINE, qkv_cols), BF),
            pltpu.VMEM((2, 4, 4, 2, PIECE, GROUP * HD), BF),
            pltpu.VMEM((2, 4, 4, 2, PIECE, 2 * HD), BF),
            pltpu.VMEM((2, 3, 4, HALF, 2 * HD), BF),
            pltpu.VMEM((2, 4, HALF, 2 * HD), BF),
            pltpu.VMEM((2, 3, HALF, 2 * HD), BF),
        ]
        + fold_scratch() * 2
        + [pltpu.VMEM((LINE, WIDTH), BF)] * 2
        + [pltpu.VMEM((ROWS, 128), F32)] * 4
        + [pltpu.VMEM(share, BF)]
        + sum_buffers((PIECE, D), BF)
        + sum_buffers((2, PIECE, HIDDEN), BF) * 2
        + sum_buffers((2, PIECE, GROUP * HD), BF)
        + sum_buffers((2, PIECE, 2 * HD), BF)
        + [
            pltpu.VMEM((3, 2, PIECE, D), BF),
            pltpu.VMEM((2, PIECE, D), BF),
            pltpu.VMEM((3, 2, PIECE, D), BF),
            pltpu.VMEM((24, 128), F32),
            pltpu.VMEM((24, 128), F32),
            pltpu.VMEM((15, 24, 128), F32),
            pltpu.VMEM((7, 24, 128), F32),
        ]
        + wire_scratch(200)
        + wire_scratch(6)
        + [pltpu.SemaphoreType.DMA((49,))],
        compiler_params=comm_params(2),
        name="backward",
    )(*operands)


CHUNK = 256


def feed_kernel(
    normed_two, cotangent, gate_low, up_low, down_low,
    output_part, back_part, grad_gate, grad_up, grad_down, output_sum, back_sum,
):
    at = pl.program_id(0)

    @pl.when(at == 0)
    def _():
        output_sum[...] = jnp.zeros(output_sum.shape, F32)
        back_sum[...] = jnp.zeros(back_sum.shape, F32)

    inputs, incoming = normed_two[...], cotangent[...]
    gate = jnp.dot(inputs, gate_low[...], preferred_element_type=F32)
    up = jnp.dot(inputs, up_low[...], preferred_element_type=F32)
    hidden_grad = lax.dot_general(
        incoming, down_low[...], (((1,), (1,)), ((), ())), preferred_element_type=F32
    )
    sigmoid = jax.nn.sigmoid(gate)
    silu = gate * sigmoid
    hidden = (silu * up).astype(BF)
    gate_back = (hidden_grad * up * sigmoid * (1.0 + gate * (1.0 - sigmoid))).astype(BF)
    up_back = (hidden_grad * silu).astype(BF)
    both_back = jnp.concatenate([gate_back, up_back], axis=1)
    for k in range(4):
        cols = slice(k * D // 4, (k + 1) * D // 4)
        output_sum[:, cols] += jnp.dot(hidden, down_low[:, cols], preferred_element_type=F32)
        back_sum[:, cols] += lax.dot_general(
            gate_back, gate_low[cols, :], (((1,), (1,)), ((), ())), preferred_element_type=F32
        ) + lax.dot_general(
            up_back, up_low[cols, :], (((1,), (1,)), ((), ())), preferred_element_type=F32
        )
        grad_down[:, cols] = outer_rows(hidden, incoming[:, cols], BF)
        both = outer_rows(inputs[:, cols], both_back, BF)
        grad_gate[cols, :] = both[:, :CHUNK]
        grad_up[cols, :] = both[:, CHUNK:]

    @pl.when(at == HIDDEN // CHUNK - 1)
    def _():
        output_part[...] = output_sum[...].astype(BF)
        back_part[...] = back_sum[...].astype(BF)


def call_feed(normed_two, cotangent, gate_low, up_low, down_low):
    rows = pl.BlockSpec((LINE, D), lambda j: (0, 0))
    tall = pl.BlockSpec((D, CHUNK), lambda j: (0, j))
    wide = pl.BlockSpec((CHUNK, D), lambda j: (j, 0))
    return pl.pallas_call(
        feed_kernel,
        out_shape=(
            jax.ShapeDtypeStruct((LINE, D), BF),
            jax.ShapeDtypeStruct((LINE, D), BF),
            jax.ShapeDtypeStruct((D, HIDDEN), BF),
            jax.ShapeDtypeStruct((D, HIDDEN), BF),
            jax.ShapeDtypeStruct((HIDDEN, D), BF),
        ),
        grid=(HIDDEN // CHUNK,),
        in_specs=[rows, rows, tall, tall, wide],
        out_specs=(rows, rows, tall, tall, wide),
        scratch_shapes=[pltpu.VMEM((LINE, D), F32), pltpu.VMEM((LINE, D), F32)],
        compiler_params=pltpu.CompilerParams(vmem_limit_bytes=VMEM_LIMIT),
        name="feed_forward",
    )(normed_two, cotangent, gate_low, up_low, down_low)


def rope_inverse():
    half_size = HD // 2
    column = np.arange(half_size, dtype=np.float32)
    inverse = np.exp(-(np.float32(2.0) * column / HD) * np.float32(math.log(ROPE_THETA)))
    wavelength = np.float32(2.0 * math.pi) / inverse
    smooth = (np.float32(OLD_CONTEXT) / wavelength - LOW_FREQ) / (HIGH_FREQ - LOW_FREQ)
    blended = (1.0 - smooth) * inverse / ROPE_FACTOR + smooth * inverse
    inverse = np.where(
        wavelength < OLD_CONTEXT / HIGH_FREQ,
        inverse,
        np.where(wavelength > OLD_CONTEXT / LOW_FREQ, inverse / ROPE_FACTOR, blended),
    )
    return np.broadcast_to(inverse.astype(np.float32)[:, None], (half_size, 128))


def outer_rows(left, right, kind):
    return lax.dot_general(
        left, right, (((0,), (0,)), ((), ())), preferred_element_type=F32
    ).astype(kind)


def adam(weight, moment, second, gradient, rate, decay):
    moment_next = BETA_ONE * moment + (1.0 - BETA_ONE) * gradient
    second_next = BETA_TWO * second + (1.0 - BETA_TWO) * gradient * gradient
    unbiased = moment_next / (1.0 - BETA_ONE**ADAM_STEP)
    divisor = jnp.sqrt(second_next / (1.0 - BETA_TWO**ADAM_STEP)) + ADAM_EPS
    return (weight - rate * (unbiased / divisor + decay * weight), moment_next, second_next)


def shards(
    block_input,
    out_grad,
    qkv_weight,
    qkv_moment,
    qkv_second,
    gate_up_weight,
    gate_up_moment,
    gate_up_second,
    out_weight,
    out_moment,
    out_second,
    down_weight,
    down_moment,
    down_second,
    norm_gains,
    gains_moment,
    gains_second,
    doc_lengths,
):
    (
        cosine,
        sine,
        scale_one,
        normed,
        qkv_whole,
        query_columns,
        mixed,
        logs,
        attended,
        keys,
        cotangent_all,
        out_whole,
        gate_whole,
        up_whole,
        down_whole,
        middle,
        scale_two,
        normed_two,
    ) = call_forward(
        doc_lengths,
        jnp.asarray(rope_inverse()),
        block_input,
        qkv_weight,
        gate_up_weight,
        down_weight,
        out_weight,
        norm_gains,
        out_grad,
    )
    output_part, back_part, grad_gate, grad_up, grad_down = call_feed(
        normed_two,
        cotangent_all,
        gate_whole.reshape(D, HIDDEN),
        up_whole.reshape(D, HIDDEN),
        down_whole.reshape(HIDDEN, D),
    )
    input_grad, output, grad_qkv, grad_gate_up, grad_down, grad_out, totals = call_backward(
        doc_lengths,
        cosine,
        sine,
        back_part,
        output_part,
        middle,
        scale_two,
        scale_one,
        norm_gains,
        block_input,
        out_grad,
        query_columns,
        mixed,
        logs,
        attended,
        keys,
        out_whole,
        qkv_whole,
        normed,
        grad_down.reshape(down_whole.shape),
        grad_up.reshape(up_whole.shape),
        grad_gate.reshape(gate_whole.shape),
    )
    shares = (grad_qkv, grad_gate_up, grad_out, grad_down)
    gains_grad = totals[:16].reshape(2, WIDTH)
    grad_norm = jnp.sqrt(totals[16, 0])
    factor = CLIP_NORM / jnp.maximum(grad_norm, CLIP_NORM)
    weights = (qkv_weight, gate_up_weight, out_weight, down_weight)
    moments = (qkv_moment, gate_up_moment, out_moment, down_moment)
    seconds = (qkv_second, gate_up_second, out_second, down_second)
    out_rate = OUTPUT_RATE * (TOKENS / (HQ * HD)) ** 0.5
    down_rate = DOWN_RATE * FF ** (-0.5)
    rates = (MATRIX_RATE, MATRIX_RATE, out_rate, down_rate)
    results = []
    for weight, moment, second, gradient, rate in zip(weights, moments, seconds, shares, rates):
        results.extend(adam(weight, moment, second, gradient * factor, rate, WEIGHT_DECAY))
    gains_new = adam(norm_gains, gains_moment, gains_second, gains_grad * factor, GAIN_RATE, 0.0)
    return (output, input_grad, grad_norm, *results, *gains_new)


def solution(mesh):
    placed = (
        P(("seq", "wide"), "narrow"),
        P(("seq", "wide"), "narrow"),
        P(("narrow", "seq"), "wide", None),
        P(("narrow", "seq"), "wide", None),
        P(("narrow", "seq"), "wide", None),
        P(("narrow", "seq"), None, "wide"),
        P(("narrow", "seq"), None, "wide"),
        P(("narrow", "seq"), None, "wide"),
        P(("wide", "seq"), "narrow"),
        P(("wide", "seq"), "narrow"),
        P(("wide", "seq"), "narrow"),
        P(("wide", "seq"), "narrow"),
        P(("wide", "seq"), "narrow"),
        P(("wide", "seq"), "narrow"),
        P(None, "narrow"),
        P(None, "narrow"),
        P(None, "narrow"),
        P(),
    )
    return jax.shard_map(
        shards,
        mesh=mesh,
        in_specs=placed,
        out_specs=(
            P(("seq", "wide"), "narrow"),
            P(("seq", "wide"), "narrow"),
            P(),
            P(("narrow", "seq"), "wide", None),
            P(("narrow", "seq"), "wide", None),
            P(("narrow", "seq"), "wide", None),
            P(("narrow", "seq"), None, "wide"),
            P(("narrow", "seq"), None, "wide"),
            P(("narrow", "seq"), None, "wide"),
            P(("wide", "seq"), "narrow"),
            P(("wide", "seq"), "narrow"),
            P(("wide", "seq"), "narrow"),
            P(("wide", "seq"), "narrow"),
            P(("wide", "seq"), "narrow"),
            P(("wide", "seq"), "narrow"),
            P(None, "narrow"),
            P(None, "narrow"),
            P(None, "narrow"),
        ),
        check_vma=False,
    )
```

time: 387 us -> 364 us (0.941); the launches traced: 379 us -> 361 us
  Pallas kernels: 304 us -> 341 us
  matrix products: 34.1 us -> 0 us
  local copies, waits for them, and re-layouts: 19.5 us -> 4.24 us
  other arithmetic: 18.6 us -> 12.8 us
    dot_general x9 -> x0, matrix products: 34.1 us -> none  [the longest x3 13.2 us: outer_rows(): lax.dot_general(left, right, (((0,), (0,)), ((), ())), preferred_element_...]
    pallas_call x0 -> x1, Pallas kernels: none -> 31.9 us  [call_feed(): pl.pallas_call(feed_kernel, out_shape=(jax.ShapeDtypeStruct((LINE, D), BF...]
    pallas_call x1, Pallas kernels: 161 us -> 174 us  [call_backward(): pl.pallas_call(backward_kernel, out_shape=tuple((jax.ShapeDtypeStruct(sha...]
    pallas_call x1, Pallas kernels: 143 us -> 135 us  [call_forward(): pl.pallas_call(forward_kernel, out_shape=tuple((jax.ShapeDtypeStruct(shap...]
    unnamed x52 -> x38, local copies, waits for them, and re-layouts: 5.6 us -> 1.59 us
where the time goes in v5:
time: 364 us; the launch traced here: 361 us
  Pallas kernels  341 us (94%)
  other arithmetic  12.8 us (4%)
  local copies, waits for them, and re-layouts  4.24 us (1%)
    pallas_call x1, Pallas kernels, call_backward(): pl.pallas_call(backward_kernel, out_shape=tuple((jax.ShapeDtypeStruct(sha...  174 us
    pallas_call x1, Pallas kernels, call_forward(): pl.pallas_call(forward_kernel, out_shape=tuple((jax.ShapeDtypeStruct(shap...  135 us
    pallas_call x1, Pallas kernels, call_feed(): pl.pallas_call(feed_kernel, out_shape=(jax.ShapeDtypeStruct((LINE, D), BF...  31.9 us
    sub x5, other arithmetic, adam(): weight - rate * (unbiased / divisor + decay * weight)  12.1 us

profile of v5, /device:TPU:1, one launch (start us, length us, event | category | flops | bytes accessed | tf_op | source)
XLA Modules:
  0.0 360.6 jit_solution(10011252856799464373)
XLA Ops:
  0.7 1.3 jit_solution_.3.inverse
  2.0 135.0 %forward.1 = (f32[32,512]{1,0:T(8,128)}, f32[32,512]{1,0:T(8,128)}, f32[128,128]{1,0:T(8,128)}, bf16[512,2048]{1,0:T(8,128)(2,1)}, bf16[2,4,4,2,32,384]{5,4,3,2,...) custom-call(s32[4]{0:T(128)} %lengths.3, ...), custom_call_target="tpu_custom_call" | custom-call | tf_op jit(solution)/shard_map/forward/pallas_call | solution.py:1156
  137.0 31.9 %feed_forward.1 = (bf16[512,2048]{1,0:T(8,128)(2,1)}, bf16[512,2048]{1,0:T(8,128)(2,1)}, bf16[2048,1024]{1,0:T(8,128)(2,1)}, bf16[2048,1024]{1,0:T(8,128)(2,1)}, bf16[1024,2048]{1,0:T(8,128)(2,1)}) custom-call(bf16[512,2048]{1,0:T(8,128)(2,1)} %get-tuple-element.50.normed_two, bf16[512,2048]{1,0:T(8,128)(2,1)} %get-tuple-element.51.cotangent, ...), custom_call_target="tpu_custom_call" | custom-call | tf_op jit(solution)/shard_map/feed_forward/pallas_call | solution.py:1736
  168.9 0.0 copy-start.15
  168.9 0.0 copy-start.16
  168.9 0.0 copy-start.17
  169.0 0.0 copy-start.9
  169.0 0.0 copy-start.13
  169.0 0.0 copy-start.14
  169.0 0.0 copy-start.5
  169.0 0.0 copy-start.11
  169.0 0.0 copy-start.12
  169.0 173.7 %backward.1 = (f32[128,1024]{1,0:T(8,128)}, bf16[128,1024]{1,0:T(8,128)(2,1)}, f32[32,4,384]{2,1,0:T(4,128)}, f32[32,2,4096]{2,1,0:T(2,128)}, f32[128,1024]{1,0:...) custom-call(s32[4]{0:T(128)} %lengths.3, f32[32,512]{1,0:T(8,128)} %get-tuple-element.48.cosine, ...), custom_call_target="tpu_custom_call" | custom-call | tf_op jit(solution)/shard_map/backward/pallas_call | solution.py:1630
  342.7 0.0 copy-start.1
  342.7 0.0 copy-start.7
  342.7 0.0 copy-start.8
  342.8 1.3 slice.6
  344.8 0.7 slice_multiply_fusion
  345.5 0.0 copy-done.15
  345.5 0.0 copy-done.16
  345.5 0.0 copy-done.17
  345.5 0.6 multiply_subtract_fusion.4
  346.2 0.0 copy-done.9
  346.2 0.0 copy-done.13
  346.2 0.0 copy-done.14
  346.2 1.7 multiply_subtract_fusion.3
  347.9 0.0 copy-done.5
  347.9 0.0 copy-done.11
  347.9 0.0 copy-done.12
  347.9 0.0 copy-start.4
  347.9 2.1 multiply_subtract_fusion.2
  350.0 0.0 copy-start
  350.0 0.0 copy-start.2
  350.0 0.0 copy-start.3
  350.0 0.0 copy-done.1
  350.0 0.0 copy-done.7
  350.0 0.0 copy-done.8
  350.1 2.6 multiply_subtract_fusion.1
  352.7 0.0 copy-done.4
  352.7 0.0 copy-done
  352.7 0.0 copy-done.2
  352.7 0.0 copy-done.3
  352.7 0.0 copy-start.10
  352.7 0.0 copy-start.6
  352.7 5.0 %multiply_subtract_fusion = (f32[32,2,4096]{2,1,0:T(2,128)}, f32[32,2,4096]{2,1,0:T(2,128)}, f32[32,2,4096]{2,1,0:T(2,128)}) fusion(f32[32,2,4096]{2,1,0:T(2,128)S(1)} %copy-done, f32[32,2,4096]{2,1,0:T(2,128)S(1)} %copy-done.4, f32[]{:T(128)S(6)} %div.78, f32[32,2,4096]{2,1,0:T(2,128)S(1)} %copy-done.2, f32[32,2,4096]{2,1,0:T(2,128)S(1)} %copy-done.3), kind=kLoop, calls=%fused_computation.2 | loop fusion | flops 4194304 | bytes 7340036 | tf_op jit(solution)/shard_map/sub | solution.py:1780
  357.7 0.0 copy-done.10
  357.7 0.7 copy.39
  358.4 0.0 copy-done.6
  358.4 0.8 copy.40
  (1 shorter events, 0.0 us)
Async XLA Ops:
  168.9 176.6 %copy-start.15 = (f32[2,1024]{1,0:T(2,128)S(1)}, f32[2,1024]{1,0:T(2,128)}, u32[]{:S(2)}) copy-start(f32[2,1024]{1,0:T(2,128)} %gains.3) | copy-start | bytes 24580
  168.9 176.6 %copy-start.16 = (f32[2,1024]{1,0:T(2,128)S(1)}, f32[2,1024]{1,0:T(2,128)}, u32[]{:S(2)}) copy-start(f32[2,1024]{1,0:T(2,128)} %param.34) | copy-start | bytes 24580
  168.9 176.6 %copy-start.17 = (f32[2,1024]{1,0:T(2,128)S(1)}, f32[2,1024]{1,0:T(2,128)}, u32[]{:S(2)}) copy-start(f32[2,1024]{1,0:T(2,128)} %param.35) | copy-start | bytes 24580
  169.0 177.2 %copy-start.9 = (f32[32,1024]{1,0:T(8,128)S(1)}, f32[32,1024]{1,0:T(8,128)}, u32[]{:S(2)}) copy-start(f32[32,1024]{1,0:T(8,128)} %out_weight.1) | copy-start | bytes 393220
  169.0 177.2 %copy-start.13 = (f32[32,1024]{1,0:T(8,128)S(1)}, f32[32,1024]{1,0:T(8,128)}, u32[]{:S(2)}) copy-start(f32[32,1024]{1,0:T(8,128)} %param.28) | copy-start | bytes 393220
  169.0 177.2 %copy-start.14 = (f32[32,1024]{1,0:T(8,128)S(1)}, f32[32,1024]{1,0:T(8,128)}, u32[]{:S(2)}) copy-start(f32[32,1024]{1,0:T(8,128)} %param.29) | copy-start | bytes 393220
  169.0 178.9 %copy-start.5 = (f32[32,4,384]{2,1,0:T(4,128)S(1)}, f32[32,4,384]{2,1,0:T(4,128)}, u32[]{:S(2)}) copy-start(f32[32,4,384]{2,1,0:T(4,128)} %qkv_weight.1) | copy-start | bytes 589828
  169.0 178.9 %copy-start.11 = (f32[32,4,384]{2,1,0:T(4,128)S(1)}, f32[32,4,384]{2,1,0:T(4,128)}, u32[]{:S(2)}) copy-start(f32[32,4,384]{2,1,0:T(4,128)} %param.22) | copy-start | bytes 589828
  169.0 178.9 %copy-start.12 = (f32[32,4,384]{2,1,0:T(4,128)S(1)}, f32[32,4,384]{2,1,0:T(4,128)}, u32[]{:S(2)}) copy-start(f32[32,4,384]{2,1,0:T(4,128)} %param.23) | copy-start | bytes 589828
  342.7 7.3 %copy-start.1 = (f32[128,1024]{1,0:T(8,128)S(1)}, f32[128,1024]{1,0:T(8,128)}, u32[]{:S(2)}) copy-start(f32[128,1024]{1,0:T(8,128)} %down_weight.1) | copy-start | bytes 1572868
  342.7 7.3 %copy-start.7 = (f32[128,1024]{1,0:T(8,128)S(1)}, f32[128,1024]{1,0:T(8,128)}, u32[]{:S(2)}) copy-start(f32[128,1024]{1,0:T(8,128)} %param.31) | copy-start | bytes 1572868
  342.7 7.3 %copy-start.8 = (f32[128,1024]{1,0:T(8,128)S(1)}, f32[128,1024]{1,0:T(8,128)}, u32[]{:S(2)}) copy-start(f32[128,1024]{1,0:T(8,128)} %param.32) | copy-start | bytes 1572868
  347.9 4.8 %copy-start.4 = (f32[32,2,4096]{2,1,0:T(2,128)S(1)}, f32[32,2,4096]{2,1,0:T(2,128)}, u32[]{:S(2)}) copy-start(f32[32,2,4096]{2,1,0:T(2,128)} %get-tuple-element.75) | copy-start | bytes 3145732
  350.0 2.6 copy-start
  350.0 2.6 copy-start.2
  350.0 2.6 copy-start.3
  352.7 5.0 %copy-start.10 = (bf16[128,1024]{1,0:T(8,128)(2,1)S(1)}, bf16[128,1024]{1,0:T(8,128)(2,1)}, u32[]{:S(2)}) copy-start(bf16[128,1024]{1,0:T(8,128)(2,1)} %get-tuple-element.111) | copy-start | bytes 786436
  352.7 5.7 %copy-start.6 = (f32[128,1024]{1,0:T(8,128)S(1)}, f32[128,1024]{1,0:T(8,128)}, u32[]{:S(2)}) copy-start(f32[128,1024]{1,0:T(8,128)} %get-tuple-element.112) | copy-start | bytes 1572868

commit v6 on v5

--- a/solution.py
+++ b/solution.py
@@ -1424,50 +1424,6 @@
     up_swap = deal(up_buffers[5], up_out)
     gate_swap = deal(gate_buffers[5], gate_out)
 
-    def turn_back(values, tokens, scale):
-        for g in range(GROUP):
-            turned = rope(values.at[:, head_cols(g)], 0, cosine[:, tokens], -sine[:, tokens])
-            for i, value in enumerate(turned):
-                at = g * HD + i * (HD // 2)
-                columns[at : at + HD // 2, tokens] = value * scale
-
-    turn_back(sums.at[0], slice(0, HALF), HD ** (-0.5))
-    wires.landed(back_at, across)
-    turn_back(across, slice(HALF, LINE), 1.0)
-
-    def take_rows(cols):
-        for r in range(4):
-            rows = slice(r * ROWS, (r + 1) * ROWS)
-            rows_back[rows, cols] = columns[cols, rows].T.astype(BF)
-
-    def weight_terms(cols, result):
-        back_part = rows_back[:, cols]
-        for n, half in enumerate((part_own, output_own)):
-
-            def body(i, carry):
-                at = pl.ds(pl.multiple_of(i * 256, 256), 256)
-                value = lax.dot_general(
-                    half[:, at], back_part, (((0,), (0,)), ((), ())), preferred_element_type=F32
-                )
-                result[n, i] = value.astype(BF).reshape(result.shape[2:])
-                return carry
-
-            lax.fori_loop(0, 4, body, 0)
-
-    q_cols, kv_cols = slice(0, GROUP * HD), slice(GROUP * HD, (GROUP + 2) * HD)
-    take_rows(q_cols)
-    own_parts[3].wait()
-    wires.settle(relayed)
-    weight = q_terms[...].reshape(D, GROUP * HD)
-    for r in range(4):
-        rows = slice(r * ROWS, (r + 1) * ROWS)
-        middle_all[rows, :] = lax.dot_general(
-            rows_back[rows, q_cols], weight, (((1,), (1,)), ((), ())), preferred_element_type=F32
-        ).astype(BF)
-    for copy in normed_parts:
-        copy.wait()
-    weight_terms(q_cols, q_terms)
-    run_bulk((q_sum,), ('start', 'direct'))
     second = [[], []]
     for s in (0, 1):
         for k in range(3):
@@ -1485,7 +1441,50 @@
                     first_device(here, s, by),
                 )
             )
-    run_bulk((q_sum,), ('relay',))
+    def turn_back(values, tokens, scale):
+        for g in range(GROUP):
+            turned = rope(values.at[:, head_cols(g)], 0, cosine[:, tokens], -sine[:, tokens])
+            for i, value in enumerate(turned):
+                at = g * HD + i * (HD // 2)
+                columns[at : at + HD // 2, tokens] = value * scale
+
+    turn_back(sums.at[0], slice(0, HALF), HD ** (-0.5))
+    wires.landed(back_at, across)
+    turn_back(across, slice(HALF, LINE), 1.0)
+
+    def take_rows(cols):
+        for r in range(4):
+            rows = slice(r * ROWS, (r + 1) * ROWS)
+            rows_back[rows, cols] = columns[cols, rows].T.astype(BF)
+
+    def weight_terms(cols, result):
+        back_part = rows_back[:, cols]
+        for n, half in enumerate((part_own, output_own)):
+
+            def body(i, carry):
+                at = pl.ds(pl.multiple_of(i * 256, 256), 256)
+                value = lax.dot_general(
+                    half[:, at], back_part, (((0,), (0,)), ((), ())), preferred_element_type=F32
+                )
+                result[n, i] = value.astype(BF).reshape(result.shape[2:])
+                return carry
+
+            lax.fori_loop(0, 4, body, 0)
+
+    q_cols, kv_cols = slice(0, GROUP * HD), slice(GROUP * HD, (GROUP + 2) * HD)
+    take_rows(q_cols)
+    own_parts[3].wait()
+    wires.settle(relayed)
+    weight = q_terms[...].reshape(D, GROUP * HD)
+    for r in range(4):
+        rows = slice(r * ROWS, (r + 1) * ROWS)
+        middle_all[rows, :] = lax.dot_general(
+            rows_back[rows, q_cols], weight, (((1,), (1,)), ((), ())), preferred_element_type=F32
+        ).astype(BF)
+    for copy in normed_parts:
+        copy.wait()
+    weight_terms(q_cols, q_terms)
+    run_bulk((q_sum,), ('start', 'direct'))
     for s in (0, 1):
         tokens = slice(s * HALF, (s + 1) * HALF)
         value = key_sums[s, first_at(here, s)].astype(F32)
@@ -1498,6 +1497,8 @@
             at = GROUP * HD + i * (HD // 2)
             columns[at : at + HD // 2, tokens] = value
         columns[(GROUP + 1) * HD :, tokens] = pair_columns[HD:]
+
+    run_bulk((q_sum,), ('relay',))
 
     take_rows(kv_cols)
     own_parts[4].wait()
@@ -1684,7 +1685,7 @@
     )(*operands)
 
 
-CHUNK = 256
+CHUNK = 512
 
 
 def feed_kernel(

time: 364 us -> 360 us (0.989)
  Pallas kernels: 341 us -> 336 us
where the time goes in v6:
time: 360 us; the launch traced here: 356 us
  Pallas kernels  336 us (93%)
  other arithmetic  12.8 us (4%)
  local copies, waits for them, and re-layouts  4.24 us (1%)
    pallas_call x1, Pallas kernels, call_backward(): pl.pallas_call(backward_kernel, out_shape=tuple((jax.ShapeDtypeStruct(sha...  171 us
    pallas_call x1, Pallas kernels, call_forward(): pl.pallas_call(forward_kernel, out_shape=tuple((jax.ShapeDtypeStruct(shap...  135 us
    pallas_call x1, Pallas kernels, call_feed(): pl.pallas_call(feed_kernel, out_shape=(jax.ShapeDtypeStruct((LINE, D), BF...  30.4 us
    sub x5, other arithmetic, adam(): weight - rate * (unbiased / divisor + decay * weight)  12.1 us

profile of v6, /device:TPU:1, one launch (start us, length us, event | category | flops | bytes accessed | tf_op | source)
XLA Modules:
  0.0 356.2 jit_solution(9548696924479834859)
XLA Ops:
  0.7 1.3 jit_solution_.3.inverse
  2.0 135.0 %forward.1 = (f32[32,512]{1,0:T(8,128)}, f32[32,512]{1,0:T(8,128)}, f32[128,128]{1,0:T(8,128)}, bf16[512,2048]{1,0:T(8,128)(2,1)}, bf16[2,4,4,2,32,384]{5,4,3,2,...) custom-call(s32[4]{0:T(128)} %lengths.3, ...), custom_call_target="tpu_custom_call" | custom-call | tf_op jit(solution)/shard_map/forward/pallas_call | solution.py:1156
  137.0 30.4 %feed_forward.1 = (bf16[512,2048]{1,0:T(8,128)(2,1)}, bf16[512,2048]{1,0:T(8,128)(2,1)}, bf16[2048,1024]{1,0:T(8,128)(2,1)}, bf16[2048,1024]{1,0:T(8,128)(2,1)}, bf16[1024,2048]{1,0:T(8,128)(2,1)}) custom-call(bf16[512,2048]{1,0:T(8,128)(2,1)} %get-tuple-element.50.normed_two, bf16[512,2048]{1,0:T(8,128)(2,1)} %get-tuple-element.51.cotangent, ...), custom_call_target="tpu_custom_call" | custom-call | tf_op jit(solution)/shard_map/feed_forward/pallas_call | solution.py:1737
  167.4 0.0 copy-start.15
  167.4 0.0 copy-start.16
  167.5 0.0 copy-start.17
  167.5 0.0 copy-start.9
  167.5 0.0 copy-start.13
  167.5 0.0 copy-start.14
  167.5 0.0 copy-start.5
  167.5 0.0 copy-start.11
  167.5 0.0 copy-start.12
  167.5 170.8 %backward.1 = (f32[128,1024]{1,0:T(8,128)}, bf16[128,1024]{1,0:T(8,128)(2,1)}, f32[32,4,384]{2,1,0:T(4,128)}, f32[32,2,4096]{2,1,0:T(2,128)}, f32[128,1024]{1,0:...) custom-call(s32[4]{0:T(128)} %lengths.3, f32[32,512]{1,0:T(8,128)} %get-tuple-element.48.cosine, ...), custom_call_target="tpu_custom_call" | custom-call | tf_op jit(solution)/shard_map/backward/pallas_call | solution.py:1631
  338.4 0.0 copy-start.1
  338.4 0.0 copy-start.7
  338.4 0.0 copy-start.8
  338.4 1.3 slice.6
  340.4 0.7 slice_multiply_fusion
  341.2 0.0 copy-done.15
  341.2 0.0 copy-done.16
  341.2 0.0 copy-done.17
  341.2 0.6 multiply_subtract_fusion.4
  341.8 0.0 copy-done.9
  341.8 0.0 copy-done.13
  341.8 0.0 copy-done.14
  341.8 1.7 multiply_subtract_fusion.3
  343.5 0.0 copy-done.5
  343.5 0.0 copy-done.11
  343.5 0.0 copy-done.12
  343.6 0.0 copy-start.4
  343.6 2.1 multiply_subtract_fusion.2
  345.7 0.0 copy-start
  345.7 0.0 copy-start.2
  345.7 0.0 copy-start.3
  345.7 0.0 copy-done.1
  345.7 0.0 copy-done.7
  345.7 0.0 copy-done.8
  345.7 2.6 multiply_subtract_fusion.1
  348.3 0.0 copy-done.4
  348.3 0.0 copy-done
  348.3 0.0 copy-done.2
  348.3 0.0 copy-done.3
  348.3 0.0 copy-start.10
  348.3 0.0 copy-start.6
  348.4 5.0 %multiply_subtract_fusion = (f32[32,2,4096]{2,1,0:T(2,128)}, f32[32,2,4096]{2,1,0:T(2,128)}, f32[32,2,4096]{2,1,0:T(2,128)}) fusion(f32[32,2,4096]{2,1,0:T(2,128)S(1)} %copy-done, f32[32,2,4096]{2,1,0:T(2,128)S(1)} %copy-done.4, f32[]{:T(128)S(6)} %div.78, f32[32,2,4096]{2,1,0:T(2,128)S(1)} %copy-done.2, f32[32,2,4096]{2,1,0:T(2,128)S(1)} %copy-done.3), kind=kLoop, calls=%fused_computation.2 | loop fusion | flops 4194304 | bytes 7340036 | tf_op jit(solution)/shard_map/sub | solution.py:1781
  353.4 0.0 copy-done.10
  353.4 0.7 copy.39
  354.1 0.0 copy-done.6
  354.1 0.8 copy.40
  (1 shorter events, 0.0 us)
Async XLA Ops:
  167.4 173.7 %copy-start.15 = (f32[2,1024]{1,0:T(2,128)S(1)}, f32[2,1024]{1,0:T(2,128)}, u32[]{:S(2)}) copy-start(f32[2,1024]{1,0:T(2,128)} %gains.3) | copy-start | bytes 24580
  167.4 173.7 %copy-start.16 = (f32[2,1024]{1,0:T(2,128)S(1)}, f32[2,1024]{1,0:T(2,128)}, u32[]{:S(2)}) copy-start(f32[2,1024]{1,0:T(2,128)} %param.34) | copy-start | bytes 24580
  167.5 173.7 %copy-start.17 = (f32[2,1024]{1,0:T(2,128)S(1)}, f32[2,1024]{1,0:T(2,128)}, u32[]{:S(2)}) copy-start(f32[2,1024]{1,0:T(2,128)} %param.35) | copy-start | bytes 24580
  167.5 174.4 %copy-start.9 = (f32[32,1024]{1,0:T(8,128)S(1)}, f32[32,1024]{1,0:T(8,128)}, u32[]{:S(2)}) copy-start(f32[32,1024]{1,0:T(8,128)} %out_weight.1) | copy-start | bytes 393220
  167.5 174.3 %copy-start.13 = (f32[32,1024]{1,0:T(8,128)S(1)}, f32[32,1024]{1,0:T(8,128)}, u32[]{:S(2)}) copy-start(f32[32,1024]{1,0:T(8,128)} %param.28) | copy-start | bytes 393220
  167.5 174.3 %copy-start.14 = (f32[32,1024]{1,0:T(8,128)S(1)}, f32[32,1024]{1,0:T(8,128)}, u32[]{:S(2)}) copy-start(f32[32,1024]{1,0:T(8,128)} %param.29) | copy-start | bytes 393220
  167.5 176.0 %copy-start.5 = (f32[32,4,384]{2,1,0:T(4,128)S(1)}, f32[32,4,384]{2,1,0:T(4,128)}, u32[]{:S(2)}) copy-start(f32[32,4,384]{2,1,0:T(4,128)} %qkv_weight.1) | copy-start | bytes 589828
  167.5 176.0 %copy-start.11 = (f32[32,4,384]{2,1,0:T(4,128)S(1)}, f32[32,4,384]{2,1,0:T(4,128)}, u32[]{:S(2)}) copy-start(f32[32,4,384]{2,1,0:T(4,128)} %param.22) | copy-start | bytes 589828
  167.5 176.0 %copy-start.12 = (f32[32,4,384]{2,1,0:T(4,128)S(1)}, f32[32,4,384]{2,1,0:T(4,128)}, u32[]{:S(2)}) copy-start(f32[32,4,384]{2,1,0:T(4,128)} %param.23) | copy-start | bytes 589828
  338.4 7.3 %copy-start.1 = (f32[128,1024]{1,0:T(8,128)S(1)}, f32[128,1024]{1,0:T(8,128)}, u32[]{:S(2)}) copy-start(f32[128,1024]{1,0:T(8,128)} %down_weight.1) | copy-start | bytes 1572868
  338.4 7.3 %copy-start.7 = (f32[128,1024]{1,0:T(8,128)S(1)}, f32[128,1024]{1,0:T(8,128)}, u32[]{:S(2)}) copy-start(f32[128,1024]{1,0:T(8,128)} %param.31) | copy-start | bytes 1572868
  338.4 7.3 %copy-start.8 = (f32[128,1024]{1,0:T(8,128)S(1)}, f32[128,1024]{1,0:T(8,128)}, u32[]{:S(2)}) copy-start(f32[128,1024]{1,0:T(8,128)} %param.32) | copy-start | bytes 1572868
  343.6 4.8 %copy-start.4 = (f32[32,2,4096]{2,1,0:T(2,128)S(1)}, f32[32,2,4096]{2,1,0:T(2,128)}, u32[]{:S(2)}) copy-start(f32[32,2,4096]{2,1,0:T(2,128)} %get-tuple-element.75) | copy-start | bytes 3145732
  345.7 2.6 copy-start
  345.7 2.6 copy-start.2
  345.7 2.6 copy-start.3
  348.3 5.0 %copy-start.10 = (bf16[128,1024]{1,0:T(8,128)(2,1)S(1)}, bf16[128,1024]{1,0:T(8,128)(2,1)}, u32[]{:S(2)}) copy-start(bf16[128,1024]{1,0:T(8,128)(2,1)} %get-tuple-element.111) | copy-start | bytes 786436
  348.3 5.7 %copy-start.6 = (f32[128,1024]{1,0:T(8,128)S(1)}, f32[128,1024]{1,0:T(8,128)}, u32[]{:S(2)}) copy-start(f32[128,1024]{1,0:T(8,128)} %get-tuple-element.112) | copy-start | bytes 1572868

commit v7 on v6

--- a/solution.py
+++ b/solution.py
@@ -1291,9 +1291,9 @@
     grads[:, :HD, :] = jnp.zeros((2, HD, GROUP * HALF), BF)
     terms[...] = jnp.zeros(terms.shape, F32)
     sums[...] = jnp.zeros(sums.shape, F32)
+    relayed = gather_relay(wires, sends, middle_all, here)
     in_turn(c, bulk, True)(*('middle',))
     in_turn(c, bulk, False)(*('start', 'direct'))
-    relayed = gather_relay(wires, sends, middle_all, here)
     kept[0].wait()
 
     own_parts[2].wait()
@@ -1331,7 +1331,6 @@
 
     lax.fori_loop(0, D // HALF, out_columns, 0)
     out_sum.start()
-    in_turn(c, bulk, False)(*('relay',))
     output_numbers = fold_sends(wires, output_part, output_fold[0], here)
 
     ends = ends_of(lengths)
@@ -1376,6 +1375,7 @@
         prepare(1)
 
     tour.run(step, between, 0, 4)
+    in_turn(c, bulk, False)(*('relay',))
     tour.run(step, between, 4, 8)
     own_parts[1].wait()
     output_moves = fold_moves(
@@ -1394,8 +1394,8 @@
         copy.start()
     out_sum.deal()
     in_turn(c, bulk, True)(*('finish',))
+    tour.run(step, between, 20, 26)
     in_turn(c, bulk, False)(*('middle',))
-    tour.run(step, between, 20, 26)
     tour.run(step, between, 26, 33)
 
     for s in (0, 1):

time: 360 us -> 361 us (level)
  no operation moved by 1% of the time
where the time goes in v7:
time: 361 us; the launch traced here: 358 us
  Pallas kernels  338 us (94%)
  other arithmetic  12.8 us (4%)
  local copies, waits for them, and re-layouts  4.24 us (1%)
    pallas_call x1, Pallas kernels, call_backward(): pl.pallas_call(backward_kernel, out_shape=tuple((jax.ShapeDtypeStruct(sha...  172 us
    pallas_call x1, Pallas kernels, call_forward(): pl.pallas_call(forward_kernel, out_shape=tuple((jax.ShapeDtypeStruct(shap...  135 us
    pallas_call x1, Pallas kernels, call_feed(): pl.pallas_call(feed_kernel, out_shape=(jax.ShapeDtypeStruct((LINE, D), BF...  30.4 us
    sub x5, other arithmetic, adam(): weight - rate * (unbiased / divisor + decay * weight)  12.1 us

profile of v7, /device:TPU:1, one launch (start us, length us, event | category | flops | bytes accessed | tf_op | source)
XLA Modules:
  0.0 357.7 jit_solution(16276738708698553844)
XLA Ops:
  0.7 1.3 jit_solution_.3.inverse
  2.0 135.0 %forward.1 = (f32[32,512]{1,0:T(8,128)}, f32[32,512]{1,0:T(8,128)}, f32[128,128]{1,0:T(8,128)}, bf16[512,2048]{1,0:T(8,128)(2,1)}, bf16[2,4,4,2,32,384]{5,4,3,2,...) custom-call(s32[4]{0:T(128)} %lengths.3, ...), custom_call_target="tpu_custom_call" | custom-call | tf_op jit(solution)/shard_map/forward/pallas_call | solution.py:1156
  137.0 30.4 %feed_forward.1 = (bf16[512,2048]{1,0:T(8,128)(2,1)}, bf16[512,2048]{1,0:T(8,128)(2,1)}, bf16[2048,1024]{1,0:T(8,128)(2,1)}, bf16[2048,1024]{1,0:T(8,128)(2,1)}, bf16[1024,2048]{1,0:T(8,128)(2,1)}) custom-call(bf16[512,2048]{1,0:T(8,128)(2,1)} %get-tuple-element.50.normed_two, bf16[512,2048]{1,0:T(8,128)(2,1)} %get-tuple-element.51.cotangent, ...), custom_call_target="tpu_custom_call" | custom-call | tf_op jit(solution)/shard_map/feed_forward/pallas_call | solution.py:1737
  167.4 0.0 copy-start.15
  167.4 0.0 copy-start.16
  167.5 0.0 copy-start.17
  167.5 0.0 copy-start.9
  167.5 0.0 copy-start.13
  167.5 0.0 copy-start.14
  167.5 0.0 copy-start.5
  167.5 0.0 copy-start.11
  167.5 0.0 copy-start.12
  167.5 172.3 %backward.1 = (f32[128,1024]{1,0:T(8,128)}, bf16[128,1024]{1,0:T(8,128)(2,1)}, f32[32,4,384]{2,1,0:T(4,128)}, f32[32,2,4096]{2,1,0:T(2,128)}, f32[128,1024]{1,0:...) custom-call(s32[4]{0:T(128)} %lengths.3, f32[32,512]{1,0:T(8,128)} %get-tuple-element.48.cosine, ...), custom_call_target="tpu_custom_call" | custom-call | tf_op jit(solution)/shard_map/backward/pallas_call | solution.py:1631
  339.8 0.0 copy-start.1
  339.8 0.0 copy-start.7
  339.8 0.0 copy-start.8
  339.8 1.3 slice.6
  341.9 0.7 slice_multiply_fusion
  342.6 0.0 copy-done.15
  342.6 0.0 copy-done.16
  342.6 0.0 copy-done.17
  342.6 0.6 multiply_subtract_fusion.4
  343.3 0.0 copy-done.9
  343.3 0.0 copy-done.13
  343.3 0.0 copy-done.14
  343.3 1.7 multiply_subtract_fusion.3
  345.0 0.0 copy-done.5
  345.0 0.0 copy-done.11
  345.0 0.0 copy-done.12
  345.0 0.0 copy-start.4
  345.0 2.1 multiply_subtract_fusion.2
  347.1 0.0 copy-start
  347.1 0.0 copy-start.2
  347.1 0.0 copy-start.3
  347.1 0.0 copy-done.1
  347.1 0.0 copy-done.7
  347.1 0.0 copy-done.8
  347.1 2.6 multiply_subtract_fusion.1
  349.7 0.0 copy-done.4
  349.7 0.0 copy-done
  349.7 0.0 copy-done.2
  349.8 0.0 copy-done.3
  349.8 0.0 copy-start.10
  349.8 0.0 copy-start.6
  349.8 5.0 %multiply_subtract_fusion = (f32[32,2,4096]{2,1,0:T(2,128)}, f32[32,2,4096]{2,1,0:T(2,128)}, f32[32,2,4096]{2,1,0:T(2,128)}) fusion(f32[32,2,4096]{2,1,0:T(2,128)S(1)} %copy-done, f32[32,2,4096]{2,1,0:T(2,128)S(1)} %copy-done.4, f32[]{:T(128)S(6)} %div.78, f32[32,2,4096]{2,1,0:T(2,128)S(1)} %copy-done.2, f32[32,2,4096]{2,1,0:T(2,128)S(1)} %copy-done.3), kind=kLoop, calls=%fused_computation.2 | loop fusion | flops 4194304 | bytes 7340036 | tf_op jit(solution)/shard_map/sub | solution.py:1781
  354.8 0.0 copy-done.10
  354.8 0.7 copy.39
  355.5 0.0 copy-done.6
  355.5 0.8 copy.40
  (1 shorter events, 0.0 us)
Async XLA Ops:
  167.4 175.2 %copy-start.15 = (f32[2,1024]{1,0:T(2,128)S(1)}, f32[2,1024]{1,0:T(2,128)}, u32[]{:S(2)}) copy-start(f32[2,1024]{1,0:T(2,128)} %gains.3) | copy-start | bytes 24580
  167.4 175.2 %copy-start.16 = (f32[2,1024]{1,0:T(2,128)S(1)}, f32[2,1024]{1,0:T(2,128)}, u32[]{:S(2)}) copy-start(f32[2,1024]{1,0:T(2,128)} %param.34) | copy-start | bytes 24580
  167.5 175.2 %copy-start.17 = (f32[2,1024]{1,0:T(2,128)S(1)}, f32[2,1024]{1,0:T(2,128)}, u32[]{:S(2)}) copy-start(f32[2,1024]{1,0:T(2,128)} %param.35) | copy-start | bytes 24580
  167.5 175.8 %copy-start.9 = (f32[32,1024]{1,0:T(8,128)S(1)}, f32[32,1024]{1,0:T(8,128)}, u32[]{:S(2)}) copy-start(f32[32,1024]{1,0:T(8,128)} %out_weight.1) | copy-start | bytes 393220
  167.5 175.8 %copy-start.13 = (f32[32,1024]{1,0:T(8,128)S(1)}, f32[32,1024]{1,0:T(8,128)}, u32[]{:S(2)}) copy-start(f32[32,1024]{1,0:T(8,128)} %param.28) | copy-start | bytes 393220
  167.5 175.8 %copy-start.14 = (f32[32,1024]{1,0:T(8,128)S(1)}, f32[32,1024]{1,0:T(8,128)}, u32[]{:S(2)}) copy-start(f32[32,1024]{1,0:T(8,128)} %param.29) | copy-start | bytes 393220
  167.5 177.5 %copy-start.5 = (f32[32,4,384]{2,1,0:T(4,128)S(1)}, f32[32,4,384]{2,1,0:T(4,128)}, u32[]{:S(2)}) copy-start(f32[32,4,384]{2,1,0:T(4,128)} %qkv_weight.1) | copy-start | bytes 589828
  167.5 177.5 %copy-start.11 = (f32[32,4,384]{2,1,0:T(4,128)S(1)}, f32[32,4,384]{2,1,0:T(4,128)}, u32[]{:S(2)}) copy-start(f32[32,4,384]{2,1,0:T(4,128)} %param.22) | copy-start | bytes 589828
  167.5 177.5 %copy-start.12 = (f32[32,4,384]{2,1,0:T(4,128)S(1)}, f32[32,4,384]{2,1,0:T(4,128)}, u32[]{:S(2)}) copy-start(f32[32,4,384]{2,1,0:T(4,128)} %param.23) | copy-start | bytes 589828
  339.8 7.3 %copy-start.1 = (f32[128,1024]{1,0:T(8,128)S(1)}, f32[128,1024]{1,0:T(8,128)}, u32[]{:S(2)}) copy-start(f32[128,1024]{1,0:T(8,128)} %down_weight.1) | copy-start | bytes 1572868
  339.8 7.3 %copy-start.7 = (f32[128,1024]{1,0:T(8,128)S(1)}, f32[128,1024]{1,0:T(8,128)}, u32[]{:S(2)}) copy-start(f32[128,1024]{1,0:T(8,128)} %param.31) | copy-start | bytes 1572868
  339.8 7.3 %copy-start.8 = (f32[128,1024]{1,0:T(8,128)S(1)}, f32[128,1024]{1,0:T(8,128)}, u32[]{:S(2)}) copy-start(f32[128,1024]{1,0:T(8,128)} %param.32) | copy-start | bytes 1572868
  345.0 4.8 %copy-start.4 = (f32[32,2,4096]{2,1,0:T(2,128)S(1)}, f32[32,2,4096]{2,1,0:T(2,128)}, u32[]{:S(2)}) copy-start(f32[32,2,4096]{2,1,0:T(2,128)} %get-tuple-element.75) | copy-start | bytes 3145732
  347.1 2.6 copy-start
  347.1 2.6 copy-start.2
  347.1 2.6 copy-start.3
  349.8 5.0 %copy-start.10 = (bf16[128,1024]{1,0:T(8,128)(2,1)S(1)}, bf16[128,1024]{1,0:T(8,128)(2,1)}, u32[]{:S(2)}) copy-start(bf16[128,1024]{1,0:T(8,128)(2,1)} %get-tuple-element.111) | copy-start | bytes 786436
  349.8 5.7 %copy-start.6 = (f32[128,1024]{1,0:T(8,128)S(1)}, f32[128,1024]{1,0:T(8,128)}, u32[]{:S(2)}) copy-start(f32[128,1024]{1,0:T(8,128)} %get-tuple-element.112) | copy-start | bytes 1572868
